TPU v7x, 256 devices: a whole 4x4x8 slice. The times are simulated.
256 devices in a mesh: blk: 16 (over y, x_hi, core), head: 8 (over z), rep: 2 (over x_lo).
Axes of the slice: x: 4 (x_hi: 2, x_lo: 2; x = x_hi * 2 + x_lo), y: 4, z: 8, core: 2. Of those that a mesh axis runs over, the one named last changes fastest.
Arguments:
- video_q: bfloat16 [32768, 3072], P(('blk', 'head', 'rep')), may hold values from -6 to 6
- video_k: bfloat16 [32768, 3072], P(('blk', 'head', 'rep')), may hold values from -6 to 6
- video_v: bfloat16 [32768, 3072], P(('blk', 'head', 'rep')), may hold values from -15 to 15
- text_q: bfloat16 [512, 3072], P(('blk', 'rep'), 'head'), may hold values from -6 to 6
- text_k: bfloat16 [512, 3072], P(('blk', 'rep'), 'head'), may hold values from -6 to 6
- text_v: bfloat16 [512, 3072], P(('blk', 'rep'), 'head'), may hold values from -15 to 15
- gain_video_q: float32 [128], replicated, may hold values from 1.5 to 2.4
- gain_video_k: float32 [128], replicated, may hold values from 1.5 to 2.4
- gain_text_q: float32 [128], replicated, may hold values from 1.5 to 2.4
- gain_text_k: float32 [128], replicated, may hold values from 1.5 to 2.4
- window: int32 [4], replicated, may hold values from 0 to 255
- grad_out_video: bfloat16 [512, 3072], P(('blk', 'rep'), 'head'), may hold values from -6 to 6
- grad_out_text: bfloat16 [512, 3072], P(('blk', 'rep'), 'head'), may hold values from -6 to 6
Outputs:
- out_video: bfloat16 [512, 3072], P(('blk', 'rep'), 'head')
- out_text: bfloat16 [512, 3072], P(('blk', 'rep'), 'head')
- grad_window_q: bfloat16 [512, 3072], P(('blk', 'rep'), 'head')
- grad_text_q: bfloat16 [512, 3072], P(('blk', 'rep'), 'head')
- grad_video_k: bfloat16 [32768, 3072], P(('blk', 'head', 'rep'))
- grad_video_v: bfloat16 [32768, 3072], P(('blk', 'head', 'rep'))
- grad_text_k: bfloat16 [512, 3072], P(('blk', 'rep'), 'head')
- grad_text_v: bfloat16 [512, 3072], P(('blk', 'rep'), 'head')
Inputs may be any that keep to these rules, and one draw needn't show every extreme that they name: `window`: each entry names a block of 128 video rows; entries may repeat.
All inputs are finite; a program needn't handle non-finite values.
Results may differ from a plain program's by a relative error of at most 0.018.
Values may be sent and summed in bfloat16 or wider, within the bound.
No kernel may reach another device: no remote copies, remote signals or barrier semaphores. Data moves between devices by JAX's collectives and lax.ppermute only.
A program may use at most 64 MiB of HBM per device.

v0:
```python
import math

import jax
import jax.numpy as jnp
from jax import lax
from jax.sharding import PartitionSpec as P

QBLK = 128
NWIN = 4


NORM_EPSILON = 1e-06


def broadcast(value, axis, source):
    kept = jnp.where(lax.axis_index(axis) == source, value, 0).astype(value.dtype)
    return lax.psum(kept, axis)


def head_norm(flat_rows, gain_vec):
    row_count = flat_rows.shape[0]
    per_head = flat_rows.reshape(row_count, -1, gain_vec.shape[0])
    inverse = lax.rsqrt(jnp.mean(per_head * per_head, axis=-1, keepdims=True) + NORM_EPSILON)
    return (per_head * inverse * gain_vec).reshape(row_count, -1)


def norm_input(raw_rows, gain_vec):
    return head_norm(raw_rows.astype(jnp.float32), gain_vec)


def norm_pullback(raw_rows, gain_vec, cotangent):
    _, pullback = jax.vjp(
        lambda inner_rows: head_norm(inner_rows, gain_vec), raw_rows.astype(jnp.float32)
    )
    return pullback(cotangent)[0]


def alternate(first_part, second_part, groups):
    feature_width = first_part.shape[1]
    joined = jnp.concatenate(
        (
            first_part.reshape(groups, -1, feature_width),
            second_part.reshape(groups, -1, feature_width),
        ),
        axis=1,
    )
    return joined.reshape(-1, feature_width)


def local(
    video_q,
    video_k,
    video_v,
    text_q,
    text_k,
    text_v,
    gain_video_q,
    gain_video_k,
    gain_text_q,
    gain_text_k,
    window,
    grad_out_video,
    grad_out_text,
):
    head_count = lax.axis_size("head")
    rep_size = lax.axis_size("rep")
    groups = lax.axis_size("blk") * rep_size
    head_dim = gain_video_q.shape[0]
    local_rows = video_q.shape[0]
    columns = video_q.shape[1] // head_count
    local_heads = columns // head_dim
    group_index = lax.axis_index("blk") * rep_size + lax.axis_index("rep")
    inv_root = 1.0 / math.sqrt(head_dim)
    picked = []
    moved_q, moved_k, moved_v = (
        lax.all_to_all(video_q, "head", split_axis=1, concat_axis=0, tiled=True),
        lax.all_to_all(video_k, "head", split_axis=1, concat_axis=0, tiled=True),
        lax.all_to_all(video_v, "head", split_axis=1, concat_axis=0, tiled=True),
    )
    for window_slot in range(NWIN):
        first_row = window[window_slot] * QBLK
        owner_index = first_row // local_rows
        offset = first_row % local_rows
        source = owner_index // (head_count * rep_size) * rep_size + owner_index % rep_size
        position = owner_index // rep_size % head_count * local_rows + offset
        block_rows = lax.dynamic_slice_in_dim(moved_q, position, QBLK, 0)
        picked.append(broadcast(block_rows, ("blk", "rep"), source))
    window_rows = jnp.concatenate(picked, axis=0)
    text_rows = lax.all_gather(text_q, ("blk", "rep"), axis=0, tiled=True)
    queries = alternate(
        norm_input(window_rows, gain_video_q).astype(jnp.bfloat16),
        norm_input(text_rows, gain_text_q).astype(jnp.bfloat16),
        groups,
    )
    normed_keys = jnp.concatenate(
        (norm_input(moved_k, gain_video_k), norm_input(text_k, gain_text_k)), axis=0
    ).astype(jnp.bfloat16)
    values = jnp.concatenate((moved_v, text_v), axis=0)
    total_rows = queries.shape[0]
    block_size = 512
    block_count = total_rows // block_size
    key_heads = normed_keys.reshape(-1, local_heads, head_dim)
    value_heads = values.reshape(-1, local_heads, head_dim)
    query_blocks = queries.reshape(block_count, block_size, local_heads, head_dim)

    def weights_of(query_block):
        scores = (
            jnp.einsum("khd,qhd->khq", key_heads, query_block, preferred_element_type=jnp.float32)
            * inv_root
        )
        return jnp.exp(scores)

    def forward_block(query_block):
        weights = weights_of(query_block)
        numerator = jnp.einsum(
            "khq,khd->qhd",
            weights.astype(jnp.bfloat16),
            value_heads,
            preferred_element_type=jnp.float32,
        )
        return (numerator.reshape(block_size, columns), jnp.sum(weights, axis=0).T)

    numerator, denominator = lax.map(forward_block, query_blocks)
    numerator = numerator.reshape(total_rows, columns)
    denominator = denominator.reshape(total_rows, local_heads)
    own_rows = total_rows // groups
    own_cotangent = jnp.concatenate((grad_out_video, grad_out_text), axis=0)
    cotangent = lax.all_gather(own_cotangent, ("blk", "rep"), axis=0, tiled=True)
    numer_all, denom_all = lax.psum((numerator, denominator), ("blk", "rep"))
    outputs = (
        (numer_all.reshape(-1, local_heads, head_dim) / denom_all[:, :, None])
        .reshape(-1, columns)
        .astype(jnp.bfloat16)
    )
    product = cotangent.astype(jnp.float32) * outputs.astype(jnp.float32)
    delta_all = jnp.sum(product.reshape(-1, local_heads, head_dim), axis=-1)
    own_out = lax.dynamic_slice_in_dim(outputs, group_index * own_rows, own_rows, 0)
    cot_blocks = cotangent.reshape(block_count, block_size, local_heads, head_dim)
    denom_blocks = denom_all.reshape(block_count, block_size, local_heads)
    delta_blocks = delta_all.reshape(block_count, block_size, local_heads)

    def backward_block(carried, inputs):
        grad_keys, grad_values = carried
        query_block, cot_block, denom_block, delta_block = inputs
        probabilities = weights_of(query_block) / denom_block.T[None, :, :]
        grad_values = grad_values + jnp.einsum(
            "khq,qhd->khd",
            probabilities.astype(jnp.bfloat16),
            cot_block,
            preferred_element_type=jnp.float32,
        )
        dprobs = jnp.einsum(
            "khd,qhd->khq", value_heads, cot_block, preferred_element_type=jnp.float32
        )
        dscores = (probabilities * (dprobs - delta_block.T[None, :, :])).astype(jnp.bfloat16)
        grad_keys = grad_keys + jnp.einsum(
            "khq,qhd->khd", dscores, query_block, preferred_element_type=jnp.float32
        )
        grad_query = jnp.einsum(
            "khq,khd->qhd", dscores, key_heads, preferred_element_type=jnp.float32
        )
        return ((grad_keys, grad_values), grad_query.reshape(block_size, columns) * inv_root)

    empty_grads = jnp.zeros(key_heads.shape, jnp.float32)
    (grad_keys, grad_values), grad_queries = lax.scan(
        backward_block,
        (empty_grads, empty_grads),
        (query_blocks, cot_blocks, denom_blocks, delta_blocks),
    )
    own_grad = lax.psum_scatter(
        grad_queries.reshape(total_rows, columns), ("blk", "rep"), scatter_dimension=0, tiled=True
    )
    video_share = grad_out_video.shape[0]
    own_window = lax.dynamic_slice_in_dim(window_rows, group_index * video_share, video_share, 0)
    grad_window_q = norm_pullback(own_window, gain_video_q, own_grad[:video_share]).astype(
        jnp.bfloat16
    )
    grad_text_q = norm_pullback(text_q, gain_text_q, own_grad[video_share:]).astype(jnp.bfloat16)
    grad_keys = grad_keys.reshape(-1, columns) * inv_root
    grad_values = grad_values.reshape(-1, columns)
    video_keys = moved_k.shape[0]
    key_video = norm_pullback(moved_k, gain_video_k, grad_keys[:video_keys]).astype(jnp.bfloat16)
    key_text = norm_pullback(text_k, gain_text_k, grad_keys[video_keys:]).astype(jnp.bfloat16)
    value_video = grad_values[:video_keys].astype(jnp.bfloat16)
    value_text = grad_values[video_keys:].astype(jnp.bfloat16)
    grad_video_k, grad_video_v = (
        lax.all_to_all(key_video, "head", split_axis=0, concat_axis=1, tiled=True),
        lax.all_to_all(value_video, "head", split_axis=0, concat_axis=1, tiled=True),
    )
    return (
        own_out[:video_share],
        own_out[video_share:],
        grad_window_q,
        grad_text_q,
        grad_video_k,
        grad_video_v,
        key_text,
        value_text,
    )


def solution(mesh):
    return jax.shard_map(
        local,
        mesh=mesh,
        in_specs=(
            P(("blk", "head", "rep"), None),
            P(("blk", "head", "rep"), None),
            P(("blk", "head", "rep"), None),
            P(("blk", "rep"), "head"),
            P(("blk", "rep"), "head"),
            P(("blk", "rep"), "head"),
            P(),
            P(),
            P(),
            P(),
            P(),
            P(("blk", "rep"), "head"),
            P(("blk", "rep"), "head"),
        ),
        out_specs=(
            P(("blk", "rep"), "head"),
            P(("blk", "rep"), "head"),
            P(("blk", "rep"), "head"),
            P(("blk", "rep"), "head"),
            P(("blk", "head", "rep"), None),
            P(("blk", "head", "rep"), None),
            P(("blk", "rep"), "head"),
            P(("blk", "rep"), "head"),
        ),
        check_vma=False,
    )
```

profile of v0, /device:TPU:1, one launch (start us, length us, event | category | flops | bytes accessed | tf_op | source)
XLA Modules:
  0.0 672.3 jit_solution(8309458191765190212)
XLA Ops:
  7.2 2.3 copy.206
  9.5 9.1 %all-to-all-start.1 = ((bf16[128,8,384]{0,2,1:T(8,128)(2,1)}), bf16[128,8,384]{0,2,1:T(8,128)(2,1)S(1)}, u32[]{:S(2)}, u32[]{:S(2)}) async-start(bf16[128,8,384]{0,2,1:T(8,128)(2,1)} %bitcast.23), calls=%async_computation.1 | async-start | bytes 1572864 | tf_op jit(solution)/shard_map/all_to_all | solution.py:77
  23.7 65.6 %all_gather.6 = bf16[512,384]{1,0:T(8,128)(2,1)S(1)} all-gather(bf16[16,384]{1,0:T(8,128)(2,1)S(1)} %copy-done.14), channel_id=1, replica_groups=mesh['blk'=16,'head'=8,'rep'=2] {'blk','rep'}, dimensions={0}, use_global_device_ids=true | all-gather | bytes 405504 | tf_op jit(solution)/shard_map/all_gather | solution.py:89
  89.5 1.2 copy.210
  90.7 6.3 all-to-all-start.2
  100.2 1.0 copy.290
  101.5 15.9 %all-to-all-done.2 = bf16[128,8,384]{0,2,1:T(8,128)(2,1)S(1)} async-done(((bf16[128,8,384]{0,2,1:T(8,128)(2,1)}), bf16[128,8,384]{0,2,1:T(8,128)(2,1)S(1)}, u32[]{:S(2)}, u32[]{:S(2)}) %all-to-all-start.2) | async-done | bytes 786464 | tf_op jit(solution)/shard_map/all_to_all | solution.py:78
  117.4 4.2 all-to-all-start
  123.6 1.2 copy-done.2
  125.7 1.4 reshape.289
  127.1 1.9 copy.208
  129.0 2.1 multiply_reduce_fusion.1
  131.6 10.0 %all-to-all-done = bf16[128,8,384]{2,0,1:T(8,128)(2,1)} async-done(((bf16[128,8,384]{2,0,1:T(8,128)(2,1)}), bf16[128,8,384]{2,0,1:T(8,128)(2,1)}, u32[]{:S(2)}, u32[]{:S(2)}) %all-to-all-start) | async-done | bytes 786464 | tf_op jit(solution)/shard_map/all_to_all | solution.py:76
  141.6 1.9 dynamic-slice_select_fusion.3
  143.6 110.8 %all-reduce.6.cloned.1.call-done = (bf16[128,384]{1,0:T(8,128)(2,1)}, bf16[128,384]{1,0:T(8,128)(2,1)}, bf16[128,384]{1,0:T(8,128)(2,1)}, bf16[128,384]{1,0:T(8,128)(2,1)}) async-done(((bf16[128,384]{1,0:T(8,128)(2,1)}, bf16[128,384]{1,0:T(8,128)(2,1)}, bf16[128,384]{1,0:T(8,128)(2,1)}, bf16[128,384]{1,0:T(8,128)(2,1)}), (bf16[128,384]{1,0:T(8,128)(2,1)}, bf16[128,384]{1,0:T(8,128)(2,1)}, ...) | async-done | bytes 393232 | tf_op jit(solution)/shard_map/psum | solution.py:17
  254.5 1.1 copy.199
  255.5 1.5 constant_dynamic-update-slice_fusion.4
  257.1 1.0 copy.202
  258.1 1.0 copy.201
  259.1 1.0 copy.200
  263.4 1.2 fusion.32
  264.9 1.0 copy.213
  265.9 38.4 %while.27 = (s32[]{:T(128)}, f32[2,512,384]{1,0,2:T(2,128)}, f32[2,512,3]{1,2,0:T(4,128)}, bf16[2,512,3,128]{3,1,2,0:T(8,128)(2,1)}, bf16[1040,3,128]{2,0,1:T(8,...) while((s32[]{:T(128)}, f32[2,512,384]{1,0,2:T(2,128)}, ...), condition=%wide.region_10.11_spmd, body=%wide.region_8.10_spmd.sunk | while | flops 822680064 | bytes 12333161 | solution.py:123
  265.9 2.2 bitcast_reduce_fusion.2
  270.3 14.8 %dynamic_update_slice.18 = f32[2,512,384]{1,0,2:T(2,128)} dynamic-update-slice(f32[2,512,384]{1,0,2:T(2,128)} %get-tuple-element.448, f32[1,512,384]{1,0,2:T(1,128)S(1)} %copy.293, s32[]{:T(128)S(6)} %copy.308, s32[]{:T(128)} %constant.219.clone.1..sunk, s32[]{:T(128)} %constant.219.clone.1..sunk) | dynamic-update-slice | bytes 1572868 | tf_op jit(solution)/shard_map/while/body/jit(dynamic_update_index_in_dim)/dynamic_update_slice | solution.py:123
  285.1 2.2 bitcast_reduce_fusion.2
  289.5 14.8 %dynamic_update_slice.18 = f32[2,512,384]{1,0,2:T(2,128)} dynamic-update-slice(f32[2,512,384]{1,0,2:T(2,128)} %get-tuple-element.448, f32[1,512,384]{1,0,2:T(1,128)S(1)} %copy.293, s32[]{:T(128)S(6)} %copy.308, s32[]{:T(128)} %constant.219.clone.1..sunk, s32[]{:T(128)} %constant.219.clone.1..sunk) | dynamic-update-slice | bytes 1572868 | tf_op jit(solution)/shard_map/while/body/jit(dynamic_update_index_in_dim)/dynamic_update_slice | solution.py:123
  304.4 3.0 copy.268
  307.5 66.7 %all_gather.7 = bf16[1024,384]{1,0:T(8,128)(2,1)S(1)} all-gather(bf16[32,384]{1,0:T(8,128)(2,1)S(1)} %pad_maximum_fusion.3), channel_id=1, replica_groups=mesh['blk'=16,'head'=8,'rep'=2] {'blk','rep'}, dimensions={0}, use_global_device_ids=true | all-gather | bytes 811008 | tf_op jit(solution)/shard_map/all_gather | solution.py:128
  374.2 1.2 copy.217
  375.7 1.0 copy.219
  376.7 123.7 %psum.47 = f32[1024,3]{0,1:T(4,128)S(1)} all-reduce(f32[1024,3]{0,1:T(4,128)S(1)} %bitcast.275), channel_id=1, replica_groups=mesh['blk'=16,'head'=8,'rep'=2] {'blk','rep'}, use_global_device_ids=true, to_apply=%region_12.13 | all-reduce | flops 3072 | bytes 24576 | tf_op jit(solution)/shard_map/psum | solution.py:129
  500.4 2.9 convert_multiply_fusion
  503.3 26.0 %while.28 = (s32[]{:T(128)}, f32[1040,3,128]{2,0,1:T(8,128)}, f32[1040,3,128]{2,0,1:T(8,128)}, f32[2,512,384]{2,1,0:T(8,128)}, bf16[2,512,3,128]{3,1,2,0:T(8,128...) while((s32[]{:T(128)}, f32[1040,3,128]{2,0,1:T(8,128)}, ...), condition=%wide.region_15.16_spmd.clone, body=%wide.region_14.15_spmd.clone.sunk | while | flops 2056101888 | bytes 43081884 | solution.py:165
  503.4 2.0 exponential_divide_fusion.2
  505.4 3.2 fusion.91
  508.6 2.0 fusion.89
  511.4 3.2 fusion.90
  514.9 1.0 constant_dynamic-update-slice_fusion.6
  515.8 2.0 exponential_divide_fusion.2
  517.9 3.8 fusion.91
  521.6 2.0 fusion.89
  524.4 3.8 fusion.90
  528.4 0.9 constant_dynamic-update-slice_fusion.6
  529.4 1.5 convert.21
  530.9 1.0 copy-done.4
  532.4 1.0 copy.231
  533.4 6.7 %all-to-all-start.4 = ((bf16[8,128,384]{1,2,0:T(8,128)(2,1)}), bf16[8,128,384]{1,2,0:T(8,128)(2,1)}, u32[]{:S(2)}, u32[]{:S(2)}) async-start(bf16[8,128,384]{1,2,0:T(8,128)(2,1)} %copy.231), calls=%async_computation.5 | async-start | bytes 1572864 | tf_op jit(solution)/shard_map/all_to_all | solution.py:188
  540.2 1.7 copy.225
  541.8 1.9 copy.227
  543.7 1.7 broadcast_multiply_fusion
  545.6 1.6 multiply_reduce_fusion
  547.2 3.0 copy.223
  550.2 2.7 fusion.27
  552.9 2.3 copy.228
  555.2 5.4 all-to-all-done.4
  560.6 3.5 all-to-all-start.3
  564.9 1.1 constant_dynamic-slice_fusion.1
  567.5 1.3 copy_bitcast_fusion.1
  569.6 2.3 copy.240
  571.9 12.2 %all-to-all-done.3 = bf16[8,128,384]{2,1,0:T(8,128)(2,1)S(1)} async-done(((bf16[8,128,384]{2,1,0:T(8,128)(2,1)}), bf16[8,128,384]{2,1,0:T(8,128)(2,1)S(1)}, u32[]{:S(2)}, u32[]{:S(2)}) %all-to-all-start.3) | async-done | bytes 786464 | tf_op jit(solution)/shard_map/all_to_all | solution.py:187
  584.5 1.2 copy.239
  585.7 77.3 %reduce-scatter.2.cloned.1.call-done = f32[32,384]{1,0:T(8,128)} async-done(((f32[1024,384]{1,0:T(8,128)}), f32[32,384]{1,0:T(8,128)}) %reduce-scatter.2.cloned.1.call-update) | async-done | bytes 49168 | tf_op jit(solution)/shard_map/reduce_scatter | solution.py:170
  664.4 1.4 fusion.34
  (152 shorter events, 24.8 us)
Async XLA Ops:
  7.2 11.5 %copy-start.24 = (s32[4]{0:T(128)S(1)}, s32[4]{0:T(128)}, u32[]{:S(2)}) copy-start(s32[4]{0:T(128)} %param.27) | copy-start | bytes 52
  7.2 15.1 %copy-start.12 = (bf16[16,384]{1,0:T(8,128)(2,1)S(1)}, bf16[16,384]{1,0:T(8,128)(2,1)}, u32[]{:S(2)}) copy-start(bf16[16,384]{1,0:T(8,128)(2,1)} %param.21) | copy-start | bytes 36868
  7.2 15.8 %copy-start.21 = (bf16[16,384]{1,0:T(8,128)(2,1)S(1)}, bf16[16,384]{1,0:T(8,128)(2,1)}, u32[]{:S(2)}) copy-start(bf16[16,384]{1,0:T(8,128)(2,1)} %param.22) | copy-start | bytes 36868
  7.2 16.5 %copy-start.14 = (bf16[16,384]{1,0:T(8,128)(2,1)S(1)}, bf16[16,384]{1,0:T(8,128)(2,1)}, u32[]{:S(2)}) copy-start(bf16[16,384]{1,0:T(8,128)(2,1)} %param.20) | copy-start | bytes 36868
  9.5 80.0 %copy-start.6 = (bf16[128,3072]{1,0:T(8,128)(2,1)S(1)}, bf16[128,3072]{1,0:T(8,128)(2,1)}, u32[]{:S(2)}) copy-start(bf16[128,3072]{1,0:T(8,128)(2,1)} %param.19) | copy-start | bytes 2359300
  9.5 81.2 %all-to-all-start.1 = ((bf16[128,8,384]{0,2,1:T(8,128)(2,1)}), bf16[128,8,384]{0,2,1:T(8,128)(2,1)S(1)}, u32[]{:S(2)}, u32[]{:S(2)}) async-start(bf16[128,8,384]{0,2,1:T(8,128)(2,1)} %bitcast.23), calls=%async_computation.1 | async-start | bytes 1572864 | tf_op jit(solution)/shard_map/all_to_all | solution.py:77
  90.7 26.7 %all-to-all-start.2 = ((bf16[128,8,384]{0,2,1:T(8,128)(2,1)}), bf16[128,8,384]{0,2,1:T(8,128)(2,1)S(1)}, u32[]{:S(2)}, u32[]{:S(2)}) async-start(bf16[128,8,384]{0,2,1:T(8,128)(2,1)} %bitcast.26), calls=%async_computation.2 | async-start | bytes 1572864 | tf_op jit(solution)/shard_map/all_to_all | solution.py:78
  97.0 3.2 copy-start.7
  97.8 3.4 copy-start.13
  99.2 2.1 copy-start.27
  100.2 21.4 %copy-start.30 = (f32[128]{0:T(128)S(1)}, f32[128]{0:T(128)}, u32[]{:S(2)}) copy-start(f32[128]{0:T(128)} %param.23) | copy-start | bytes 1540
  101.3 20.9 %copy-start.18 = (f32[384]{0:T(512)}, f32[384]{0:T(512)S(1)}, u32[]{:S(2)}) copy-start(f32[384]{0:T(512)S(1)} %broadcast_bitcast_fusion.1) | copy-start | bytes 4612
  117.4 24.3 %all-to-all-start = ((bf16[128,8,384]{2,0,1:T(8,128)(2,1)}), bf16[128,8,384]{2,0,1:T(8,128)(2,1)}, u32[]{:S(2)}, u32[]{:S(2)}) async-start(bf16[128,8,384]{2,0,1:T(8,128)(2,1)} %bitcast.201), calls=%async_computation | async-start | bytes 1572864 | tf_op jit(solution)/shard_map/all_to_all | solution.py:76
  121.6 1.0 copy-start.8
  121.6 132.9 %all-reduce.6.cloned.1.call-start = ((), (), s32[]{:S(2)}) async-start(), calls=%async_computation.8 | async-start | bytes 786432 | tf_op jit(solution)/shard_map/psum | solution.py:17
  121.7 141.7 %copy-start.16 = (f32[384]{0:T(512)}, f32[384]{0:T(512)S(1)}, u32[]{:S(2)}) copy-start(f32[384]{0:T(512)S(1)} %broadcast_bitcast_fusion.3) | copy-start | bytes 4612
  123.6 1.2 copy-start.2
  127.1 4.1 copy-start.25
  129.0 2.7 copy-start
  143.5 356.8 %all-reduce.4.cloned.1.call-start = ((), (), s32[]{:S(2)}) async-start(), calls=%async_computation.6 | async-start | bytes 3145728 | tf_op jit(solution)/shard_map/psum | solution.py:129
  254.5 5.9 copy-start.11
  254.5 6.6 copy-start.10
  254.5 7.2 %copy-start.9 = (bf16[128,384]{1,0:T(8,128)(2,1)S(1)}, bf16[128,384]{1,0:T(8,128)(2,1)}, u32[]{:S(2)}) copy-start(bf16[128,384]{1,0:T(8,128)(2,1)} %get-tuple-element.299) | copy-start | bytes 294916
  263.4 1.2 copy-start.5
  304.4 3.1 copy-start.22
  304.4 3.1 copy-start.23
  307.4 355.5 %reduce-scatter.2.cloned.1.call-start = ((), (), s32[]{:S(2)}) async-start(), calls=%async_computation.7 | async-start | bytes 1622016 | tf_op jit(solution)/shard_map/reduce_scatter | solution.py:170
  375.4 1.3 copy-start.20
  530.9 1.0 copy-start.4
  532.4 7.8 %copy-start.3 = (f32[8,128,384]{1,2,0:T(8,128)S(1)}, f32[8,128,384]{1,2,0:T(8,128)}, u32[]{:S(2)}) copy-start(f32[8,128,384]{1,2,0:T(8,128)} %copy-done.2) | copy-start | bytes 4718596
  533.4 27.2 %all-to-all-start.4 = ((bf16[8,128,384]{1,2,0:T(8,128)(2,1)}), bf16[8,128,384]{1,2,0:T(8,128)(2,1)}, u32[]{:S(2)}, u32[]{:S(2)}) async-start(bf16[8,128,384]{1,2,0:T(8,128)(2,1)} %copy.231), calls=%async_computation.5 | async-start | bytes 1572864 | tf_op jit(solution)/shard_map/all_to_all | solution.py:188
  543.7 1.9 copy-start.1
  543.7 1.9 copy-start.26
  552.9 11.2 %copy-start.15 = (bf16[16,384]{1,0:T(8,128)(2,1)S(1)}, bf16[16,384]{1,0:T(8,128)(2,1)}, u32[]{:S(2)}) copy-start(bf16[16,384]{1,0:T(8,128)(2,1)} %param.20) | copy-start | bytes 36868
  552.9 14.5 %copy-start.28 = (f32[128]{0:T(128)S(1)}, f32[128]{0:T(128)}, u32[]{:S(2)}) copy-start(f32[128]{0:T(128)} %param.26) | copy-start | bytes 1540
  555.2 13.7 %copy-start.19 = (f32[384]{0:T(512)S(1)}, f32[384]{0:T(512)}, u32[]{:S(2)}) copy-start(f32[384]{0:T(512)} %copy-done.18) | copy-start | bytes 4612
  560.6 23.5 %all-to-all-start.3 = ((bf16[8,128,384]{2,1,0:T(8,128)(2,1)}), bf16[8,128,384]{2,1,0:T(8,128)(2,1)S(1)}, u32[]{:S(2)}, u32[]{:S(2)}) async-start(bf16[8,128,384]{2,1,0:T(8,128)(2,1)} %bitcast.40), calls=%async_computation.4 | async-start | bytes 1572864 | tf_op jit(solution)/shard_map/all_to_all | solution.py:187
  584.1 79.6 %copy-start.29 = (f32[128]{0:T(128)S(1)}, f32[128]{0:T(128)}, u32[]{:S(2)}) copy-start(f32[128]{0:T(128)} %param.25) | copy-start | bytes 1540
  584.1 79.8 %copy-start.31 = (f32[128]{0:T(128)S(1)}, f32[128]{0:T(128)}, u32[]{:S(2)}) copy-start(f32[128]{0:T(128)} %param.23) | copy-start | bytes 1540
  584.1 80.3 %copy-start.17 = (f32[384]{0:T(512)S(1)}, f32[384]{0:T(512)}, u32[]{:S(2)}) copy-start(f32[384]{0:T(512)} %copy-done.16) | copy-start | bytes 4612
Sparse Core Ops, SparseCore 0:
  143.7 110.7 all-reduce.5
  307.5 116.2 all-reduce.3
  529.5 133.3 reduce-scatter.1
where the time goes:
time: 677 us; the launch traced here: 672 us
  blocking collectives  256 us (38%)
  waiting for transfers between devices  232 us (34%)
  local copies, waits for them, and re-layouts  86.2 us (13%)
  starting transfers between devices  30.1 us (4%)
  matrix products  29.4 us (4%)
  other arithmetic  21.3 us (3%)
  between operations  17.5 us (3%)
    psum x1, blocking collectives, local(): numer_all, denom_all = lax.psum((numerator, denominator), ('blk', 'rep'))  124 us
    psum x1, waiting for transfers between devices, broadcast(): return lax.psum(kept, axis)  111 us
    reduce_scatter x1, waiting for transfers between devices, local(): lax.psum_scatter(grad_queries.reshape(total_rows, columns), ('blk', 'rep'...  77.3 us
    all_gather x1, blocking collectives, local(): lax.all_gather(own_cotangent, ('blk', 'rep'), axis=0, tiled=True)  66.7 us
    all_gather x1, blocking collectives, local(): text_rows = lax.all_gather(text_q, ('blk', 'rep'), axis=0, tiled=True)  65.6 us
    dynamic_update_slice x10, local copies, waits for them, and re-layouts, local(): numerator, denominator = lax.map(forward_block, query_blocks)  34.9 us
    unnamed x76, local copies, waits for them, and re-layouts  17.8 us
    all_to_all x1, waiting for transfers between devices, local(): lax.all_to_all(video_v, 'head', split_axis=1, concat_axis=0, tiled=True)  15.9 us
  transfers between devices with their start and end apart: 8, of which 6 were waited for; matrix products, arithmetic and copies ran while one was open for 7% of the time, Pallas kernels for 0%

commit v1 on v0

v1 whole, which is shorter than its diff:
```python
import math

import jax
import jax.numpy as jnp
from jax import lax
from jax.experimental import pallas as pl
from jax.experimental.pallas import tpu as pltpu
from jax.sharding import Mesh, PartitionSpec as P

NWIN = 4
HD = 128
EPS = 1e-06
INV_ROOT = 1.0 / math.sqrt(HD)
LOG2E = math.log2(math.e)
PLANE = ("y", "xh", "c", "xl")
CHIPS = ("y", "xh", "xl")
KEY_BLOCK = 256
NT = (((1,), (1,)), ((), ()))
NN = (((1,), (0,)), ((), ()))
TN = (((0,), (0,)), ((), ()))
F32 = jnp.float32
BF16 = jnp.bfloat16


def mm(a, b, dims):
    return lax.dot_general(a, b, dims, preferred_element_type=F32)


def inverse_rms(rows):
    return lax.rsqrt(jnp.mean(rows * rows, axis=-1, keepdims=True) + EPS)


def normed(raw, gain):
    rows = raw.astype(F32)
    return (rows * inverse_rms(rows) * gain).astype(BF16)


def pullback(raw, gain, cot):
    rows = raw.astype(F32)
    inverse = inverse_rms(rows)
    scaled = cot * gain
    along = jnp.mean(rows * scaled, axis=-1, keepdims=True)
    return inverse * (scaled - rows * (inverse * inverse * along))


def normed_queries(win_ref, text_ref, gains_ref):
    return jnp.concatenate(
        (normed(win_ref[...], gains_ref[0:1]), normed(text_ref[...], gains_ref[2:3])), axis=0
    )


def key_parts(k_ref, v_ref, tk_ref, tv_ref, gains_ref):
    parts = []
    for start in range(0, k_ref.shape[0], KEY_BLOCK):
        rows = slice(start, start + KEY_BLOCK)
        parts.append((k_ref[rows], v_ref[rows], gains_ref[1:2], rows))
    parts.append((tk_ref[...], tv_ref[...], gains_ref[3:4], None))
    return parts


def stats_kernel(win_ref, tq_ref, cot_ref, k_ref, v_ref, tk_ref, tv_ref, gains_ref, out_ref):
    queries = normed_queries(win_ref, tq_ref, gains_ref)
    cot = cot_ref[...]
    den = jnp.zeros((1, queries.shape[0]), F32)
    mixed = jnp.zeros((1, queries.shape[0]), F32)
    for raw_key, value, gain, _ in key_parts(k_ref, v_ref, tk_ref, tv_ref, gains_ref):
        key = normed(raw_key, gain)
        weights = jnp.exp2(mm(key, queries, NT) * (INV_ROOT * LOG2E))
        dprobs = mm(value, cot, NT)
        den += jnp.sum(weights, axis=0, keepdims=True)
        mixed += jnp.sum(weights * dprobs, axis=0, keepdims=True)
    out_ref[0, 0:1] = den
    out_ref[0, 1:2] = mixed


def grads_kernel(
    win_ref, tq_ref, cot_ref, k_ref, v_ref, tk_ref, tv_ref, gains_ref, stats_ref,
    rows_ref, dk_ref, dv_ref, dtk_ref, dtv_ref,
):
    queries = normed_queries(win_ref, tq_ref, gains_ref)
    cot = cot_ref[...]
    count = queries.shape[0]
    inv_den = 1.0 / stats_ref[0, 0:1]
    delta = stats_ref[0, 1:2] * inv_den
    out_t = jnp.zeros((HD, count), F32)
    dq_t = jnp.zeros((HD, count), F32)
    for raw_key, value, gain, rows in key_parts(k_ref, v_ref, tk_ref, tv_ref, gains_ref):
        key = normed(raw_key, gain)
        probs = jnp.exp2(mm(key, queries, NT) * (INV_ROOT * LOG2E)) * inv_den
        probs_16 = probs.astype(BF16)
        dvalue = mm(probs_16, cot, NN).astype(BF16)
        out_t += mm(value, probs_16, TN)
        dscores = (probs * (mm(value, cot, NT) - delta)).astype(BF16)
        dkey = pullback(raw_key, gain, mm(dscores, queries, NN) * INV_ROOT).astype(BF16)
        dq_t += mm(key, dscores, TN)
        if rows is None:
            dtk_ref[...] = dkey
            dtv_ref[...] = dvalue
        else:
            dk_ref[rows] = dkey
            dv_ref[rows] = dvalue
    half = count // 2
    outs = out_t.T.astype(BF16)
    dqs = (dq_t * INV_ROOT).T.astype(BF16)
    groups, part = rows_ref.shape[0], rows_ref.shape[1] // 4
    for place, block in enumerate((outs[:half], outs[half:], dqs[:half], dqs[half:])):
        rows_ref[:, place * part : (place + 1) * part] = block.reshape(groups, part, HD)


def column_spec(array):
    return pl.BlockSpec((array.shape[0], HD), lambda head: (0, head))


def whole_spec(array):
    return pl.BlockSpec(array.shape, lambda head: (0,) * array.ndim)


PARAMS = pltpu.CompilerParams(vmem_limit_bytes=48 * 1024 * 1024)


def attention_stats(operands, gains, heads):
    count = operands[2].shape[0]
    keys = operands[3].shape[0]
    return pl.pallas_call(
        stats_kernel,
        grid=(heads,),
        in_specs=[column_spec(a) for a in operands] + [whole_spec(gains)],
        out_specs=pl.BlockSpec((1, 2, count), lambda head: (head, 0, 0)),
        out_shape=jax.ShapeDtypeStruct((heads, 2, count), F32),
        compiler_params=PARAMS,
        cost_estimate=pl.CostEstimate(
            flops=4 * count * keys * heads * HD, bytes_accessed=6000000,
            transcendentals=count * keys * heads,
        ),
    )(*operands, gains)


def attention_grads(operands, gains, stats, heads, groups):
    count = operands[2].shape[0]
    keys = operands[3].shape[0]
    text = operands[5].shape[0]
    part = count // groups * 2
    width = heads * HD
    shapes = [
        jax.ShapeDtypeStruct((groups, part, width), BF16),
        jax.ShapeDtypeStruct((keys, width), BF16),
        jax.ShapeDtypeStruct((keys, width), BF16),
        jax.ShapeDtypeStruct((text, width), BF16),
        jax.ShapeDtypeStruct((text, width), BF16),
    ]
    return pl.pallas_call(
        grads_kernel,
        grid=(heads,),
        in_specs=[column_spec(a) for a in operands]
        + [whole_spec(gains), pl.BlockSpec((1, 2, count), lambda head: (head, 0, 0))],
        out_specs=[pl.BlockSpec((groups, part, HD), lambda head: (0, 0, head))]
        + [column_spec(s) for s in shapes[1:]],
        out_shape=shapes,
        compiler_params=PARAMS,
        cost_estimate=pl.CostEstimate(
            flops=12 * count * keys * heads * HD, bytes_accessed=9000000,
            transcendentals=count * keys * heads,
        ),
    )(*operands, gains, stats)


def swap(array, axes):
    return lax.all_to_all(array, axes, split_axis=0, concat_axis=0, tiled=True)


def split_heads(rows, groups):
    count = rows.shape[0]
    return rows.reshape(count, groups, -1).transpose(1, 0, 2)


def pick(array, index):
    return lax.dynamic_index_in_dim(array, index, 0, keepdims=False)


def local(
    video_q, video_k, video_v, text_q, text_k, text_v,
    gain_video_q, gain_video_k, gain_text_q, gain_text_k,
    window, grad_out_video, grad_out_text,
):
    z_size = lax.axis_size("z")
    rep_size = lax.axis_size("xl")
    groups = lax.axis_size(PLANE)
    own_rows, model = video_q.shape
    columns = model // z_size
    heads = columns // HD
    share = grad_out_video.shape[0]
    gains = jnp.stack((gain_video_q, gain_video_k, gain_text_q, gain_text_k))

    piece = own_rows // groups
    scattered = swap(video_q.reshape(groups, piece, model), PLANE)
    z_of = [window[s] // rep_size % z_size for s in range(NWIN)]
    plane_of = [
        window[s] // (z_size * rep_size) * rep_size + window[s] % rep_size for s in range(NWIN)
    ]
    picked = jnp.concatenate([pick(scattered, plane_of[s]) for s in range(NWIN)], axis=0)

    sent = jnp.concatenate(
        (
            split_heads(video_k, z_size),
            split_heads(video_v, z_size),
            split_heads(picked, z_size),
        ),
        axis=1,
    )
    moved = swap(sent, "z")
    moved_k = moved[:, :own_rows].reshape(-1, columns)
    moved_v = moved[:, own_rows : 2 * own_rows].reshape(-1, columns)
    moved_q = moved[:, 2 * own_rows :].reshape(z_size, NWIN, piece, columns)
    own_window = jnp.concatenate([pick(moved_q[:, s], z_of[s]) for s in range(NWIN)], axis=0)

    own = jnp.concatenate((own_window, text_q, grad_out_video, grad_out_text), axis=0)
    every = swap(jnp.broadcast_to(own[None], (groups,) + own.shape), PLANE)
    window_rows = (
        every[:, :share].reshape(groups, NWIN, piece, columns).transpose(1, 0, 2, 3)
    ).reshape(-1, columns)
    text_rows = every[:, share : 2 * share].reshape(-1, columns)
    cotangent = jnp.concatenate(
        (
            every[:, 2 * share : 3 * share].reshape(-1, columns),
            every[:, 3 * share :].reshape(-1, columns),
        ),
        axis=0,
    )
    operands = (window_rows, text_rows, cotangent, moved_k, moved_v, text_k, text_v)

    stats = attention_stats(operands, gains, heads)
    pair = lax.psum(stats, "c").reshape(-1, 128)
    chips = lax.axis_size(CHIPS)
    stats = jnp.sum(swap(jnp.broadcast_to(pair[None], (chips,) + pair.shape), CHIPS), axis=0)
    stats = stats.reshape(heads, 2, -1)

    rows, dkey, dvalue, key_text, value_text = attention_grads(
        operands, gains, stats, heads, groups
    )
    returned = swap(
        jnp.concatenate(
            (dkey.reshape(z_size, own_rows, columns), dvalue.reshape(z_size, own_rows, columns)),
            axis=1,
        ),
        "z",
    )
    grad_video_k = returned[:, :own_rows].transpose(1, 0, 2).reshape(own_rows, model)
    grad_video_v = returned[:, own_rows:].transpose(1, 0, 2).reshape(own_rows, model)

    total = jnp.sum(swap(rows, PLANE).astype(F32), axis=0)
    place = lax.axis_index(PLANE)
    own_raw = lax.dynamic_slice_in_dim(window_rows, place * share, share, 0)

    def query_grad(raw, gain, cot):
        shape = (raw.shape[0], heads, HD)
        return pullback(raw.reshape(shape), gain, cot.reshape(shape)).reshape(raw.shape)

    return (
        total[:share].astype(BF16),
        total[share : 2 * share].astype(BF16),
        query_grad(own_raw, gain_video_q, total[2 * share : 3 * share]).astype(BF16),
        query_grad(text_q, gain_text_q, total[3 * share :]).astype(BF16),
        grad_video_k,
        grad_video_v,
        key_text,
        value_text,
    )


def solution(mesh):
    fine = Mesh(mesh.devices.reshape(4, 2, 2, 8, 2), ("y", "xh", "c", "z", "xl"))
    tokens = P(("y", "xh", "c", "z", "xl"), None)
    text = P(PLANE, "z")
    return jax.shard_map(
        local,
        mesh=fine,
        in_specs=(tokens,) * 3 + (text,) * 3 + (P(),) * 5 + (text,) * 2,
        out_specs=(text,) * 4 + (tokens,) * 2 + (text,) * 2,
        check_vma=False,
    )
```

time: 677 us -> 226 us (0.33)
  blocking collectives: 256 us -> 18.8 us
  waiting for transfers between devices: 232 us -> 115 us
  local copies, waits for them, and re-layouts: 86.2 us -> 17.6 us
  matrix products: 29.4 us -> 0 us
  Pallas kernels: 0 us -> 18.2 us
  other arithmetic: 21.3 us -> 6.57 us
    all_gather x2 -> x0, blocking collectives: 132 us -> none  [the longest x1 66.7 us: local(): lax.all_gather(own_cotangent, ('blk', 'rep'), axis=0, tiled=True)]
    psum x1, blocking collectives: 124 us -> 5.48 us  [local(): pair = lax.psum(stats, 'c').reshape(-1, 128)]
    psum x2 -> x0, waiting for transfers between devices: 111 us -> none  [the longest x1 111 us: broadcast(): return lax.psum(kept, axis)]
    reduce_scatter x1 -> x0, waiting for transfers between devices: 77.3 us -> none  [local(): lax.psum_scatter(grad_queries.reshape(total_rows, columns), ('blk', 'rep'...]
    all_to_all x5, waiting for transfers between devices: 43.5 us -> 115 us  [swap(): return lax.all_to_all(array, axes, split_axis=0, concat_axis=0, tiled=True)]
    dynamic_update_slice x10 -> x0, local copies, waits for them, and re-layouts: 34.9 us -> none  [local(): numerator, denominator = lax.map(forward_block, query_blocks)]
    dot_general x14 -> x0, matrix products: 29.4 us -> none  [the longest x4 8.43 us: weights_of(): jnp.einsum('khd,qhd->khq', key_heads, query_block, preferred_element_type...]
    pallas_call x0 -> x2, Pallas kernels: none -> 18.2 us  [the longest x1 12.8 us: attention_grads(): pl.pallas_call(grads_kernel, grid=(heads,), in_specs=[column_spec(a) for...]
  transfers between devices with their start and end apart: 8 -> 5, of which waited for: 6 -> 5; matrix products, arithmetic and copies ran while one was open for 7% -> 4% of each run, Pallas kernels for 0% -> 0%
where the time goes in v1:
time: 226 us; the launch traced here: 224 us
  waiting for transfers between devices  115 us (51%)
  starting transfers between devices  35.9 us (16%)
  blocking collectives  18.8 us (8%)
  Pallas kernels  18.2 us (8%)
  local copies, waits for them, and re-layouts  17.6 us (8%)
  between operations  11.6 us (5%)
  other arithmetic  6.57 us (3%)
    all_to_all x5, waiting for transfers between devices, swap(): return lax.all_to_all(array, axes, split_axis=0, concat_axis=0, tiled=True)  115 us
    all_to_all x5, starting transfers between devices, swap(): return lax.all_to_all(array, axes, split_axis=0, concat_axis=0, tiled=True)  35.9 us
    all_to_all x1, blocking collectives, swap(): return lax.all_to_all(array, axes, split_axis=0, concat_axis=0, tiled=True)  13.3 us
    pallas_call x1, Pallas kernels, attention_grads(): pl.pallas_call(grads_kernel, grid=(heads,), in_specs=[column_spec(a) for...  12.8 us
    psum x1, blocking collectives, local(): pair = lax.psum(stats, 'c').reshape(-1, 128)  5.48 us
    pallas_call x1, Pallas kernels, attention_stats(): pl.pallas_call(stats_kernel, grid=(heads,), in_specs=[column_spec(a) for...  5.4 us
  transfers between devices with their start and end apart: 5, of which 5 were waited for; matrix products, arithmetic and copies ran while one was open for 4% of the time, Pallas kernels for 0%

profile of v1, /device:TPU:1, one launch (start us, length us, event | category | flops | bytes accessed | tf_op | source)
XLA Modules:
  0.0 223.6 jit_solution(2422086366084233864)
XLA Ops:
  0.6 0.0 copy-start.14
  0.6 0.0 copy-start.9
  0.7 2.5 %reshape.143 = bf16[32,4,3072]{2,1,0:T(4,128)(2,1)} reshape(bf16[128,3072]{1,0:T(8,128)(2,1)} %param.13) | data formatting | bytes 1572864 | tf_op jit(solution)/shard_map/reshape | solution.py:195
  3.1 8.6 %all-to-all-start = ((bf16[32,4,3072]{2,1,0:T(4,128)(2,1)}), bf16[32,4,3072]{2,1,0:T(4,128)(2,1)S(1)}, u32[]{:S(2)}, u32[]{:S(2)}) async-start(bf16[32,4,3072]{2,1,0:T(4,128)(2,1)} %reshape.143), calls=%async_computation | async-start | bytes 1572864 | tf_op jit(solution)/shard_map/all_to_all | solution.py:168
  11.7 0.0 copy-done.14
  11.7 0.6 fusion.11
  22.8 0.0 copy-done.9
  22.8 1.4 bitcast_bitcast_fusion
  24.2 0.8 all-to-all-done
  25.0 0.1 maximum_bitcast_fusion
  25.1 1.4 pad_maximum_fusion
  26.5 8.3 %all-to-all-start.1 = ((bf16[8,272,384]{2,1,0:T(8,128)(2,1)}), bf16[8,272,384]{2,1,0:T(8,128)(2,1)S(1)}, u32[]{:S(2)}, u32[]{:S(2)}) async-start(bf16[8,272,384]{2,1,0:T(8,128)(2,1)} %pad_maximum_fusion), calls=%async_computation.1 | async-start | bytes 3342336 | tf_op jit(solution)/shard_map/all_to_all | solution.py:168
  34.8 40.1 %all-to-all-done.1 = bf16[8,272,384]{2,1,0:T(8,128)(2,1)S(1)} async-done(((bf16[8,272,384]{2,1,0:T(8,128)(2,1)}), bf16[8,272,384]{2,1,0:T(8,128)(2,1)S(1)}, u32[]{:S(2)}, u32[]{:S(2)}) %all-to-all-start.1) | async-done | bytes 1671200 | tf_op jit(solution)/shard_map/all_to_all | solution.py:168
  75.0 0.0 copy-done.10
  75.0 0.0 copy-done.12
  75.0 0.0 copy-done.13
  75.0 0.1 concatenate.30
  75.1 1.4 broadcast_in_dim.6
  76.6 9.4 %all-to-all-start.2 = ((bf16[32,64,384]{2,1,0:T(8,128)(2,1)}), bf16[32,64,384]{2,1,0:T(8,128)(2,1)}, u32[]{:S(2)}, u32[]{:S(2)}) async-start(bf16[32,64,384]{2,1,0:T(8,128)(2,1)} %broadcast_in_dim.6), calls=%async_computation.2 | async-start | bytes 3145728 | tf_op jit(solution)/shard_map/all_to_all | solution.py:168
  86.0 0.0 copy-done.8
  86.0 0.0 copy-done.15
  86.0 0.0 copy-done.17
  86.1 0.0 copy-done.19
  86.1 0.0 copy-done.20
  86.1 1.6 fusion.6
  87.7 19.6 %all-to-all-done.2 = bf16[32,64,384]{2,1,0:T(8,128)(2,1)} async-done(((bf16[32,64,384]{2,1,0:T(8,128)(2,1)}), bf16[32,64,384]{2,1,0:T(8,128)(2,1)}, u32[]{:S(2)}, u32[]{:S(2)}) %all-to-all-start.2) | async-done | bytes 1572896 | tf_op jit(solution)/shard_map/all_to_all | solution.py:168
  107.2 2.4 %fusion.7 = (bf16[32,16,384]{2,1,0:T(8,128)(2,1)}, bf16[32,16,384]{2,1,0:T(8,128)(2,1)}, bf16[32,16,384]{2,1,0:T(8,128)(2,1)S(1)}, bf16[32,16,384]{2,1,0:T(8,128)(2,1)S(1)}) fusion(bf16[32,64,384]{2,1,0:T(8,128)(2,1)} %all-to-all-done.2), kind=kLoop, calls=%fused_computation.39 | loop fusion | bytes 3145728 | tf_op jit(solution)/shard_map/slice | solution.py:224
  109.6 0.1 reshape.145
  109.7 0.0 copy-start.5
  109.7 0.0 copy-start.6
  109.7 0.1 copy.51
  109.9 0.1 reshape.146.win_ref
  110.0 1.2 pad_maximum_fusion.2.cot_ref
  111.2 0.0 copy-done.2
  111.2 0.0 copy-done.5
  111.2 0.0 copy-done.6
  111.2 5.4 %shard_map.188 = f32[3,2,1024]{2,1,0:T(2,128)S(1)} custom-call(bf16[512,384]{1,0:T(8,128)(2,1)S(1)} %reshape.146.win_ref, bf16[512,384]{1,0:T(8,128)(2,1)S(1)} %bitcast.84, bf16[1024,384]{1,0:T(8,128)(2,1)S(1)} %pad_maximum_fusion.2.cot_ref, bf16[1024,384]{1,0:T(8,128)(2,1)S(1)} %bitcast.80, bf16[1024,384]{1,0:T(8,128)(2,1)S(1)} %bitcast.78, ...), custom_call_target="tpu_custom_call" | custom-call | flops 1610612736 | bytes 6000000 | tf_op jit(solution)/shard_map/pallas_call | solution.py:124
  116.7 5.5 %psum.7 = f32[48,128]{1,0:T(8,128)S(1)} all-reduce(f32[48,128]{1,0:T(8,128)S(1)} %broadcast_in_dim.7), channel_id=1, replica_groups=mesh['y'=4,'xh'=2,'c'=2,'z'=8,'xl'=2] {'c'}, use_global_device_ids=true, to_apply=%region_0.1 | all-reduce | flops 6144 | bytes 49152 | tf_op jit(solution)/shard_map/psum | solution.py:232
  122.2 13.3 %all_to_all.30 = f32[16,48,128]{2,1,0:T(8,128)S(1)} all-to-all(f32[16,48,128]{2,1,0:T(8,128)S(1)} %broadcast_in_dim.8), channel_id=1, replica_groups=mesh['y'=4,'xh'=2,'c'=2,'z'=8,'xl'=2] {'y','xh','xl'}, dimensions={0} | all-to-all | bytes 786432 | tf_op jit(solution)/shard_map/all_to_all | solution.py:168
  135.5 0.6 reshape.152.stats_ref
  136.2 1.0 copy-done.3
  137.2 0.7 copy-done.4
  137.9 0.7 copy-done.7
  138.6 12.8 %shard_map.189 = (bf16[32,64,384]{2,1,0:T(8,128)(2,1)}, bf16[1024,384]{1,0:T(8,128)(2,1)S(1)}, bf16[1024,384]{1,0:T(8,128)(2,1)S(1)}, bf16[16,384]{1,0:T(8,128)(2,1)}, bf16[16,384]{1,0:T(8,128)(2,1)}) custom-call(bf16[512,384]{1,0:T(8,128)(2,1)S(1)} %reshape.146.win_ref, bf16[512,384]{1,0:T(8,128)(2,1)S(1)} %bitcast.85, ...), custom_call_target="tpu_custom_call" | custom-call | flops 4831838208 | bytes 9000000 | tf_op jit(solution)/shard_map/pallas_call | solution.py:151
  151.4 0.9 copy-done
  152.3 6.0 %all-to-all-start.4 = ((bf16[32,64,384]{2,1,0:T(8,128)(2,1)}), bf16[32,64,384]{2,1,0:T(8,128)(2,1)}, u32[]{:S(2)}, u32[]{:S(2)}) async-start(bf16[32,64,384]{2,1,0:T(8,128)(2,1)} %get-tuple-element.13), calls=%async_computation.4 | async-start | bytes 3145728 | tf_op jit(solution)/shard_map/all_to_all | solution.py:168
  158.3 1.4 pad_maximum_fusion.1
  159.7 19.9 %all-to-all-done.4 = bf16[32,64,384]{2,1,0:T(8,128)(2,1)} async-done(((bf16[32,64,384]{2,1,0:T(8,128)(2,1)}), bf16[32,64,384]{2,1,0:T(8,128)(2,1)}, u32[]{:S(2)}, u32[]{:S(2)}) %all-to-all-start.4) | async-done | bytes 1572896 | tf_op jit(solution)/shard_map/all_to_all | solution.py:168
  179.6 3.6 %all-to-all-start.5 = ((bf16[8,256,384]{2,1,0:T(8,128)(2,1)}), bf16[8,256,384]{2,1,0:T(8,128)(2,1)S(1)}, u32[]{:S(2)}, u32[]{:S(2)}) async-start(bf16[8,256,384]{2,1,0:T(8,128)(2,1)} %pad_maximum_fusion.1), calls=%async_computation.5 | async-start | bytes 3145728 | tf_op jit(solution)/shard_map/all_to_all | solution.py:168
  183.3 0.0 copy-done.16
  183.3 0.0 copy-done.18
  183.3 1.6 convert_reduce_fusion
  185.0 0.1 multiply_reduce_fusion.3
  185.1 0.1 multiply_reduce_fusion.1
  185.3 0.6 fusion.10
  185.9 0.1 mul.155
  186.0 0.1 mul.166
  186.1 0.1 mul.171
  186.1 0.1 mul.182
  186.2 0.6 fusion.2
  186.9 34.5 %all-to-all-done.5 = bf16[8,256,384]{2,1,0:T(8,128)(2,1)S(1)} async-done(((bf16[8,256,384]{2,1,0:T(8,128)(2,1)}), bf16[8,256,384]{2,1,0:T(8,128)(2,1)S(1)}, u32[]{:S(2)}, u32[]{:S(2)}) %all-to-all-start.5) | async-done | bytes 1572896 | tf_op jit(solution)/shard_map/all_to_all | solution.py:168
  221.4 0.2 slice_bitcast_fusion
  221.6 1.0 copy.38
  222.6 1.0 copy.39
  (41 shorter events, 0.4 us)
Async XLA Ops:
  0.6 11.1 %copy-start.14 = (s32[4]{0:T(128)S(1)}, s32[4]{0:T(128)}, u32[]{:S(2)}) copy-start(s32[4]{0:T(128)} %param.23) | copy-start | bytes 52
  0.6 22.2 %copy-start.9 = (bf16[128,3072]{1,0:T(8,128)(2,1)S(1)}, bf16[128,3072]{1,0:T(8,128)(2,1)}, u32[]{:S(2)}) copy-start(bf16[128,3072]{1,0:T(8,128)(2,1)} %param.15) | copy-start | bytes 2359300
  3.1 21.8 %all-to-all-start = ((bf16[32,4,3072]{2,1,0:T(4,128)(2,1)}), bf16[32,4,3072]{2,1,0:T(4,128)(2,1)S(1)}, u32[]{:S(2)}, u32[]{:S(2)}) async-start(bf16[32,4,3072]{2,1,0:T(4,128)(2,1)} %reshape.143), calls=%async_computation | async-start | bytes 1572864 | tf_op jit(solution)/shard_map/all_to_all | solution.py:168
  26.5 48.6 %copy-start.10 = (bf16[16,384]{1,0:T(8,128)(2,1)S(1)}, bf16[16,384]{1,0:T(8,128)(2,1)}, u32[]{:S(2)}) copy-start(bf16[16,384]{1,0:T(8,128)(2,1)} %param.16) | copy-start | bytes 36868
  26.5 48.6 %copy-start.12 = (bf16[16,384]{1,0:T(8,128)(2,1)S(1)}, bf16[16,384]{1,0:T(8,128)(2,1)}, u32[]{:S(2)}) copy-start(bf16[16,384]{1,0:T(8,128)(2,1)} %param.24) | copy-start | bytes 36868
  26.5 48.6 %copy-start.13 = (bf16[16,384]{1,0:T(8,128)(2,1)S(1)}, bf16[16,384]{1,0:T(8,128)(2,1)}, u32[]{:S(2)}) copy-start(bf16[16,384]{1,0:T(8,128)(2,1)} %param.25) | copy-start | bytes 36868
  26.5 48.4 %all-to-all-start.1 = ((bf16[8,272,384]{2,1,0:T(8,128)(2,1)}), bf16[8,272,384]{2,1,0:T(8,128)(2,1)S(1)}, u32[]{:S(2)}, u32[]{:S(2)}) async-start(bf16[8,272,384]{2,1,0:T(8,128)(2,1)} %pad_maximum_fusion), calls=%async_computation.1 | async-start | bytes 3342336 | tf_op jit(solution)/shard_map/all_to_all | solution.py:168
  74.8 11.2 %copy-start.8 = (bf16[8,272,384]{2,1,0:T(8,128)(2,1)}, bf16[8,272,384]{2,1,0:T(8,128)(2,1)S(1)}, u32[]{:S(2)}) copy-start(bf16[8,272,384]{2,1,0:T(8,128)(2,1)S(1)} %all-to-all-done.1) | copy-start | bytes 5013508
  76.6 9.5 %copy-start.15 = (f32[128]{0:T(128)S(1)}, f32[128]{0:T(128)}, u32[]{:S(2)}) copy-start(f32[128]{0:T(128)} %param.19) | copy-start | bytes 1540
  76.6 9.5 %copy-start.17 = (f32[128]{0:T(128)S(1)}, f32[128]{0:T(128)}, u32[]{:S(2)}) copy-start(f32[128]{0:T(128)} %param.21) | copy-start | bytes 1540
  76.6 9.5 %copy-start.19 = (f32[128]{0:T(128)S(1)}, f32[128]{0:T(128)}, u32[]{:S(2)}) copy-start(f32[128]{0:T(128)} %param.22) | copy-start | bytes 1540
  76.6 9.5 %copy-start.20 = (f32[128]{0:T(128)S(1)}, f32[128]{0:T(128)}, u32[]{:S(2)}) copy-start(f32[128]{0:T(128)} %param.20) | copy-start | bytes 1540
  76.6 30.6 %all-to-all-start.2 = ((bf16[32,64,384]{2,1,0:T(8,128)(2,1)}), bf16[32,64,384]{2,1,0:T(8,128)(2,1)}, u32[]{:S(2)}, u32[]{:S(2)}) async-start(bf16[32,64,384]{2,1,0:T(8,128)(2,1)} %broadcast_in_dim.6), calls=%async_computation.2 | async-start | bytes 3145728 | tf_op jit(solution)/shard_map/all_to_all | solution.py:168
  109.6 1.6 copy-start.2
  109.7 1.5 copy-start.5
  109.7 1.5 copy-start.6
  136.2 1.0 copy-start.3
  137.2 0.7 copy-start.4
  137.9 0.7 copy-start.7
  151.4 0.9 copy-start
  152.3 6.0 %copy-start.1 = (bf16[1024,384]{1,0:T(8,128)(2,1)S(1)}, bf16[1024,384]{1,0:T(8,128)(2,1)}, u32[]{:S(2)}) copy-start(bf16[1024,384]{1,0:T(8,128)(2,1)} %copy-done) | copy-start | bytes 2359300
  152.3 27.3 %all-to-all-start.4 = ((bf16[32,64,384]{2,1,0:T(8,128)(2,1)}), bf16[32,64,384]{2,1,0:T(8,128)(2,1)}, u32[]{:S(2)}, u32[]{:S(2)}) async-start(bf16[32,64,384]{2,1,0:T(8,128)(2,1)} %get-tuple-element.13), calls=%async_computation.4 | async-start | bytes 3145728 | tf_op jit(solution)/shard_map/all_to_all | solution.py:168
  159.7 23.5 %copy-start.11 = (bf16[16,384]{1,0:T(8,128)(2,1)S(1)}, bf16[16,384]{1,0:T(8,128)(2,1)}, u32[]{:S(2)}) copy-start(bf16[16,384]{1,0:T(8,128)(2,1)} %param.16) | copy-start | bytes 36868
  159.7 23.6 %copy-start.16 = (f32[128]{0:T(128)S(1)}, f32[128]{0:T(128)}, u32[]{:S(2)}) copy-start(f32[128]{0:T(128)} %param.19) | copy-start | bytes 1540
  159.7 23.6 %copy-start.18 = (f32[128]{0:T(128)S(1)}, f32[128]{0:T(128)}, u32[]{:S(2)}) copy-start(f32[128]{0:T(128)} %param.21) | copy-start | bytes 1540
  179.6 41.8 %all-to-all-start.5 = ((bf16[8,256,384]{2,1,0:T(8,128)(2,1)}), bf16[8,256,384]{2,1,0:T(8,128)(2,1)S(1)}, u32[]{:S(2)}, u32[]{:S(2)}) async-start(bf16[8,256,384]{2,1,0:T(8,128)(2,1)} %pad_maximum_fusion.1), calls=%async_computation.5 | async-start | bytes 3145728 | tf_op jit(solution)/shard_map/all_to_all | solution.py:168

commit v2 on v1

--- a/solution.py
+++ b/solution.py
@@ -14,6 +14,7 @@
 LOG2E = math.log2(math.e)
 PLANE = ("y", "xh", "c", "xl")
 CHIPS = ("y", "xh", "xl")
+ROW = ("xh", "xl")
 KEY_BLOCK = 256
 NT = (((1,), (1,)), ((), ()))
 NN = (((1,), (0,)), ((), ()))
@@ -51,9 +52,12 @@
 
 def key_parts(k_ref, v_ref, tk_ref, tv_ref, gains_ref):
     parts = []
-    for start in range(0, k_ref.shape[0], KEY_BLOCK):
-        rows = slice(start, start + KEY_BLOCK)
-        parts.append((k_ref[rows], v_ref[rows], gains_ref[1:2], rows))
+    step = KEY_BLOCK // k_ref.shape[1]
+    for start in range(0, k_ref.shape[0], step):
+        spots = slice(start, start + step)
+        key = k_ref[spots].reshape(KEY_BLOCK, HD)
+        value = v_ref[spots].reshape(KEY_BLOCK, HD)
+        parts.append((key, value, gains_ref[1:2], spots))
     parts.append((tk_ref[...], tv_ref[...], gains_ref[3:4], None))
     return parts
 
@@ -75,7 +79,7 @@
 
 def grads_kernel(
     win_ref, tq_ref, cot_ref, k_ref, v_ref, tk_ref, tv_ref, gains_ref, stats_ref,
-    rows_ref, dk_ref, dv_ref, dtk_ref, dtv_ref,
+    rows_ref, dkv_ref, dtk_ref, dtv_ref,
 ):
     queries = normed_queries(win_ref, tq_ref, gains_ref)
     cot = cot_ref[...]
@@ -84,7 +88,7 @@
     delta = stats_ref[0, 1:2] * inv_den
     out_t = jnp.zeros((HD, count), F32)
     dq_t = jnp.zeros((HD, count), F32)
-    for raw_key, value, gain, rows in key_parts(k_ref, v_ref, tk_ref, tv_ref, gains_ref):
+    for raw_key, value, gain, spots in key_parts(k_ref, v_ref, tk_ref, tv_ref, gains_ref):
         key = normed(raw_key, gain)
         probs = jnp.exp2(mm(key, queries, NT) * (INV_ROOT * LOG2E)) * inv_den
         probs_16 = probs.astype(BF16)
@@ -93,12 +97,13 @@
         dscores = (probs * (mm(value, cot, NT) - delta)).astype(BF16)
         dkey = pullback(raw_key, gain, mm(dscores, queries, NN) * INV_ROOT).astype(BF16)
         dq_t += mm(key, dscores, TN)
-        if rows is None:
+        if spots is None:
             dtk_ref[...] = dkey
             dtv_ref[...] = dvalue
         else:
-            dk_ref[rows] = dkey
-            dv_ref[rows] = dvalue
+            own = dkv_ref.shape[1] // 2
+            dkv_ref[spots, :own] = dkey.reshape(-1, own, HD)
+            dkv_ref[spots, own:] = dvalue.reshape(-1, own, HD)
     half = count // 2
     outs = out_t.T.astype(BF16)
     dqs = (dq_t * INV_ROOT).T.astype(BF16)
@@ -108,7 +113,8 @@
 
 
 def column_spec(array):
-    return pl.BlockSpec((array.shape[0], HD), lambda head: (0, head))
+    lead = array.shape[:-1]
+    return pl.BlockSpec(lead + (HD,), lambda head: (0,) * len(lead) + (head,))
 
 
 def whole_spec(array):
@@ -120,7 +126,7 @@
 
 def attention_stats(operands, gains, heads):
     count = operands[2].shape[0]
-    keys = operands[3].shape[0]
+    keys = operands[3].shape[0] * operands[3].shape[1]
     return pl.pallas_call(
         stats_kernel,
         grid=(heads,),
@@ -137,14 +143,14 @@
 
 def attention_grads(operands, gains, stats, heads, groups):
     count = operands[2].shape[0]
-    keys = operands[3].shape[0]
+    keys = operands[3].shape[0] * operands[3].shape[1]
     text = operands[5].shape[0]
     part = count // groups * 2
+    z_size = operands[3].shape[0]
     width = heads * HD
     shapes = [
         jax.ShapeDtypeStruct((groups, part, width), BF16),
-        jax.ShapeDtypeStruct((keys, width), BF16),
-        jax.ShapeDtypeStruct((keys, width), BF16),
+        jax.ShapeDtypeStruct((z_size, 2 * operands[3].shape[1], width), BF16),
         jax.ShapeDtypeStruct((text, width), BF16),
         jax.ShapeDtypeStruct((text, width), BF16),
     ]
@@ -153,8 +159,7 @@
         grid=(heads,),
         in_specs=[column_spec(a) for a in operands]
         + [whole_spec(gains), pl.BlockSpec((1, 2, count), lambda head: (head, 0, 0))],
-        out_specs=[pl.BlockSpec((groups, part, HD), lambda head: (0, 0, head))]
-        + [column_spec(s) for s in shapes[1:]],
+        out_specs=[column_spec(s) for s in shapes],
         out_shape=shapes,
         compiler_params=PARAMS,
         cost_estimate=pl.CostEstimate(
@@ -168,13 +173,79 @@
     return lax.all_to_all(array, axes, split_axis=0, concat_axis=0, tiled=True)
 
 
+def push(array, axes, step):
+    size = lax.axis_size(axes)
+    return lax.ppermute(array, axes, [(i, (i + step) % size) for i in range(size)])
+
+
+def place(array, index):
+    return lax.dynamic_index_in_dim(array, index, 0, keepdims=False, allow_negative_indices=False)
+
+
+def put(array, part, index):
+    return lax.dynamic_update_index_in_dim(array, part, index, 0, allow_negative_indices=False)
+
+
+def tie(*arrays):
+    return lax.optimization_barrier(arrays)
+
+
+def gather_stage(own, axes):
+    size, here = lax.axis_size(axes), lax.axis_index(axes)
+    whole = put(jnp.zeros((size,) + own.shape, own.dtype), own, here)
+    for step in range(1, size):
+        whole = put(whole, push(own, axes, step), (here - step) & (size - 1))
+    return whole
+
+
+def gather_plane(own):
+    whole = gather_stage(gather_stage(gather_stage(own, "y"), ROW), "c")
+    return whole.reshape((-1,) + own.shape)
+
+
+def scatter_stage(pieces, axes):
+    size, here = lax.axis_size(axes), lax.axis_index(axes)
+    return [place(pieces, here)] + [
+        push(place(pieces, (here + step) & (size - 1)), axes, step) for step in range(1, size)
+    ]
+
+
+def sum_stage(pieces, axes):
+    return sum(piece.astype(F32) for piece in scatter_stage(pieces, axes))
+
+
+def reduce_plane(pieces):
+    shape = pieces.shape[1:]
+    pieces = pieces.reshape((lax.axis_size("c"), lax.axis_size(ROW), lax.axis_size("y")) + shape)
+    pieces = sum_stage(pieces, "c").astype(BF16)
+    pieces = sum_stage(pieces, ROW).astype(BF16)
+    return sum_stage(pieces, "y")
+
+
 def split_heads(rows, groups):
     count = rows.shape[0]
     return rows.reshape(count, groups, -1).transpose(1, 0, 2)
 
 
-def pick(array, index):
-    return lax.dynamic_index_in_dim(array, index, 0, keepdims=False)
+def scatter_window(video_q, window):
+    y_size, xl_size, z_size = lax.axis_size("y"), lax.axis_size("xl"), lax.axis_size("z")
+    row, model = video_q.shape[0] // lax.axis_size(PLANE), video_q.shape[1]
+    rest = window >> (xl_size.bit_length() - 1)
+    z_of = rest & (z_size - 1)
+    plane_of = (rest >> (z_size.bit_length() - 1)) * xl_size + (window & (xl_size - 1))
+    pieces = video_q.reshape(-1, y_size, row, model).transpose(1, 0, 2, 3)
+    pieces = swap(pieces.reshape(-1, row, model), PLANE)
+    rows = jnp.concatenate([place(pieces, plane_of[slot]) for slot in range(NWIN)], axis=0)
+    return split_heads(rows, z_size), z_of
+
+
+def pick_window(came, z_of):
+    row = came.shape[1] // NWIN
+    rows = jnp.stack(
+        [place(came, z_of[s])[s * row : (s + 1) * row] for s in range(NWIN)]
+    )
+    rows = gather_stage(rows, "y")
+    return rows.transpose(1, 0, 2, 3).reshape(NWIN, row * lax.axis_size("y"), -1)
 
 
 def local(
@@ -183,7 +254,6 @@
     window, grad_out_video, grad_out_text,
 ):
     z_size = lax.axis_size("z")
-    rep_size = lax.axis_size("xl")
     groups = lax.axis_size(PLANE)
     own_rows, model = video_q.shape
     columns = model // z_size
@@ -191,40 +261,20 @@
     share = grad_out_video.shape[0]
     gains = jnp.stack((gain_video_q, gain_video_k, gain_text_q, gain_text_k))
 
-    piece = own_rows // groups
-    scattered = swap(video_q.reshape(groups, piece, model), PLANE)
-    z_of = [window[s] // rep_size % z_size for s in range(NWIN)]
-    plane_of = [
-        window[s] // (z_size * rep_size) * rep_size + window[s] % rep_size for s in range(NWIN)
-    ]
-    picked = jnp.concatenate([pick(scattered, plane_of[s]) for s in range(NWIN)], axis=0)
-
-    sent = jnp.concatenate(
-        (
-            split_heads(video_k, z_size),
-            split_heads(video_v, z_size),
-            split_heads(picked, z_size),
-        ),
-        axis=1,
-    )
+    text = jnp.stack((text_q, grad_out_video, grad_out_text))
+    every = gather_plane(text)
+    picked, z_of = scatter_window(video_q, window)
+    sent = jnp.concatenate((split_heads(video_k, z_size), picked), axis=1)
     moved = swap(sent, "z")
-    moved_k = moved[:, :own_rows].reshape(-1, columns)
-    moved_v = moved[:, own_rows : 2 * own_rows].reshape(-1, columns)
-    moved_q = moved[:, 2 * own_rows :].reshape(z_size, NWIN, piece, columns)
-    own_window = jnp.concatenate([pick(moved_q[:, s], z_of[s]) for s in range(NWIN)], axis=0)
-
-    own = jnp.concatenate((own_window, text_q, grad_out_video, grad_out_text), axis=0)
-    every = swap(jnp.broadcast_to(own[None], (groups,) + own.shape), PLANE)
-    window_rows = (
-        every[:, :share].reshape(groups, NWIN, piece, columns).transpose(1, 0, 2, 3)
-    ).reshape(-1, columns)
-    text_rows = every[:, share : 2 * share].reshape(-1, columns)
+    rows = pick_window(moved[:, own_rows:], z_of)
+    own_window = place(rows, lax.axis_index("y"))
+    sent_v, moved = tie(split_heads(video_v, z_size), moved)
+    moved_v = swap(sent_v, "z")
+    moved_k = moved[:, :own_rows]
+    window_rows = gather_stage(gather_stage(rows, ROW), "c").reshape(-1, columns)
+    text_rows = every[:, 0].reshape(-1, columns)
     cotangent = jnp.concatenate(
-        (
-            every[:, 2 * share : 3 * share].reshape(-1, columns),
-            every[:, 3 * share :].reshape(-1, columns),
-        ),
-        axis=0,
+        (every[:, 1].reshape(-1, columns), every[:, 2].reshape(-1, columns)), axis=0
     )
     operands = (window_rows, text_rows, cotangent, moved_k, moved_v, text_k, text_v)
 
@@ -234,22 +284,12 @@
     stats = jnp.sum(swap(jnp.broadcast_to(pair[None], (chips,) + pair.shape), CHIPS), axis=0)
     stats = stats.reshape(heads, 2, -1)
 
-    rows, dkey, dvalue, key_text, value_text = attention_grads(
-        operands, gains, stats, heads, groups
-    )
-    returned = swap(
-        jnp.concatenate(
-            (dkey.reshape(z_size, own_rows, columns), dvalue.reshape(z_size, own_rows, columns)),
-            axis=1,
-        ),
-        "z",
-    )
+    rows, dmoved, key_text, value_text = attention_grads(operands, gains, stats, heads, groups)
+    returned = swap(dmoved, "z")
     grad_video_k = returned[:, :own_rows].transpose(1, 0, 2).reshape(own_rows, model)
     grad_video_v = returned[:, own_rows:].transpose(1, 0, 2).reshape(own_rows, model)
 
-    total = jnp.sum(swap(rows, PLANE).astype(F32), axis=0)
-    place = lax.axis_index(PLANE)
-    own_raw = lax.dynamic_slice_in_dim(window_rows, place * share, share, 0)
+    total = reduce_plane(rows)
 
     def query_grad(raw, gain, cot):
         shape = (raw.shape[0], heads, HD)
@@ -258,7 +298,7 @@
     return (
         total[:share].astype(BF16),
         total[share : 2 * share].astype(BF16),
-        query_grad(own_raw, gain_video_q, total[2 * share : 3 * share]).astype(BF16),
+        query_grad(own_window, gain_video_q, total[2 * share : 3 * share]).astype(BF16),
         query_grad(text_q, gain_text_q, total[3 * share :]).astype(BF16),
         grad_video_k,
         grad_video_v,

time: 226 us -> 196 us (0.87)
  waiting for transfers between devices: 115 us -> 83.6 us
  starting transfers between devices: 35.9 us -> 54.8 us
  blocking collectives: 18.8 us -> 5.22 us
  between operations: 11.6 us -> 1.38 us
  local copies, waits for them, and re-layouts: 17.6 us -> 26.4 us
    all_to_all x5, waiting for transfers between devices: 115 us -> 59.2 us  [swap(): return lax.all_to_all(array, axes, split_axis=0, concat_axis=0, tiled=True)]
    ppermute x0 -> x21, starting transfers between devices: none -> 29.4 us  [push(): lax.ppermute(array, axes, [(i, (i + step) % size) for i in range(size)])]
    ppermute x0 -> x21, waiting for transfers between devices: none -> 24.5 us  [push(): lax.ppermute(array, axes, [(i, (i + step) % size) for i in range(size)])]
    all_to_all x1 -> x0, blocking collectives: 13.3 us -> none  [swap(): return lax.all_to_all(array, axes, split_axis=0, concat_axis=0, tiled=True)]
    all_to_all x5, starting transfers between devices: 35.9 us -> 25.4 us  [swap(): return lax.all_to_all(array, axes, split_axis=0, concat_axis=0, tiled=True)]
    unnamed x43 -> x50, local copies, waits for them, and re-layouts: 3.57 us -> 6.74 us
    concatenate x3 -> x2, other arithmetic: 3.94 us -> 1.12 us  [the longest x1 1.04 us: local(): sent = jnp.concatenate((split_heads(video_k, z_size), picked), axis=1)]
    dynamic_slice x1, local copies, waits for them, and re-layouts: 0.04 us -> 2.6 us  [place(): lax.dynamic_index_in_dim(array, index, 0, keepdims=False, allow_negative_...]
  transfers between devices with their start and end apart: 5 -> 26, of which waited for: 5 -> 13; matrix products, arithmetic and copies ran while one was open for 4% -> 9% of each run, Pallas kernels for 0% -> 0%
where the time goes in v2:
time: 196 us; the launch traced here: 195 us
  waiting for transfers between devices  83.6 us (43%)
  starting transfers between devices  54.8 us (28%)
  local copies, waits for them, and re-layouts  26.4 us (13%)
  Pallas kernels  18.3 us (9%)
  blocking collectives  5.22 us (3%)
  other arithmetic  5.02 us (3%)
    all_to_all x5, waiting for transfers between devices, swap(): return lax.all_to_all(array, axes, split_axis=0, concat_axis=0, tiled=True)  59.2 us
    ppermute x21, starting transfers between devices, push(): lax.ppermute(array, axes, [(i, (i + step) % size) for i in range(size)])  29.4 us
    all_to_all x5, starting transfers between devices, swap(): return lax.all_to_all(array, axes, split_axis=0, concat_axis=0, tiled=True)  25.4 us
    ppermute x21, waiting for transfers between devices, push(): lax.ppermute(array, axes, [(i, (i + step) % size) for i in range(size)])  24.5 us
    pallas_call x1, Pallas kernels, attention_grads(): pl.pallas_call(grads_kernel, grid=(heads,), in_specs=[column_spec(a) for...  12.9 us
    unnamed x50, local copies, waits for them, and re-layouts  6.74 us
    pallas_call x1, Pallas kernels, attention_stats(): pl.pallas_call(stats_kernel, grid=(heads,), in_specs=[column_spec(a) for...  5.39 us
    psum x1, blocking collectives, local(): pair = lax.psum(stats, 'c').reshape(-1, 128)  5.22 us
  transfers between devices with their start and end apart: 26, of which 13 were waited for; matrix products, arithmetic and copies ran while one was open for 9% of the time, Pallas kernels for 0%

profile of v2, /device:TPU:1, one launch (start us, length us, event | category | flops | bytes accessed | tf_op | source)
XLA Modules:
  0.0 194.7 jit_solution(7515411017069471869)
XLA Ops:
  0.6 0.8 pad_maximum_fusion.2
  1.4 2.2 %collective-permute-start.7 = (bf16[3,16,384]{2,1,0:T(8,128)(2,1)S(1)}, bf16[3,16,384]{2,1,0:T(8,128)(2,1)S(1)}, u32[]{:S(2)}, u32[]{:S(2)}) collective-permute-start(bf16[3,16,384]{2,1,0:T(8,128)(2,1)S(1)} %pad_maximum_fusion.2), channel_id=1, source_target_pairs={{0,64},{64,128},{128,192},{192,0},{1,65},{65,129},{129,193},{193,1... | collective-permute-start | bytes 110600 | tf_op jit(solution)/shard_map/ppermute | solution.py:178
  3.6 2.6 %collective-permute-start.8 = (bf16[3,16,384]{2,1,0:T(8,128)(2,1)S(1)}, bf16[3,16,384]{2,1,0:T(8,128)(2,1)S(1)}, u32[]{:S(2)}, u32[]{:S(2)}) collective-permute-start(bf16[3,16,384]{2,1,0:T(8,128)(2,1)S(1)} %pad_maximum_fusion.2), channel_id=1, source_target_pairs={{0,128},{64,192},{128,0},{192,64},{1,129},{65,193},{129,1},{193,65... | collective-permute-start | bytes 110600 | tf_op jit(solution)/shard_map/ppermute | solution.py:178
  6.2 1.1 collective-permute-start.9
  7.3 1.7 reshape.145
  9.0 0.4 copy.98
  9.5 1.5 copy.72
  11.0 6.1 %all-to-all-start = ((bf16[32,4,3072]{2,1,0:T(4,128)(2,1)}), bf16[32,4,3072]{2,1,0:T(4,128)(2,1)S(1)}, u32[]{:S(2)}, u32[]{:S(2)}) async-start(bf16[32,4,3072]{2,1,0:T(4,128)(2,1)} %copy.72), calls=%async_computation | async-start | bytes 1572864 | tf_op jit(solution)/shard_map/all_to_all | solution.py:173
  17.2 0.6 fusion.16
  18.6 1.5 collective-permute-start.10
  20.1 2.4 %collective-permute-start.11 = (bf16[4,3,16,384]{3,2,1,0:T(8,128)(2,1)S(1)}, bf16[4,3,16,384]{3,2,1,0:T(8,128)(2,1)S(1)}, u32[]{:S(2)}, u32[]{:S(2)}) collective-permute-start(bf16[4,3,16,384]{3,2,1,0:T(8,128)(2,1)S(1)} %bitcast_dynamic-update-slice_fusion.9), channel_id=1, source_target_pairs={{0,32},{1,33},{32,0},{33,1},{2,34},{3,35},{34,2},{35,3},{4,36},{5,... | collective-permute-start | bytes 442376 | tf_op jit(solution)/shard_map/ppermute | solution.py:178
  22.5 1.2 collective-permute-start.12
  23.7 8.4 %collective-permute-done.10 = bf16[4,3,16,384]{3,2,1,0:T(8,128)(2,1)S(1)} collective-permute-done((bf16[4,3,16,384]{3,2,1,0:T(8,128)(2,1)S(1)}, bf16[4,3,16,384]{3,2,1,0:T(8,128)(2,1)S(1)}, u32[]{:S(2)}, u32[]{:S(2)}) %collective-permute-start.10) | collective-permute-done | bytes 147488 | tf_op jit(solution)/shard_map/ppermute | solution.py:178
  32.1 2.6 %constant_dynamic-slice_fusion.7 = (bf16[1,4,3072]{2,1,0:T(4,128)(2,1)S(1)}, bf16[1,4,3072]{2,1,0:T(4,128)(2,1)S(1)}, bf16[1,4,3072]{2,1,0:T(4,128)(2,1)S(1)}, bf16[1,4,3072]{2,1,0:T(4,128)(2,1)S(1)}) fusion(bf16[32,4,3072]{2,1,0:T(4,128)(2,1)S(1)} %all-to-all-done, s32[]{:T(128)} %bitcast.4, s32[]{:T(128)} %bitcast.10, s32[]{:T(128)} %bitcast.8, s32[]{:T(128)} %bitcast.6), kind=kLoop, calls=%fused_computation.64 | loop fusion | bytes 196624 | tf_op jit(solution)/shard_map/jit(dynamic_index_in_dim)/dynamic_slice | solution.py:182
  34.8 1.0 pad_maximum_fusion
  35.9 8.3 %all-to-all-start.1 = ((bf16[8,144,384]{2,1,0:T(8,128)(2,1)}), bf16[8,144,384]{2,1,0:T(8,128)(2,1)S(1)}, u32[]{:S(2)}, u32[]{:S(2)}) async-start(bf16[8,144,384]{2,1,0:T(8,128)(2,1)} %pad_maximum_fusion), calls=%async_computation.1 | async-start | bytes 1769472 | tf_op jit(solution)/shard_map/all_to_all | solution.py:173
  44.3 1.4 collective-permute-start.13
  45.7 0.4 copy.81
  46.1 1.2 copy.82
  47.6 1.2 copy_dynamic-update-slice_fusion
  49.0 20.8 %all-to-all-done.1 = bf16[8,144,384]{2,1,0:T(8,128)(2,1)S(1)} async-done(((bf16[8,144,384]{2,1,0:T(8,128)(2,1)}), bf16[8,144,384]{2,1,0:T(8,128)(2,1)S(1)}, u32[]{:S(2)}, u32[]{:S(2)}) %all-to-all-start.1) | async-done | bytes 884768 | tf_op jit(solution)/shard_map/all_to_all | solution.py:173
  69.9 2.6 %constant_dynamic-slice_fusion.3 = (bf16[1,4,384]{2,1,0:T(4,128)(2,1)S(1)}, bf16[1,4,384]{2,1,0:T(4,128)(2,1)S(1)}, bf16[1,4,384]{2,1,0:T(4,128)(2,1)S(1)}, bf16[1,4,384]{2,1,0:T(4,128)(2,1)S(1)}) fusion(bf16[8,16,384]{2,1,0:T(8,128)(2,1)S(1)} %slice.98, s32[]{:T(128)} %bitcast.13, s32[]{:T(128)} %bitcast.16, s32[]{:T(128)S(6)} %add.101, s32[]{:T(128)} %bitcast.15, ...), kind=kLoop, calls=%fused_computation.60 | loop fusion | bytes 24604 | tf_op jit(solution)/shard_map/slice | solution.py:245
  72.5 1.3 collective-permute-start
  73.8 2.5 %collective-permute-start.1 = (bf16[4,4,384]{2,1,0:T(4,128)(2,1)S(1)}, bf16[4,4,384]{2,1,0:T(4,128)(2,1)S(1)}, u32[]{:S(2)}, u32[]{:S(2)}) collective-permute-start(bf16[4,4,384]{2,1,0:T(4,128)(2,1)S(1)} %pad_maximum_fusion.3), channel_id=1, source_target_pairs={{0,128},{64,192},{128,0},{192,64},{1,129},{65,193},{129,1},{193,65... | collective-permute-start | bytes 36872 | tf_op jit(solution)/shard_map/ppermute | solution.py:178
  76.2 1.1 collective-permute-start.2
  77.5 3.7 %all-to-all-start.2 = ((bf16[8,128,384]{2,1,0:T(8,128)(2,1)}), bf16[8,128,384]{2,1,0:T(8,128)(2,1)S(1)}, u32[]{:S(2)}, u32[]{:S(2)}) async-start(bf16[8,128,384]{2,1,0:T(8,128)(2,1)} %bitcast.146), calls=%async_computation.2 | async-start | bytes 1572864 | tf_op jit(solution)/shard_map/all_to_all | solution.py:173
  81.6 1.7 collective-permute-start.4
  83.3 0.9 collective-permute-start.5
  84.3 2.0 %collective-permute-done.3 = bf16[4,16,384]{2,1,0:T(8,128)(2,1)S(1)} collective-permute-done((bf16[4,16,384]{2,1,0:T(8,128)(2,1)S(1)}, bf16[4,16,384]{2,1,0:T(8,128)(2,1)S(1)}, u32[]{:S(2)}, u32[]{:S(2)}) %collective-permute-start.3) | collective-permute-done | bytes 49184 | tf_op jit(solution)/shard_map/ppermute | solution.py:178
  86.3 0.8 collective-permute-done.5
  87.1 2.6 %collective-permute-start.6 = (bf16[4,4,16,384]{3,2,1,0:T(8,128)(2,1)S(1)}, bf16[4,4,16,384]{3,2,1,0:T(8,128)(2,1)S(1)}, u32[]{:S(2)}, u32[]{:S(2)}) collective-permute-start(bf16[4,4,16,384]{3,2,1,0:T(8,128)(2,1)S(1)} %bitcast_dynamic-update-slice_fusion.6), channel_id=1, source_target_pairs={{0,16},{16,0},{1,17},{17,1},{2,18},{18,2},{3,19},{19,3},{4,20},{20... | collective-permute-start | bytes 589832 | tf_op jit(solution)/shard_map/ppermute | solution.py:178
  89.7 1.0 collective-permute-done.6
  90.8 12.3 %all-to-all-done.2.v_ref = bf16[8,128,384]{2,1,0:T(8,128)(2,1)S(1)} async-done(((bf16[8,128,384]{2,1,0:T(8,128)(2,1)}), bf16[8,128,384]{2,1,0:T(8,128)(2,1)S(1)}, u32[]{:S(2)}, u32[]{:S(2)}) %all-to-all-start.2) | async-done | bytes 786464 | tf_op jit(solution)/shard_map/all_to_all | solution.py:173
  103.1 5.4 %shard_map.188 = f32[3,2,1024]{2,1,0:T(2,128)S(1)} custom-call(bf16[512,384]{1,0:T(8,128)(2,1)S(1)} %bitcast.142, bf16[512,384]{1,0:T(8,128)(2,1)S(1)} %bitcast.140, bf16[1024,384]{1,0:T(8,128)(2,1)S(1)} %pad_maximum_fusion.1.cot_ref, bf16[8,128,384]{2,1,0:T(8,128)(2,1)S(1)} %slice.91.k_ref, bf16[8,128,384]{2,1,0:T(8,128)(2,1)S(1)} %all-to-all-done.2.v_ref, ...), custom_call_target="tpu_custom_call" | custom-call | flops 1610612736 | bytes 6000000 | tf_op jit(solution)/shard_map/pallas_call | solution.py:130
  108.6 5.2 %psum.7 = f32[48,128]{1,0:T(8,128)S(1)} all-reduce(f32[48,128]{1,0:T(8,128)S(1)} %broadcast_in_dim.123), channel_id=1, replica_groups=mesh['y'=4,'xh'=2,'c'=2,'z'=8,'xl'=2] {'c'}, use_global_device_ids=true, to_apply=%region_0.1 | all-reduce | flops 6144 | bytes 49152 | tf_op jit(solution)/shard_map/psum | solution.py:282
  113.8 0.8 broadcast_in_dim.124
  114.6 3.6 %all-to-all-start.3 = ((f32[16,48,128]{2,1,0:T(8,128)}), f32[16,48,128]{2,1,0:T(8,128)S(1)}, u32[]{:S(2)}, u32[]{:S(2)}) async-start(f32[16,48,128]{2,1,0:T(8,128)} %broadcast_in_dim.124), calls=%async_computation.3 | async-start | bytes 786432 | tf_op jit(solution)/shard_map/all_to_all | solution.py:173
  118.1 9.8 %all-to-all-done.3 = f32[16,48,128]{2,1,0:T(8,128)S(1)} async-done(((f32[16,48,128]{2,1,0:T(8,128)}), f32[16,48,128]{2,1,0:T(8,128)S(1)}, u32[]{:S(2)}, u32[]{:S(2)}) %all-to-all-start.3) | async-done | bytes 393248 | tf_op jit(solution)/shard_map/all_to_all | solution.py:173
  127.9 0.6 reshape.151.stats_ref
  128.6 1.1 copy-done.1
  129.7 1.0 copy-done.3
  130.7 0.7 copy-done.4
  131.4 0.7 copy-done.7
  132.1 12.9 %shard_map.189 = (bf16[32,64,384]{2,1,0:T(8,128)(2,1)S(1)}, bf16[8,256,384]{2,1,0:T(8,128)(2,1)}, bf16[16,384]{1,0:T(8,128)(2,1)}, bf16[16,384]{1,0:T(8,128)(2,1)}) custom-call(bf16[512,384]{1,0:T(8,128)(2,1)S(1)} %bitcast.143, bf16[512,384]{1,0:T(8,128)(2,1)S(1)} %bitcast.141, bf16[1024,384]{1,0:T(8,128)(2,1)S(1)} %pad_maximum_fusion.1.cot_ref, ...), custom_call_target="tpu_custom_call" | custom-call | flops 4831838208 | bytes 9000000 | tf_op jit(solution)/shard_map/pallas_call | solution.py:157
  145.1 1.0 dynamic-slice_bitcast_fusion
  146.0 1.3 collective-permute-start.14
  147.3 3.7 %all-to-all-start.4 = ((bf16[8,256,384]{2,1,0:T(8,128)(2,1)}), bf16[8,256,384]{2,1,0:T(8,128)(2,1)S(1)}, u32[]{:S(2)}, u32[]{:S(2)}) async-start(bf16[8,256,384]{2,1,0:T(8,128)(2,1)} %get-tuple-element.17), calls=%async_computation.4 | async-start | bytes 3145728 | tf_op jit(solution)/shard_map/all_to_all | solution.py:173
  151.1 1.4 fusion
  152.9 1.1 collective-permute-start.16
  154.1 1.4 collective-permute-start.17
  155.4 9.2 %collective-permute-done.15 = bf16[4,64,384]{2,1,0:T(8,128)(2,1)S(1)} collective-permute-done((bf16[4,64,384]{2,1,0:T(8,128)(2,1)S(1)}, bf16[4,64,384]{2,1,0:T(8,128)(2,1)S(1)}, u32[]{:S(2)}, u32[]{:S(2)}) %collective-permute-start.15) | collective-permute-done | bytes 196640 | tf_op jit(solution)/shard_map/ppermute | solution.py:178
  165.1 1.7 collective-permute-start.19
  166.9 0.9 collective-permute-start.20
  167.8 2.1 %collective-permute-done.18 = bf16[64,384]{1,0:T(8,128)(2,1)S(1)} collective-permute-done((bf16[64,384]{1,0:T(8,128)(2,1)S(1)}, bf16[64,384]{1,0:T(8,128)(2,1)S(1)}, u32[]{:S(2)}, u32[]{:S(2)}) %collective-permute-start.18) | collective-permute-done | bytes 49184 | tf_op jit(solution)/shard_map/ppermute | solution.py:178
  170.3 0.4 collective-permute-done.20
  171.0 0.6 fusion.8
  171.8 0.6 fusion.15
  172.6 0.6 fusion.11
  173.2 16.2 %all-to-all-done.4 = bf16[8,256,384]{2,1,0:T(8,128)(2,1)S(1)} async-done(((bf16[8,256,384]{2,1,0:T(8,128)(2,1)}), bf16[8,256,384]{2,1,0:T(8,128)(2,1)S(1)}, u32[]{:S(2)}, u32[]{:S(2)}) %all-to-all-start.4) | async-done | bytes 1572896 | tf_op jit(solution)/shard_map/all_to_all | solution.py:173
  189.4 1.1 slice_bitcast_fusion
  190.5 1.5 copy.83
  192.0 1.2 copy.85
  193.2 0.4 copy.84
  193.6 1.2 copy.86
  (120 shorter events, 4.2 us)
Async XLA Ops:
  1.4 17.1 %collective-permute-start.7 = (bf16[3,16,384]{2,1,0:T(8,128)(2,1)S(1)}, bf16[3,16,384]{2,1,0:T(8,128)(2,1)S(1)}, u32[]{:S(2)}, u32[]{:S(2)}) collective-permute-start(bf16[3,16,384]{2,1,0:T(8,128)(2,1)S(1)} %pad_maximum_fusion.2), channel_id=1, source_target_pairs={{0,64},{64,128},{128,192},{192,0},{1,65},{65,129},{129,193},{193,1... | collective-permute-start | bytes 110600 | tf_op jit(solution)/shard_map/ppermute | solution.py:178
  3.6 15.0 %collective-permute-start.8 = (bf16[3,16,384]{2,1,0:T(8,128)(2,1)S(1)}, bf16[3,16,384]{2,1,0:T(8,128)(2,1)S(1)}, u32[]{:S(2)}, u32[]{:S(2)}) collective-permute-start(bf16[3,16,384]{2,1,0:T(8,128)(2,1)S(1)} %pad_maximum_fusion.2), channel_id=1, source_target_pairs={{0,128},{64,192},{128,0},{192,64},{1,129},{65,193},{129,1},{193,65... | collective-permute-start | bytes 110600 | tf_op jit(solution)/shard_map/ppermute | solution.py:178
  6.2 12.4 %collective-permute-start.9 = (bf16[3,16,384]{2,1,0:T(8,128)(2,1)S(1)}, bf16[3,16,384]{2,1,0:T(8,128)(2,1)S(1)}, u32[]{:S(2)}, u32[]{:S(2)}) collective-permute-start(bf16[3,16,384]{2,1,0:T(8,128)(2,1)S(1)} %pad_maximum_fusion.2), channel_id=1, source_target_pairs={{0,192},{64,0},{128,64},{192,128},{1,193},{65,1},{129,65},{193,129... | collective-permute-start | bytes 110600 | tf_op jit(solution)/shard_map/ppermute | solution.py:178
  9.4 7.7 %copy-start.22 = (s32[4]{0:T(128)S(1)}, s32[4]{0:T(128)}, u32[]{:S(2)}) copy-start(s32[4]{0:T(128)} %param.23) | copy-start | bytes 52
  9.4 7.7 %copy-start.10 = (bf16[16,384]{1,0:T(8,128)(2,1)S(1)}, bf16[16,384]{1,0:T(8,128)(2,1)}, u32[]{:S(2)}) copy-start(bf16[16,384]{1,0:T(8,128)(2,1)} %param.16) | copy-start | bytes 36868
  9.4 7.7 %copy-start.14 = (bf16[16,384]{1,0:T(8,128)(2,1)S(1)}, bf16[16,384]{1,0:T(8,128)(2,1)}, u32[]{:S(2)}) copy-start(bf16[16,384]{1,0:T(8,128)(2,1)} %param.25) | copy-start | bytes 36868
  9.4 7.7 %copy-start.15 = (bf16[16,384]{1,0:T(8,128)(2,1)S(1)}, bf16[16,384]{1,0:T(8,128)(2,1)}, u32[]{:S(2)}) copy-start(bf16[16,384]{1,0:T(8,128)(2,1)} %param.24) | copy-start | bytes 36868
  9.5 8.3 %copy-start.8 = (bf16[128,3072]{1,0:T(8,128)(2,1)S(1)}, bf16[128,3072]{1,0:T(8,128)(2,1)}, u32[]{:S(2)}) copy-start(bf16[128,3072]{1,0:T(8,128)(2,1)} %param.14) | copy-start | bytes 2359300
  11.0 21.2 %all-to-all-start = ((bf16[32,4,3072]{2,1,0:T(4,128)(2,1)}), bf16[32,4,3072]{2,1,0:T(4,128)(2,1)S(1)}, u32[]{:S(2)}, u32[]{:S(2)}) async-start(bf16[32,4,3072]{2,1,0:T(4,128)(2,1)} %copy.72), calls=%async_computation | async-start | bytes 1572864 | tf_op jit(solution)/shard_map/all_to_all | solution.py:173
  18.6 13.5 %collective-permute-start.10 = (bf16[4,3,16,384]{3,2,1,0:T(8,128)(2,1)S(1)}, bf16[4,3,16,384]{3,2,1,0:T(8,128)(2,1)S(1)}, u32[]{:S(2)}, u32[]{:S(2)}) collective-permute-start(bf16[4,3,16,384]{3,2,1,0:T(8,128)(2,1)S(1)} %bitcast_dynamic-update-slice_fusion.9), channel_id=1, source_target_pairs={{0,1},{1,32},{32,33},{33,0},{2,3},{3,34},{34,35},{35,2},{4,5},{5,3... | collective-permute-start | bytes 442376 | tf_op jit(solution)/shard_map/ppermute | solution.py:178
  20.1 24.1 %collective-permute-start.11 = (bf16[4,3,16,384]{3,2,1,0:T(8,128)(2,1)S(1)}, bf16[4,3,16,384]{3,2,1,0:T(8,128)(2,1)S(1)}, u32[]{:S(2)}, u32[]{:S(2)}) collective-permute-start(bf16[4,3,16,384]{3,2,1,0:T(8,128)(2,1)S(1)} %bitcast_dynamic-update-slice_fusion.9), channel_id=1, source_target_pairs={{0,32},{1,33},{32,0},{33,1},{2,34},{3,35},{34,2},{35,3},{4,36},{5,... | collective-permute-start | bytes 442376 | tf_op jit(solution)/shard_map/ppermute | solution.py:178
  22.5 21.8 %collective-permute-start.12 = (bf16[4,3,16,384]{3,2,1,0:T(8,128)(2,1)S(1)}, bf16[4,3,16,384]{3,2,1,0:T(8,128)(2,1)S(1)}, u32[]{:S(2)}, u32[]{:S(2)}) collective-permute-start(bf16[4,3,16,384]{3,2,1,0:T(8,128)(2,1)S(1)} %bitcast_dynamic-update-slice_fusion.9), channel_id=1, source_target_pairs={{0,33},{1,0},{32,1},{33,32},{2,35},{3,2},{34,3},{35,34},{4,37},{5,... | collective-permute-start | bytes 442376 | tf_op jit(solution)/shard_map/ppermute | solution.py:178
  35.9 9.8 %copy-start.9 = (bf16[128,3072]{1,0:T(8,128)(2,1)S(1)}, bf16[128,3072]{1,0:T(8,128)(2,1)}, u32[]{:S(2)}) copy-start(bf16[128,3072]{1,0:T(8,128)(2,1)} %param.15) | copy-start | bytes 2359300
  35.9 34.0 %all-to-all-start.1 = ((bf16[8,144,384]{2,1,0:T(8,128)(2,1)}), bf16[8,144,384]{2,1,0:T(8,128)(2,1)S(1)}, u32[]{:S(2)}, u32[]{:S(2)}) async-start(bf16[8,144,384]{2,1,0:T(8,128)(2,1)} %pad_maximum_fusion), calls=%async_computation.1 | async-start | bytes 1769472 | tf_op jit(solution)/shard_map/all_to_all | solution.py:173
  44.3 3.3 %collective-permute-start.13 = (bf16[4,4,3,16,384]{4,3,2,1,0:T(8,128)(2,1)S(1)}, bf16[4,4,3,16,384]{4,3,2,1,0:T(8,128)(2,1)}, u32[]{:S(2)}, u32[]{:S(2)}) collective-permute-start(bf16[4,4,3,16,384]{4,3,2,1,0:T(8,128)(2,1)S(1)} %bitcast_dynamic-update-slice_fusion.2), channel_id=1, source_target_pairs={{0,16},{16,0},{1,17},{17,1},{2,18},{18,2},{3,19},{19,3},{4,20},{20... | collective-permute-start | bytes 1769480 | tf_op jit(solution)/shard_map/ppermute | solution.py:178
  45.7 1.6 copy-start.16
  45.7 1.6 copy-start.18
  45.7 1.6 copy-start.20
  45.7 1.6 copy-start.21
  72.5 8.8 %collective-permute-start = (bf16[4,4,384]{2,1,0:T(4,128)(2,1)S(1)}, bf16[4,4,384]{2,1,0:T(4,128)(2,1)S(1)}, u32[]{:S(2)}, u32[]{:S(2)}) collective-permute-start(bf16[4,4,384]{2,1,0:T(4,128)(2,1)S(1)} %pad_maximum_fusion.3), channel_id=1, source_target_pairs={{0,64},{64,128},{128,192},{192,0},{1,65},{65,129},{129,193},{193,1... | collective-permute-start | bytes 36872 | tf_op jit(solution)/shard_map/ppermute | solution.py:178
  73.8 7.5 %collective-permute-start.1 = (bf16[4,4,384]{2,1,0:T(4,128)(2,1)S(1)}, bf16[4,4,384]{2,1,0:T(4,128)(2,1)S(1)}, u32[]{:S(2)}, u32[]{:S(2)}) collective-permute-start(bf16[4,4,384]{2,1,0:T(4,128)(2,1)S(1)} %pad_maximum_fusion.3), channel_id=1, source_target_pairs={{0,128},{64,192},{128,0},{192,64},{1,129},{65,193},{129,1},{193,65... | collective-permute-start | bytes 36872 | tf_op jit(solution)/shard_map/ppermute | solution.py:178
  76.2 5.1 %collective-permute-start.2 = (bf16[4,4,384]{2,1,0:T(4,128)(2,1)S(1)}, bf16[4,4,384]{2,1,0:T(4,128)(2,1)S(1)}, u32[]{:S(2)}, u32[]{:S(2)}) collective-permute-start(bf16[4,4,384]{2,1,0:T(4,128)(2,1)S(1)} %pad_maximum_fusion.3), channel_id=1, source_target_pairs={{0,192},{64,0},{128,64},{192,128},{1,193},{65,1},{129,65},{193,129... | collective-permute-start | bytes 36872 | tf_op jit(solution)/shard_map/ppermute | solution.py:178
  77.5 25.6 %copy-start.5 = (bf16[16,384]{1,0:T(8,128)(2,1)S(1)}, bf16[16,384]{1,0:T(8,128)(2,1)}, u32[]{:S(2)}) copy-start(bf16[16,384]{1,0:T(8,128)(2,1)} %tk_ref.3) | copy-start | bytes 36868
  77.5 25.6 %copy-start.6 = (bf16[16,384]{1,0:T(8,128)(2,1)S(1)}, bf16[16,384]{1,0:T(8,128)(2,1)}, u32[]{:S(2)}) copy-start(bf16[16,384]{1,0:T(8,128)(2,1)} %tv_ref.3) | copy-start | bytes 36868
  77.5 25.6 %all-to-all-start.2 = ((bf16[8,128,384]{2,1,0:T(8,128)(2,1)}), bf16[8,128,384]{2,1,0:T(8,128)(2,1)S(1)}, u32[]{:S(2)}, u32[]{:S(2)}) async-start(bf16[8,128,384]{2,1,0:T(8,128)(2,1)} %bitcast.146), calls=%async_computation.2 | async-start | bytes 1572864 | tf_op jit(solution)/shard_map/all_to_all | solution.py:173
  81.5 27.1 %copy-start.12 = (bf16[4,16,384]{2,1,0:T(8,128)(2,1)}, bf16[4,16,384]{2,1,0:T(8,128)(2,1)S(1)}, u32[]{:S(2)}) copy-start(bf16[4,16,384]{2,1,0:T(8,128)(2,1)S(1)} %reshape.147) | copy-start | bytes 147460
  81.5 4.8 %collective-permute-start.3 = (bf16[4,16,384]{2,1,0:T(8,128)(2,1)S(1)}, bf16[4,16,384]{2,1,0:T(8,128)(2,1)S(1)}, u32[]{:S(2)}, u32[]{:S(2)}) collective-permute-start(bf16[4,16,384]{2,1,0:T(8,128)(2,1)S(1)} %reshape.147), channel_id=1, source_target_pairs={{0,1},{1,32},{32,33},{33,0},{2,3},{3,34},{34,35},{35,2},{4,5},{5,3... | collective-permute-start | bytes 147464 | tf_op jit(solution)/shard_map/ppermute | solution.py:178
  81.6 4.7 %collective-permute-start.4 = (bf16[4,16,384]{2,1,0:T(8,128)(2,1)S(1)}, bf16[4,16,384]{2,1,0:T(8,128)(2,1)S(1)}, u32[]{:S(2)}, u32[]{:S(2)}) collective-permute-start(bf16[4,16,384]{2,1,0:T(8,128)(2,1)S(1)} %reshape.147), channel_id=1, source_target_pairs={{0,32},{1,33},{32,0},{33,1},{2,34},{3,35},{34,2},{35,3},{4,36},{5,... | collective-permute-start | bytes 147464 | tf_op jit(solution)/shard_map/ppermute | solution.py:178
  83.3 3.8 %collective-permute-start.5 = (bf16[4,16,384]{2,1,0:T(8,128)(2,1)S(1)}, bf16[4,16,384]{2,1,0:T(8,128)(2,1)S(1)}, u32[]{:S(2)}, u32[]{:S(2)}) collective-permute-start(bf16[4,16,384]{2,1,0:T(8,128)(2,1)S(1)} %reshape.147), channel_id=1, source_target_pairs={{0,33},{1,0},{32,1},{33,32},{2,35},{3,2},{34,3},{35,34},{4,37},{5,... | collective-permute-start | bytes 147464 | tf_op jit(solution)/shard_map/ppermute | solution.py:178
  87.1 3.6 %collective-permute-start.6 = (bf16[4,4,16,384]{3,2,1,0:T(8,128)(2,1)S(1)}, bf16[4,4,16,384]{3,2,1,0:T(8,128)(2,1)S(1)}, u32[]{:S(2)}, u32[]{:S(2)}) collective-permute-start(bf16[4,4,16,384]{3,2,1,0:T(8,128)(2,1)S(1)} %bitcast_dynamic-update-slice_fusion.6), channel_id=1, source_target_pairs={{0,16},{16,0},{1,17},{17,1},{2,18},{18,2},{3,19},{19,3},{4,20},{20... | collective-permute-start | bytes 589832 | tf_op jit(solution)/shard_map/ppermute | solution.py:178
  90.8 17.8 %copy-start.2 = (bf16[2,4,4,16,384]{4,3,2,1,0:T(8,128)(2,1)}, bf16[2,4,4,16,384]{4,3,2,1,0:T(8,128)(2,1)S(1)}, u32[]{:S(2)}) copy-start(bf16[2,4,4,16,384]{4,3,2,1,0:T(8,128)(2,1)S(1)} %bitcast_dynamic-update-slice_fusion) | copy-start | bytes 1179652
  103.1 5.4 %copy-start = (bf16[8,128,384]{2,1,0:T(8,128)(2,1)}, bf16[8,128,384]{2,1,0:T(8,128)(2,1)S(1)}, u32[]{:S(2)}) copy-start(bf16[8,128,384]{2,1,0:T(8,128)(2,1)S(1)} %all-to-all-done.2.v_ref) | copy-start | bytes 2359300
  114.6 13.3 %all-to-all-start.3 = ((f32[16,48,128]{2,1,0:T(8,128)}), f32[16,48,128]{2,1,0:T(8,128)S(1)}, u32[]{:S(2)}, u32[]{:S(2)}) async-start(f32[16,48,128]{2,1,0:T(8,128)} %broadcast_in_dim.124), calls=%async_computation.3 | async-start | bytes 786432 | tf_op jit(solution)/shard_map/all_to_all | solution.py:173
  128.6 1.1 copy-start.1
  129.7 1.0 copy-start.3
  130.7 0.7 copy-start.4
  131.4 0.7 copy-start.7
  146.0 5.1 %collective-permute-start.14 = (bf16[4,4,64,384]{3,2,1,0:T(8,128)(2,1)}, bf16[4,4,64,384]{3,2,1,0:T(8,128)(2,1)}, u32[]{:S(2)}, u32[]{:S(2)}) collective-permute-start(bf16[4,4,64,384]{3,2,1,0:T(8,128)(2,1)} %dynamic-slice_bitcast_fusion), channel_id=1, source_target_pairs={{0,16},{16,0},{1,17},{17,1},{2,18},{18,2},{3,19},{19,3},{4,20},{20... | collective-permute-start | bytes 2359304 | tf_op jit(solution)/shard_map/ppermute | solution.py:178
  147.3 3.7 %copy-start.17 = (f32[128]{0:T(128)S(1)}, f32[128]{0:T(128)}, u32[]{:S(2)}) copy-start(f32[128]{0:T(128)} %param.21) | copy-start | bytes 1540
  147.3 3.7 %copy-start.11 = (bf16[16,384]{1,0:T(8,128)(2,1)S(1)}, bf16[16,384]{1,0:T(8,128)(2,1)}, u32[]{:S(2)}) copy-start(bf16[16,384]{1,0:T(8,128)(2,1)} %param.16) | copy-start | bytes 36868
  147.3 42.1 %all-to-all-start.4 = ((bf16[8,256,384]{2,1,0:T(8,128)(2,1)}), bf16[8,256,384]{2,1,0:T(8,128)(2,1)S(1)}, u32[]{:S(2)}, u32[]{:S(2)}) async-start(bf16[8,256,384]{2,1,0:T(8,128)(2,1)} %get-tuple-element.17), calls=%async_computation.4 | async-start | bytes 3145728 | tf_op jit(solution)/shard_map/all_to_all | solution.py:173
  151.1 4.3 %copy-start.19 = (f32[128]{0:T(128)S(1)}, f32[128]{0:T(128)}, u32[]{:S(2)}) copy-start(f32[128]{0:T(128)} %param.19) | copy-start | bytes 1540
  152.5 15.3 %copy-start.13 = (bf16[4,16,384]{2,1,0:T(8,128)(2,1)S(1)}, bf16[4,16,384]{2,1,0:T(8,128)(2,1)}, u32[]{:S(2)}) copy-start(bf16[4,16,384]{2,1,0:T(8,128)(2,1)} %copy-done.12) | copy-start | bytes 147460
  152.6 12.0 %collective-permute-start.15 = (bf16[4,64,384]{2,1,0:T(8,128)(2,1)S(1)}, bf16[4,64,384]{2,1,0:T(8,128)(2,1)S(1)}, u32[]{:S(2)}, u32[]{:S(2)}) collective-permute-start(bf16[4,64,384]{2,1,0:T(8,128)(2,1)S(1)} %get-tuple-element.63), channel_id=1, source_target_pairs={{0,1},{1,32},{32,33},{33,0},{2,3},{3,34},{34,35},{35,2},{4,5},{5,3... | collective-permute-start | bytes 589832 | tf_op jit(solution)/shard_map/ppermute | solution.py:178
  152.9 11.7 %collective-permute-start.16 = (bf16[4,64,384]{2,1,0:T(8,128)(2,1)S(1)}, bf16[4,64,384]{2,1,0:T(8,128)(2,1)S(1)}, u32[]{:S(2)}, u32[]{:S(2)}) collective-permute-start(bf16[4,64,384]{2,1,0:T(8,128)(2,1)S(1)} %get-tuple-element.65), channel_id=1, source_target_pairs={{0,32},{1,33},{32,0},{33,1},{2,34},{3,35},{34,2},{35,3},{4,36},{5,... | collective-permute-start | bytes 589832 | tf_op jit(solution)/shard_map/ppermute | solution.py:178
  154.1 10.9 %collective-permute-start.17 = (bf16[4,64,384]{2,1,0:T(8,128)(2,1)S(1)}, bf16[4,64,384]{2,1,0:T(8,128)(2,1)S(1)}, u32[]{:S(2)}, u32[]{:S(2)}) collective-permute-start(bf16[4,64,384]{2,1,0:T(8,128)(2,1)S(1)} %get-tuple-element.64), channel_id=1, source_target_pairs={{0,33},{1,0},{32,1},{33,32},{2,35},{3,2},{34,3},{35,34},{4,37},{5,... | collective-permute-start | bytes 589832 | tf_op jit(solution)/shard_map/ppermute | solution.py:178
  165.1 4.9 %collective-permute-start.18 = (bf16[64,384]{1,0:T(8,128)(2,1)S(1)}, bf16[64,384]{1,0:T(8,128)(2,1)S(1)}, u32[]{:S(2)}, u32[]{:S(2)}) collective-permute-start(bf16[64,384]{1,0:T(8,128)(2,1)S(1)} %get-tuple-element.70), channel_id=1, source_target_pairs={{0,64},{64,128},{128,192},{192,0},{1,65},{65,129},{129,193},{193,1... | collective-permute-start | bytes 147464 | tf_op jit(solution)/shard_map/ppermute | solution.py:178
  165.1 5.1 %collective-permute-start.19 = (bf16[64,384]{1,0:T(8,128)(2,1)S(1)}, bf16[64,384]{1,0:T(8,128)(2,1)S(1)}, u32[]{:S(2)}, u32[]{:S(2)}) collective-permute-start(bf16[64,384]{1,0:T(8,128)(2,1)S(1)} %get-tuple-element.72), channel_id=1, source_target_pairs={{0,128},{64,192},{128,0},{192,64},{1,129},{65,193},{129,1},{193,65... | collective-permute-start | bytes 147464 | tf_op jit(solution)/shard_map/ppermute | solution.py:178
  166.9 3.8 %collective-permute-start.20 = (bf16[64,384]{1,0:T(8,128)(2,1)S(1)}, bf16[64,384]{1,0:T(8,128)(2,1)S(1)}, u32[]{:S(2)}, u32[]{:S(2)}) collective-permute-start(bf16[64,384]{1,0:T(8,128)(2,1)S(1)} %get-tuple-element.71), channel_id=1, source_target_pairs={{0,192},{64,0},{128,64},{192,128},{1,193},{65,1},{129,65},{193,129... | collective-permute-start | bytes 147464 | tf_op jit(solution)/shard_map/ppermute | solution.py:178

commit v3 on v2

--- a/solution.py
+++ b/solution.py
@@ -13,7 +13,7 @@
 INV_ROOT = 1.0 / math.sqrt(HD)
 LOG2E = math.log2(math.e)
 PLANE = ("y", "xh", "c", "xl")
-CHIPS = ("y", "xh", "xl")
+FLAT = ("xh", "c", "xl")
 ROW = ("xh", "xl")
 KEY_BLOCK = 256
 NT = (((1,), (1,)), ((), ()))
@@ -52,8 +52,8 @@
 
 def key_parts(k_ref, v_ref, tk_ref, tv_ref, gains_ref):
     parts = []
-    step = KEY_BLOCK // k_ref.shape[1]
-    for start in range(0, k_ref.shape[0], step):
+    step = KEY_BLOCK // v_ref.shape[1]
+    for start in range(0, v_ref.shape[0], step):
         spots = slice(start, start + step)
         key = k_ref[spots].reshape(KEY_BLOCK, HD)
         value = v_ref[spots].reshape(KEY_BLOCK, HD)
@@ -112,60 +112,61 @@
         rows_ref[:, place * part : (place + 1) * part] = block.reshape(groups, part, HD)
 
 
-def column_spec(array):
-    lead = array.shape[:-1]
+def column_spec(shape):
+    lead = tuple(shape[:-1])
     return pl.BlockSpec(lead + (HD,), lambda head: (0,) * len(lead) + (head,))
 
 
-def whole_spec(array):
-    return pl.BlockSpec(array.shape, lambda head: (0,) * array.ndim)
-
-
 PARAMS = pltpu.CompilerParams(vmem_limit_bytes=48 * 1024 * 1024)
+
+
+def operand_specs(operands, gains):
+    win, text, cot, moved_k, moved_v, text_k, text_v = operands
+    shapes = [win.shape, text.shape, cot.shape, moved_v.shape, moved_v.shape]
+    specs = [column_spec(shape) for shape in shapes + [text_k.shape, text_v.shape]]
+    return specs + [pl.BlockSpec(gains.shape, lambda head: (0, 0))]
+
+
+def cost(operands, heads, dots):
+    work = operands[2].shape[0] * operands[4].shape[0] * operands[4].shape[1] * heads
+    return pl.CostEstimate(
+        flops=2 * dots * work * HD, bytes_accessed=2000000 * heads, transcendentals=work
+    )
 
 
 def attention_stats(operands, gains, heads):
     count = operands[2].shape[0]
-    keys = operands[3].shape[0] * operands[3].shape[1]
     return pl.pallas_call(
         stats_kernel,
         grid=(heads,),
-        in_specs=[column_spec(a) for a in operands] + [whole_spec(gains)],
+        in_specs=operand_specs(operands, gains),
         out_specs=pl.BlockSpec((1, 2, count), lambda head: (head, 0, 0)),
         out_shape=jax.ShapeDtypeStruct((heads, 2, count), F32),
         compiler_params=PARAMS,
-        cost_estimate=pl.CostEstimate(
-            flops=4 * count * keys * heads * HD, bytes_accessed=6000000,
-            transcendentals=count * keys * heads,
-        ),
+        cost_estimate=cost(operands, heads, 2),
     )(*operands, gains)
 
 
 def attention_grads(operands, gains, stats, heads, groups):
     count = operands[2].shape[0]
-    keys = operands[3].shape[0] * operands[3].shape[1]
+    z_size, own = operands[4].shape[:2]
     text = operands[5].shape[0]
-    part = count // groups * 2
-    z_size = operands[3].shape[0]
     width = heads * HD
     shapes = [
-        jax.ShapeDtypeStruct((groups, part, width), BF16),
-        jax.ShapeDtypeStruct((z_size, 2 * operands[3].shape[1], width), BF16),
+        jax.ShapeDtypeStruct((groups, count // groups * 2, width), BF16),
+        jax.ShapeDtypeStruct((z_size, 2 * own, width), BF16),
         jax.ShapeDtypeStruct((text, width), BF16),
         jax.ShapeDtypeStruct((text, width), BF16),
     ]
     return pl.pallas_call(
         grads_kernel,
         grid=(heads,),
-        in_specs=[column_spec(a) for a in operands]
-        + [whole_spec(gains), pl.BlockSpec((1, 2, count), lambda head: (head, 0, 0))],
-        out_specs=[column_spec(s) for s in shapes],
+        in_specs=operand_specs(operands, gains)
+        + [pl.BlockSpec((1, 2, count), lambda head: (head, 0, 0))],
+        out_specs=[column_spec(s.shape) for s in shapes],
         out_shape=shapes,
         compiler_params=PARAMS,
-        cost_estimate=pl.CostEstimate(
-            flops=12 * count * keys * heads * HD, bytes_accessed=9000000,
-            transcendentals=count * keys * heads,
-        ),
+        cost_estimate=cost(operands, heads, 6),
     )(*operands, gains, stats)
 
 
@@ -174,6 +175,8 @@
 
 
 def push(array, axes, step):
+    if step == 0:
+        return array
     size = lax.axis_size(axes)
     return lax.ppermute(array, axes, [(i, (i + step) % size) for i in range(size)])
 
@@ -214,38 +217,114 @@
     return sum(piece.astype(F32) for piece in scatter_stage(pieces, axes))
 
 
-def reduce_plane(pieces):
+def reduce_row(pieces):
     shape = pieces.shape[1:]
     pieces = pieces.reshape((lax.axis_size("c"), lax.axis_size(ROW), lax.axis_size("y")) + shape)
     pieces = sum_stage(pieces, "c").astype(BF16)
-    pieces = sum_stage(pieces, ROW).astype(BF16)
-    return sum_stage(pieces, "y")
-
-
-def split_heads(rows, groups):
-    count = rows.shape[0]
-    return rows.reshape(count, groups, -1).transpose(1, 0, 2)
-
-
-def scatter_window(video_q, window):
-    y_size, xl_size, z_size = lax.axis_size("y"), lax.axis_size("xl"), lax.axis_size("z")
-    row, model = video_q.shape[0] // lax.axis_size(PLANE), video_q.shape[1]
-    rest = window >> (xl_size.bit_length() - 1)
-    z_of = rest & (z_size - 1)
-    plane_of = (rest >> (z_size.bit_length() - 1)) * xl_size + (window & (xl_size - 1))
-    pieces = video_q.reshape(-1, y_size, row, model).transpose(1, 0, 2, 3)
-    pieces = swap(pieces.reshape(-1, row, model), PLANE)
-    rows = jnp.concatenate([place(pieces, plane_of[slot]) for slot in range(NWIN)], axis=0)
-    return split_heads(rows, z_size), z_of
-
-
-def pick_window(came, z_of):
-    row = came.shape[1] // NWIN
-    rows = jnp.stack(
-        [place(came, z_of[s])[s * row : (s + 1) * row] for s in range(NWIN)]
-    )
-    rows = gather_stage(rows, "y")
-    return rows.transpose(1, 0, 2, 3).reshape(NWIN, row * lax.axis_size("y"), -1)
+    return sum_stage(pieces, ROW).astype(BF16)
+
+
+def sum_plane(part):
+    for axes in ("c", ROW, "y"):
+        size = lax.axis_size(axes)
+        bit = 1
+        while bit < size:
+            part = part + lax.ppermute(part, axes, [(i, i ^ bit) for i in range(size)])
+            bit *= 2
+    return part
+
+
+def pack_kernel(flat_ref, pieces_ref, k_ref, out_ref):
+    own, rows = k_ref.shape[0], pieces_ref.shape[1]
+    out_ref[0, :own] = k_ref[...]
+    for slot in range(NWIN):
+        start = own + slot * rows
+        out_ref[0, start : start + rows] = pieces_ref[flat_ref[slot]]
+
+
+def pack(flat_of, pieces, video_k, z_size):
+    count, rows, model = pieces.shape
+    own = video_k.shape[0]
+    columns = model // z_size
+    total = own + NWIN * rows
+    return pl.pallas_call(
+        pack_kernel,
+        grid_spec=pltpu.PrefetchScalarGridSpec(
+            num_scalar_prefetch=1,
+            grid=(z_size,),
+            in_specs=[
+                pl.BlockSpec((count, rows, columns), lambda z, _: (0, 0, z)),
+                pl.BlockSpec((own, columns), lambda z, _: (0, z)),
+            ],
+            out_specs=pl.BlockSpec((1, total, columns), lambda z, _: (z, 0, 0)),
+        ),
+        out_shape=jax.ShapeDtypeStruct((z_size, total, columns), BF16),
+    )(flat_of, pieces, video_k)
+
+
+def unpack_kernel(_, came_ref, out_ref):
+    out_ref[...] = came_ref[...]
+
+
+def unpack(z_of, came, own, rows):
+    columns = came.shape[2]
+    first = own // rows
+    return pl.pallas_call(
+        unpack_kernel,
+        grid_spec=pltpu.PrefetchScalarGridSpec(
+            num_scalar_prefetch=1,
+            grid=(NWIN,),
+            in_specs=[
+                pl.BlockSpec((1, rows, columns), lambda s, z_ref: (z_ref[s], first + s, 0))
+            ],
+            out_specs=pl.BlockSpec((1, rows, columns), lambda s, _: (s, 0, 0)),
+        ),
+        out_shape=jax.ShapeDtypeStruct((NWIN, rows, columns), BF16),
+    )(z_of, came)
+
+
+def choose_kernel(info_ref, *refs):
+    parts, (out_ref, own_ref) = refs[:-2], refs[-2:]
+    for slot in range(NWIN):
+        source = info_ref[slot]
+        for index, part in enumerate(parts):
+
+            @pl.when(source == index)
+            def _():
+                out_ref[slot] = part[slot]
+
+    own_ref[...] = out_ref[info_ref[NWIN]]
+
+
+def choose(info, parts):
+    shape = parts[0].shape
+    whole = pl.BlockSpec(memory_space=pltpu.VMEM)
+    return pl.pallas_call(
+        choose_kernel,
+        in_specs=[pl.BlockSpec(memory_space=pltpu.SMEM)] + [whole] * len(parts),
+        out_specs=[whole, whole],
+        out_shape=[
+            jax.ShapeDtypeStruct(shape, BF16), jax.ShapeDtypeStruct(shape[1:], BF16)
+        ],
+    )(info, *parts)
+
+
+def merge_kernel(came_ref, k_ref, v_ref):
+    own = k_ref.shape[0]
+    k_ref[...] = came_ref[0, :own]
+    v_ref[...] = came_ref[0, own:]
+
+
+def merge(came):
+    z_size, rows, width = came.shape
+    out = pl.BlockSpec((rows // 2, width), lambda z: (0, z))
+    return pl.pallas_call(
+        merge_kernel,
+        grid=(z_size,),
+        in_specs=[pl.BlockSpec((1, rows, width), lambda z: (z, 0, 0))],
+        out_specs=[out, out],
+        out_shape=[jax.ShapeDtypeStruct((rows // 2, z_size * width), BF16)] * 2,
+    )(came)
 
 
 def local(
@@ -253,43 +332,52 @@
     gain_video_q, gain_video_k, gain_text_q, gain_text_k,
     window, grad_out_video, grad_out_text,
 ):
-    z_size = lax.axis_size("z")
+    z_size, xl_size = lax.axis_size("z"), lax.axis_size("xl")
+    flat_size, y_size = lax.axis_size(FLAT), lax.axis_size("y")
     groups = lax.axis_size(PLANE)
     own_rows, model = video_q.shape
     columns = model // z_size
     heads = columns // HD
     share = grad_out_video.shape[0]
     gains = jnp.stack((gain_video_q, gain_video_k, gain_text_q, gain_text_k))
+    y = lax.axis_index("y")
+
+    rest = window >> (xl_size.bit_length() - 1)
+    z_of = rest & (z_size - 1)
+    rest = rest >> (z_size.bit_length() - 1)
+    flat_of = (rest & (flat_size // xl_size - 1)) * xl_size + (window & (xl_size - 1))
+    from_y = (y - (rest >> ((flat_size // xl_size).bit_length() - 1))) & (y_size - 1)
+
+    pieces = swap(video_q.reshape(flat_size, -1, model), FLAT)
+    rows = pieces.shape[1]
+    moved_k = swap(pack(flat_of, pieces, video_k, z_size), "z")
 
     text = jnp.stack((text_q, grad_out_video, grad_out_text))
-    every = gather_plane(text)
-    picked, z_of = scatter_window(video_q, window)
-    sent = jnp.concatenate((split_heads(video_k, z_size), picked), axis=1)
-    moved = swap(sent, "z")
-    rows = pick_window(moved[:, own_rows:], z_of)
-    own_window = place(rows, lax.axis_index("y"))
-    sent_v, moved = tie(split_heads(video_v, z_size), moved)
-    moved_v = swap(sent_v, "z")
-    moved_k = moved[:, :own_rows]
-    window_rows = gather_stage(gather_stage(rows, ROW), "c").reshape(-1, columns)
-    text_rows = every[:, 0].reshape(-1, columns)
-    cotangent = jnp.concatenate(
-        (every[:, 1].reshape(-1, columns), every[:, 2].reshape(-1, columns)), axis=0
-    )
+    text, pieces = tie(text, pieces)
+    text = gather_stage(gather_stage(text, "y"), ROW)
+    own = unpack(z_of, moved_k, own_rows, rows)
+    video_v, moved_k = tie(video_v, moved_k)
+    sent = video_v.reshape(own_rows, z_size, columns).transpose(1, 0, 2)
+    moved_v = swap(sent, "z")
+
+    own, own_window = choose(
+        jnp.concatenate((from_y, y[None])), [push(own, "y", step) for step in range(y_size)]
+    )
+    own = gather_stage(own, ROW)
+    own, moved_v = tie(own, moved_v)
+    text = text.transpose(2, 0, 1, 3, 4)
+    halves = gather_stage(jnp.concatenate((own[None], text.reshape((-1,) + own.shape)), 0), "c")
+    window_rows, text_rows, *cotangent = (
+        halves[:, kind].reshape(-1, columns) for kind in range(4)
+    )
+    cotangent = jnp.concatenate(cotangent, axis=0)
     operands = (window_rows, text_rows, cotangent, moved_k, moved_v, text_k, text_v)
 
-    stats = attention_stats(operands, gains, heads)
-    pair = lax.psum(stats, "c").reshape(-1, 128)
-    chips = lax.axis_size(CHIPS)
-    stats = jnp.sum(swap(jnp.broadcast_to(pair[None], (chips,) + pair.shape), CHIPS), axis=0)
-    stats = stats.reshape(heads, 2, -1)
-
-    rows, dmoved, key_text, value_text = attention_grads(operands, gains, stats, heads, groups)
-    returned = swap(dmoved, "z")
-    grad_video_k = returned[:, :own_rows].transpose(1, 0, 2).reshape(own_rows, model)
-    grad_video_v = returned[:, own_rows:].transpose(1, 0, 2).reshape(own_rows, model)
-
-    total = reduce_plane(rows)
+    stats = sum_plane(attention_stats(operands, gains, heads))
+    out, dmoved, key_text, value_text = attention_grads(operands, gains, stats, heads, groups)
+    back = swap(dmoved, "z")
+    total = sum_stage(reduce_row(out), "y")
+    grad_video_k, grad_video_v = merge(back)
 
     def query_grad(raw, gain, cot):
         shape = (raw.shape[0], heads, HD)

time: 196 us -> 196 us (level)
  Pallas kernels: 18.3 us -> 34.7 us
  local copies, waits for them, and re-layouts: 26.4 us -> 18.3 us
  waiting for transfers between devices: 83.6 us -> 76.5 us
  starting transfers between devices: 54.8 us -> 61.2 us
  blocking collectives: 5.22 us -> 0 us
    pallas_call x2 -> x6, Pallas kernels: 18.3 us -> 34.7 us  [the longest x1 12.9 us: attention_grads(): pl.pallas_call(grads_kernel, grid=(heads,), in_specs=operand_specs(operan...]
    ppermute x0 -> x5, starting transfers between devices: none -> 7.73 us  [sum_plane(): part = part + lax.ppermute(part, axes, [(i, i ^ bit) for i in range(size)])]
    ppermute x0 -> x5, waiting for transfers between devices: none -> 7.65 us  [sum_plane(): part = part + lax.ppermute(part, axes, [(i, i ^ bit) for i in range(size)])]
    ppermute x21 -> x20, waiting for transfers between devices: 24.5 us -> 17 us  [push(): lax.ppermute(array, axes, [(i, (i + step) % size) for i in range(size)])]
    all_to_all x5 -> x4, waiting for transfers between devices: 59.2 us -> 51.8 us  [swap(): return lax.all_to_all(array, axes, split_axis=0, concat_axis=0, tiled=True)]
    dynamic_update_slice x19 -> x13, local copies, waits for them, and re-layouts: 1.69 us -> 7.25 us  [put(): lax.dynamic_update_index_in_dim(array, part, index, 0, allow_negative_ind...]
    psum x1 -> x0, blocking collectives: 5.22 us -> none  [local(): pair = lax.psum(stats, 'c').reshape(-1, 128)]
    reshape x6 -> x1, local copies, waits for them, and re-layouts: 5.35 us -> 1.17 us  [local(): sent = video_v.reshape(own_rows, z_size, columns).transpose(1, 0, 2)]
  transfers between devices with their start and end apart: 26 -> 29, of which waited for: 13 -> 20; matrix products, arithmetic and copies ran while one was open for 9% -> 7% of each run, Pallas kernels for 0% -> 3%
where the time goes in v3:
time: 196 us; the launch traced here: 195 us
  waiting for transfers between devices  76.5 us (39%)
  starting transfers between devices  61.2 us (31%)
  Pallas kernels  34.7 us (18%)
  local copies, waits for them, and re-layouts  18.3 us (9%)
  other arithmetic  3.4 us (2%)
    all_to_all x4, waiting for transfers between devices, swap(): return lax.all_to_all(array, axes, split_axis=0, concat_axis=0, tiled=True)  51.8 us
    ppermute x20, starting transfers between devices, push(): lax.ppermute(array, axes, [(i, (i + step) % size) for i in range(size)])  29.2 us
    all_to_all x4, starting transfers between devices, swap(): return lax.all_to_all(array, axes, split_axis=0, concat_axis=0, tiled=True)  24.2 us
    ppermute x20, waiting for transfers between devices, push(): lax.ppermute(array, axes, [(i, (i + step) % size) for i in range(size)])  17 us
    pallas_call x1, Pallas kernels, attention_grads(): pl.pallas_call(grads_kernel, grid=(heads,), in_specs=operand_specs(operan...  12.9 us
    ppermute x5, starting transfers between devices, sum_plane(): part = part + lax.ppermute(part, axes, [(i, i ^ bit) for i in range(size)])  7.73 us
    ppermute x5, waiting for transfers between devices, sum_plane(): part = part + lax.ppermute(part, axes, [(i, i ^ bit) for i in range(size)])  7.65 us
    dynamic_update_slice x13, local copies, waits for them, and re-layouts, put(): lax.dynamic_update_index_in_dim(array, part, index, 0, allow_negative_ind...  7.25 us
  transfers between devices with their start and end apart: 29, of which 20 were waited for; matrix products, arithmetic and copies ran while one was open for 7% of the time, Pallas kernels for 3%

profile of v3, /device:TPU:1, one launch (start us, length us, event | category | flops | bytes accessed | tf_op | source)
XLA Modules:
  0.0 195.1 jit_solution(17791672380621940408)
XLA Ops:
  0.6 6.7 %all-to-all-start = ((bf16[8,16,3072]{2,1,0:T(8,128)(2,1)}), bf16[8,16,3072]{2,1,0:T(8,128)(2,1)S(1)}, u32[]{:S(2)}, u32[]{:S(2)}) async-start(bf16[8,16,3072]{2,1,0:T(8,128)(2,1)} %bitcast.127), calls=%async_computation | async-start | bytes 1572864 | tf_op jit(solution)/shard_map/all_to_all | solution.py:174
  7.9 11.8 %all-to-all-done.pieces_ref = bf16[8,16,3072]{2,1,0:T(8,128)(2,1)S(1)} async-done(((bf16[8,16,3072]{2,1,0:T(8,128)(2,1)}), bf16[8,16,3072]{2,1,0:T(8,128)(2,1)S(1)}, u32[]{:S(2)}, u32[]{:S(2)}) %all-to-all-start) | async-done | bytes 786464 | tf_op jit(solution)/shard_map/all_to_all | solution.py:174
  19.7 0.9 copy-done.11
  20.6 6.1 %shard_map.188 = bf16[8,192,384]{2,1,0:T(8,128)(2,1)} custom-call(s32[4]{0:T(128)} %get-tuple-element.58.flat_ref, bf16[8,16,3072]{2,1,0:T(8,128)(2,1)} %copy-done.11, bf16[128,3072]{1,0:T(8,128)(2,1)} %k_ref.1), custom_call_target="tpu_custom_call" | custom-call | tf_op jit(solution)/shard_map/pallas_call | solution.py:250
  26.7 7.4 %all-to-all-start.1 = ((bf16[8,192,384]{2,1,0:T(8,128)(2,1)}), bf16[8,192,384]{2,1,0:T(8,128)(2,1)S(1)}, u32[]{:S(2)}, u32[]{:S(2)}) async-start(bf16[8,192,384]{2,1,0:T(8,128)(2,1)} %shard_map.188), calls=%async_computation.1 | async-start | bytes 2359296 | tf_op jit(solution)/shard_map/all_to_all | solution.py:174
  34.7 1.4 collective-permute-start.6
  36.1 2.6 %collective-permute-start.7 = (bf16[3,16,384]{2,1,0:T(8,128)(2,1)S(1)}, bf16[3,16,384]{2,1,0:T(8,128)(2,1)S(1)}, u32[]{:S(2)}, u32[]{:S(2)}) collective-permute-start(bf16[3,16,384]{2,1,0:T(8,128)(2,1)S(1)} %pad_maximum_fusion.2), channel_id=1, source_target_pairs={{0,128},{64,192},{128,0},{192,64},{1,129},{65,193},{129,1},{193,65... | collective-permute-start | bytes 110600 | tf_op jit(solution)/shard_map/ppermute | solution.py:181
  38.7 1.1 collective-permute-start.8
  39.8 0.7 broadcast_in_dim.79
  40.4 0.6 bitcast_dynamic-update-slice_fusion.13
  41.1 0.6 bitcast_dynamic-update-slice_fusion.12
  41.7 0.6 bitcast_dynamic-update-slice_fusion.11
  42.3 0.6 bitcast_dynamic-update-slice_fusion.10
  43.2 1.8 collective-permute-start.10
  45.7 0.9 bitcast_dynamic-update-slice_fusion.4
  46.6 19.5 %all-to-all-done.1.came_ref.k_ref = bf16[8,192,384]{2,1,0:T(8,128)(2,1)S(1)} async-done(((bf16[8,192,384]{2,1,0:T(8,128)(2,1)}), bf16[8,192,384]{2,1,0:T(8,128)(2,1)S(1)}, u32[]{:S(2)}, u32[]{:S(2)}) %all-to-all-start.1) | async-done | bytes 1179680 | tf_op jit(solution)/shard_map/all_to_all | solution.py:174
  66.5 1.2 copy.30
  67.7 3.5 %all-to-all-start.2 = ((bf16[8,128,384]{2,1,0:T(8,128)(2,1)}), bf16[8,128,384]{2,1,0:T(8,128)(2,1)S(1)}, u32[]{:S(2)}, u32[]{:S(2)}) async-start(bf16[8,128,384]{2,1,0:T(8,128)(2,1)} %bitcast.7), calls=%async_computation.2 | async-start | bytes 1572864 | tf_op jit(solution)/shard_map/all_to_all | solution.py:174
  71.3 0.9 bitcast_dynamic-update-slice_fusion.3
  72.2 0.9 bitcast_dynamic-update-slice_fusion.2
  73.2 3.3 %shard_map.189.refs_0_ = bf16[4,16,384]{2,1,0:T(8,128)(2,1)} custom-call(s32[4]{0:T(128)} %get-tuple-element.59._, bf16[8,192,384]{2,1,0:T(8,128)(2,1)} %copy-done), custom_call_target="tpu_custom_call" | custom-call | tf_op jit(solution)/shard_map/pallas_call | solution.py:272
  76.5 1.4 collective-permute-start
  77.9 2.6 %collective-permute-start.1 = (bf16[4,16,384]{2,1,0:T(8,128)(2,1)}, bf16[4,16,384]{2,1,0:T(8,128)(2,1)S(1)}, u32[]{:S(2)}, u32[]{:S(2)}) collective-permute-start(bf16[4,16,384]{2,1,0:T(8,128)(2,1)} %shard_map.189.refs_0_), channel_id=1, source_target_pairs={{0,128},{64,192},{128,0},{192,64},{1,129},{65,193},{129,1},{193,65... | collective-permute-start | bytes 147464 | tf_op jit(solution)/shard_map/ppermute | solution.py:181
  80.5 1.1 collective-permute-start.2
  81.5 0.9 bitcast_dynamic-update-slice_fusion.5
  83.0 0.9 collective-permute-done.2.refs_3_
  83.9 0.6 copy-done.18
  84.6 1.6 shard_map.190
  86.4 1.8 collective-permute-start.4
  88.2 0.6 collective-permute-start.5
  88.9 0.8 bitcast_dynamic-update-slice_fusion.9
  89.7 1.1 collective-permute-done.3
  91.9 2.9 %all-to-all-done.2.v_ref = bf16[8,128,384]{2,1,0:T(8,128)(2,1)S(1)} async-done(((bf16[8,128,384]{2,1,0:T(8,128)(2,1)}), bf16[8,128,384]{2,1,0:T(8,128)(2,1)S(1)}, u32[]{:S(2)}, u32[]{:S(2)}) %all-to-all-start.2) | async-done | bytes 786464 | tf_op jit(solution)/shard_map/all_to_all | solution.py:174
  94.9 0.8 collective-permute-start.12
  96.1 1.5 collective-permute-done.12
  98.1 1.7 copy-done.1
  99.8 5.4 %shard_map.191 = f32[3,2,1024]{2,1,0:T(2,128)S(1)} custom-call(bf16[512,384]{1,0:T(8,128)(2,1)S(1)} %bitcast.118, bf16[512,384]{1,0:T(8,128)(2,1)S(1)} %bitcast.116, bf16[1024,384]{1,0:T(8,128)(2,1)S(1)} %pad_maximum_fusion.1.cot_ref, bf16[8,192,384]{2,1,0:T(8,128)(2,1)S(1)} %copy-done.1, bf16[8,128,384]{2,1,0:T(8,128)(2,1)S(1)} %all-to-all-done.2.v_ref, ...), custom_call_target="tpu_custom_call" | custom-call | flops 1610612736 | bytes 6000000 | tf_op jit(solution)/shard_map/pallas_call | solution.py:139
  105.7 0.8 collective-permute-done.13
  106.5 1.0 collective-permute-start.14
  107.5 1.8 collective-permute-done.14
  109.3 1.9 collective-permute-start.15
  111.2 2.4 %collective-permute-done.15 = f32[3,2,1024]{2,1,0:T(2,128)S(1)} collective-permute-done((f32[3,2,1024]{2,1,0:T(2,128)S(1)}, f32[3,2,1024]{2,1,0:T(2,128)S(1)}, u32[]{:S(2)}, u32[]{:S(2)}) %collective-permute-start.15) | collective-permute-done | bytes 24608 | tf_op jit(solution)/shard_map/ppermute | solution.py:232
  113.6 1.4 collective-permute-start.16
  115.0 1.4 collective-permute-done.16
  116.4 3.0 %collective-permute-start.17 = (f32[3,2,1024]{2,1,0:T(2,128)S(1)}, f32[3,2,1024]{2,1,0:T(2,128)S(1)}, u32[]{:S(2)}, u32[]{:S(2)}) collective-permute-start(f32[3,2,1024]{2,1,0:T(2,128)S(1)} %add.99), channel_id=1, source_target_pairs={{0,128},{64,192},{128,0},{192,64},{1,129},{65,193},{129,1},{193,65... | collective-permute-start | bytes 73736 | tf_op jit(solution)/shard_map/ppermute | solution.py:232
  119.4 1.3 collective-permute-done.17
  120.7 1.1 copy-done.3
  121.8 1.0 copy-done.5
  122.8 1.0 copy-done.7
  123.8 0.7 copy-done.10
  124.5 12.9 %shard_map.192 = (bf16[32,64,384]{2,1,0:T(8,128)(2,1)S(1)}, bf16[8,256,384]{2,1,0:T(8,128)(2,1)}, bf16[16,384]{1,0:T(8,128)(2,1)}, bf16[16,384]{1,0:T(8,128)(2,1)}) custom-call(bf16[512,384]{1,0:T(8,128)(2,1)S(1)} %bitcast.119, bf16[512,384]{1,0:T(8,128)(2,1)S(1)} %bitcast.117, bf16[1024,384]{1,0:T(8,128)(2,1)S(1)} %copy-done.3, ...), custom_call_target="tpu_custom_call" | custom-call | flops 4831838208 | bytes 6000000 | tf_op jit(solution)/shard_map/pallas_call | solution.py:161
  137.5 5.0 %collective-permute-start.18 = (bf16[4,4,64,384]{3,2,1,0:T(8,128)(2,1)S(1)}, bf16[4,4,64,384]{3,2,1,0:T(8,128)(2,1)S(1)}, u32[]{:S(2)}, u32[]{:S(2)}) collective-permute-start(bf16[4,4,64,384]{3,2,1,0:T(8,128)(2,1)S(1)} %dynamic-slice_bitcast_fusion), channel_id=1, source_target_pairs={{0,16},{16,0},{1,17},{17,1},{2,18},{18,2},{3,19},{19,3},{4,20},{20... | collective-permute-start | bytes 2359304 | tf_op jit(solution)/shard_map/ppermute | solution.py:181
  142.5 6.6 %all-to-all-start.3 = ((bf16[8,256,384]{2,1,0:T(8,128)(2,1)}), bf16[8,256,384]{2,1,0:T(8,128)(2,1)}, u32[]{:S(2)}, u32[]{:S(2)}) async-start(bf16[8,256,384]{2,1,0:T(8,128)(2,1)} %get-tuple-element.29), calls=%async_computation.3 | async-start | bytes 3145728 | tf_op jit(solution)/shard_map/all_to_all | solution.py:174
  149.5 1.3 collective-permute-start.19
  150.7 2.4 %collective-permute-start.20 = (bf16[4,64,384]{2,1,0:T(8,128)(2,1)S(1)}, bf16[4,64,384]{2,1,0:T(8,128)(2,1)S(1)}, u32[]{:S(2)}, u32[]{:S(2)}) collective-permute-start(bf16[4,64,384]{2,1,0:T(8,128)(2,1)S(1)} %get-tuple-element.46), channel_id=1, source_target_pairs={{0,32},{1,33},{32,0},{33,1},{2,34},{3,35},{34,2},{35,3},{4,36},{5,... | collective-permute-start | bytes 589832 | tf_op jit(solution)/shard_map/ppermute | solution.py:181
  153.4 3.6 %collective-permute-done.19 = bf16[4,64,384]{2,1,0:T(8,128)(2,1)S(1)} collective-permute-done((bf16[4,64,384]{2,1,0:T(8,128)(2,1)S(1)}, bf16[4,64,384]{2,1,0:T(8,128)(2,1)S(1)}, u32[]{:S(2)}, u32[]{:S(2)}) %collective-permute-start.19) | collective-permute-done | bytes 196640 | tf_op jit(solution)/shard_map/ppermute | solution.py:181
  157.0 5.1 %collective-permute-done.20 = bf16[4,64,384]{2,1,0:T(8,128)(2,1)S(1)} collective-permute-done((bf16[4,64,384]{2,1,0:T(8,128)(2,1)S(1)}, bf16[4,64,384]{2,1,0:T(8,128)(2,1)S(1)}, u32[]{:S(2)}, u32[]{:S(2)}) %collective-permute-start.20) | collective-permute-done | bytes 196640 | tf_op jit(solution)/shard_map/ppermute | solution.py:181
  162.8 2.9 %collective-permute-start.23 = (bf16[64,384]{1,0:T(8,128)(2,1)S(1)}, bf16[64,384]{1,0:T(8,128)(2,1)S(1)}, u32[]{:S(2)}, u32[]{:S(2)}) collective-permute-start(bf16[64,384]{1,0:T(8,128)(2,1)S(1)} %get-tuple-element.49), channel_id=1, source_target_pairs={{0,128},{64,192},{128,0},{192,64},{1,129},{65,193},{129,1},{193,65... | collective-permute-start | bytes 147464 | tf_op jit(solution)/shard_map/ppermute | solution.py:181
  166.9 1.1 collective-permute-done.23
  168.0 1.5 collective-permute-done.24
  169.9 0.6 fusion.8
  171.4 0.6 fusion.11
  172.0 17.6 %all-to-all-done.3.came_ref = bf16[8,256,384]{2,1,0:T(8,128)(2,1)} async-done(((bf16[8,256,384]{2,1,0:T(8,128)(2,1)}), bf16[8,256,384]{2,1,0:T(8,128)(2,1)}, u32[]{:S(2)}, u32[]{:S(2)}) %all-to-all-start.3) | async-done | bytes 1572896 | tf_op jit(solution)/shard_map/all_to_all | solution.py:174
  189.7 5.4 %shard_map.193 = (bf16[128,3072]{1,0:T(8,128)(2,1)}, bf16[128,3072]{1,0:T(8,128)(2,1)}) custom-call(bf16[8,256,384]{2,1,0:T(8,128)(2,1)} %all-to-all-done.3.came_ref), custom_call_target="tpu_custom_call" | custom-call | tf_op jit(solution)/shard_map/pallas_call | solution.py:321
  (112 shorter events, 9.6 us)
Async XLA Ops:
  0.6 6.7 %copy-start.25 = (s32[4]{0:T(128)S(1)}, s32[4]{0:T(128)}, u32[]{:S(2)}) copy-start(s32[4]{0:T(128)} %param.23) | copy-start | bytes 52
  0.6 19.1 %all-to-all-start = ((bf16[8,16,3072]{2,1,0:T(8,128)(2,1)}), bf16[8,16,3072]{2,1,0:T(8,128)(2,1)S(1)}, u32[]{:S(2)}, u32[]{:S(2)}) async-start(bf16[8,16,3072]{2,1,0:T(8,128)(2,1)} %bitcast.127), calls=%async_computation | async-start | bytes 1572864 | tf_op jit(solution)/shard_map/all_to_all | solution.py:174
  19.7 0.9 copy-start.11
  26.7 8.0 %copy-start.13 = (bf16[16,384]{1,0:T(8,128)(2,1)S(1)}, bf16[16,384]{1,0:T(8,128)(2,1)}, u32[]{:S(2)}) copy-start(bf16[16,384]{1,0:T(8,128)(2,1)} %param.16) | copy-start | bytes 36868
  26.7 8.0 %copy-start.19 = (bf16[16,384]{1,0:T(8,128)(2,1)S(1)}, bf16[16,384]{1,0:T(8,128)(2,1)}, u32[]{:S(2)}) copy-start(bf16[16,384]{1,0:T(8,128)(2,1)} %param.25) | copy-start | bytes 36868
  26.7 8.0 %copy-start.20 = (bf16[16,384]{1,0:T(8,128)(2,1)S(1)}, bf16[16,384]{1,0:T(8,128)(2,1)}, u32[]{:S(2)}) copy-start(bf16[16,384]{1,0:T(8,128)(2,1)} %param.24) | copy-start | bytes 36868
  26.7 39.5 %copy-start.12 = (bf16[128,3072]{1,0:T(8,128)(2,1)S(1)}, bf16[128,3072]{1,0:T(8,128)(2,1)}, u32[]{:S(2)}) copy-start(bf16[128,3072]{1,0:T(8,128)(2,1)} %param.15) | copy-start | bytes 2359300
  26.7 39.5 %all-to-all-start.1 = ((bf16[8,192,384]{2,1,0:T(8,128)(2,1)}), bf16[8,192,384]{2,1,0:T(8,128)(2,1)S(1)}, u32[]{:S(2)}, u32[]{:S(2)}) async-start(bf16[8,192,384]{2,1,0:T(8,128)(2,1)} %shard_map.188), calls=%async_computation.1 | async-start | bytes 2359296 | tf_op jit(solution)/shard_map/all_to_all | solution.py:174
  34.7 6.4 %collective-permute-start.6 = (bf16[3,16,384]{2,1,0:T(8,128)(2,1)S(1)}, bf16[3,16,384]{2,1,0:T(8,128)(2,1)S(1)}, u32[]{:S(2)}, u32[]{:S(2)}) collective-permute-start(bf16[3,16,384]{2,1,0:T(8,128)(2,1)S(1)} %pad_maximum_fusion.2), channel_id=1, source_target_pairs={{0,64},{64,128},{128,192},{192,0},{1,65},{65,129},{129,193},{193,1... | collective-permute-start | bytes 110600 | tf_op jit(solution)/shard_map/ppermute | solution.py:181
  36.1 5.6 %collective-permute-start.7 = (bf16[3,16,384]{2,1,0:T(8,128)(2,1)S(1)}, bf16[3,16,384]{2,1,0:T(8,128)(2,1)S(1)}, u32[]{:S(2)}, u32[]{:S(2)}) collective-permute-start(bf16[3,16,384]{2,1,0:T(8,128)(2,1)S(1)} %pad_maximum_fusion.2), channel_id=1, source_target_pairs={{0,128},{64,192},{128,0},{192,64},{1,129},{65,193},{129,1},{193,65... | collective-permute-start | bytes 110600 | tf_op jit(solution)/shard_map/ppermute | solution.py:181
  38.7 3.6 %collective-permute-start.8 = (bf16[3,16,384]{2,1,0:T(8,128)(2,1)S(1)}, bf16[3,16,384]{2,1,0:T(8,128)(2,1)S(1)}, u32[]{:S(2)}, u32[]{:S(2)}) collective-permute-start(bf16[3,16,384]{2,1,0:T(8,128)(2,1)S(1)} %pad_maximum_fusion.2), channel_id=1, source_target_pairs={{0,192},{64,0},{128,64},{192,128},{1,193},{65,1},{129,65},{193,129... | collective-permute-start | bytes 110600 | tf_op jit(solution)/shard_map/ppermute | solution.py:181
  42.9 28.3 %collective-permute-start.9 = (bf16[4,3,16,384]{3,2,0,1:T(8,128)(2,1)}, bf16[4,3,16,384]{3,2,0,1:T(8,128)(2,1)}, u32[]{:S(2)}, u32[]{:S(2)}) collective-permute-start(bf16[4,3,16,384]{3,2,0,1:T(8,128)(2,1)} %bitcast_dynamic-update-slice_fusion.10), channel_id=1, source_target_pairs={{0,1},{1,32},{32,33},{33,0},{2,3},{3,34},{34,35},{35,2},{4,5},{5,3... | collective-permute-start | bytes 442376 | tf_op jit(solution)/shard_map/ppermute | solution.py:181
  43.2 29.0 %collective-permute-start.10 = (bf16[4,3,16,384]{3,2,0,1:T(8,128)(2,1)}, bf16[4,3,16,384]{3,2,0,1:T(8,128)(2,1)}, u32[]{:S(2)}, u32[]{:S(2)}) collective-permute-start(bf16[4,3,16,384]{3,2,0,1:T(8,128)(2,1)} %bitcast_dynamic-update-slice_fusion.10), channel_id=1, source_target_pairs={{0,32},{1,33},{32,0},{33,1},{2,34},{3,35},{34,2},{35,3},{4,36},{5,... | collective-permute-start | bytes 442376 | tf_op jit(solution)/shard_map/ppermute | solution.py:181
  45.0 36.5 %collective-permute-start.11 = (bf16[4,3,16,384]{3,2,0,1:T(8,128)(2,1)}, bf16[4,3,16,384]{3,2,0,1:T(8,128)(2,1)}, u32[]{:S(2)}, u32[]{:S(2)}) collective-permute-start(bf16[4,3,16,384]{3,2,0,1:T(8,128)(2,1)} %bitcast_dynamic-update-slice_fusion.10), channel_id=1, source_target_pairs={{0,33},{1,0},{32,1},{33,32},{2,35},{3,2},{34,3},{35,34},{4,37},{5,... | collective-permute-start | bytes 442376 | tf_op jit(solution)/shard_map/ppermute | solution.py:181
  66.2 1.5 copy-start
  67.7 27.1 %all-to-all-start.2 = ((bf16[8,128,384]{2,1,0:T(8,128)(2,1)}), bf16[8,128,384]{2,1,0:T(8,128)(2,1)S(1)}, u32[]{:S(2)}, u32[]{:S(2)}) async-start(bf16[8,128,384]{2,1,0:T(8,128)(2,1)} %bitcast.7), calls=%async_computation.2 | async-start | bytes 1572864 | tf_op jit(solution)/shard_map/all_to_all | solution.py:174
  76.5 19.2 %copy-start.21 = (f32[128]{0:T(128)S(1)}, f32[128]{0:T(128)}, u32[]{:S(2)}) copy-start(f32[128]{0:T(128)} %param.21) | copy-start | bytes 1540
  76.5 19.2 %copy-start.23 = (f32[128]{0:T(128)S(1)}, f32[128]{0:T(128)}, u32[]{:S(2)}) copy-start(f32[128]{0:T(128)} %param.19) | copy-start | bytes 1540
  76.5 19.2 %copy-start.26 = (f32[128]{0:T(128)S(1)}, f32[128]{0:T(128)}, u32[]{:S(2)}) copy-start(f32[128]{0:T(128)} %param.22) | copy-start | bytes 1540
  76.5 19.2 %copy-start.27 = (f32[128]{0:T(128)S(1)}, f32[128]{0:T(128)}, u32[]{:S(2)}) copy-start(f32[128]{0:T(128)} %param.20) | copy-start | bytes 1540
  76.5 6.0 %collective-permute-start = (bf16[4,16,384]{2,1,0:T(8,128)(2,1)}, bf16[4,16,384]{2,1,0:T(8,128)(2,1)S(1)}, u32[]{:S(2)}, u32[]{:S(2)}) collective-permute-start(bf16[4,16,384]{2,1,0:T(8,128)(2,1)} %shard_map.189.refs_0_), channel_id=1, source_target_pairs={{0,64},{64,128},{128,192},{192,0},{1,65},{65,129},{129,193},{193,1... | collective-permute-start | bytes 147464 | tf_op jit(solution)/shard_map/ppermute | solution.py:181
  77.9 5.1 %collective-permute-start.1 = (bf16[4,16,384]{2,1,0:T(8,128)(2,1)}, bf16[4,16,384]{2,1,0:T(8,128)(2,1)S(1)}, u32[]{:S(2)}, u32[]{:S(2)}) collective-permute-start(bf16[4,16,384]{2,1,0:T(8,128)(2,1)} %shard_map.189.refs_0_), channel_id=1, source_target_pairs={{0,128},{64,192},{128,0},{192,64},{1,129},{65,193},{129,1},{193,65... | collective-permute-start | bytes 147464 | tf_op jit(solution)/shard_map/ppermute | solution.py:181
  80.5 3.4 %collective-permute-start.2 = (bf16[4,16,384]{2,1,0:T(8,128)(2,1)}, bf16[4,16,384]{2,1,0:T(8,128)(2,1)S(1)}, u32[]{:S(2)}, u32[]{:S(2)}) collective-permute-start(bf16[4,16,384]{2,1,0:T(8,128)(2,1)} %shard_map.189.refs_0_), channel_id=1, source_target_pairs={{0,192},{64,0},{128,64},{192,128},{1,193},{65,1},{129,65},{193,129... | collective-permute-start | bytes 147464 | tf_op jit(solution)/shard_map/ppermute | solution.py:181
  82.5 1.4 copy-start.16
  83.0 0.9 copy-start.17
  83.9 0.6 copy-start.18
  86.1 4.7 %collective-permute-start.3 = (bf16[4,16,384]{2,1,0:T(8,128)(2,1)}, bf16[4,16,384]{2,1,0:T(8,128)(2,1)S(1)}, u32[]{:S(2)}, u32[]{:S(2)}) collective-permute-start(bf16[4,16,384]{2,1,0:T(8,128)(2,1)} %get-tuple-element.21), channel_id=1, source_target_pairs={{0,1},{1,32},{32,33},{33,0},{2,3},{3,34},{34,35},{35,2},{4,5},{5,3... | collective-permute-start | bytes 147464 | tf_op jit(solution)/shard_map/ppermute | solution.py:181
  86.4 5.0 %collective-permute-start.4 = (bf16[4,16,384]{2,1,0:T(8,128)(2,1)}, bf16[4,16,384]{2,1,0:T(8,128)(2,1)S(1)}, u32[]{:S(2)}, u32[]{:S(2)}) collective-permute-start(bf16[4,16,384]{2,1,0:T(8,128)(2,1)} %get-tuple-element.21), channel_id=1, source_target_pairs={{0,32},{1,33},{32,0},{33,1},{2,34},{3,35},{34,2},{35,3},{4,36},{5,... | collective-permute-start | bytes 147464 | tf_op jit(solution)/shard_map/ppermute | solution.py:181
  88.2 3.7 %collective-permute-start.5 = (bf16[4,16,384]{2,1,0:T(8,128)(2,1)}, bf16[4,16,384]{2,1,0:T(8,128)(2,1)S(1)}, u32[]{:S(2)}, u32[]{:S(2)}) collective-permute-start(bf16[4,16,384]{2,1,0:T(8,128)(2,1)} %get-tuple-element.21), channel_id=1, source_target_pairs={{0,33},{1,0},{32,1},{33,32},{2,35},{3,2},{34,3},{35,34},{4,37},{5,... | collective-permute-start | bytes 147464 | tf_op jit(solution)/shard_map/ppermute | solution.py:181
  94.9 2.7 %collective-permute-start.12 = (bf16[4,4,4,16,384]{4,3,2,1,0:T(8,128)(2,1)S(1)}, bf16[4,4,4,16,384]{4,3,2,1,0:T(8,128)(2,1)S(1)}, u32[]{:S(2)}, u32[]{:S(2)}) collective-permute-start(bf16[4,4,4,16,384]{4,3,2,1,0:T(8,128)(2,1)S(1)} %pad_maximum_fusion), channel_id=1, source_target_pairs={{0,16},{16,0},{1,17},{17,1},{2,18},{18,2},{3,19},{19,3},{4,20},{20... | collective-permute-start | bytes 2359304 | tf_op jit(solution)/shard_map/ppermute | solution.py:181
  97.9 7.3 %copy-start.4 = (bf16[2,1,4,4,16,384]{5,4,3,2,0,1:T(8,128)(2,1)}, bf16[2,1,4,4,16,384]{5,4,3,2,0,1:T(8,128)(2,1)S(1)}, u32[]{:S(2)}) copy-start(bf16[2,1,4,4,16,384]{5,4,3,2,0,1:T(8,128)(2,1)S(1)} %get-tuple-element.42) | copy-start | bytes 1179652
  97.9 7.3 %copy-start.6 = (bf16[2,1,4,4,16,384]{5,4,3,2,0,1:T(8,128)(2,1)}, bf16[2,1,4,4,16,384]{5,4,3,2,0,1:T(8,128)(2,1)S(1)}, u32[]{:S(2)}) copy-start(bf16[2,1,4,4,16,384]{5,4,3,2,0,1:T(8,128)(2,1)S(1)} %get-tuple-element.43) | copy-start | bytes 1179652
  97.9 1.8 copy-start.1
  97.9 1.8 copy-start.8
  98.0 1.8 copy-start.9
  98.1 7.1 %copy-start.2 = (bf16[1024,384]{1,0:T(8,128)(2,1)}, bf16[1024,384]{1,0:T(8,128)(2,1)S(1)}, u32[]{:S(2)}) copy-start(bf16[1024,384]{1,0:T(8,128)(2,1)S(1)} %pad_maximum_fusion.1.cot_ref) | copy-start | bytes 2359300
  105.2 1.3 collective-permute-start.13
  106.5 2.8 %collective-permute-start.14 = (f32[3,2,1024]{2,1,0:T(2,128)S(1)}, f32[3,2,1024]{2,1,0:T(2,128)S(1)}, u32[]{:S(2)}, u32[]{:S(2)}) collective-permute-start(f32[3,2,1024]{2,1,0:T(2,128)S(1)} %add.96), channel_id=1, source_target_pairs={{0,1},{1,0},{32,33},{33,32},{2,3},{3,2},{34,35},{35,34},{4,5},{5,4... | collective-permute-start | bytes 73736 | tf_op jit(solution)/shard_map/ppermute | solution.py:232
  109.3 4.3 %collective-permute-start.15 = (f32[3,2,1024]{2,1,0:T(2,128)S(1)}, f32[3,2,1024]{2,1,0:T(2,128)S(1)}, u32[]{:S(2)}, u32[]{:S(2)}) collective-permute-start(f32[3,2,1024]{2,1,0:T(2,128)S(1)} %add.97), channel_id=1, source_target_pairs={{0,32},{1,33},{32,0},{33,1},{2,34},{3,35},{34,2},{35,3},{4,36},{5,... | collective-permute-start | bytes 73736 | tf_op jit(solution)/shard_map/ppermute | solution.py:232
  113.6 2.8 %collective-permute-start.16 = (f32[3,2,1024]{2,1,0:T(2,128)S(1)}, f32[3,2,1024]{2,1,0:T(2,128)S(1)}, u32[]{:S(2)}, u32[]{:S(2)}) collective-permute-start(f32[3,2,1024]{2,1,0:T(2,128)S(1)} %add.98), channel_id=1, source_target_pairs={{0,64},{64,0},{128,192},{192,128},{1,65},{65,1},{129,193},{193,129... | collective-permute-start | bytes 73736 | tf_op jit(solution)/shard_map/ppermute | solution.py:232
  116.4 4.3 %collective-permute-start.17 = (f32[3,2,1024]{2,1,0:T(2,128)S(1)}, f32[3,2,1024]{2,1,0:T(2,128)S(1)}, u32[]{:S(2)}, u32[]{:S(2)}) collective-permute-start(f32[3,2,1024]{2,1,0:T(2,128)S(1)} %add.99), channel_id=1, source_target_pairs={{0,128},{64,192},{128,0},{192,64},{1,129},{65,193},{129,1},{193,65... | collective-permute-start | bytes 73736 | tf_op jit(solution)/shard_map/ppermute | solution.py:232
  120.7 1.1 copy-start.3
  121.8 1.0 copy-start.5
  122.8 1.0 copy-start.7
  123.8 0.7 copy-start.10
  137.5 11.6 %collective-permute-start.18 = (bf16[4,4,64,384]{3,2,1,0:T(8,128)(2,1)S(1)}, bf16[4,4,64,384]{3,2,1,0:T(8,128)(2,1)S(1)}, u32[]{:S(2)}, u32[]{:S(2)}) collective-permute-start(bf16[4,4,64,384]{3,2,1,0:T(8,128)(2,1)S(1)} %dynamic-slice_bitcast_fusion), channel_id=1, source_target_pairs={{0,16},{16,0},{1,17},{17,1},{2,18},{18,2},{3,19},{19,3},{4,20},{20... | collective-permute-start | bytes 2359304 | tf_op jit(solution)/shard_map/ppermute | solution.py:181
  142.5 47.1 %all-to-all-start.3 = ((bf16[8,256,384]{2,1,0:T(8,128)(2,1)}), bf16[8,256,384]{2,1,0:T(8,128)(2,1)}, u32[]{:S(2)}, u32[]{:S(2)}) async-start(bf16[8,256,384]{2,1,0:T(8,128)(2,1)} %get-tuple-element.29), calls=%async_computation.3 | async-start | bytes 3145728 | tf_op jit(solution)/shard_map/all_to_all | solution.py:174
  149.1 4.3 %copy-start.22 = (f32[128]{0:T(128)S(1)}, f32[128]{0:T(128)}, u32[]{:S(2)}) copy-start(f32[128]{0:T(128)} %param.21) | copy-start | bytes 1540
  149.4 16.9 %copy-start.24 = (f32[128]{0:T(128)S(1)}, f32[128]{0:T(128)}, u32[]{:S(2)}) copy-start(f32[128]{0:T(128)} %param.19) | copy-start | bytes 1540
  149.4 16.9 %copy-start.14 = (bf16[16,384]{1,0:T(8,128)(2,1)S(1)}, bf16[16,384]{1,0:T(8,128)(2,1)}, u32[]{:S(2)}) copy-start(bf16[16,384]{1,0:T(8,128)(2,1)} %param.16) | copy-start | bytes 36868
  149.4 16.9 %copy-start.15 = (bf16[16,384]{1,0:T(8,128)(2,1)S(1)}, bf16[16,384]{1,0:T(8,128)(2,1)}, u32[]{:S(2)}) copy-start(bf16[16,384]{1,0:T(8,128)(2,1)} %get-tuple-element.28) | copy-start | bytes 36868
  149.5 7.6 %collective-permute-start.19 = (bf16[4,64,384]{2,1,0:T(8,128)(2,1)S(1)}, bf16[4,64,384]{2,1,0:T(8,128)(2,1)S(1)}, u32[]{:S(2)}, u32[]{:S(2)}) collective-permute-start(bf16[4,64,384]{2,1,0:T(8,128)(2,1)S(1)} %get-tuple-element.44), channel_id=1, source_target_pairs={{0,1},{1,32},{32,33},{33,0},{2,3},{3,34},{34,35},{35,2},{4,5},{5,3... | collective-permute-start | bytes 589832 | tf_op jit(solution)/shard_map/ppermute | solution.py:181
  150.7 11.4 %collective-permute-start.20 = (bf16[4,64,384]{2,1,0:T(8,128)(2,1)S(1)}, bf16[4,64,384]{2,1,0:T(8,128)(2,1)S(1)}, u32[]{:S(2)}, u32[]{:S(2)}) collective-permute-start(bf16[4,64,384]{2,1,0:T(8,128)(2,1)S(1)} %get-tuple-element.46), channel_id=1, source_target_pairs={{0,32},{1,33},{32,0},{33,1},{2,34},{3,35},{34,2},{35,3},{4,36},{5,... | collective-permute-start | bytes 589832 | tf_op jit(solution)/shard_map/ppermute | solution.py:181
  153.1 9.0 %collective-permute-start.21 = (bf16[4,64,384]{2,1,0:T(8,128)(2,1)S(1)}, bf16[4,64,384]{2,1,0:T(8,128)(2,1)S(1)}, u32[]{:S(2)}, u32[]{:S(2)}) collective-permute-start(bf16[4,64,384]{2,1,0:T(8,128)(2,1)S(1)} %get-tuple-element.45), channel_id=1, source_target_pairs={{0,33},{1,0},{32,1},{33,32},{2,35},{3,2},{34,3},{35,34},{4,37},{5,... | collective-permute-start | bytes 589832 | tf_op jit(solution)/shard_map/ppermute | solution.py:181
  162.3 4.6 %collective-permute-start.22 = (bf16[64,384]{1,0:T(8,128)(2,1)S(1)}, bf16[64,384]{1,0:T(8,128)(2,1)S(1)}, u32[]{:S(2)}, u32[]{:S(2)}) collective-permute-start(bf16[64,384]{1,0:T(8,128)(2,1)S(1)} %get-tuple-element.47), channel_id=1, source_target_pairs={{0,64},{64,128},{128,192},{192,0},{1,65},{65,129},{129,193},{193,1... | collective-permute-start | bytes 147464 | tf_op jit(solution)/shard_map/ppermute | solution.py:181
  162.8 5.2 %collective-permute-start.23 = (bf16[64,384]{1,0:T(8,128)(2,1)S(1)}, bf16[64,384]{1,0:T(8,128)(2,1)S(1)}, u32[]{:S(2)}, u32[]{:S(2)}) collective-permute-start(bf16[64,384]{1,0:T(8,128)(2,1)S(1)} %get-tuple-element.49), channel_id=1, source_target_pairs={{0,128},{64,192},{128,0},{192,64},{1,129},{65,193},{129,1},{193,65... | collective-permute-start | bytes 147464 | tf_op jit(solution)/shard_map/ppermute | solution.py:181
  165.8 3.7 %collective-permute-start.24 = (bf16[64,384]{1,0:T(8,128)(2,1)S(1)}, bf16[64,384]{1,0:T(8,128)(2,1)S(1)}, u32[]{:S(2)}, u32[]{:S(2)}) collective-permute-start(bf16[64,384]{1,0:T(8,128)(2,1)S(1)} %get-tuple-element.48), channel_id=1, source_target_pairs={{0,192},{64,0},{128,64},{192,128},{1,193},{65,1},{129,65},{193,129... | collective-permute-start | bytes 147464 | tf_op jit(solution)/shard_map/ppermute | solution.py:181

commit v4 on v3

--- a/solution.py
+++ b/solution.py
@@ -13,9 +13,9 @@
 INV_ROOT = 1.0 / math.sqrt(HD)
 LOG2E = math.log2(math.e)
 PLANE = ("y", "xh", "c", "xl")
-FLAT = ("xh", "c", "xl")
 ROW = ("xh", "xl")
 KEY_BLOCK = 256
+VMEM = 48 * 1024 * 1024
 NT = (((1,), (1,)), ((), ()))
 NN = (((1,), (0,)), ((), ()))
 TN = (((0,), (0,)), ((), ()))
@@ -117,7 +117,7 @@
     return pl.BlockSpec(lead + (HD,), lambda head: (0,) * len(lead) + (head,))
 
 
-PARAMS = pltpu.CompilerParams(vmem_limit_bytes=48 * 1024 * 1024)
+PARAMS = pltpu.CompilerParams(vmem_limit_bytes=VMEM)
 
 
 def operand_specs(operands, gains):
@@ -234,96 +234,71 @@
     return part
 
 
-def pack_kernel(flat_ref, pieces_ref, k_ref, out_ref):
-    own, rows = k_ref.shape[0], pieces_ref.shape[1]
-    out_ref[0, :own] = k_ref[...]
-    for slot in range(NWIN):
-        start = own + slot * rows
-        out_ref[0, start : start + rows] = pieces_ref[flat_ref[slot]]
-
-
-def pack(flat_of, pieces, video_k, z_size):
-    count, rows, model = pieces.shape
-    own = video_k.shape[0]
-    columns = model // z_size
-    total = own + NWIN * rows
-    return pl.pallas_call(
-        pack_kernel,
-        grid_spec=pltpu.PrefetchScalarGridSpec(
-            num_scalar_prefetch=1,
-            grid=(z_size,),
-            in_specs=[
-                pl.BlockSpec((count, rows, columns), lambda z, _: (0, 0, z)),
-                pl.BlockSpec((own, columns), lambda z, _: (0, z)),
-            ],
-            out_specs=pl.BlockSpec((1, total, columns), lambda z, _: (z, 0, 0)),
-        ),
-        out_shape=jax.ShapeDtypeStruct((z_size, total, columns), BF16),
-    )(flat_of, pieces, video_k)
-
-
-def unpack_kernel(_, came_ref, out_ref):
-    out_ref[...] = came_ref[...]
-
-
-def unpack(z_of, came, own, rows):
-    columns = came.shape[2]
-    first = own // rows
-    return pl.pallas_call(
-        unpack_kernel,
-        grid_spec=pltpu.PrefetchScalarGridSpec(
-            num_scalar_prefetch=1,
-            grid=(NWIN,),
-            in_specs=[
-                pl.BlockSpec((1, rows, columns), lambda s, z_ref: (z_ref[s], first + s, 0))
-            ],
-            out_specs=pl.BlockSpec((1, rows, columns), lambda s, _: (s, 0, 0)),
-        ),
-        out_shape=jax.ShapeDtypeStruct((NWIN, rows, columns), BF16),
-    )(z_of, came)
-
-
-def choose_kernel(info_ref, *refs):
-    parts, (out_ref, own_ref) = refs[:-2], refs[-2:]
-    for slot in range(NWIN):
-        source = info_ref[slot]
-        for index, part in enumerate(parts):
-
-            @pl.when(source == index)
-            def _():
-                out_ref[slot] = part[slot]
-
-    own_ref[...] = out_ref[info_ref[NWIN]]
-
-
-def choose(info, parts):
-    shape = parts[0].shape
-    whole = pl.BlockSpec(memory_space=pltpu.VMEM)
-    return pl.pallas_call(
-        choose_kernel,
-        in_specs=[pl.BlockSpec(memory_space=pltpu.SMEM)] + [whole] * len(parts),
-        out_specs=[whole, whole],
-        out_shape=[
-            jax.ShapeDtypeStruct(shape, BF16), jax.ShapeDtypeStruct(shape[1:], BF16)
-        ],
-    )(info, *parts)
-
-
-def merge_kernel(came_ref, k_ref, v_ref):
+def fetch_window(video_q, window):
+    y, x, c = (lax.axis_index(axes) for axes in ("y", ROW, "c"))
+    xl_size, z_size = lax.axis_size("xl"), lax.axis_size("z")
+    y_size, x_size, c_size = lax.axis_size("y"), lax.axis_size(ROW), lax.axis_size("c")
+    xh_size = x_size // xl_size
+    model = video_q.shape[1]
+
+    block = lax.dynamic_slice_in_dim(
+        jnp.concatenate((window, window)), y, NWIN, 0, allow_negative_indices=False
+    )
+    xl_of = block & (xl_size - 1)
+    rest = block >> (xl_size.bit_length() - 1)
+    z_of = rest & (z_size - 1)
+    rest = rest >> (z_size.bit_length() - 1)
+    c_of = rest & (c_size - 1)
+    rest = rest >> (c_size.bit_length() - 1)
+    xh_of = rest & (xh_size - 1)
+    y_of = rest >> (xh_size.bit_length() - 1)
+    from_x = (x - xh_of * xl_size - xl_of) & (x_size - 1)
+    source = from_x * c_size + ((c - c_of) & (c_size - 1))
+    from_y = (y - y_of[0]) & (y_size - 1)
+
+    pieces = video_q.reshape(xh_size, c_size, xl_size, -1, model).transpose(1, 0, 2, 3, 4)
+    pieces = pieces.reshape(c_size, x_size, -1, model)
+    pieces = jnp.stack(scatter_stage(pieces, "c"), axis=1)
+    pieces = jnp.concatenate(scatter_stage(pieces, ROW), axis=0)
+    came = [place(pieces, source[0])] + [
+        push(place(pieces, source[step]), "y", step) for step in range(1, y_size)
+    ]
+    return place(jnp.stack(came), from_y), z_of[0]
+
+
+def split_heads(rows, groups):
+    count = rows.shape[0]
+    return rows.reshape(count, groups, -1).transpose(1, 0, 2)
+
+
+def merge_kernel(came_ref, k_ref, v_ref, sems):
     own = k_ref.shape[0]
-    k_ref[...] = came_ref[0, :own]
-    v_ref[...] = came_ref[0, own:]
+    z_size, _, width = came_ref.shape
+    copies = []
+    for z in range(z_size):
+        for part, ref in enumerate((k_ref, v_ref)):
+            copies.append(
+                pltpu.make_async_copy(
+                    came_ref.at[z, pl.ds(part * own, own)],
+                    ref.at[:, pl.ds(z * width, width)],
+                    sems.at[z, part],
+                )
+            )
+    for copy in copies:
+        copy.start()
+    for copy in copies:
+        copy.wait()
 
 
 def merge(came):
     z_size, rows, width = came.shape
-    out = pl.BlockSpec((rows // 2, width), lambda z: (0, z))
+    anywhere = pl.BlockSpec(memory_space=pl.ANY)
     return pl.pallas_call(
         merge_kernel,
-        grid=(z_size,),
-        in_specs=[pl.BlockSpec((1, rows, width), lambda z: (z, 0, 0))],
-        out_specs=[out, out],
+        in_specs=[pl.BlockSpec(memory_space=pltpu.VMEM)],
+        out_specs=[anywhere, anywhere],
         out_shape=[jax.ShapeDtypeStruct((rows // 2, z_size * width), BF16)] * 2,
+        scratch_shapes=[pltpu.SemaphoreType.DMA((z_size, 2))],
     )(came)
 
 
@@ -332,44 +307,26 @@
     gain_video_q, gain_video_k, gain_text_q, gain_text_k,
     window, grad_out_video, grad_out_text,
 ):
-    z_size, xl_size = lax.axis_size("z"), lax.axis_size("xl")
-    flat_size, y_size = lax.axis_size(FLAT), lax.axis_size("y")
+    z_size = lax.axis_size("z")
     groups = lax.axis_size(PLANE)
     own_rows, model = video_q.shape
     columns = model // z_size
     heads = columns // HD
     share = grad_out_video.shape[0]
     gains = jnp.stack((gain_video_q, gain_video_k, gain_text_q, gain_text_k))
-    y = lax.axis_index("y")
-
-    rest = window >> (xl_size.bit_length() - 1)
-    z_of = rest & (z_size - 1)
-    rest = rest >> (z_size.bit_length() - 1)
-    flat_of = (rest & (flat_size // xl_size - 1)) * xl_size + (window & (xl_size - 1))
-    from_y = (y - (rest >> ((flat_size // xl_size).bit_length() - 1))) & (y_size - 1)
-
-    pieces = swap(video_q.reshape(flat_size, -1, model), FLAT)
-    rows = pieces.shape[1]
-    moved_k = swap(pack(flat_of, pieces, video_k, z_size), "z")
-
-    text = jnp.stack((text_q, grad_out_video, grad_out_text))
-    text, pieces = tie(text, pieces)
-    text = gather_stage(gather_stage(text, "y"), ROW)
-    own = unpack(z_of, moved_k, own_rows, rows)
-    video_v, moved_k = tie(video_v, moved_k)
-    sent = video_v.reshape(own_rows, z_size, columns).transpose(1, 0, 2)
-    moved_v = swap(sent, "z")
-
-    own, own_window = choose(
-        jnp.concatenate((from_y, y[None])), [push(own, "y", step) for step in range(y_size)]
-    )
-    own = gather_stage(own, ROW)
+
+    moved_k = swap(split_heads(video_k, z_size), "z")
+    picked, z_of = fetch_window(video_q, window)
+    picked, moved_k = tie(picked, moved_k)
+    came = swap(split_heads(picked, z_size), "z")
+    own_window = place(came, z_of)
+    sent_v, own_window = tie(split_heads(video_v, z_size), own_window)
+    moved_v = swap(sent_v, "z")
+    own = jnp.stack((own_window, text_q, grad_out_video, grad_out_text))
+    own = gather_stage(gather_stage(own, "y"), ROW)
     own, moved_v = tie(own, moved_v)
-    text = text.transpose(2, 0, 1, 3, 4)
-    halves = gather_stage(jnp.concatenate((own[None], text.reshape((-1,) + own.shape)), 0), "c")
-    window_rows, text_rows, *cotangent = (
-        halves[:, kind].reshape(-1, columns) for kind in range(4)
-    )
+    own = gather_stage(own.transpose(2, 0, 1, 3, 4), "c")
+    window_rows, text_rows, *cotangent = (own[:, kind].reshape(-1, columns) for kind in range(4))
     cotangent = jnp.concatenate(cotangent, axis=0)
     operands = (window_rows, text_rows, cotangent, moved_k, moved_v, text_k, text_v)
 

time: 196 us -> 174 us (0.89)
  Pallas kernels: 34.7 us -> 21 us
  waiting for transfers between devices: 76.5 us -> 67.4 us
  local copies, waits for them, and re-layouts: 18.3 us -> 13.3 us
  starting transfers between devices: 61.2 us -> 65.7 us
    all_to_all x4, waiting for transfers between devices: 51.8 us -> 31.4 us  [swap(): return lax.all_to_all(array, axes, split_axis=0, concat_axis=0, tiled=True)]
    pallas_call x4 -> x1, Pallas kernels: 16.4 us -> 2.67 us  [merge(): pl.pallas_call(merge_kernel, in_specs=[pl.BlockSpec(memory_space=pltpu.VM...]
    ppermute x20 -> x21, waiting for transfers between devices: 17 us -> 28.5 us  [push(): lax.ppermute(array, axes, [(i, (i + step) % size) for i in range(size)])]
    ppermute x20 -> x21, starting transfers between devices: 29.2 us -> 37.7 us  [push(): lax.ppermute(array, axes, [(i, (i + step) % size) for i in range(size)])]
    dynamic_update_slice x13 -> x9, local copies, waits for them, and re-layouts: 7.25 us -> 0.51 us  [put(): lax.dynamic_update_index_in_dim(array, part, index, 0, allow_negative_ind...]
    unnamed x56 -> x29, local copies, waits for them, and re-layouts: 7.13 us -> 2.6 us
    all_to_all x4, starting transfers between devices: 24.2 us -> 20.1 us  [swap(): return lax.all_to_all(array, axes, split_axis=0, concat_axis=0, tiled=True)]
    squeeze x3 -> x6, local copies, waits for them, and re-layouts: 0.19 us -> 3.86 us  [place(): lax.dynamic_index_in_dim(array, index, 0, keepdims=False, allow_negative_...]
  transfers between devices with their start and end apart: 29 -> 30, of which waited for: 20 -> 20; matrix products, arithmetic and copies ran while one was open for 7% -> 7% of each run, Pallas kernels for 3% -> 0%
where the time goes in v4:
time: 174 us; the launch traced here: 172 us
  waiting for transfers between devices  67.4 us (39%)
  starting transfers between devices  65.7 us (38%)
  Pallas kernels  21 us (12%)
  local copies, waits for them, and re-layouts  13.3 us (8%)
  other arithmetic  3.6 us (2%)
    ppermute x21, starting transfers between devices, push(): lax.ppermute(array, axes, [(i, (i + step) % size) for i in range(size)])  37.7 us
    all_to_all x4, waiting for transfers between devices, swap(): return lax.all_to_all(array, axes, split_axis=0, concat_axis=0, tiled=True)  31.4 us
    ppermute x21, waiting for transfers between devices, push(): lax.ppermute(array, axes, [(i, (i + step) % size) for i in range(size)])  28.5 us
    all_to_all x4, starting transfers between devices, swap(): return lax.all_to_all(array, axes, split_axis=0, concat_axis=0, tiled=True)  20.1 us
    pallas_call x1, Pallas kernels, attention_grads(): pl.pallas_call(grads_kernel, grid=(heads,), in_specs=operand_specs(operan...  12.9 us
    ppermute x5, starting transfers between devices, sum_plane(): part = part + lax.ppermute(part, axes, [(i, i ^ bit) for i in range(size)])  7.91 us
    ppermute x5, waiting for transfers between devices, sum_plane(): part = part + lax.ppermute(part, axes, [(i, i ^ bit) for i in range(size)])  7.47 us
    pallas_call x1, Pallas kernels, attention_stats(): pl.pallas_call(stats_kernel, grid=(heads,), in_specs=operand_specs(operan...  5.39 us
  transfers between devices with their start and end apart: 30, of which 20 were waited for; matrix products, arithmetic and copies ran while one was open for 7% of the time, Pallas kernels for 0%

profile of v4, /device:TPU:1, one launch (start us, length us, event | category | flops | bytes accessed | tf_op | source)
XLA Modules:
  0.0 172.4 jit_solution(16511922329184714152)
XLA Ops:
  0.6 1.3 copy.56
  2.0 3.3 %collective-permute-start = (bf16[4,16,3072]{2,1,0:T(8,128)(2,1)S(1)}, bf16[4,16,3072]{2,1,0:T(8,128)(2,1)S(1)}, u32[]{:S(2)}, u32[]{:S(2)}) collective-permute-start(bf16[4,16,3072]{2,1,0:T(8,128)(2,1)S(1)} %get-tuple-element.53), channel_id=1, source_target_pairs={{0,16},{16,0},{1,17},{17,1},{2,18},{18,2},{3,19},{19,3},{4,20},{20... | collective-permute-start | bytes 1179656 | tf_op jit(solution)/shard_map/ppermute | solution.py:181
  5.3 0.4 copy.57
  5.7 1.2 copy.58
  6.9 6.5 %all-to-all-start = ((bf16[8,128,384]{2,1,0:T(8,128)(2,1)}), bf16[8,128,384]{2,1,0:T(8,128)(2,1)S(1)}, u32[]{:S(2)}, u32[]{:S(2)}) async-start(bf16[8,128,384]{2,1,0:T(8,128)(2,1)} %bitcast.25), calls=%async_computation | async-start | bytes 1572864 | tf_op jit(solution)/shard_map/all_to_all | solution.py:174
  13.5 1.3 collective-permute-start.1
  14.8 2.5 %collective-permute-start.2 = (bf16[2,16,3072]{2,1,0:T(8,128)(2,1)S(1)}, bf16[2,16,3072]{2,1,0:T(8,128)(2,1)S(1)}, u32[]{:S(2)}, u32[]{:S(2)}) collective-permute-start(bf16[2,16,3072]{2,1,0:T(8,128)(2,1)S(1)} %get-tuple-element.51), channel_id=1, source_target_pairs={{0,32},{1,33},{32,0},{33,1},{2,34},{3,35},{34,2},{35,3},{4,36},{5,... | collective-permute-start | bytes 589832 | tf_op jit(solution)/shard_map/ppermute | solution.py:181
  17.2 1.2 collective-permute-start.3
  18.5 0.6 fusion.28
  19.1 1.9 %collective-permute-done.1 = bf16[2,16,3072]{2,1,0:T(8,128)(2,1)S(1)} collective-permute-done((bf16[2,16,3072]{2,1,0:T(8,128)(2,1)S(1)}, bf16[2,16,3072]{2,1,0:T(8,128)(2,1)S(1)}, u32[]{:S(2)}, u32[]{:S(2)}) %collective-permute-start.1) | collective-permute-done | bytes 196640 | tf_op jit(solution)/shard_map/ppermute | solution.py:181
  21.0 5.2 %collective-permute-done.2 = bf16[2,16,3072]{2,1,0:T(8,128)(2,1)S(1)} collective-permute-done((bf16[2,16,3072]{2,1,0:T(8,128)(2,1)S(1)}, bf16[2,16,3072]{2,1,0:T(8,128)(2,1)S(1)}, u32[]{:S(2)}, u32[]{:S(2)}) %collective-permute-start.2) | collective-permute-done | bytes 196640 | tf_op jit(solution)/shard_map/ppermute | solution.py:181
  26.3 2.7 %dynamic-slice_bitcast_fusion.6 = (bf16[16,3072]{1,0:T(8,128)(2,1)S(1)}, bf16[16,3072]{1,0:T(8,128)(2,1)S(1)}, bf16[16,3072]{1,0:T(8,128)(2,1)S(1)}, bf16[1,16,3072]{2,1,0:T(8,128)(2,1)S(1)}) fusion(bf16[8,16,3072]{2,1,0:T(8,128)(2,1)S(1)} %pad_maximum_fusion, s32[]{:T(128)} %bitcast.19, s32[]{:T(128)} %bitcast.16, s32[]{:T(128)} %bitcast.13, s32[]{:T(128)} %bitcast.12), kind=kLoop, calls=%fused_computation.47 | loop fusion | bytes 786448 | tf_op jit(solution)/shard_map/jit(dynamic_index_in_dim)/squeeze | solution.py:185
  29.0 1.4 collective-permute-start.4
  30.3 2.6 %collective-permute-start.5 = (bf16[16,3072]{1,0:T(8,128)(2,1)S(1)}, bf16[16,3072]{1,0:T(8,128)(2,1)S(1)}, u32[]{:S(2)}, u32[]{:S(2)}) collective-permute-start(bf16[16,3072]{1,0:T(8,128)(2,1)S(1)} %get-tuple-element.46), channel_id=1, source_target_pairs={{0,128},{64,192},{128,0},{192,64},{1,129},{65,193},{129,1},{193,65... | collective-permute-start | bytes 294920 | tf_op jit(solution)/shard_map/ppermute | solution.py:181
  33.0 1.1 collective-permute-start.6
  34.1 2.7 %collective-permute-done.5 = bf16[16,3072]{1,0:T(8,128)(2,1)S(1)} collective-permute-done((bf16[16,3072]{1,0:T(8,128)(2,1)S(1)}, bf16[16,3072]{1,0:T(8,128)(2,1)S(1)}, u32[]{:S(2)}, u32[]{:S(2)}) %collective-permute-start.5) | collective-permute-done | bytes 98336 | tf_op jit(solution)/shard_map/ppermute | solution.py:181
  36.8 0.7 collective-permute-done.6
  37.6 0.7 copy.59
  38.3 6.5 %all-to-all-start.1 = ((bf16[8,16,384]{2,1,0:T(8,128)(2,1)}), bf16[8,16,384]{2,1,0:T(8,128)(2,1)S(1)}, u32[]{:S(2)}, u32[]{:S(2)}) async-start(bf16[8,16,384]{2,1,0:T(8,128)(2,1)} %copy.59), calls=%async_computation.1 | async-start | bytes 196608 | tf_op jit(solution)/shard_map/all_to_all | solution.py:174
  44.8 0.4 copy.54
  45.2 1.2 copy.55
  46.4 6.1 %all-to-all-done.1 = bf16[8,16,384]{2,1,0:T(8,128)(2,1)S(1)} async-done(((bf16[8,16,384]{2,1,0:T(8,128)(2,1)}), bf16[8,16,384]{2,1,0:T(8,128)(2,1)S(1)}, u32[]{:S(2)}, u32[]{:S(2)}) %all-to-all-start.1) | async-done | bytes 98336 | tf_op jit(solution)/shard_map/all_to_all | solution.py:174
  52.7 3.3 %collective-permute-start.8 = (bf16[4,16,384]{2,1,0:T(8,128)(2,1)S(1)}, bf16[4,16,384]{2,1,0:T(8,128)(2,1)S(1)}, u32[]{:S(2)}, u32[]{:S(2)}) collective-permute-start(bf16[4,16,384]{2,1,0:T(8,128)(2,1)S(1)} %pad_maximum_fusion.2), channel_id=1, source_target_pairs={{0,128},{64,192},{128,0},{192,64},{1,129},{65,193},{129,1},{193,65... | collective-permute-start | bytes 147464 | tf_op jit(solution)/shard_map/ppermute | solution.py:181
  56.1 3.6 %all-to-all-start.2 = ((bf16[8,128,384]{2,1,0:T(8,128)(2,1)}), bf16[8,128,384]{2,1,0:T(8,128)(2,1)S(1)}, u32[]{:S(2)}, u32[]{:S(2)}) async-start(bf16[8,128,384]{2,1,0:T(8,128)(2,1)} %bitcast.1), calls=%async_computation.2 | async-start | bytes 1572864 | tf_op jit(solution)/shard_map/all_to_all | solution.py:174
  59.8 1.3 collective-permute-start.10
  61.1 2.9 %collective-permute-start.11 = (bf16[4,4,16,384]{3,2,0,1:T(8,128)(2,1)S(1)}, bf16[4,4,16,384]{3,2,0,1:T(8,128)(2,1)S(1)}, u32[]{:S(2)}, u32[]{:S(2)}) collective-permute-start(bf16[4,4,16,384]{3,2,0,1:T(8,128)(2,1)S(1)} %bitcast_dynamic-update-slice_fusion.6), channel_id=1, source_target_pairs={{0,32},{1,33},{32,0},{33,1},{2,34},{3,35},{34,2},{35,3},{4,36},{5,... | collective-permute-start | bytes 589832 | tf_op jit(solution)/shard_map/ppermute | solution.py:181
  64.2 1.7 %collective-permute-done.10 = bf16[4,4,16,384]{3,2,0,1:T(8,128)(2,1)S(1)} collective-permute-done((bf16[4,4,16,384]{3,2,0,1:T(8,128)(2,1)S(1)}, bf16[4,4,16,384]{3,2,0,1:T(8,128)(2,1)S(1)}, u32[]{:S(2)}, u32[]{:S(2)}) %collective-permute-start.10) | collective-permute-done | bytes 196640 | tf_op jit(solution)/shard_map/ppermute | solution.py:181
  65.9 3.3 %collective-permute-done.11 = bf16[4,4,16,384]{3,2,0,1:T(8,128)(2,1)S(1)} collective-permute-done((bf16[4,4,16,384]{3,2,0,1:T(8,128)(2,1)S(1)}, bf16[4,4,16,384]{3,2,0,1:T(8,128)(2,1)S(1)}, u32[]{:S(2)}, u32[]{:S(2)}) %collective-permute-start.11) | collective-permute-done | bytes 196640 | tf_op jit(solution)/shard_map/ppermute | solution.py:181
  69.4 10.2 %all-to-all-done.2.v_ref = bf16[8,128,384]{2,1,0:T(8,128)(2,1)S(1)} async-done(((bf16[8,128,384]{2,1,0:T(8,128)(2,1)}), bf16[8,128,384]{2,1,0:T(8,128)(2,1)S(1)}, u32[]{:S(2)}, u32[]{:S(2)}) %all-to-all-start.2) | async-done | bytes 786464 | tf_op jit(solution)/shard_map/all_to_all | solution.py:174
  79.6 4.1 %collective-permute-start.13 = (bf16[4,4,4,16,384]{4,3,2,1,0:T(8,128)(2,1)S(1)}, bf16[4,4,4,16,384]{4,3,2,1,0:T(8,128)(2,1)S(1)}, u32[]{:S(2)}, u32[]{:S(2)}) collective-permute-start(bf16[4,4,4,16,384]{4,3,2,1,0:T(8,128)(2,1)S(1)} %bitcast.157), channel_id=1, source_target_pairs={{0,16},{16,0},{1,17},{17,1},{2,18},{18,2},{3,19},{19,3},{4,20},{20... | collective-permute-start | bytes 2359304 | tf_op jit(solution)/shard_map/ppermute | solution.py:181
  84.1 1.5 collective-permute-done.13
  86.0 0.6 copy-done
  86.6 5.4 %shard_map.188 = f32[3,2,1024]{2,1,0:T(2,128)S(1)} custom-call(bf16[512,384]{1,0:T(8,128)(2,1)S(1)} %bitcast.153, bf16[512,384]{1,0:T(8,128)(2,1)S(1)} %bitcast.151, bf16[1024,384]{1,0:T(8,128)(2,1)S(1)} %pad_maximum_fusion.1.cot_ref, bf16[8,128,384]{2,1,0:T(8,128)(2,1)S(1)} %all-to-all-done.k_ref, bf16[8,128,384]{2,1,0:T(8,128)(2,1)S(1)} %all-to-all-done.2.v_ref, ...), custom_call_target="tpu_custom_call" | custom-call | flops 1610612736 | bytes 6000000 | tf_op jit(solution)/shard_map/pallas_call | solution.py:139
  92.0 0.5 collective-permute-start.14
  92.5 0.8 collective-permute-done.14
  93.4 1.3 collective-permute-start.15
  94.7 1.4 collective-permute-done.15
  96.1 2.8 %collective-permute-start.16 = (f32[3,2,1024]{2,1,0:T(2,128)S(1)}, f32[3,2,1024]{2,1,0:T(2,128)S(1)}, u32[]{:S(2)}, u32[]{:S(2)}) collective-permute-start(f32[3,2,1024]{2,1,0:T(2,128)S(1)} %add.106), channel_id=1, source_target_pairs={{0,32},{1,33},{32,0},{33,1},{2,34},{3,35},{34,2},{35,3},{4,36},{5,... | collective-permute-start | bytes 73736 | tf_op jit(solution)/shard_map/ppermute | solution.py:232
  98.9 1.5 collective-permute-done.16
  100.4 1.6 collective-permute-start.17
  102.0 1.2 collective-permute-done.17
  103.2 1.8 %collective-permute-start.18 = (f32[3,2,1024]{2,1,0:T(2,128)S(1)}, f32[3,2,1024]{2,1,0:T(2,128)S(1)}, u32[]{:S(2)}, u32[]{:S(2)}) collective-permute-start(f32[3,2,1024]{2,1,0:T(2,128)S(1)} %add.108), channel_id=1, source_target_pairs={{0,128},{64,192},{128,0},{192,64},{1,129},{65,193},{129,1},{193,65... | collective-permute-start | bytes 73736 | tf_op jit(solution)/shard_map/ppermute | solution.py:232
  105.0 2.5 %collective-permute-done.18 = f32[3,2,1024]{2,1,0:T(2,128)S(1)} collective-permute-done((f32[3,2,1024]{2,1,0:T(2,128)S(1)}, f32[3,2,1024]{2,1,0:T(2,128)S(1)}, u32[]{:S(2)}, u32[]{:S(2)}) %collective-permute-start.18) | collective-permute-done | bytes 24608 | tf_op jit(solution)/shard_map/ppermute | solution.py:232
  107.5 12.9 %shard_map.189 = (bf16[32,64,384]{2,1,0:T(8,128)(2,1)S(1)}, bf16[8,256,384]{2,1,0:T(8,128)(2,1)}, bf16[16,384]{1,0:T(8,128)(2,1)}, bf16[16,384]{1,0:T(8,128)(2,1)}) custom-call(bf16[512,384]{1,0:T(8,128)(2,1)S(1)} %bitcast.154, bf16[512,384]{1,0:T(8,128)(2,1)S(1)} %bitcast.152, bf16[1024,384]{1,0:T(8,128)(2,1)S(1)} %pad_maximum_fusion.1.cot_ref, ...), custom_call_target="tpu_custom_call" | custom-call | flops 4831838208 | bytes 6000000 | tf_op jit(solution)/shard_map/pallas_call | solution.py:161
  120.4 1.0 dynamic-slice_bitcast_fusion
  121.4 4.9 %collective-permute-start.19 = (bf16[4,4,64,384]{3,2,1,0:T(8,128)(2,1)}, bf16[4,4,64,384]{3,2,1,0:T(8,128)(2,1)}, u32[]{:S(2)}, u32[]{:S(2)}) collective-permute-start(bf16[4,4,64,384]{3,2,1,0:T(8,128)(2,1)} %dynamic-slice_bitcast_fusion), channel_id=1, source_target_pairs={{0,16},{16,0},{1,17},{17,1},{2,18},{18,2},{3,19},{19,3},{4,20},{20... | collective-permute-start | bytes 2359304 | tf_op jit(solution)/shard_map/ppermute | solution.py:181
  126.4 3.6 %all-to-all-start.3 = ((bf16[8,256,384]{2,1,0:T(8,128)(2,1)}), bf16[8,256,384]{2,1,0:T(8,128)(2,1)S(1)}, u32[]{:S(2)}, u32[]{:S(2)}) async-start(bf16[8,256,384]{2,1,0:T(8,128)(2,1)} %get-tuple-element.27), calls=%async_computation.3 | async-start | bytes 3145728 | tf_op jit(solution)/shard_map/all_to_all | solution.py:174
  130.0 1.4 fusion
  131.4 1.3 collective-permute-start.20
  132.7 2.9 %collective-permute-start.21 = (bf16[4,64,384]{2,1,0:T(8,128)(2,1)S(1)}, bf16[4,64,384]{2,1,0:T(8,128)(2,1)S(1)}, u32[]{:S(2)}, u32[]{:S(2)}) collective-permute-start(bf16[4,64,384]{2,1,0:T(8,128)(2,1)S(1)} %get-tuple-element.44), channel_id=1, source_target_pairs={{0,32},{1,33},{32,0},{33,1},{2,34},{3,35},{34,2},{35,3},{4,36},{5,... | collective-permute-start | bytes 589832 | tf_op jit(solution)/shard_map/ppermute | solution.py:181
  135.6 0.3 collective-permute-start.22
  136.0 3.8 %collective-permute-done.20 = bf16[4,64,384]{2,1,0:T(8,128)(2,1)S(1)} collective-permute-done((bf16[4,64,384]{2,1,0:T(8,128)(2,1)S(1)}, bf16[4,64,384]{2,1,0:T(8,128)(2,1)S(1)}, u32[]{:S(2)}, u32[]{:S(2)}) %collective-permute-start.20) | collective-permute-done | bytes 196640 | tf_op jit(solution)/shard_map/ppermute | solution.py:181
  139.7 5.2 %collective-permute-done.21 = bf16[4,64,384]{2,1,0:T(8,128)(2,1)S(1)} collective-permute-done((bf16[4,64,384]{2,1,0:T(8,128)(2,1)S(1)}, bf16[4,64,384]{2,1,0:T(8,128)(2,1)S(1)}, u32[]{:S(2)}, u32[]{:S(2)}) %collective-permute-start.21) | collective-permute-done | bytes 196640 | tf_op jit(solution)/shard_map/ppermute | solution.py:181
  145.1 0.7 collective-permute-start.23
  145.8 0.6 collective-permute-start.24
  146.3 1.9 %collective-permute-start.25 = (bf16[64,384]{1,0:T(8,128)(2,1)S(1)}, bf16[64,384]{1,0:T(8,128)(2,1)S(1)}, u32[]{:S(2)}, u32[]{:S(2)}) collective-permute-start(bf16[64,384]{1,0:T(8,128)(2,1)S(1)} %get-tuple-element.56), channel_id=1, source_target_pairs={{0,192},{64,0},{128,64},{192,128},{1,193},{65,1},{129,65},{193,129... | collective-permute-start | bytes 147464 | tf_op jit(solution)/shard_map/ppermute | solution.py:181
  148.3 1.3 collective-permute-done.23
  149.6 0.9 collective-permute-done.24
  151.0 0.6 fusion.20
  151.8 0.6 fusion.27
  152.6 0.6 fusion.23
  153.2 15.1 %all-to-all-done.3.came_ref = bf16[8,256,384]{2,1,0:T(8,128)(2,1)S(1)} async-done(((bf16[8,256,384]{2,1,0:T(8,128)(2,1)}), bf16[8,256,384]{2,1,0:T(8,128)(2,1)S(1)}, u32[]{:S(2)}, u32[]{:S(2)}) %all-to-all-start.3) | async-done | bytes 1572896 | tf_op jit(solution)/shard_map/all_to_all | solution.py:174
  168.3 1.2 copy-done.2
  169.5 2.7 %shard_map.190 = (bf16[128,3072]{1,0:T(8,128)(2,1)}, bf16[128,3072]{1,0:T(8,128)(2,1)}) custom-call(bf16[8,256,384]{2,1,0:T(8,128)(2,1)} %copy-done.2), custom_call_target="tpu_custom_call" | custom-call | tf_op jit(solution)/shard_map/pallas_call | solution.py:296
  (87 shorter events, 3.0 us)
Async XLA Ops:
  0.6 4.7 %copy-start.3 = (bf16[128,3072]{1,0:T(8,128)(2,1)S(1)}, bf16[128,3072]{1,0:T(8,128)(2,1)}, u32[]{:S(2)}) copy-start(bf16[128,3072]{1,0:T(8,128)(2,1)} %param.14) | copy-start | bytes 2359300
  2.0 11.4 %collective-permute-start = (bf16[4,16,3072]{2,1,0:T(8,128)(2,1)S(1)}, bf16[4,16,3072]{2,1,0:T(8,128)(2,1)S(1)}, u32[]{:S(2)}, u32[]{:S(2)}) collective-permute-start(bf16[4,16,3072]{2,1,0:T(8,128)(2,1)S(1)} %get-tuple-element.53), channel_id=1, source_target_pairs={{0,16},{16,0},{1,17},{17,1},{2,18},{18,2},{3,19},{19,3},{4,20},{20... | collective-permute-start | bytes 1179656 | tf_op jit(solution)/shard_map/ppermute | solution.py:181
  5.7 7.6 %copy-start.12 = (s32[4]{0:T(128)S(1)}, s32[4]{0:T(128)}, u32[]{:S(2)}) copy-start(s32[4]{0:T(128)} %param.23) | copy-start | bytes 52
  6.9 30.7 %all-to-all-start = ((bf16[8,128,384]{2,1,0:T(8,128)(2,1)}), bf16[8,128,384]{2,1,0:T(8,128)(2,1)S(1)}, u32[]{:S(2)}, u32[]{:S(2)}) async-start(bf16[8,128,384]{2,1,0:T(8,128)(2,1)} %bitcast.25), calls=%async_computation | async-start | bytes 1572864 | tf_op jit(solution)/shard_map/all_to_all | solution.py:174
  13.5 7.5 %collective-permute-start.1 = (bf16[2,16,3072]{2,1,0:T(8,128)(2,1)S(1)}, bf16[2,16,3072]{2,1,0:T(8,128)(2,1)S(1)}, u32[]{:S(2)}, u32[]{:S(2)}) collective-permute-start(bf16[2,16,3072]{2,1,0:T(8,128)(2,1)S(1)} %get-tuple-element.50), channel_id=1, source_target_pairs={{0,1},{1,32},{32,33},{33,0},{2,3},{3,34},{34,35},{35,2},{4,5},{5,3... | collective-permute-start | bytes 589832 | tf_op jit(solution)/shard_map/ppermute | solution.py:181
  14.8 11.4 %collective-permute-start.2 = (bf16[2,16,3072]{2,1,0:T(8,128)(2,1)S(1)}, bf16[2,16,3072]{2,1,0:T(8,128)(2,1)S(1)}, u32[]{:S(2)}, u32[]{:S(2)}) collective-permute-start(bf16[2,16,3072]{2,1,0:T(8,128)(2,1)S(1)} %get-tuple-element.51), channel_id=1, source_target_pairs={{0,32},{1,33},{32,0},{33,1},{2,34},{3,35},{34,2},{35,3},{4,36},{5,... | collective-permute-start | bytes 589832 | tf_op jit(solution)/shard_map/ppermute | solution.py:181
  17.2 8.9 %collective-permute-start.3 = (bf16[2,16,3072]{2,1,0:T(8,128)(2,1)S(1)}, bf16[2,16,3072]{2,1,0:T(8,128)(2,1)S(1)}, u32[]{:S(2)}, u32[]{:S(2)}) collective-permute-start(bf16[2,16,3072]{2,1,0:T(8,128)(2,1)S(1)} %get-tuple-element.52), channel_id=1, source_target_pairs={{0,33},{1,0},{32,1},{33,32},{2,35},{3,2},{34,3},{35,34},{4,37},{5,... | collective-permute-start | bytes 589832 | tf_op jit(solution)/shard_map/ppermute | solution.py:181
  26.2 18.6 %copy-start.4 = (bf16[128,3072]{1,0:T(8,128)(2,1)S(1)}, bf16[128,3072]{1,0:T(8,128)(2,1)}, u32[]{:S(2)}) copy-start(bf16[128,3072]{1,0:T(8,128)(2,1)} %param.15) | copy-start | bytes 2359300
  29.0 5.1 %collective-permute-start.4 = (bf16[16,3072]{1,0:T(8,128)(2,1)S(1)}, bf16[16,3072]{1,0:T(8,128)(2,1)S(1)}, u32[]{:S(2)}, u32[]{:S(2)}) collective-permute-start(bf16[16,3072]{1,0:T(8,128)(2,1)S(1)} %get-tuple-element.47), channel_id=1, source_target_pairs={{0,64},{64,128},{128,192},{192,0},{1,65},{65,129},{129,193},{193,1... | collective-permute-start | bytes 294920 | tf_op jit(solution)/shard_map/ppermute | solution.py:181
  30.3 6.4 %collective-permute-start.5 = (bf16[16,3072]{1,0:T(8,128)(2,1)S(1)}, bf16[16,3072]{1,0:T(8,128)(2,1)S(1)}, u32[]{:S(2)}, u32[]{:S(2)}) collective-permute-start(bf16[16,3072]{1,0:T(8,128)(2,1)S(1)} %get-tuple-element.46), channel_id=1, source_target_pairs={{0,128},{64,192},{128,0},{192,64},{1,129},{65,193},{129,1},{193,65... | collective-permute-start | bytes 294920 | tf_op jit(solution)/shard_map/ppermute | solution.py:181
  33.0 4.5 %collective-permute-start.6 = (bf16[16,3072]{1,0:T(8,128)(2,1)S(1)}, bf16[16,3072]{1,0:T(8,128)(2,1)S(1)}, u32[]{:S(2)}, u32[]{:S(2)}) collective-permute-start(bf16[16,3072]{1,0:T(8,128)(2,1)S(1)} %get-tuple-element.45), channel_id=1, source_target_pairs={{0,192},{64,0},{128,64},{192,128},{1,193},{65,1},{129,65},{193,129... | collective-permute-start | bytes 294920 | tf_op jit(solution)/shard_map/ppermute | solution.py:181
  38.3 14.2 %all-to-all-start.1 = ((bf16[8,16,384]{2,1,0:T(8,128)(2,1)}), bf16[8,16,384]{2,1,0:T(8,128)(2,1)S(1)}, u32[]{:S(2)}, u32[]{:S(2)}) async-start(bf16[8,16,384]{2,1,0:T(8,128)(2,1)} %copy.59), calls=%async_computation.1 | async-start | bytes 196608 | tf_op jit(solution)/shard_map/all_to_all | solution.py:174
  44.8 7.7 %copy-start.5 = (bf16[16,384]{1,0:T(8,128)(2,1)S(1)}, bf16[16,384]{1,0:T(8,128)(2,1)}, u32[]{:S(2)}) copy-start(bf16[16,384]{1,0:T(8,128)(2,1)} %param.16) | copy-start | bytes 36868
  44.8 7.7 %copy-start.6 = (bf16[16,384]{1,0:T(8,128)(2,1)S(1)}, bf16[16,384]{1,0:T(8,128)(2,1)}, u32[]{:S(2)}) copy-start(bf16[16,384]{1,0:T(8,128)(2,1)} %param.25) | copy-start | bytes 36868
  44.8 7.7 %copy-start.7 = (bf16[16,384]{1,0:T(8,128)(2,1)S(1)}, bf16[16,384]{1,0:T(8,128)(2,1)}, u32[]{:S(2)}) copy-start(bf16[16,384]{1,0:T(8,128)(2,1)} %param.24) | copy-start | bytes 36868
  52.6 7.1 %collective-permute-start.7 = (bf16[4,16,384]{2,1,0:T(8,128)(2,1)S(1)}, bf16[4,16,384]{2,1,0:T(8,128)(2,1)S(1)}, u32[]{:S(2)}, u32[]{:S(2)}) collective-permute-start(bf16[4,16,384]{2,1,0:T(8,128)(2,1)S(1)} %pad_maximum_fusion.2), channel_id=1, source_target_pairs={{0,64},{64,128},{128,192},{192,0},{1,65},{65,129},{129,193},{193,1... | collective-permute-start | bytes 147464 | tf_op jit(solution)/shard_map/ppermute | solution.py:181
  52.7 7.0 %collective-permute-start.8 = (bf16[4,16,384]{2,1,0:T(8,128)(2,1)S(1)}, bf16[4,16,384]{2,1,0:T(8,128)(2,1)S(1)}, u32[]{:S(2)}, u32[]{:S(2)}) collective-permute-start(bf16[4,16,384]{2,1,0:T(8,128)(2,1)S(1)} %pad_maximum_fusion.2), channel_id=1, source_target_pairs={{0,128},{64,192},{128,0},{192,64},{1,129},{65,193},{129,1},{193,65... | collective-permute-start | bytes 147464 | tf_op jit(solution)/shard_map/ppermute | solution.py:181
  56.0 3.7 %collective-permute-start.9 = (bf16[4,16,384]{2,1,0:T(8,128)(2,1)S(1)}, bf16[4,16,384]{2,1,0:T(8,128)(2,1)S(1)}, u32[]{:S(2)}, u32[]{:S(2)}) collective-permute-start(bf16[4,16,384]{2,1,0:T(8,128)(2,1)S(1)} %pad_maximum_fusion.2), channel_id=1, source_target_pairs={{0,192},{64,0},{128,64},{192,128},{1,193},{65,1},{129,65},{193,129... | collective-permute-start | bytes 147464 | tf_op jit(solution)/shard_map/ppermute | solution.py:181
  56.1 23.5 %all-to-all-start.2 = ((bf16[8,128,384]{2,1,0:T(8,128)(2,1)}), bf16[8,128,384]{2,1,0:T(8,128)(2,1)S(1)}, u32[]{:S(2)}, u32[]{:S(2)}) async-start(bf16[8,128,384]{2,1,0:T(8,128)(2,1)} %bitcast.1), calls=%async_computation.2 | async-start | bytes 1572864 | tf_op jit(solution)/shard_map/all_to_all | solution.py:174
  59.6 24.0 %copy-start.8 = (f32[128]{0:T(128)S(1)}, f32[128]{0:T(128)}, u32[]{:S(2)}) copy-start(f32[128]{0:T(128)} %param.21) | copy-start | bytes 1540
  59.6 24.0 %copy-start.9 = (f32[128]{0:T(128)S(1)}, f32[128]{0:T(128)}, u32[]{:S(2)}) copy-start(f32[128]{0:T(128)} %param.19) | copy-start | bytes 1540
  59.7 24.0 %copy-start.10 = (f32[128]{0:T(128)S(1)}, f32[128]{0:T(128)}, u32[]{:S(2)}) copy-start(f32[128]{0:T(128)} %param.22) | copy-start | bytes 1540
  59.7 24.0 %copy-start.11 = (f32[128]{0:T(128)S(1)}, f32[128]{0:T(128)}, u32[]{:S(2)}) copy-start(f32[128]{0:T(128)} %param.20) | copy-start | bytes 1540
  59.8 6.1 %collective-permute-start.10 = (bf16[4,4,16,384]{3,2,0,1:T(8,128)(2,1)S(1)}, bf16[4,4,16,384]{3,2,0,1:T(8,128)(2,1)S(1)}, u32[]{:S(2)}, u32[]{:S(2)}) collective-permute-start(bf16[4,4,16,384]{3,2,0,1:T(8,128)(2,1)S(1)} %bitcast_dynamic-update-slice_fusion.6), channel_id=1, source_target_pairs={{0,1},{1,32},{32,33},{33,0},{2,3},{3,34},{34,35},{35,2},{4,5},{5,3... | collective-permute-start | bytes 589832 | tf_op jit(solution)/shard_map/ppermute | solution.py:181
  61.1 8.2 %collective-permute-start.11 = (bf16[4,4,16,384]{3,2,0,1:T(8,128)(2,1)S(1)}, bf16[4,4,16,384]{3,2,0,1:T(8,128)(2,1)S(1)}, u32[]{:S(2)}, u32[]{:S(2)}) collective-permute-start(bf16[4,4,16,384]{3,2,0,1:T(8,128)(2,1)S(1)} %bitcast_dynamic-update-slice_fusion.6), channel_id=1, source_target_pairs={{0,32},{1,33},{32,0},{33,1},{2,34},{3,35},{34,2},{35,3},{4,36},{5,... | collective-permute-start | bytes 589832 | tf_op jit(solution)/shard_map/ppermute | solution.py:181
  64.0 5.3 %collective-permute-start.12 = (bf16[4,4,16,384]{3,2,0,1:T(8,128)(2,1)S(1)}, bf16[4,4,16,384]{3,2,0,1:T(8,128)(2,1)S(1)}, u32[]{:S(2)}, u32[]{:S(2)}) collective-permute-start(bf16[4,4,16,384]{3,2,0,1:T(8,128)(2,1)S(1)} %bitcast_dynamic-update-slice_fusion.6), channel_id=1, source_target_pairs={{0,33},{1,0},{32,1},{33,32},{2,35},{3,2},{34,3},{35,34},{4,37},{5,... | collective-permute-start | bytes 589832 | tf_op jit(solution)/shard_map/ppermute | solution.py:181
  79.6 6.0 %collective-permute-start.13 = (bf16[4,4,4,16,384]{4,3,2,1,0:T(8,128)(2,1)S(1)}, bf16[4,4,4,16,384]{4,3,2,1,0:T(8,128)(2,1)S(1)}, u32[]{:S(2)}, u32[]{:S(2)}) collective-permute-start(bf16[4,4,4,16,384]{4,3,2,1,0:T(8,128)(2,1)S(1)} %bitcast.157), channel_id=1, source_target_pairs={{0,16},{16,0},{1,17},{17,1},{2,18},{18,2},{3,19},{19,3},{4,20},{20... | collective-permute-start | bytes 2359304 | tf_op jit(solution)/shard_map/ppermute | solution.py:181
  85.9 0.7 copy-start
  85.9 0.7 copy-start.1
  92.0 1.3 collective-permute-start.14
  93.4 2.8 %collective-permute-start.15 = (f32[3,2,1024]{2,1,0:T(2,128)S(1)}, f32[3,2,1024]{2,1,0:T(2,128)S(1)}, u32[]{:S(2)}, u32[]{:S(2)}) collective-permute-start(f32[3,2,1024]{2,1,0:T(2,128)S(1)} %add.105), channel_id=1, source_target_pairs={{0,1},{1,0},{32,33},{33,32},{2,3},{3,2},{34,35},{35,34},{4,5},{5,4... | collective-permute-start | bytes 73736 | tf_op jit(solution)/shard_map/ppermute | solution.py:232
  96.1 4.3 %collective-permute-start.16 = (f32[3,2,1024]{2,1,0:T(2,128)S(1)}, f32[3,2,1024]{2,1,0:T(2,128)S(1)}, u32[]{:S(2)}, u32[]{:S(2)}) collective-permute-start(f32[3,2,1024]{2,1,0:T(2,128)S(1)} %add.106), channel_id=1, source_target_pairs={{0,32},{1,33},{32,0},{33,1},{2,34},{3,35},{34,2},{35,3},{4,36},{5,... | collective-permute-start | bytes 73736 | tf_op jit(solution)/shard_map/ppermute | solution.py:232
  100.4 2.8 %collective-permute-start.17 = (f32[3,2,1024]{2,1,0:T(2,128)S(1)}, f32[3,2,1024]{2,1,0:T(2,128)S(1)}, u32[]{:S(2)}, u32[]{:S(2)}) collective-permute-start(f32[3,2,1024]{2,1,0:T(2,128)S(1)} %add.107), channel_id=1, source_target_pairs={{0,64},{64,0},{128,192},{192,128},{1,65},{65,1},{129,193},{193,129... | collective-permute-start | bytes 73736 | tf_op jit(solution)/shard_map/ppermute | solution.py:232
  103.2 4.3 %collective-permute-start.18 = (f32[3,2,1024]{2,1,0:T(2,128)S(1)}, f32[3,2,1024]{2,1,0:T(2,128)S(1)}, u32[]{:S(2)}, u32[]{:S(2)}) collective-permute-start(f32[3,2,1024]{2,1,0:T(2,128)S(1)} %add.108), channel_id=1, source_target_pairs={{0,128},{64,192},{128,0},{192,64},{1,129},{65,193},{129,1},{193,65... | collective-permute-start | bytes 73736 | tf_op jit(solution)/shard_map/ppermute | solution.py:232
  121.4 8.5 %collective-permute-start.19 = (bf16[4,4,64,384]{3,2,1,0:T(8,128)(2,1)}, bf16[4,4,64,384]{3,2,1,0:T(8,128)(2,1)}, u32[]{:S(2)}, u32[]{:S(2)}) collective-permute-start(bf16[4,4,64,384]{3,2,1,0:T(8,128)(2,1)} %dynamic-slice_bitcast_fusion), channel_id=1, source_target_pairs={{0,16},{16,0},{1,17},{17,1},{2,18},{18,2},{3,19},{19,3},{4,20},{20... | collective-permute-start | bytes 2359304 | tf_op jit(solution)/shard_map/ppermute | solution.py:181
  126.4 42.0 %all-to-all-start.3 = ((bf16[8,256,384]{2,1,0:T(8,128)(2,1)}), bf16[8,256,384]{2,1,0:T(8,128)(2,1)S(1)}, u32[]{:S(2)}, u32[]{:S(2)}) async-start(bf16[8,256,384]{2,1,0:T(8,128)(2,1)} %get-tuple-element.27), calls=%async_computation.3 | async-start | bytes 3145728 | tf_op jit(solution)/shard_map/all_to_all | solution.py:174
  131.4 8.3 %collective-permute-start.20 = (bf16[4,64,384]{2,1,0:T(8,128)(2,1)S(1)}, bf16[4,64,384]{2,1,0:T(8,128)(2,1)S(1)}, u32[]{:S(2)}, u32[]{:S(2)}) collective-permute-start(bf16[4,64,384]{2,1,0:T(8,128)(2,1)S(1)} %get-tuple-element.42), channel_id=1, source_target_pairs={{0,1},{1,32},{32,33},{33,0},{2,3},{3,34},{34,35},{35,2},{4,5},{5,3... | collective-permute-start | bytes 589832 | tf_op jit(solution)/shard_map/ppermute | solution.py:181
  132.7 12.2 %collective-permute-start.21 = (bf16[4,64,384]{2,1,0:T(8,128)(2,1)S(1)}, bf16[4,64,384]{2,1,0:T(8,128)(2,1)S(1)}, u32[]{:S(2)}, u32[]{:S(2)}) collective-permute-start(bf16[4,64,384]{2,1,0:T(8,128)(2,1)S(1)} %get-tuple-element.44), channel_id=1, source_target_pairs={{0,32},{1,33},{32,0},{33,1},{2,34},{3,35},{34,2},{35,3},{4,36},{5,... | collective-permute-start | bytes 589832 | tf_op jit(solution)/shard_map/ppermute | solution.py:181
  135.6 9.3 %collective-permute-start.22 = (bf16[4,64,384]{2,1,0:T(8,128)(2,1)S(1)}, bf16[4,64,384]{2,1,0:T(8,128)(2,1)S(1)}, u32[]{:S(2)}, u32[]{:S(2)}) collective-permute-start(bf16[4,64,384]{2,1,0:T(8,128)(2,1)S(1)} %get-tuple-element.43), channel_id=1, source_target_pairs={{0,33},{1,0},{32,1},{33,32},{2,35},{3,2},{34,3},{35,34},{4,37},{5,... | collective-permute-start | bytes 589832 | tf_op jit(solution)/shard_map/ppermute | solution.py:181
  145.1 4.5 %collective-permute-start.23 = (bf16[64,384]{1,0:T(8,128)(2,1)S(1)}, bf16[64,384]{1,0:T(8,128)(2,1)S(1)}, u32[]{:S(2)}, u32[]{:S(2)}) collective-permute-start(bf16[64,384]{1,0:T(8,128)(2,1)S(1)} %get-tuple-element.55), channel_id=1, source_target_pairs={{0,64},{64,128},{128,192},{192,0},{1,65},{65,129},{129,193},{193,1... | collective-permute-start | bytes 147464 | tf_op jit(solution)/shard_map/ppermute | solution.py:181
  145.8 4.7 %collective-permute-start.24 = (bf16[64,384]{1,0:T(8,128)(2,1)S(1)}, bf16[64,384]{1,0:T(8,128)(2,1)S(1)}, u32[]{:S(2)}, u32[]{:S(2)}) collective-permute-start(bf16[64,384]{1,0:T(8,128)(2,1)S(1)} %get-tuple-element.57), channel_id=1, source_target_pairs={{0,128},{64,192},{128,0},{192,64},{1,129},{65,193},{129,1},{193,65... | collective-permute-start | bytes 147464 | tf_op jit(solution)/shard_map/ppermute | solution.py:181
  146.3 4.4 %collective-permute-start.25 = (bf16[64,384]{1,0:T(8,128)(2,1)S(1)}, bf16[64,384]{1,0:T(8,128)(2,1)S(1)}, u32[]{:S(2)}, u32[]{:S(2)}) collective-permute-start(bf16[64,384]{1,0:T(8,128)(2,1)S(1)} %get-tuple-element.56), channel_id=1, source_target_pairs={{0,192},{64,0},{128,64},{192,128},{1,193},{65,1},{129,65},{193,129... | collective-permute-start | bytes 147464 | tf_op jit(solution)/shard_map/ppermute | solution.py:181
  168.3 1.2 copy-start.2

commit v5 on v4

--- a/solution.py
+++ b/solution.py
@@ -112,23 +112,23 @@
         rows_ref[:, place * part : (place + 1) * part] = block.reshape(groups, part, HD)
 
 
-def column_spec(shape):
+def column_spec(shape, first=0):
     lead = tuple(shape[:-1])
-    return pl.BlockSpec(lead + (HD,), lambda head: (0,) * len(lead) + (head,))
+    return pl.BlockSpec(lead + (HD,), lambda head: (0,) * len(lead) + (head + first,))
 
 
 PARAMS = pltpu.CompilerParams(vmem_limit_bytes=VMEM)
 
 
-def operand_specs(operands, gains):
-    win, text, cot, moved_k, moved_v, text_k, text_v = operands
-    shapes = [win.shape, text.shape, cot.shape, moved_v.shape, moved_v.shape]
-    specs = [column_spec(shape) for shape in shapes + [text_k.shape, text_v.shape]]
+def operand_specs(operands, gains, first):
+    specs = [column_spec(array.shape, first) for array in operands]
     return specs + [pl.BlockSpec(gains.shape, lambda head: (0, 0))]
 
 
 def cost(operands, heads, dots):
-    work = operands[2].shape[0] * operands[4].shape[0] * operands[4].shape[1] * heads
+    _, _, cot, moved_k, moved_v, *_ = operands
+    keys = moved_k.shape[0] * (moved_k.shape[1] + moved_v.shape[1]) // 2
+    work = cot.shape[0] * keys * heads
     return pl.CostEstimate(
         flops=2 * dots * work * HD, bytes_accessed=2000000 * heads, transcendentals=work
     )
@@ -139,7 +139,7 @@
     return pl.pallas_call(
         stats_kernel,
         grid=(heads,),
-        in_specs=operand_specs(operands, gains),
+        in_specs=operand_specs(operands, gains, 0),
         out_specs=pl.BlockSpec((1, 2, count), lambda head: (head, 0, 0)),
         out_shape=jax.ShapeDtypeStruct((heads, 2, count), F32),
         compiler_params=PARAMS,
@@ -147,22 +147,23 @@
     )(*operands, gains)
 
 
-def attention_grads(operands, gains, stats, heads, groups):
-    count = operands[2].shape[0]
-    z_size, own = operands[4].shape[:2]
-    text = operands[5].shape[0]
+def attention_grads(operands, gains, stats, first, last, groups):
+    _, _, cot, moved_k, moved_v, text_k, _ = operands
+    count, heads = cot.shape[0], last - first
     width = heads * HD
     shapes = [
         jax.ShapeDtypeStruct((groups, count // groups * 2, width), BF16),
-        jax.ShapeDtypeStruct((z_size, 2 * own, width), BF16),
-        jax.ShapeDtypeStruct((text, width), BF16),
-        jax.ShapeDtypeStruct((text, width), BF16),
+        jax.ShapeDtypeStruct(
+            (moved_k.shape[0], moved_k.shape[1] + moved_v.shape[1], width), BF16
+        ),
+        jax.ShapeDtypeStruct((text_k.shape[0], width), BF16),
+        jax.ShapeDtypeStruct((text_k.shape[0], width), BF16),
     ]
     return pl.pallas_call(
         grads_kernel,
         grid=(heads,),
-        in_specs=operand_specs(operands, gains)
-        + [pl.BlockSpec((1, 2, count), lambda head: (head, 0, 0))],
+        in_specs=operand_specs(operands, gains, first)
+        + [pl.BlockSpec((1, 2, count), lambda head: (head + first, 0, 0))],
         out_specs=[column_spec(s.shape) for s in shapes],
         out_shape=shapes,
         compiler_params=PARAMS,
@@ -226,12 +227,30 @@
 
 def sum_plane(part):
     for axes in ("c", ROW, "y"):
-        size = lax.axis_size(axes)
-        bit = 1
-        while bit < size:
-            part = part + lax.ppermute(part, axes, [(i, i ^ bit) for i in range(size)])
-            bit *= 2
+        part = sum(push(part, axes, step) for step in range(lax.axis_size(axes)))
     return part
+
+
+def choose_kernel(source_ref, *refs):
+    parts, outs = refs[:-NWIN], refs[-NWIN:]
+    count = parts[0].shape[0]
+    for step, out in enumerate(outs):
+        source = source_ref[step]
+        for index in range(len(parts) * count):
+
+            @pl.when(source == index)
+            def _():
+                out[...] = parts[index // count][index % count]
+
+
+def choose(source, parts):
+    whole = pl.BlockSpec(memory_space=pltpu.VMEM)
+    return pl.pallas_call(
+        choose_kernel,
+        in_specs=[pl.BlockSpec(memory_space=pltpu.SMEM)] + [whole] * len(parts),
+        out_specs=[whole] * NWIN,
+        out_shape=[jax.ShapeDtypeStruct(parts[0].shape[1:], BF16)] * NWIN,
+    )(source, *parts)
 
 
 def fetch_window(video_q, window):
@@ -256,13 +275,15 @@
     source = from_x * c_size + ((c - c_of) & (c_size - 1))
     from_y = (y - y_of[0]) & (y_size - 1)
 
-    pieces = video_q.reshape(xh_size, c_size, xl_size, -1, model).transpose(1, 0, 2, 3, 4)
-    pieces = pieces.reshape(c_size, x_size, -1, model)
-    pieces = jnp.stack(scatter_stage(pieces, "c"), axis=1)
-    pieces = jnp.concatenate(scatter_stage(pieces, ROW), axis=0)
-    came = [place(pieces, source[0])] + [
-        push(place(pieces, source[step]), "y", step) for step in range(1, y_size)
-    ]
+    pieces = video_q.reshape(xh_size, c_size, xl_size, -1, model)
+
+    def side(index):
+        part = lax.dynamic_index_in_dim(pieces, index, 1, False, allow_negative_indices=False)
+        return part.reshape(x_size, -1, model)
+
+    pieces = jnp.stack((side(c), push(side(c ^ 1), "c", 1)), axis=1)
+    chosen = choose(source, scatter_stage(pieces, ROW))
+    came = [chosen[0]] + [push(chosen[step], "y", step) for step in range(1, y_size)]
     return place(jnp.stack(came), from_y), z_of[0]
 
 
@@ -271,35 +292,38 @@
     return rows.reshape(count, groups, -1).transpose(1, 0, 2)
 
 
-def merge_kernel(came_ref, k_ref, v_ref, sems):
+def merge_kernel(lead_ref, late_ref, k_ref, v_ref, sems):
     own = k_ref.shape[0]
-    z_size, _, width = came_ref.shape
+    z_size, _, first = lead_ref.shape
+    width = first + late_ref.shape[2]
     copies = []
     for z in range(z_size):
         for part, ref in enumerate((k_ref, v_ref)):
-            copies.append(
-                pltpu.make_async_copy(
-                    came_ref.at[z, pl.ds(part * own, own)],
-                    ref.at[:, pl.ds(z * width, width)],
-                    sems.at[z, part],
+            for half, (source, start) in enumerate(((lead_ref, 0), (late_ref, first))):
+                copies.append(
+                    pltpu.make_async_copy(
+                        source.at[z, pl.ds(part * own, own)],
+                        ref.at[:, pl.ds(z * width + start, source.shape[2])],
+                        sems.at[z, part, half],
+                    )
                 )
-            )
     for copy in copies:
         copy.start()
     for copy in copies:
         copy.wait()
 
 
-def merge(came):
-    z_size, rows, width = came.shape
+def merge(lead, late):
+    z_size, rows, first = lead.shape
+    width = first + late.shape[2]
     anywhere = pl.BlockSpec(memory_space=pl.ANY)
     return pl.pallas_call(
         merge_kernel,
-        in_specs=[pl.BlockSpec(memory_space=pltpu.VMEM)],
+        in_specs=[pl.BlockSpec(memory_space=pltpu.VMEM)] * 2,
         out_specs=[anywhere, anywhere],
         out_shape=[jax.ShapeDtypeStruct((rows // 2, z_size * width), BF16)] * 2,
-        scratch_shapes=[pltpu.SemaphoreType.DMA((z_size, 2))],
-    )(came)
+        scratch_shapes=[pltpu.SemaphoreType.DMA((z_size, 2, 2))],
+    )(lead, late)
 
 
 def local(
@@ -324,17 +348,25 @@
     moved_v = swap(sent_v, "z")
     own = jnp.stack((own_window, text_q, grad_out_video, grad_out_text))
     own = gather_stage(gather_stage(own, "y"), ROW)
-    own, moved_v = tie(own, moved_v)
-    own = gather_stage(own.transpose(2, 0, 1, 3, 4), "c")
-    window_rows, text_rows, *cotangent = (own[:, kind].reshape(-1, columns) for kind in range(4))
+    text = gather_stage(own[:, :, 1:].transpose(2, 0, 1, 3, 4), "c")
+    own, moved_v = tie(own[:, :, 0], moved_v)
+    window_rows = gather_stage(own, "c").reshape(-1, columns)
+    text_rows, *cotangent = (text[:, kind].reshape(-1, columns) for kind in range(3))
     cotangent = jnp.concatenate(cotangent, axis=0)
     operands = (window_rows, text_rows, cotangent, moved_k, moved_v, text_k, text_v)
 
     stats = sum_plane(attention_stats(operands, gains, heads))
-    out, dmoved, key_text, value_text = attention_grads(operands, gains, stats, heads, groups)
-    back = swap(dmoved, "z")
+    outs, backs, *dtext = zip(
+        *(
+            attention_grads(operands, gains, stats, first, last, groups)
+            for first, last in ((0, 1), (1, heads))
+        )
+    )
+    backs = [swap(back, "z") for back in backs]
+    out, backs[0] = tie(jnp.concatenate(outs, axis=2), backs[0])
     total = sum_stage(reduce_row(out), "y")
-    grad_video_k, grad_video_v = merge(back)
+    grad_video_k, grad_video_v = merge(*backs)
+    key_text, value_text = (jnp.concatenate(parts, axis=1) for parts in dtext)
 
     def query_grad(raw, gain, cot):
         shape = (raw.shape[0], heads, HD)

time: 174 us -> 172 us (0.989)
  waiting for transfers between devices: 67.4 us -> 53.9 us
  starting transfers between devices: 65.7 us -> 73.4 us
  other arithmetic: 3.6 us -> 7.36 us
  Pallas kernels: 21 us -> 23.4 us
    ppermute x21 -> x29, starting transfers between devices: 37.7 us -> 48.8 us  [push(): lax.ppermute(array, axes, [(i, (i + step) % size) for i in range(size)])]
    all_to_all x4 -> x5, waiting for transfers between devices: 31.4 us -> 22.2 us  [swap(): return lax.all_to_all(array, axes, split_axis=0, concat_axis=0, tiled=True)]
    ppermute x5 -> x0, starting transfers between devices: 7.91 us -> none  [sum_plane(): part = part + lax.ppermute(part, axes, [(i, i ^ bit) for i in range(size)])]
    ppermute x5 -> x0, waiting for transfers between devices: 7.47 us -> none  [sum_plane(): part = part + lax.ppermute(part, axes, [(i, i ^ bit) for i in range(size)])]
    all_to_all x4 -> x5, starting transfers between devices: 20.1 us -> 24.6 us  [swap(): return lax.all_to_all(array, axes, split_axis=0, concat_axis=0, tiled=True)]
    ppermute x21 -> x29, waiting for transfers between devices: 28.5 us -> 31.7 us  [push(): lax.ppermute(array, axes, [(i, (i + step) % size) for i in range(size)])]
    pallas_call x0 -> x1, Pallas kernels: none -> 2.17 us  [choose(): pl.pallas_call(choose_kernel, in_specs=[pl.BlockSpec(memory_space=pltpu.S...]
    squeeze x6 -> x4, local copies, waits for them, and re-layouts: 3.86 us -> 2.21 us  [place(): lax.dynamic_index_in_dim(array, index, 0, keepdims=False, allow_negative_...]
  transfers between devices with their start and end apart: 30 -> 34, of which waited for: 20 -> 21; matrix products, arithmetic and copies ran while one was open for 7% -> 6% of each run, Pallas kernels for 0% -> 8%
where the time goes in v5:
time: 172 us; the launch traced here: 171 us
  starting transfers between devices  73.4 us (43%)
  waiting for transfers between devices  53.9 us (31%)
  Pallas kernels  23.4 us (14%)
  local copies, waits for them, and re-layouts  12.1 us (7%)
  other arithmetic  7.36 us (4%)
    ppermute x29, starting transfers between devices, push(): lax.ppermute(array, axes, [(i, (i + step) % size) for i in range(size)])  48.8 us
    ppermute x29, waiting for transfers between devices, push(): lax.ppermute(array, axes, [(i, (i + step) % size) for i in range(size)])  31.7 us
    all_to_all x5, starting transfers between devices, swap(): return lax.all_to_all(array, axes, split_axis=0, concat_axis=0, tiled=True)  24.6 us
    all_to_all x5, waiting for transfers between devices, swap(): return lax.all_to_all(array, axes, split_axis=0, concat_axis=0, tiled=True)  22.2 us
    pallas_call x2, Pallas kernels, attention_grads(): pl.pallas_call(grads_kernel, grid=(heads,), in_specs=operand_specs(operan...  13 us
    pallas_call x1, Pallas kernels, attention_stats(): pl.pallas_call(stats_kernel, grid=(heads,), in_specs=operand_specs(operan...  5.4 us
    unnamed x47, local copies, waits for them, and re-layouts  3.61 us
  transfers between devices with their start and end apart: 34, of which 21 were waited for; matrix products, arithmetic and copies ran while one was open for 6% of the time, Pallas kernels for 8%

profile of v5, /device:TPU:1, one launch (start us, length us, event | category | flops | bytes accessed | tf_op | source)
XLA Modules:
  0.0 171.4 jit_solution(112238428250336678)
XLA Ops:
  0.6 1.3 constant_dynamic-slice_fusion
  1.9 3.3 %collective-permute-start = (bf16[4,16,3072]{2,1,0:T(8,128)(2,1)S(1)}, bf16[4,16,3072]{2,1,0:T(8,128)(2,1)S(1)}, u32[]{:S(2)}, u32[]{:S(2)}) collective-permute-start(bf16[4,16,3072]{2,1,0:T(8,128)(2,1)S(1)} %bitcast.159), channel_id=1, source_target_pairs={{0,16},{16,0},{1,17},{17,1},{2,18},{18,2},{3,19},{19,3},{4,20},{20... | collective-permute-start | bytes 1179656 | tf_op jit(solution)/shard_map/ppermute | solution.py:182
  5.6 1.2 copy.56
  6.8 6.6 %all-to-all-start = ((bf16[8,128,384]{2,1,0:T(8,128)(2,1)}), bf16[8,128,384]{2,1,0:T(8,128)(2,1)S(1)}, u32[]{:S(2)}, u32[]{:S(2)}) async-start(bf16[8,128,384]{2,1,0:T(8,128)(2,1)} %bitcast.17), calls=%async_computation | async-start | bytes 1572864 | tf_op jit(solution)/shard_map/all_to_all | solution.py:175
  13.4 0.8 fusion.5
  14.1 1.2 collective-permute-start.1
  15.4 2.5 %collective-permute-start.2 = (bf16[2,16,3072]{2,1,0:T(8,128)(2,1)S(1)}, bf16[2,16,3072]{2,1,0:T(8,128)(2,1)S(1)}, u32[]{:S(2)}, u32[]{:S(2)}) collective-permute-start(bf16[2,16,3072]{2,1,0:T(8,128)(2,1)S(1)} %get-tuple-element.67), channel_id=1, source_target_pairs={{0,32},{1,33},{32,0},{33,1},{2,34},{3,35},{34,2},{35,3},{4,36},{5,... | collective-permute-start | bytes 589832 | tf_op jit(solution)/shard_map/ppermute | solution.py:182
  17.8 1.2 collective-permute-start.3
  19.0 0.6 shift-right-arithmetic_and_fusion
  19.6 1.9 %collective-permute-done.1.refs_1_ = bf16[2,16,3072]{2,1,0:T(8,128)(2,1)S(1)} collective-permute-done((bf16[2,16,3072]{2,1,0:T(8,128)(2,1)S(1)}, bf16[2,16,3072]{2,1,0:T(8,128)(2,1)S(1)}, u32[]{:S(2)}, u32[]{:S(2)}) %collective-permute-start.1) | collective-permute-done | bytes 196640 | tf_op jit(solution)/shard_map/ppermute | solution.py:182
  21.6 5.2 %collective-permute-done.2.refs_2_ = bf16[2,16,3072]{2,1,0:T(8,128)(2,1)S(1)} collective-permute-done((bf16[2,16,3072]{2,1,0:T(8,128)(2,1)S(1)}, bf16[2,16,3072]{2,1,0:T(8,128)(2,1)S(1)}, u32[]{:S(2)}, u32[]{:S(2)}) %collective-permute-start.2) | collective-permute-done | bytes 196640 | tf_op jit(solution)/shard_map/ppermute | solution.py:182
  26.8 0.7 copy-done.10
  27.5 2.2 %shard_map.188 = (bf16[16,3072]{1,0:T(8,128)(2,1)}, bf16[16,3072]{1,0:T(8,128)(2,1)}, bf16[16,3072]{1,0:T(8,128)(2,1)}, bf16[16,3072]{1,0:T(8,128)(2,1)}) custom-call(s32[4]{0:T(128)} %get-tuple-element.82.source_ref, bf16[2,16,3072]{2,1,0:T(8,128)(2,1)} %get-tuple-element.65.refs_0_, bf16[2,16,3072]{2,1,0:T(8,128)(2,1)} %copy-done.9, ...), custom_call_target="tpu_custom_call" | custom-call | tf_op jit(solution)/shard_map/pallas_call | solution.py:248
  29.7 1.3 collective-permute-start.4
  31.0 2.6 %collective-permute-start.5 = (bf16[16,3072]{1,0:T(8,128)(2,1)}, bf16[16,3072]{1,0:T(8,128)(2,1)S(1)}, u32[]{:S(2)}, u32[]{:S(2)}) collective-permute-start(bf16[16,3072]{1,0:T(8,128)(2,1)} %get-tuple-element.32), channel_id=1, source_target_pairs={{0,128},{64,192},{128,0},{192,64},{1,129},{65,193},{129,1},{193,65... | collective-permute-start | bytes 294920 | tf_op jit(solution)/shard_map/ppermute | solution.py:182
  33.6 1.1 collective-permute-start.6
  34.9 2.4 %collective-permute-done.5 = bf16[16,3072]{1,0:T(8,128)(2,1)S(1)} collective-permute-done((bf16[16,3072]{1,0:T(8,128)(2,1)}, bf16[16,3072]{1,0:T(8,128)(2,1)S(1)}, u32[]{:S(2)}, u32[]{:S(2)}) %collective-permute-start.5) | collective-permute-done | bytes 98336 | tf_op jit(solution)/shard_map/ppermute | solution.py:182
  37.3 1.0 collective-permute-done.6
  38.5 0.7 copy.57
  39.1 6.5 %all-to-all-start.1 = ((bf16[8,16,384]{2,1,0:T(8,128)(2,1)}), bf16[8,16,384]{2,1,0:T(8,128)(2,1)S(1)}, u32[]{:S(2)}, u32[]{:S(2)}) async-start(bf16[8,16,384]{2,1,0:T(8,128)(2,1)} %copy.57), calls=%async_computation.1 | async-start | bytes 196608 | tf_op jit(solution)/shard_map/all_to_all | solution.py:175
  46.1 1.2 copy.54
  47.2 6.1 %all-to-all-done.1 = bf16[8,16,384]{2,1,0:T(8,128)(2,1)S(1)} async-done(((bf16[8,16,384]{2,1,0:T(8,128)(2,1)}), bf16[8,16,384]{2,1,0:T(8,128)(2,1)S(1)}, u32[]{:S(2)}, u32[]{:S(2)}) %all-to-all-start.1) | async-done | bytes 98336 | tf_op jit(solution)/shard_map/all_to_all | solution.py:175
  53.5 4.2 %collective-permute-start.8 = (bf16[4,16,384]{2,1,0:T(8,128)(2,1)S(1)}, bf16[4,16,384]{2,1,0:T(8,128)(2,1)S(1)}, u32[]{:S(2)}, u32[]{:S(2)}) collective-permute-start(bf16[4,16,384]{2,1,0:T(8,128)(2,1)S(1)} %pad_maximum_fusion.2), channel_id=1, source_target_pairs={{0,128},{64,192},{128,0},{192,64},{1,129},{65,193},{129,1},{193,65... | collective-permute-start | bytes 147464 | tf_op jit(solution)/shard_map/ppermute | solution.py:182
  57.8 3.6 %all-to-all-start.2 = ((bf16[8,128,384]{2,1,0:T(8,128)(2,1)}), bf16[8,128,384]{2,1,0:T(8,128)(2,1)S(1)}, u32[]{:S(2)}, u32[]{:S(2)}) async-start(bf16[8,128,384]{2,1,0:T(8,128)(2,1)} %bitcast.1), calls=%async_computation.2 | async-start | bytes 1572864 | tf_op jit(solution)/shard_map/all_to_all | solution.py:175
  61.5 1.2 collective-permute-start.10
  62.7 2.0 %collective-permute-start.11 = (bf16[4,4,16,384]{3,2,0,1:T(8,128)(2,1)S(1)}, bf16[4,4,16,384]{3,2,0,1:T(8,128)(2,1)S(1)}, u32[]{:S(2)}, u32[]{:S(2)}) collective-permute-start(bf16[4,4,16,384]{3,2,0,1:T(8,128)(2,1)S(1)} %bitcast_dynamic-update-slice_fusion.8), channel_id=1, source_target_pairs={{0,32},{1,33},{32,0},{33,1},{2,34},{3,35},{34,2},{35,3},{4,36},{5,... | collective-permute-start | bytes 589832 | tf_op jit(solution)/shard_map/ppermute | solution.py:182
  65.5 1.8 %collective-permute-done.10 = bf16[4,4,16,384]{3,2,0,1:T(8,128)(2,1)S(1)} collective-permute-done((bf16[4,4,16,384]{3,2,0,1:T(8,128)(2,1)S(1)}, bf16[4,4,16,384]{3,2,0,1:T(8,128)(2,1)S(1)}, u32[]{:S(2)}, u32[]{:S(2)}) %collective-permute-start.10) | collective-permute-done | bytes 196640 | tf_op jit(solution)/shard_map/ppermute | solution.py:182
  67.3 2.6 %collective-permute-done.11 = bf16[4,4,16,384]{3,2,0,1:T(8,128)(2,1)S(1)} collective-permute-done((bf16[4,4,16,384]{3,2,0,1:T(8,128)(2,1)S(1)}, bf16[4,4,16,384]{3,2,0,1:T(8,128)(2,1)S(1)}, u32[]{:S(2)}, u32[]{:S(2)}) %collective-permute-start.11) | collective-permute-done | bytes 196640 | tf_op jit(solution)/shard_map/ppermute | solution.py:182
  70.4 5.6 %collective-permute-start.14 = (bf16[3,4,4,16,384]{4,3,2,1,0:T(8,128)(2,1)S(1)}, bf16[3,4,4,16,384]{4,3,2,1,0:T(8,128)(2,1)S(1)}, u32[]{:S(2)}, u32[]{:S(2)}) collective-permute-start(bf16[3,4,4,16,384]{4,3,2,1,0:T(8,128)(2,1)S(1)} %slice_bitcast_fusion), channel_id=1, source_target_pairs={{0,16},{16,0},{1,17},{17,1},{2,18},{18,2},{3,19},{19,3},{4,20},{20... | collective-permute-start | bytes 1769480 | tf_op jit(solution)/shard_map/ppermute | solution.py:182
  76.4 1.3 collective-permute-done.14
  78.0 3.3 %all-to-all-done.2.v_ref = bf16[8,128,384]{2,1,0:T(8,128)(2,1)S(1)} async-done(((bf16[8,128,384]{2,1,0:T(8,128)(2,1)}), bf16[8,128,384]{2,1,0:T(8,128)(2,1)S(1)}, u32[]{:S(2)}, u32[]{:S(2)}) %all-to-all-start.2) | async-done | bytes 786464 | tf_op jit(solution)/shard_map/all_to_all | solution.py:175
  81.3 4.1 %collective-permute-start.13 = (bf16[4,4,16,384]{3,2,1,0:T(8,128)(2,1)S(1)}, bf16[4,4,16,384]{3,2,1,0:T(8,128)(2,1)S(1)}, u32[]{:S(2)}, u32[]{:S(2)}) collective-permute-start(bf16[4,4,16,384]{3,2,1,0:T(8,128)(2,1)S(1)} %slice_bitcast_fusion.1), channel_id=1, source_target_pairs={{0,16},{16,0},{1,17},{17,1},{2,18},{18,2},{3,19},{19,3},{4,20},{20... | collective-permute-start | bytes 589832 | tf_op jit(solution)/shard_map/ppermute | solution.py:182
  85.5 1.0 collective-permute-done.13
  86.5 5.4 %shard_map.189 = f32[3,2,1024]{2,1,0:T(2,128)S(1)} custom-call(bf16[512,384]{1,0:T(8,128)(2,1)S(1)} %bitcast.145, bf16[512,384]{1,0:T(8,128)(2,1)S(1)} %bitcast.142, bf16[1024,384]{1,0:T(8,128)(2,1)S(1)} %pad_maximum_fusion.1.cot_ref, bf16[8,128,384]{2,1,0:T(8,128)(2,1)S(1)} %all-to-all-done.k_ref, bf16[8,128,384]{2,1,0:T(8,128)(2,1)S(1)} %all-to-all-done.2.v_ref, ...), custom_call_target="tpu_custom_call" | custom-call | flops 1610612736 | bytes 6000000 | tf_op jit(solution)/shard_map/pallas_call | solution.py:139
  92.4 0.8 collective-permute-done.15
  93.3 1.2 collective-permute-start.16
  94.5 2.0 %collective-permute-start.17 = (f32[3,2,1024]{2,1,0:T(2,128)S(1)}, f32[3,2,1024]{2,1,0:T(2,128)S(1)}, u32[]{:S(2)}, u32[]{:S(2)}) collective-permute-start(f32[3,2,1024]{2,1,0:T(2,128)S(1)} %add.109), channel_id=1, source_target_pairs={{0,32},{1,33},{32,0},{33,1},{2,34},{3,35},{34,2},{35,3},{4,36},{5,... | collective-permute-start | bytes 73736 | tf_op jit(solution)/shard_map/ppermute | solution.py:182
  97.2 1.6 collective-permute-done.17
  98.8 0.7 collective-permute-done.18
  99.6 1.5 collective-permute-start.19
  101.0 2.5 %collective-permute-start.21 = (f32[3,2,1024]{2,1,0:T(2,128)S(1)}, f32[3,2,1024]{2,1,0:T(2,128)S(1)}, u32[]{:S(2)}, u32[]{:S(2)}) collective-permute-start(f32[3,2,1024]{2,1,0:T(2,128)S(1)} %add_add_fusion.1), channel_id=1, source_target_pairs={{0,192},{64,0},{128,64},{192,128},{1,193},{65,1},{129,65},{193,129... | collective-permute-start | bytes 73736 | tf_op jit(solution)/shard_map/ppermute | solution.py:182
  103.5 1.7 collective-permute-done.20
  105.3 4.2 %shard_map.190 = (bf16[32,64,128]{2,1,0:T(8,128)(2,1)S(1)}, bf16[8,256,128]{2,1,0:T(8,128)(2,1)}, bf16[16,128]{1,0:T(8,128)(2,1)S(1)}, bf16[16,128]{1,0:T(8,128)(2,1)S(1)}) custom-call(bf16[512,384]{1,0:T(8,128)(2,1)S(1)} %bitcast.146, bf16[512,384]{1,0:T(8,128)(2,1)S(1)} %bitcast.143, bf16[1024,384]{1,0:T(8,128)(2,1)S(1)} %pad_maximum_fusion.1.cot_ref, ...), custom_call_target="tpu_custom_call" | custom-call | flops 1610612736 | bytes 2000000 | tf_op jit(solution)/shard_map/pallas_call | solution.py:162
  109.4 4.4 %all-to-all-start.3 = ((bf16[8,256,128]{2,1,0:T(8,128)(2,1)}), bf16[8,256,128]{2,1,0:T(8,128)(2,1)}, u32[]{:S(2)}, u32[]{:S(2)}) async-start(bf16[8,256,128]{2,1,0:T(8,128)(2,1)} %get-tuple-element.42), calls=%async_computation.3 | async-start | bytes 1048576 | tf_op jit(solution)/shard_map/all_to_all | solution.py:175
  113.8 1.0 copy-done.1
  114.8 8.9 %shard_map.191 = (bf16[32,64,256]{2,1,0:T(8,128)(2,1)S(1)}, bf16[8,256,256]{2,1,0:T(8,128)(2,1)}, bf16[16,256]{1,0:T(8,128)(2,1)S(1)}, bf16[16,256]{1,0:T(8,128)(2,1)S(1)}) custom-call(bf16[512,384]{1,0:T(8,128)(2,1)S(1)} %bitcast.147, bf16[512,384]{1,0:T(8,128)(2,1)S(1)} %bitcast.144, bf16[1024,384]{1,0:T(8,128)(2,1)S(1)} %pad_maximum_fusion.1.cot_ref, ...), custom_call_target="tpu_custom_call" | custom-call | flops 3221225472 | bytes 4000000 | tf_op jit(solution)/shard_map/pallas_call | solution.py:162
  123.9 4.8 %all-to-all-done.3.lead_ref = bf16[8,256,128]{2,1,0:T(8,128)(2,1)} async-done(((bf16[8,256,128]{2,1,0:T(8,128)(2,1)}), bf16[8,256,128]{2,1,0:T(8,128)(2,1)}, u32[]{:S(2)}, u32[]{:S(2)}) %all-to-all-start.3) | async-done | bytes 524320 | tf_op jit(solution)/shard_map/all_to_all | solution.py:175
  128.7 1.0 dynamic-slice_bitcast_fusion
  129.7 2.6 %collective-permute-start.22 = (bf16[4,4,64,384]{3,2,1,0:T(8,128)(2,1)}, bf16[4,4,64,384]{3,2,1,0:T(8,128)(2,1)}, u32[]{:S(2)}, u32[]{:S(2)}) collective-permute-start(bf16[4,4,64,384]{3,2,1,0:T(8,128)(2,1)} %dynamic-slice_bitcast_fusion), channel_id=1, source_target_pairs={{0,16},{16,0},{1,17},{17,1},{2,18},{18,2},{3,19},{19,3},{4,20},{20... | collective-permute-start | bytes 2359304 | tf_op jit(solution)/shard_map/ppermute | solution.py:182
  132.3 3.6 %all-to-all-start.4 = ((bf16[8,256,256]{2,1,0:T(8,128)(2,1)}), bf16[8,256,256]{2,1,0:T(8,128)(2,1)S(1)}, u32[]{:S(2)}, u32[]{:S(2)}) async-start(bf16[8,256,256]{2,1,0:T(8,128)(2,1)} %get-tuple-element.45), calls=%async_computation.4 | async-start | bytes 2097152 | tf_op jit(solution)/shard_map/all_to_all | solution.py:175
  135.9 2.2 %fusion = bf16[4,4,64,384]{3,2,1,0:T(8,128)(2,1)} fusion(bf16[4,4,64,384]{3,2,1,0:T(8,128)(2,1)} %collective-permute-done.22, bf16[2,4,4,64,384]{4,3,2,1,0:T(8,128)(2,1)S(1)} %bitcast.149, s32[]{:T(128)S(6)} %axis_index.35), kind=kLoop, calls=%fused_computation.2 | loop fusion | flops 1572864 | bytes 2359300 | tf_op jit(solution)/shard_map/convert_element_type | solution.py:224
  138.2 1.2 dynamic-slice_bitcast_fusion.3
  139.5 3.0 %collective-permute-start.24 = (bf16[4,64,384]{2,1,0:T(8,128)(2,1)S(1)}, bf16[4,64,384]{2,1,0:T(8,128)(2,1)S(1)}, u32[]{:S(2)}, u32[]{:S(2)}) collective-permute-start(bf16[4,64,384]{2,1,0:T(8,128)(2,1)S(1)} %get-tuple-element.63), channel_id=1, source_target_pairs={{0,32},{1,33},{32,0},{33,1},{2,34},{3,35},{34,2},{35,3},{4,36},{5,... | collective-permute-start | bytes 589832 | tf_op jit(solution)/shard_map/ppermute | solution.py:182
  142.7 4.5 %collective-permute-done.23 = bf16[4,64,384]{2,1,0:T(8,128)(2,1)S(1)} collective-permute-done((bf16[4,64,384]{2,1,0:T(8,128)(2,1)S(1)}, bf16[4,64,384]{2,1,0:T(8,128)(2,1)S(1)}, u32[]{:S(2)}, u32[]{:S(2)}) %collective-permute-start.23) | collective-permute-done | bytes 196640 | tf_op jit(solution)/shard_map/ppermute | solution.py:182
  147.2 4.5 %collective-permute-done.24 = bf16[4,64,384]{2,1,0:T(8,128)(2,1)S(1)} collective-permute-done((bf16[4,64,384]{2,1,0:T(8,128)(2,1)S(1)}, bf16[4,64,384]{2,1,0:T(8,128)(2,1)S(1)}, u32[]{:S(2)}, u32[]{:S(2)}) %collective-permute-start.24) | collective-permute-done | bytes 196640 | tf_op jit(solution)/shard_map/ppermute | solution.py:182
  151.7 1.0 fusion.3
  153.2 3.0 %collective-permute-start.27 = (bf16[64,384]{1,0:T(8,128)(2,1)S(1)}, bf16[64,384]{1,0:T(8,128)(2,1)S(1)}, u32[]{:S(2)}, u32[]{:S(2)}) collective-permute-start(bf16[64,384]{1,0:T(8,128)(2,1)S(1)} %get-tuple-element.72), channel_id=1, source_target_pairs={{0,128},{64,192},{128,0},{192,64},{1,129},{65,193},{129,1},{193,65... | collective-permute-start | bytes 147464 | tf_op jit(solution)/shard_map/ppermute | solution.py:182
  156.4 0.6 pad_maximum_fusion.3
  157.0 8.0 %all-to-all-done.4.late_ref = bf16[8,256,256]{2,1,0:T(8,128)(2,1)S(1)} async-done(((bf16[8,256,256]{2,1,0:T(8,128)(2,1)}), bf16[8,256,256]{2,1,0:T(8,128)(2,1)S(1)}, u32[]{:S(2)}, u32[]{:S(2)}) %all-to-all-start.4) | async-done | bytes 1048608 | tf_op jit(solution)/shard_map/all_to_all | solution.py:175
  165.1 1.0 copy-done.4
  166.1 2.8 %shard_map.192 = (bf16[128,3072]{1,0:T(8,128)(2,1)}, bf16[128,3072]{1,0:T(8,128)(2,1)}) custom-call(bf16[8,256,128]{2,1,0:T(8,128)(2,1)} %all-to-all-done.3.lead_ref, bf16[8,256,256]{2,1,0:T(8,128)(2,1)} %copy-done.4), custom_call_target="tpu_custom_call" | custom-call | tf_op jit(solution)/shard_map/pallas_call | solution.py:320
  169.3 0.6 fusion.20
  169.9 0.6 fusion.27
  170.8 0.6 fusion.23
  (116 shorter events, 6.6 us)
Async XLA Ops:
  0.6 4.6 %copy-start.5 = (bf16[128,3072]{1,0:T(8,128)(2,1)S(1)}, bf16[128,3072]{1,0:T(8,128)(2,1)}, u32[]{:S(2)}) copy-start(bf16[128,3072]{1,0:T(8,128)(2,1)} %param.14) | copy-start | bytes 2359300
  1.9 11.5 %collective-permute-start = (bf16[4,16,3072]{2,1,0:T(8,128)(2,1)S(1)}, bf16[4,16,3072]{2,1,0:T(8,128)(2,1)S(1)}, u32[]{:S(2)}, u32[]{:S(2)}) collective-permute-start(bf16[4,16,3072]{2,1,0:T(8,128)(2,1)S(1)} %bitcast.159), channel_id=1, source_target_pairs={{0,16},{16,0},{1,17},{17,1},{2,18},{18,2},{3,19},{19,3},{4,20},{20... | collective-permute-start | bytes 1179656 | tf_op jit(solution)/shard_map/ppermute | solution.py:182
  6.8 12.2 %copy-start.21 = (s32[4]{0:T(128)S(1)}, s32[4]{0:T(128)}, u32[]{:S(2)}) copy-start(s32[4]{0:T(128)} %param.23) | copy-start | bytes 52
  6.8 31.6 %all-to-all-start = ((bf16[8,128,384]{2,1,0:T(8,128)(2,1)}), bf16[8,128,384]{2,1,0:T(8,128)(2,1)S(1)}, u32[]{:S(2)}, u32[]{:S(2)}) async-start(bf16[8,128,384]{2,1,0:T(8,128)(2,1)} %bitcast.17), calls=%async_computation | async-start | bytes 1572864 | tf_op jit(solution)/shard_map/all_to_all | solution.py:175
  13.4 32.3 %copy-start.6 = (bf16[128,3072]{1,0:T(8,128)(2,1)S(1)}, bf16[128,3072]{1,0:T(8,128)(2,1)}, u32[]{:S(2)}) copy-start(bf16[128,3072]{1,0:T(8,128)(2,1)} %param.15) | copy-start | bytes 2359300
  14.1 7.4 %collective-permute-start.1 = (bf16[2,16,3072]{2,1,0:T(8,128)(2,1)S(1)}, bf16[2,16,3072]{2,1,0:T(8,128)(2,1)S(1)}, u32[]{:S(2)}, u32[]{:S(2)}) collective-permute-start(bf16[2,16,3072]{2,1,0:T(8,128)(2,1)S(1)} %get-tuple-element.66), channel_id=1, source_target_pairs={{0,1},{1,32},{32,33},{33,0},{2,3},{3,34},{34,35},{35,2},{4,5},{5,3... | collective-permute-start | bytes 589832 | tf_op jit(solution)/shard_map/ppermute | solution.py:182
  15.4 11.4 %collective-permute-start.2 = (bf16[2,16,3072]{2,1,0:T(8,128)(2,1)S(1)}, bf16[2,16,3072]{2,1,0:T(8,128)(2,1)S(1)}, u32[]{:S(2)}, u32[]{:S(2)}) collective-permute-start(bf16[2,16,3072]{2,1,0:T(8,128)(2,1)S(1)} %get-tuple-element.67), channel_id=1, source_target_pairs={{0,32},{1,33},{32,0},{33,1},{2,34},{3,35},{34,2},{35,3},{4,36},{5,... | collective-permute-start | bytes 589832 | tf_op jit(solution)/shard_map/ppermute | solution.py:182
  17.8 8.9 %collective-permute-start.3 = (bf16[2,16,3072]{2,1,0:T(8,128)(2,1)S(1)}, bf16[2,16,3072]{2,1,0:T(8,128)(2,1)S(1)}, u32[]{:S(2)}, u32[]{:S(2)}) collective-permute-start(bf16[2,16,3072]{2,1,0:T(8,128)(2,1)S(1)} %get-tuple-element.64), channel_id=1, source_target_pairs={{0,33},{1,0},{32,1},{33,32},{2,35},{3,2},{34,3},{35,34},{4,37},{5,... | collective-permute-start | bytes 589832 | tf_op jit(solution)/shard_map/ppermute | solution.py:182
  21.6 5.2 %copy-start.9 = (bf16[2,16,3072]{2,1,0:T(8,128)(2,1)}, bf16[2,16,3072]{2,1,0:T(8,128)(2,1)S(1)}, u32[]{:S(2)}) copy-start(bf16[2,16,3072]{2,1,0:T(8,128)(2,1)S(1)} %collective-permute-done.1.refs_1_) | copy-start | bytes 589828
  26.8 0.7 copy-start.10
  26.8 0.8 copy-start.11
  29.7 5.2 %collective-permute-start.4 = (bf16[16,3072]{1,0:T(8,128)(2,1)}, bf16[16,3072]{1,0:T(8,128)(2,1)S(1)}, u32[]{:S(2)}, u32[]{:S(2)}) collective-permute-start(bf16[16,3072]{1,0:T(8,128)(2,1)} %get-tuple-element.31), channel_id=1, source_target_pairs={{0,64},{64,128},{128,192},{192,0},{1,65},{65,129},{129,193},{193,1... | collective-permute-start | bytes 294920 | tf_op jit(solution)/shard_map/ppermute | solution.py:182
  31.0 6.3 %collective-permute-start.5 = (bf16[16,3072]{1,0:T(8,128)(2,1)}, bf16[16,3072]{1,0:T(8,128)(2,1)S(1)}, u32[]{:S(2)}, u32[]{:S(2)}) collective-permute-start(bf16[16,3072]{1,0:T(8,128)(2,1)} %get-tuple-element.32), channel_id=1, source_target_pairs={{0,128},{64,192},{128,0},{192,64},{1,129},{65,193},{129,1},{193,65... | collective-permute-start | bytes 294920 | tf_op jit(solution)/shard_map/ppermute | solution.py:182
  33.6 4.8 %collective-permute-start.6 = (bf16[16,3072]{1,0:T(8,128)(2,1)}, bf16[16,3072]{1,0:T(8,128)(2,1)S(1)}, u32[]{:S(2)}, u32[]{:S(2)}) collective-permute-start(bf16[16,3072]{1,0:T(8,128)(2,1)} %get-tuple-element.33), channel_id=1, source_target_pairs={{0,192},{64,0},{128,64},{192,128},{1,193},{65,1},{129,65},{193,129... | collective-permute-start | bytes 294920 | tf_op jit(solution)/shard_map/ppermute | solution.py:182
  39.1 14.2 %all-to-all-start.1 = ((bf16[8,16,384]{2,1,0:T(8,128)(2,1)}), bf16[8,16,384]{2,1,0:T(8,128)(2,1)S(1)}, u32[]{:S(2)}, u32[]{:S(2)}) async-start(bf16[8,16,384]{2,1,0:T(8,128)(2,1)} %copy.57), calls=%async_computation.1 | async-start | bytes 196608 | tf_op jit(solution)/shard_map/all_to_all | solution.py:175
  45.7 7.7 %copy-start.12 = (bf16[16,384]{1,0:T(8,128)(2,1)S(1)}, bf16[16,384]{1,0:T(8,128)(2,1)}, u32[]{:S(2)}) copy-start(bf16[16,384]{1,0:T(8,128)(2,1)} %param.16) | copy-start | bytes 36868
  45.7 7.7 %copy-start.14 = (bf16[16,384]{1,0:T(8,128)(2,1)S(1)}, bf16[16,384]{1,0:T(8,128)(2,1)}, u32[]{:S(2)}) copy-start(bf16[16,384]{1,0:T(8,128)(2,1)} %param.25) | copy-start | bytes 36868
  45.7 7.7 %copy-start.15 = (bf16[16,384]{1,0:T(8,128)(2,1)S(1)}, bf16[16,384]{1,0:T(8,128)(2,1)}, u32[]{:S(2)}) copy-start(bf16[16,384]{1,0:T(8,128)(2,1)} %param.24) | copy-start | bytes 36868
  53.4 4.4 %copy-start.7 = (bf16[16,384]{1,0:T(8,128)(2,1)}, bf16[16,384]{1,0:T(8,128)(2,1)S(1)}, u32[]{:S(2)}) copy-start(bf16[16,384]{1,0:T(8,128)(2,1)S(1)} %dynamic-slice_bitcast_fusion.7) | copy-start | bytes 36868
  53.4 7.9 %collective-permute-start.7 = (bf16[4,16,384]{2,1,0:T(8,128)(2,1)S(1)}, bf16[4,16,384]{2,1,0:T(8,128)(2,1)S(1)}, u32[]{:S(2)}, u32[]{:S(2)}) collective-permute-start(bf16[4,16,384]{2,1,0:T(8,128)(2,1)S(1)} %pad_maximum_fusion.2), channel_id=1, source_target_pairs={{0,64},{64,128},{128,192},{192,0},{1,65},{65,129},{129,193},{193,1... | collective-permute-start | bytes 147464 | tf_op jit(solution)/shard_map/ppermute | solution.py:182
  53.5 7.9 %collective-permute-start.8 = (bf16[4,16,384]{2,1,0:T(8,128)(2,1)S(1)}, bf16[4,16,384]{2,1,0:T(8,128)(2,1)S(1)}, u32[]{:S(2)}, u32[]{:S(2)}) collective-permute-start(bf16[4,16,384]{2,1,0:T(8,128)(2,1)S(1)} %pad_maximum_fusion.2), channel_id=1, source_target_pairs={{0,128},{64,192},{128,0},{192,64},{1,129},{65,193},{129,1},{193,65... | collective-permute-start | bytes 147464 | tf_op jit(solution)/shard_map/ppermute | solution.py:182
  57.8 3.7 %collective-permute-start.9 = (bf16[4,16,384]{2,1,0:T(8,128)(2,1)S(1)}, bf16[4,16,384]{2,1,0:T(8,128)(2,1)S(1)}, u32[]{:S(2)}, u32[]{:S(2)}) collective-permute-start(bf16[4,16,384]{2,1,0:T(8,128)(2,1)S(1)} %pad_maximum_fusion.2), channel_id=1, source_target_pairs={{0,192},{64,0},{128,64},{192,128},{1,193},{65,1},{129,65},{193,129... | collective-permute-start | bytes 147464 | tf_op jit(solution)/shard_map/ppermute | solution.py:182
  57.8 23.5 %all-to-all-start.2 = ((bf16[8,128,384]{2,1,0:T(8,128)(2,1)}), bf16[8,128,384]{2,1,0:T(8,128)(2,1)S(1)}, u32[]{:S(2)}, u32[]{:S(2)}) async-start(bf16[8,128,384]{2,1,0:T(8,128)(2,1)} %bitcast.1), calls=%async_computation.2 | async-start | bytes 1572864 | tf_op jit(solution)/shard_map/all_to_all | solution.py:175
  61.5 5.8 %collective-permute-start.10 = (bf16[4,4,16,384]{3,2,0,1:T(8,128)(2,1)S(1)}, bf16[4,4,16,384]{3,2,0,1:T(8,128)(2,1)S(1)}, u32[]{:S(2)}, u32[]{:S(2)}) collective-permute-start(bf16[4,4,16,384]{3,2,0,1:T(8,128)(2,1)S(1)} %bitcast_dynamic-update-slice_fusion.8), channel_id=1, source_target_pairs={{0,1},{1,32},{32,33},{33,0},{2,3},{3,34},{34,35},{35,2},{4,5},{5,3... | collective-permute-start | bytes 589832 | tf_op jit(solution)/shard_map/ppermute | solution.py:182
  62.7 7.2 %collective-permute-start.11 = (bf16[4,4,16,384]{3,2,0,1:T(8,128)(2,1)S(1)}, bf16[4,4,16,384]{3,2,0,1:T(8,128)(2,1)S(1)}, u32[]{:S(2)}, u32[]{:S(2)}) collective-permute-start(bf16[4,4,16,384]{3,2,0,1:T(8,128)(2,1)S(1)} %bitcast_dynamic-update-slice_fusion.8), channel_id=1, source_target_pairs={{0,32},{1,33},{32,0},{33,1},{2,34},{3,35},{34,2},{35,3},{4,36},{5,... | collective-permute-start | bytes 589832 | tf_op jit(solution)/shard_map/ppermute | solution.py:182
  64.8 5.5 %collective-permute-start.12 = (bf16[4,4,16,384]{3,2,0,1:T(8,128)(2,1)S(1)}, bf16[4,4,16,384]{3,2,0,1:T(8,128)(2,1)S(1)}, u32[]{:S(2)}, u32[]{:S(2)}) collective-permute-start(bf16[4,4,16,384]{3,2,0,1:T(8,128)(2,1)S(1)} %bitcast_dynamic-update-slice_fusion.8), channel_id=1, source_target_pairs={{0,33},{1,0},{32,1},{33,32},{2,35},{3,2},{34,3},{35,34},{4,37},{5,... | collective-permute-start | bytes 589832 | tf_op jit(solution)/shard_map/ppermute | solution.py:182
  65.4 10.6 %copy-start.16 = (f32[128]{0:T(128)S(1)}, f32[128]{0:T(128)}, u32[]{:S(2)}) copy-start(f32[128]{0:T(128)} %param.21) | copy-start | bytes 1540
  65.4 10.6 %copy-start.17 = (f32[128]{0:T(128)S(1)}, f32[128]{0:T(128)}, u32[]{:S(2)}) copy-start(f32[128]{0:T(128)} %param.19) | copy-start | bytes 1540
  65.4 10.6 %copy-start.19 = (f32[128]{0:T(128)S(1)}, f32[128]{0:T(128)}, u32[]{:S(2)}) copy-start(f32[128]{0:T(128)} %param.22) | copy-start | bytes 1540
  65.5 10.6 %copy-start.20 = (f32[128]{0:T(128)S(1)}, f32[128]{0:T(128)}, u32[]{:S(2)}) copy-start(f32[128]{0:T(128)} %param.20) | copy-start | bytes 1540
  70.4 7.3 %collective-permute-start.14 = (bf16[3,4,4,16,384]{4,3,2,1,0:T(8,128)(2,1)S(1)}, bf16[3,4,4,16,384]{4,3,2,1,0:T(8,128)(2,1)S(1)}, u32[]{:S(2)}, u32[]{:S(2)}) collective-permute-start(bf16[3,4,4,16,384]{4,3,2,1,0:T(8,128)(2,1)S(1)} %slice_bitcast_fusion), channel_id=1, source_target_pairs={{0,16},{16,0},{1,17},{17,1},{2,18},{18,2},{3,19},{19,3},{4,20},{20... | collective-permute-start | bytes 1769480 | tf_op jit(solution)/shard_map/ppermute | solution.py:182
  77.9 8.6 %copy-start.2 = (bf16[16,384]{1,0:T(8,128)(2,1)S(1)}, bf16[16,384]{1,0:T(8,128)(2,1)}, u32[]{:S(2)}) copy-start(bf16[16,384]{1,0:T(8,128)(2,1)} %tk_ref.5) | copy-start | bytes 36868
  77.9 8.6 %copy-start.3 = (bf16[16,384]{1,0:T(8,128)(2,1)S(1)}, bf16[16,384]{1,0:T(8,128)(2,1)}, u32[]{:S(2)}) copy-start(bf16[16,384]{1,0:T(8,128)(2,1)} %tv_ref.5) | copy-start | bytes 36868
  81.3 5.2 %collective-permute-start.13 = (bf16[4,4,16,384]{3,2,1,0:T(8,128)(2,1)S(1)}, bf16[4,4,16,384]{3,2,1,0:T(8,128)(2,1)S(1)}, u32[]{:S(2)}, u32[]{:S(2)}) collective-permute-start(bf16[4,4,16,384]{3,2,1,0:T(8,128)(2,1)S(1)} %slice_bitcast_fusion.1), channel_id=1, source_target_pairs={{0,16},{16,0},{1,17},{17,1},{2,18},{18,2},{3,19},{19,3},{4,20},{20... | collective-permute-start | bytes 589832 | tf_op jit(solution)/shard_map/ppermute | solution.py:182
  86.5 18.7 %copy-start = (bf16[2,4,4,16,384]{4,3,2,1,0:T(8,128)(2,1)}, bf16[2,4,4,16,384]{4,3,2,1,0:T(8,128)(2,1)S(1)}, u32[]{:S(2)}) copy-start(bf16[2,4,4,16,384]{4,3,2,1,0:T(8,128)(2,1)S(1)} %bitcast_dynamic-update-slice_fusion.5) | copy-start | bytes 1179652
  92.0 1.3 collective-permute-start.15
  93.3 4.0 %collective-permute-start.16 = (f32[3,2,1024]{2,1,0:T(2,128)S(1)}, f32[3,2,1024]{2,1,0:T(2,128)S(1)}, u32[]{:S(2)}, u32[]{:S(2)}) collective-permute-start(f32[3,2,1024]{2,1,0:T(2,128)S(1)} %add.109), channel_id=1, source_target_pairs={{0,1},{1,32},{32,33},{33,0},{2,3},{3,34},{34,35},{35,2},{4,5},{5,3... | collective-permute-start | bytes 73736 | tf_op jit(solution)/shard_map/ppermute | solution.py:182
  94.5 4.3 %collective-permute-start.17 = (f32[3,2,1024]{2,1,0:T(2,128)S(1)}, f32[3,2,1024]{2,1,0:T(2,128)S(1)}, u32[]{:S(2)}, u32[]{:S(2)}) collective-permute-start(f32[3,2,1024]{2,1,0:T(2,128)S(1)} %add.109), channel_id=1, source_target_pairs={{0,32},{1,33},{32,0},{33,1},{2,34},{3,35},{34,2},{35,3},{4,36},{5,... | collective-permute-start | bytes 73736 | tf_op jit(solution)/shard_map/ppermute | solution.py:182
  96.6 3.0 %collective-permute-start.18 = (f32[3,2,1024]{2,1,0:T(2,128)S(1)}, f32[3,2,1024]{2,1,0:T(2,128)S(1)}, u32[]{:S(2)}, u32[]{:S(2)}) collective-permute-start(f32[3,2,1024]{2,1,0:T(2,128)S(1)} %add.109), channel_id=1, source_target_pairs={{0,33},{1,0},{32,1},{33,32},{2,35},{3,2},{34,3},{35,34},{4,37},{5,... | collective-permute-start | bytes 73736 | tf_op jit(solution)/shard_map/ppermute | solution.py:182
  99.6 4.0 %collective-permute-start.19 = (f32[3,2,1024]{2,1,0:T(2,128)S(1)}, f32[3,2,1024]{2,1,0:T(2,128)S(1)}, u32[]{:S(2)}, u32[]{:S(2)}) collective-permute-start(f32[3,2,1024]{2,1,0:T(2,128)S(1)} %add_add_fusion.1), channel_id=1, source_target_pairs={{0,64},{64,128},{128,192},{192,0},{1,65},{65,129},{129,193},{193,1... | collective-permute-start | bytes 73736 | tf_op jit(solution)/shard_map/ppermute | solution.py:182
  101.0 4.2 %collective-permute-start.20 = (f32[3,2,1024]{2,1,0:T(2,128)S(1)}, f32[3,2,1024]{2,1,0:T(2,128)S(1)}, u32[]{:S(2)}, u32[]{:S(2)}) collective-permute-start(f32[3,2,1024]{2,1,0:T(2,128)S(1)} %add_add_fusion.1), channel_id=1, source_target_pairs={{0,128},{64,192},{128,0},{192,64},{1,129},{65,193},{129,1},{193,65... | collective-permute-start | bytes 73736 | tf_op jit(solution)/shard_map/ppermute | solution.py:182
  101.0 4.2 %collective-permute-start.21 = (f32[3,2,1024]{2,1,0:T(2,128)S(1)}, f32[3,2,1024]{2,1,0:T(2,128)S(1)}, u32[]{:S(2)}, u32[]{:S(2)}) collective-permute-start(f32[3,2,1024]{2,1,0:T(2,128)S(1)} %add_add_fusion.1), channel_id=1, source_target_pairs={{0,192},{64,0},{128,64},{192,128},{1,193},{65,1},{129,65},{193,129... | collective-permute-start | bytes 73736 | tf_op jit(solution)/shard_map/ppermute | solution.py:182
  109.4 19.3 %all-to-all-start.3 = ((bf16[8,256,128]{2,1,0:T(8,128)(2,1)}), bf16[8,256,128]{2,1,0:T(8,128)(2,1)}, u32[]{:S(2)}, u32[]{:S(2)}) async-start(bf16[8,256,128]{2,1,0:T(8,128)(2,1)} %get-tuple-element.42), calls=%async_computation.3 | async-start | bytes 1048576 | tf_op jit(solution)/shard_map/all_to_all | solution.py:175
  113.8 1.0 copy-start.1
  128.7 7.2 %copy-start.13 = (bf16[16,384]{1,0:T(8,128)(2,1)S(1)}, bf16[16,384]{1,0:T(8,128)(2,1)}, u32[]{:S(2)}) copy-start(bf16[16,384]{1,0:T(8,128)(2,1)} %param.16) | copy-start | bytes 36868
  129.7 6.3 %collective-permute-start.22 = (bf16[4,4,64,384]{3,2,1,0:T(8,128)(2,1)}, bf16[4,4,64,384]{3,2,1,0:T(8,128)(2,1)}, u32[]{:S(2)}, u32[]{:S(2)}) collective-permute-start(bf16[4,4,64,384]{3,2,1,0:T(8,128)(2,1)} %dynamic-slice_bitcast_fusion), channel_id=1, source_target_pairs={{0,16},{16,0},{1,17},{17,1},{2,18},{18,2},{3,19},{19,3},{4,20},{20... | collective-permute-start | bytes 2359304 | tf_op jit(solution)/shard_map/ppermute | solution.py:182
  132.3 32.8 %all-to-all-start.4 = ((bf16[8,256,256]{2,1,0:T(8,128)(2,1)}), bf16[8,256,256]{2,1,0:T(8,128)(2,1)S(1)}, u32[]{:S(2)}, u32[]{:S(2)}) async-start(bf16[8,256,256]{2,1,0:T(8,128)(2,1)} %get-tuple-element.45), calls=%async_computation.4 | async-start | bytes 2097152 | tf_op jit(solution)/shard_map/all_to_all | solution.py:175
  135.9 6.8 %copy-start.18 = (f32[128]{0:T(128)S(1)}, f32[128]{0:T(128)}, u32[]{:S(2)}) copy-start(f32[128]{0:T(128)} %param.19) | copy-start | bytes 1540
  135.9 6.8 %copy-start.8 = (bf16[16,384]{1,0:T(8,128)(2,1)S(1)}, bf16[16,384]{1,0:T(8,128)(2,1)}, u32[]{:S(2)}) copy-start(bf16[16,384]{1,0:T(8,128)(2,1)} %copy-done.7) | copy-start | bytes 36868
  139.4 7.8 %collective-permute-start.23 = (bf16[4,64,384]{2,1,0:T(8,128)(2,1)S(1)}, bf16[4,64,384]{2,1,0:T(8,128)(2,1)S(1)}, u32[]{:S(2)}, u32[]{:S(2)}) collective-permute-start(bf16[4,64,384]{2,1,0:T(8,128)(2,1)S(1)} %get-tuple-element.61), channel_id=1, source_target_pairs={{0,1},{1,32},{32,33},{33,0},{2,3},{3,34},{34,35},{35,2},{4,5},{5,3... | collective-permute-start | bytes 589832 | tf_op jit(solution)/shard_map/ppermute | solution.py:182
  139.5 12.3 %collective-permute-start.24 = (bf16[4,64,384]{2,1,0:T(8,128)(2,1)S(1)}, bf16[4,64,384]{2,1,0:T(8,128)(2,1)S(1)}, u32[]{:S(2)}, u32[]{:S(2)}) collective-permute-start(bf16[4,64,384]{2,1,0:T(8,128)(2,1)S(1)} %get-tuple-element.63), channel_id=1, source_target_pairs={{0,32},{1,33},{32,0},{33,1},{2,34},{3,35},{34,2},{35,3},{4,36},{5,... | collective-permute-start | bytes 589832 | tf_op jit(solution)/shard_map/ppermute | solution.py:182
  142.5 9.3 %collective-permute-start.25 = (bf16[4,64,384]{2,1,0:T(8,128)(2,1)S(1)}, bf16[4,64,384]{2,1,0:T(8,128)(2,1)S(1)}, u32[]{:S(2)}, u32[]{:S(2)}) collective-permute-start(bf16[4,64,384]{2,1,0:T(8,128)(2,1)S(1)} %get-tuple-element.62), channel_id=1, source_target_pairs={{0,33},{1,0},{32,1},{33,32},{2,35},{3,2},{34,3},{35,34},{4,37},{5,... | collective-permute-start | bytes 589832 | tf_op jit(solution)/shard_map/ppermute | solution.py:182
  152.8 16.1 %collective-permute-start.26 = (bf16[64,384]{1,0:T(8,128)(2,1)S(1)}, bf16[64,384]{1,0:T(8,128)(2,1)S(1)}, u32[]{:S(2)}, u32[]{:S(2)}) collective-permute-start(bf16[64,384]{1,0:T(8,128)(2,1)S(1)} %get-tuple-element.70), channel_id=1, source_target_pairs={{0,64},{64,128},{128,192},{192,0},{1,65},{65,129},{129,193},{193,1... | collective-permute-start | bytes 147464 | tf_op jit(solution)/shard_map/ppermute | solution.py:182
  153.2 15.6 %collective-permute-start.27 = (bf16[64,384]{1,0:T(8,128)(2,1)S(1)}, bf16[64,384]{1,0:T(8,128)(2,1)S(1)}, u32[]{:S(2)}, u32[]{:S(2)}) collective-permute-start(bf16[64,384]{1,0:T(8,128)(2,1)S(1)} %get-tuple-element.72), channel_id=1, source_target_pairs={{0,128},{64,192},{128,0},{192,64},{1,129},{65,193},{129,1},{193,65... | collective-permute-start | bytes 147464 | tf_op jit(solution)/shard_map/ppermute | solution.py:182
  156.3 12.6 %collective-permute-start.28 = (bf16[64,384]{1,0:T(8,128)(2,1)S(1)}, bf16[64,384]{1,0:T(8,128)(2,1)S(1)}, u32[]{:S(2)}, u32[]{:S(2)}) collective-permute-start(bf16[64,384]{1,0:T(8,128)(2,1)S(1)} %get-tuple-element.71), channel_id=1, source_target_pairs={{0,192},{64,0},{128,64},{192,128},{1,193},{65,1},{129,65},{193,129... | collective-permute-start | bytes 147464 | tf_op jit(solution)/shard_map/ppermute | solution.py:182
  165.1 1.0 copy-start.4

commit v6 on v4

--- a/solution.py
+++ b/solution.py
@@ -14,7 +14,8 @@
 LOG2E = math.log2(math.e)
 PLANE = ("y", "xh", "c", "xl")
 ROW = ("xh", "xl")
-KEY_BLOCK = 256
+KEY_BLOCK = 1024
+EARLY = 48
 VMEM = 48 * 1024 * 1024
 NT = (((1,), (1,)), ((), ()))
 NN = (((1,), (0,)), ((), ()))
@@ -52,11 +53,13 @@
 
 def key_parts(k_ref, v_ref, tk_ref, tv_ref, gains_ref):
     parts = []
-    step = KEY_BLOCK // v_ref.shape[1]
+    own = (k_ref.shape[1] + v_ref.shape[1]) // 2
+    step = KEY_BLOCK // own
     for start in range(0, v_ref.shape[0], step):
         spots = slice(start, start + step)
-        key = k_ref[spots].reshape(KEY_BLOCK, HD)
-        value = v_ref[spots].reshape(KEY_BLOCK, HD)
+        key = k_ref[spots, :own].reshape(KEY_BLOCK, HD)
+        value = jnp.concatenate((k_ref[spots, own:], v_ref[spots]), axis=1)
+        value = value.reshape(KEY_BLOCK, HD)
         parts.append((key, value, gains_ref[1:2], spots))
     parts.append((tk_ref[...], tv_ref[...], gains_ref[3:4], None))
     return parts
@@ -121,14 +124,14 @@
 
 
 def operand_specs(operands, gains):
-    win, text, cot, moved_k, moved_v, text_k, text_v = operands
-    shapes = [win.shape, text.shape, cot.shape, moved_v.shape, moved_v.shape]
-    specs = [column_spec(shape) for shape in shapes + [text_k.shape, text_v.shape]]
+    specs = [column_spec(array.shape) for array in operands]
     return specs + [pl.BlockSpec(gains.shape, lambda head: (0, 0))]
 
 
 def cost(operands, heads, dots):
-    work = operands[2].shape[0] * operands[4].shape[0] * operands[4].shape[1] * heads
+    _, _, cot, moved_k, moved_v, *_ = operands
+    keys = moved_k.shape[0] * (moved_k.shape[1] + moved_v.shape[1]) // 2
+    work = cot.shape[0] * keys * heads
     return pl.CostEstimate(
         flops=2 * dots * work * HD, bytes_accessed=2000000 * heads, transcendentals=work
     )
@@ -148,15 +151,16 @@
 
 
 def attention_grads(operands, gains, stats, heads, groups):
-    count = operands[2].shape[0]
-    z_size, own = operands[4].shape[:2]
-    text = operands[5].shape[0]
+    _, _, cot, moved_k, moved_v, text_k, _ = operands
+    count = cot.shape[0]
     width = heads * HD
     shapes = [
         jax.ShapeDtypeStruct((groups, count // groups * 2, width), BF16),
-        jax.ShapeDtypeStruct((z_size, 2 * own, width), BF16),
-        jax.ShapeDtypeStruct((text, width), BF16),
-        jax.ShapeDtypeStruct((text, width), BF16),
+        jax.ShapeDtypeStruct(
+            (moved_k.shape[0], moved_k.shape[1] + moved_v.shape[1], width), BF16
+        ),
+        jax.ShapeDtypeStruct((text_k.shape[0], width), BF16),
+        jax.ShapeDtypeStruct((text_k.shape[0], width), BF16),
     ]
     return pl.pallas_call(
         grads_kernel,
@@ -226,12 +230,30 @@
 
 def sum_plane(part):
     for axes in ("c", ROW, "y"):
-        size = lax.axis_size(axes)
-        bit = 1
-        while bit < size:
-            part = part + lax.ppermute(part, axes, [(i, i ^ bit) for i in range(size)])
-            bit *= 2
+        part = sum(push(part, axes, step) for step in range(lax.axis_size(axes)))
     return part
+
+
+def choose_kernel(source_ref, *refs):
+    parts, outs = refs[:-NWIN], refs[-NWIN:]
+    count = parts[0].shape[0]
+    for step, out in enumerate(outs):
+        source = source_ref[step]
+        for index in range(len(parts) * count):
+
+            @pl.when(source == index)
+            def _():
+                out[...] = parts[index // count][index % count]
+
+
+def choose(source, parts):
+    whole = pl.BlockSpec(memory_space=pltpu.VMEM)
+    return pl.pallas_call(
+        choose_kernel,
+        in_specs=[pl.BlockSpec(memory_space=pltpu.SMEM)] + [whole] * len(parts),
+        out_specs=[whole] * NWIN,
+        out_shape=[jax.ShapeDtypeStruct(parts[0].shape[1:], BF16)] * NWIN,
+    )(source, *parts)
 
 
 def fetch_window(video_q, window):
@@ -256,13 +278,15 @@
     source = from_x * c_size + ((c - c_of) & (c_size - 1))
     from_y = (y - y_of[0]) & (y_size - 1)
 
-    pieces = video_q.reshape(xh_size, c_size, xl_size, -1, model).transpose(1, 0, 2, 3, 4)
-    pieces = pieces.reshape(c_size, x_size, -1, model)
-    pieces = jnp.stack(scatter_stage(pieces, "c"), axis=1)
-    pieces = jnp.concatenate(scatter_stage(pieces, ROW), axis=0)
-    came = [place(pieces, source[0])] + [
-        push(place(pieces, source[step]), "y", step) for step in range(1, y_size)
-    ]
+    pieces = video_q.reshape(xh_size, c_size, xl_size, -1, model)
+
+    def side(index):
+        part = lax.dynamic_index_in_dim(pieces, index, 1, False, allow_negative_indices=False)
+        return part.reshape(x_size, -1, model)
+
+    pieces = jnp.stack((side(c), push(side(c ^ 1), "c", 1)), axis=1)
+    chosen = choose(source, scatter_stage(pieces, ROW))
+    came = [chosen[0]] + [push(chosen[step], "y", step) for step in range(1, y_size)]
     return place(jnp.stack(came), from_y), z_of[0]
 
 
@@ -315,12 +339,13 @@
     share = grad_out_video.shape[0]
     gains = jnp.stack((gain_video_q, gain_video_k, gain_text_q, gain_text_k))
 
-    moved_k = swap(split_heads(video_k, z_size), "z")
+    first_v, last_v = video_v[:EARLY], video_v[EARLY:]
+    moved_k = swap(split_heads(jnp.concatenate((video_k, first_v), axis=0), z_size), "z")
     picked, z_of = fetch_window(video_q, window)
     picked, moved_k = tie(picked, moved_k)
     came = swap(split_heads(picked, z_size), "z")
     own_window = place(came, z_of)
-    sent_v, own_window = tie(split_heads(video_v, z_size), own_window)
+    sent_v, own_window = tie(split_heads(last_v, z_size), own_window)
     moved_v = swap(sent_v, "z")
     own = jnp.stack((own_window, text_q, grad_out_video, grad_out_text))
     own = gather_stage(gather_stage(own, "y"), ROW)
@@ -331,8 +356,8 @@
     operands = (window_rows, text_rows, cotangent, moved_k, moved_v, text_k, text_v)
 
     stats = sum_plane(attention_stats(operands, gains, heads))
-    out, dmoved, key_text, value_text = attention_grads(operands, gains, stats, heads, groups)
-    back = swap(dmoved, "z")
+    out, back, key_text, value_text = attention_grads(operands, gains, stats, heads, groups)
+    back = swap(back, "z")
     total = sum_stage(reduce_row(out), "y")
     grad_video_k, grad_video_v = merge(back)
 

time: 174 us -> 171 us (0.983); the launches traced: 172 us -> 171 us
  waiting for transfers between devices: 67.4 us -> 64.6 us
  other arithmetic: 3.6 us -> 5.88 us
    ppermute x5 -> x0, starting transfers between devices: 7.91 us -> none  [sum_plane(): part = part + lax.ppermute(part, axes, [(i, i ^ bit) for i in range(size)])]
    ppermute x5 -> x0, waiting for transfers between devices: 7.47 us -> none  [sum_plane(): part = part + lax.ppermute(part, axes, [(i, i ^ bit) for i in range(size)])]
    ppermute x21 -> x28, waiting for transfers between devices: 28.5 us -> 35 us  [push(): lax.ppermute(array, axes, [(i, (i + step) % size) for i in range(size)])]
    ppermute x21 -> x28, starting transfers between devices: 37.7 us -> 43.2 us  [push(): lax.ppermute(array, axes, [(i, (i + step) % size) for i in range(size)])]
    unnamed x29 -> x43, local copies, waits for them, and re-layouts: 2.6 us -> 5.72 us
    squeeze x6 -> x4, local copies, waits for them, and re-layouts: 3.86 us -> 1.11 us  [place(): lax.dynamic_index_in_dim(array, index, 0, keepdims=False, allow_negative_...]
    pallas_call x0 -> x1, Pallas kernels: none -> 2.16 us  [choose(): pl.pallas_call(choose_kernel, in_specs=[pl.BlockSpec(memory_space=pltpu.S...]
    all_to_all x4, waiting for transfers between devices: 31.4 us -> 29.6 us  [swap(): return lax.all_to_all(array, axes, split_axis=0, concat_axis=0, tiled=True)]
  transfers between devices with their start and end apart: 30 -> 32, of which waited for: 20 -> 22; matrix products, arithmetic and copies ran while one was open for 7% -> 4% of each run, Pallas kernels for 0% -> 1%
where the time goes in v6:
time: 171 us
  starting transfers between devices  64.6 us (38%)
  waiting for transfers between devices  64.6 us (38%)
  Pallas kernels  22.4 us (13%)
  local copies, waits for them, and re-layouts  12.5 us (7%)
  other arithmetic  5.88 us (3%)
    ppermute x28, starting transfers between devices, push(): lax.ppermute(array, axes, [(i, (i + step) % size) for i in range(size)])  43.2 us
    ppermute x28, waiting for transfers between devices, push(): lax.ppermute(array, axes, [(i, (i + step) % size) for i in range(size)])  35 us
    all_to_all x4, waiting for transfers between devices, swap(): return lax.all_to_all(array, axes, split_axis=0, concat_axis=0, tiled=True)  29.6 us
    all_to_all x4, starting transfers between devices, swap(): return lax.all_to_all(array, axes, split_axis=0, concat_axis=0, tiled=True)  21.4 us
    pallas_call x1, Pallas kernels, attention_grads(): pl.pallas_call(grads_kernel, grid=(heads,), in_specs=operand_specs(operan...  12.2 us
    unnamed x43, local copies, waits for them, and re-layouts  5.72 us
    pallas_call x1, Pallas kernels, attention_stats(): pl.pallas_call(stats_kernel, grid=(heads,), in_specs=operand_specs(operan...  5.36 us
  transfers between devices with their start and end apart: 32, of which 22 were waited for; matrix products, arithmetic and copies ran while one was open for 4% of the time, Pallas kernels for 1%

profile of v6, /device:TPU:1, one launch (start us, length us, event | category | flops | bytes accessed | tf_op | source)
XLA Modules:
  0.0 171.3 jit_solution(13135456010145996624)
XLA Ops:
  0.6 1.0 slice.40
  1.6 1.2 pad_maximum_fusion
  2.8 1.1 copy.73
  4.0 9.1 %all-to-all-start = ((bf16[8,176,384]{2,1,0:T(8,128)(2,1)}), bf16[8,176,384]{2,1,0:T(8,128)(2,1)S(1)}, u32[]{:S(2)}, u32[]{:S(2)}) async-start(bf16[8,176,384]{2,1,0:T(8,128)(2,1)} %bitcast.140), calls=%async_computation | async-start | bytes 2162688 | tf_op jit(solution)/shard_map/all_to_all | solution.py:178
  13.2 1.0 collective-permute-start
  14.2 1.3 collective-permute-done
  15.6 0.7 fusion.5
  16.3 1.2 collective-permute-start.1
  17.6 2.5 %collective-permute-start.2 = (bf16[2,16,3072]{2,1,0:T(8,128)(2,1)S(1)}, bf16[2,16,3072]{2,1,0:T(8,128)(2,1)S(1)}, u32[]{:S(2)}, u32[]{:S(2)}) collective-permute-start(bf16[2,16,3072]{2,1,0:T(8,128)(2,1)S(1)} %get-tuple-element.56), channel_id=1, source_target_pairs={{0,32},{1,33},{32,0},{33,1},{2,34},{3,35},{34,2},{35,3},{4,36},{5,... | collective-permute-start | bytes 589832 | tf_op jit(solution)/shard_map/ppermute | solution.py:185
  20.0 1.2 collective-permute-start.3
  21.8 1.8 %collective-permute-done.1.refs_1_ = bf16[2,16,3072]{2,1,0:T(8,128)(2,1)S(1)} collective-permute-done((bf16[2,16,3072]{2,1,0:T(8,128)(2,1)S(1)}, bf16[2,16,3072]{2,1,0:T(8,128)(2,1)S(1)}, u32[]{:S(2)}, u32[]{:S(2)}) %collective-permute-start.1) | collective-permute-done | bytes 196640 | tf_op jit(solution)/shard_map/ppermute | solution.py:185
  23.7 5.2 %collective-permute-done.2.refs_2_ = bf16[2,16,3072]{2,1,0:T(8,128)(2,1)S(1)} collective-permute-done((bf16[2,16,3072]{2,1,0:T(8,128)(2,1)S(1)}, bf16[2,16,3072]{2,1,0:T(8,128)(2,1)S(1)}, u32[]{:S(2)}, u32[]{:S(2)}) %collective-permute-start.2) | collective-permute-done | bytes 196640 | tf_op jit(solution)/shard_map/ppermute | solution.py:185
  28.9 0.7 copy-done.11
  29.6 2.2 %shard_map.188 = (bf16[16,3072]{1,0:T(8,128)(2,1)}, bf16[16,3072]{1,0:T(8,128)(2,1)}, bf16[16,3072]{1,0:T(8,128)(2,1)}, bf16[16,3072]{1,0:T(8,128)(2,1)}) custom-call(s32[4]{0:T(128)} %get-tuple-element.71.source_ref, bf16[2,16,3072]{2,1,0:T(8,128)(2,1)} %get-tuple-element.54.refs_0_, bf16[2,16,3072]{2,1,0:T(8,128)(2,1)} %copy-done.10, ...), custom_call_target="tpu_custom_call" | custom-call | tf_op jit(solution)/shard_map/pallas_call | solution.py:251
  31.8 1.4 collective-permute-start.4
  33.2 2.6 %collective-permute-start.5 = (bf16[16,3072]{1,0:T(8,128)(2,1)}, bf16[16,3072]{1,0:T(8,128)(2,1)S(1)}, u32[]{:S(2)}, u32[]{:S(2)}) collective-permute-start(bf16[16,3072]{1,0:T(8,128)(2,1)} %get-tuple-element.26), channel_id=1, source_target_pairs={{0,128},{64,192},{128,0},{192,64},{1,129},{65,193},{129,1},{193,65... | collective-permute-start | bytes 294920 | tf_op jit(solution)/shard_map/ppermute | solution.py:185
  35.8 1.1 collective-permute-start.6
  36.9 2.8 %collective-permute-done.5 = bf16[16,3072]{1,0:T(8,128)(2,1)S(1)} collective-permute-done((bf16[16,3072]{1,0:T(8,128)(2,1)}, bf16[16,3072]{1,0:T(8,128)(2,1)S(1)}, u32[]{:S(2)}, u32[]{:S(2)}) %collective-permute-start.5) | collective-permute-done | bytes 98336 | tf_op jit(solution)/shard_map/ppermute | solution.py:185
  39.7 0.9 collective-permute-done.6
  40.7 2.3 %all-to-all-done.k_ref = bf16[8,176,384]{2,1,0:T(8,128)(2,1)S(1)} async-done(((bf16[8,176,384]{2,1,0:T(8,128)(2,1)}), bf16[8,176,384]{2,1,0:T(8,128)(2,1)S(1)}, u32[]{:S(2)}, u32[]{:S(2)}) %all-to-all-start) | async-done | bytes 1081376 | tf_op jit(solution)/shard_map/all_to_all | solution.py:178
  43.0 0.7 copy.51
  43.7 4.6 %all-to-all-start.1 = ((bf16[8,16,384]{2,1,0:T(8,128)(2,1)}), bf16[8,16,384]{2,1,0:T(8,128)(2,1)S(1)}, u32[]{:S(2)}, u32[]{:S(2)}) async-start(bf16[8,16,384]{2,1,0:T(8,128)(2,1)} %copy.51), calls=%async_computation.1 | async-start | bytes 196608 | tf_op jit(solution)/shard_map/all_to_all | solution.py:178
  48.3 0.8 copy.74
  49.1 6.9 %all-to-all-done.1 = bf16[8,16,384]{2,1,0:T(8,128)(2,1)S(1)} async-done(((bf16[8,16,384]{2,1,0:T(8,128)(2,1)}), bf16[8,16,384]{2,1,0:T(8,128)(2,1)S(1)}, u32[]{:S(2)}, u32[]{:S(2)}) %all-to-all-start.1) | async-done | bytes 98336 | tf_op jit(solution)/shard_map/all_to_all | solution.py:178
  56.2 4.3 %collective-permute-start.8 = (bf16[4,16,384]{2,1,0:T(8,128)(2,1)S(1)}, bf16[4,16,384]{2,1,0:T(8,128)(2,1)S(1)}, u32[]{:S(2)}, u32[]{:S(2)}) collective-permute-start(bf16[4,16,384]{2,1,0:T(8,128)(2,1)S(1)} %pad_maximum_fusion.2), channel_id=1, source_target_pairs={{0,128},{64,192},{128,0},{192,64},{1,129},{65,193},{129,1},{193,65... | collective-permute-start | bytes 147464 | tf_op jit(solution)/shard_map/ppermute | solution.py:185
  60.5 3.5 %all-to-all-start.2 = ((bf16[8,80,384]{2,1,0:T(8,128)(2,1)}), bf16[8,80,384]{2,1,0:T(8,128)(2,1)S(1)}, u32[]{:S(2)}, u32[]{:S(2)}) async-start(bf16[8,80,384]{2,1,0:T(8,128)(2,1)} %bitcast.142), calls=%async_computation.2 | async-start | bytes 983040 | tf_op jit(solution)/shard_map/all_to_all | solution.py:178
  64.2 1.1 collective-permute-start.10
  65.2 2.5 %collective-permute-start.11 = (bf16[4,4,16,384]{3,2,0,1:T(8,128)(2,1)S(1)}, bf16[4,4,16,384]{3,2,0,1:T(8,128)(2,1)S(1)}, u32[]{:S(2)}, u32[]{:S(2)}) collective-permute-start(bf16[4,4,16,384]{3,2,0,1:T(8,128)(2,1)S(1)} %bitcast_dynamic-update-slice_fusion.6), channel_id=1, source_target_pairs={{0,32},{1,33},{32,0},{33,1},{2,34},{3,35},{34,2},{35,3},{4,36},{5,... | collective-permute-start | bytes 589832 | tf_op jit(solution)/shard_map/ppermute | solution.py:185
  67.7 0.6 collective-permute-start.12
  68.5 1.5 collective-permute-done.10
  70.0 2.9 %collective-permute-done.11 = bf16[4,4,16,384]{3,2,0,1:T(8,128)(2,1)S(1)} collective-permute-done((bf16[4,4,16,384]{3,2,0,1:T(8,128)(2,1)S(1)}, bf16[4,4,16,384]{3,2,0,1:T(8,128)(2,1)S(1)}, u32[]{:S(2)}, u32[]{:S(2)}) %collective-permute-start.11) | collective-permute-done | bytes 196640 | tf_op jit(solution)/shard_map/ppermute | solution.py:185
  73.0 3.5 %all-to-all-done.2.v_ref = bf16[8,80,384]{2,1,0:T(8,128)(2,1)S(1)} async-done(((bf16[8,80,384]{2,1,0:T(8,128)(2,1)}), bf16[8,80,384]{2,1,0:T(8,128)(2,1)S(1)}, u32[]{:S(2)}, u32[]{:S(2)}) %all-to-all-start.2) | async-done | bytes 491552 | tf_op jit(solution)/shard_map/all_to_all | solution.py:178
  76.5 5.2 %collective-permute-start.13 = (bf16[4,4,4,16,384]{4,3,2,1,0:T(8,128)(2,1)S(1)}, bf16[4,4,4,16,384]{4,3,2,1,0:T(8,128)(2,1)S(1)}, u32[]{:S(2)}, u32[]{:S(2)}) collective-permute-start(bf16[4,4,4,16,384]{4,3,2,1,0:T(8,128)(2,1)S(1)} %bitcast.152), channel_id=1, source_target_pairs={{0,16},{16,0},{1,17},{17,1},{2,18},{18,2},{3,19},{19,3},{4,20},{20... | collective-permute-start | bytes 2359304 | tf_op jit(solution)/shard_map/ppermute | solution.py:185
  82.1 1.5 collective-permute-done.13
  84.1 0.6 copy-done.6
  84.7 5.4 %shard_map.189 = f32[3,2,1024]{2,1,0:T(2,128)S(1)} custom-call(bf16[512,384]{1,0:T(8,128)(2,1)S(1)} %bitcast.149, bf16[512,384]{1,0:T(8,128)(2,1)S(1)} %bitcast.147, bf16[1024,384]{1,0:T(8,128)(2,1)S(1)} %pad_maximum_fusion.1.cot_ref, bf16[8,176,384]{2,1,0:T(8,128)(2,1)S(1)} %all-to-all-done.k_ref, bf16[8,80,384]{2,1,0:T(8,128)(2,1)S(1)} %all-to-all-done.2.v_ref, ...), custom_call_target="tpu_custom_call" | custom-call | flops 1610612736 | bytes 6000000 | tf_op jit(solution)/shard_map/pallas_call | solution.py:142
  90.6 0.8 collective-permute-done.14
  91.5 1.1 collective-permute-start.15
  92.5 2.5 %collective-permute-start.16 = (f32[3,2,1024]{2,1,0:T(2,128)S(1)}, f32[3,2,1024]{2,1,0:T(2,128)S(1)}, u32[]{:S(2)}, u32[]{:S(2)}) collective-permute-start(f32[3,2,1024]{2,1,0:T(2,128)S(1)} %add.109), channel_id=1, source_target_pairs={{0,32},{1,33},{32,0},{33,1},{2,34},{3,35},{34,2},{35,3},{4,36},{5,... | collective-permute-start | bytes 73736 | tf_op jit(solution)/shard_map/ppermute | solution.py:185
  95.6 1.1 collective-permute-done.16
  96.7 1.2 collective-permute-done.17
  98.0 1.2 collective-permute-start.18
  99.3 2.4 %collective-permute-start.20 = (f32[3,2,1024]{2,1,0:T(2,128)S(1)}, f32[3,2,1024]{2,1,0:T(2,128)S(1)}, u32[]{:S(2)}, u32[]{:S(2)}) collective-permute-start(f32[3,2,1024]{2,1,0:T(2,128)S(1)} %add_add_fusion.1), channel_id=1, source_target_pairs={{0,192},{64,0},{128,64},{192,128},{1,193},{65,1},{129,65},{193,129... | collective-permute-start | bytes 73736 | tf_op jit(solution)/shard_map/ppermute | solution.py:185
  102.0 1.4 collective-permute-done.19
  103.4 1.0 copy-done.1
  104.5 1.0 copy-done.3
  105.5 1.0 copy-done.5
  106.5 12.2 %shard_map.190 = (bf16[32,64,384]{2,1,0:T(8,128)(2,1)S(1)}, bf16[8,256,384]{2,1,0:T(8,128)(2,1)}, bf16[16,384]{1,0:T(8,128)(2,1)}, bf16[16,384]{1,0:T(8,128)(2,1)}) custom-call(bf16[512,384]{1,0:T(8,128)(2,1)S(1)} %bitcast.150, bf16[512,384]{1,0:T(8,128)(2,1)S(1)} %bitcast.148, bf16[1024,384]{1,0:T(8,128)(2,1)S(1)} %pad_maximum_fusion.1.cot_ref, ...), custom_call_target="tpu_custom_call" | custom-call | flops 4831838208 | bytes 6000000 | tf_op jit(solution)/shard_map/pallas_call | solution.py:165
  118.7 1.0 dynamic-slice_bitcast_fusion
  119.7 3.0 %collective-permute-start.21 = (bf16[4,4,64,384]{3,2,1,0:T(8,128)(2,1)}, bf16[4,4,64,384]{3,2,1,0:T(8,128)(2,1)}, u32[]{:S(2)}, u32[]{:S(2)}) collective-permute-start(bf16[4,4,64,384]{3,2,1,0:T(8,128)(2,1)} %dynamic-slice_bitcast_fusion), channel_id=1, source_target_pairs={{0,16},{16,0},{1,17},{17,1},{2,18},{18,2},{3,19},{19,3},{4,20},{20... | collective-permute-start | bytes 2359304 | tf_op jit(solution)/shard_map/ppermute | solution.py:185
  122.7 4.1 %all-to-all-start.3 = ((bf16[8,256,384]{2,1,0:T(8,128)(2,1)}), bf16[8,256,384]{2,1,0:T(8,128)(2,1)S(1)}, u32[]{:S(2)}, u32[]{:S(2)}) async-start(bf16[8,256,384]{2,1,0:T(8,128)(2,1)} %get-tuple-element.35), calls=%async_computation.3 | async-start | bytes 3145728 | tf_op jit(solution)/shard_map/all_to_all | solution.py:178
  126.9 1.4 fusion
  128.4 3.3 %collective-permute-start.23 = (bf16[4,64,384]{2,1,0:T(8,128)(2,1)S(1)}, bf16[4,64,384]{2,1,0:T(8,128)(2,1)S(1)}, u32[]{:S(2)}, u32[]{:S(2)}) collective-permute-start(bf16[4,64,384]{2,1,0:T(8,128)(2,1)S(1)} %get-tuple-element.52), channel_id=1, source_target_pairs={{0,32},{1,33},{32,0},{33,1},{2,34},{3,35},{34,2},{35,3},{4,36},{5,... | collective-permute-start | bytes 589832 | tf_op jit(solution)/shard_map/ppermute | solution.py:185
  131.7 4.1 %collective-permute-done.22 = bf16[4,64,384]{2,1,0:T(8,128)(2,1)S(1)} collective-permute-done((bf16[4,64,384]{2,1,0:T(8,128)(2,1)S(1)}, bf16[4,64,384]{2,1,0:T(8,128)(2,1)S(1)}, u32[]{:S(2)}, u32[]{:S(2)}) %collective-permute-start.22) | collective-permute-done | bytes 196640 | tf_op jit(solution)/shard_map/ppermute | solution.py:185
  135.8 4.9 %collective-permute-done.23 = bf16[4,64,384]{2,1,0:T(8,128)(2,1)S(1)} collective-permute-done((bf16[4,64,384]{2,1,0:T(8,128)(2,1)S(1)}, bf16[4,64,384]{2,1,0:T(8,128)(2,1)S(1)}, u32[]{:S(2)}, u32[]{:S(2)}) %collective-permute-start.23) | collective-permute-done | bytes 196640 | tf_op jit(solution)/shard_map/ppermute | solution.py:185
  140.9 0.7 collective-permute-start.25
  141.6 2.7 %collective-permute-start.26 = (bf16[64,384]{1,0:T(8,128)(2,1)S(1)}, bf16[64,384]{1,0:T(8,128)(2,1)S(1)}, u32[]{:S(2)}, u32[]{:S(2)}) collective-permute-start(bf16[64,384]{1,0:T(8,128)(2,1)S(1)} %get-tuple-element.61), channel_id=1, source_target_pairs={{0,128},{64,192},{128,0},{192,64},{1,129},{65,193},{129,1},{193,65... | collective-permute-start | bytes 147464 | tf_op jit(solution)/shard_map/ppermute | solution.py:185
  145.4 1.2 collective-permute-done.26
  146.6 1.3 collective-permute-done.27
  148.2 0.6 fusion.20
  149.8 0.6 fusion.23
  150.4 16.9 %all-to-all-done.3.came_ref = bf16[8,256,384]{2,1,0:T(8,128)(2,1)S(1)} async-done(((bf16[8,256,384]{2,1,0:T(8,128)(2,1)}), bf16[8,256,384]{2,1,0:T(8,128)(2,1)S(1)}, u32[]{:S(2)}, u32[]{:S(2)}) %all-to-all-start.3) | async-done | bytes 1572896 | tf_op jit(solution)/shard_map/all_to_all | solution.py:178
  167.3 1.2 copy-done.8
  168.5 2.7 %shard_map.191 = (bf16[128,3072]{1,0:T(8,128)(2,1)}, bf16[128,3072]{1,0:T(8,128)(2,1)}) custom-call(bf16[8,256,384]{2,1,0:T(8,128)(2,1)} %copy-done.8), custom_call_target="tpu_custom_call" | custom-call | tf_op jit(solution)/shard_map/pallas_call | solution.py:320
  (104 shorter events, 6.3 us)
Async XLA Ops:
  4.0 9.2 %copy-start.9 = (bf16[128,3072]{1,0:T(8,128)(2,1)S(1)}, bf16[128,3072]{1,0:T(8,128)(2,1)}, u32[]{:S(2)}) copy-start(bf16[128,3072]{1,0:T(8,128)(2,1)} %param.13) | copy-start | bytes 2359300
  4.0 39.1 %all-to-all-start = ((bf16[8,176,384]{2,1,0:T(8,128)(2,1)}), bf16[8,176,384]{2,1,0:T(8,128)(2,1)S(1)}, u32[]{:S(2)}, u32[]{:S(2)}) async-start(bf16[8,176,384]{2,1,0:T(8,128)(2,1)} %bitcast.140), calls=%async_computation | async-start | bytes 2162688 | tf_op jit(solution)/shard_map/all_to_all | solution.py:178
  13.1 8.0 %copy-start.20 = (s32[4]{0:T(128)S(1)}, s32[4]{0:T(128)}, u32[]{:S(2)}) copy-start(s32[4]{0:T(128)} %param.23) | copy-start | bytes 52
  13.2 2.4 %collective-permute-start = (bf16[4,16,3072]{2,1,0:T(8,128)(2,1)S(1)}, bf16[4,16,3072]{2,1,0:T(8,128)(2,1)S(1)}, u32[]{:S(2)}, u32[]{:S(2)}) collective-permute-start(bf16[4,16,3072]{2,1,0:T(8,128)(2,1)S(1)} %bitcast.161), channel_id=1, source_target_pairs={{0,16},{16,0},{1,17},{17,1},{2,18},{18,2},{3,19},{19,3},{4,20},{20... | collective-permute-start | bytes 1179656 | tf_op jit(solution)/shard_map/ppermute | solution.py:185
  16.3 32.0 %slice-start = ((bf16[128,3072]{1,0:T(8,128)(2,1)}), bf16[80,3072]{1,0:T(8,128)(2,1)S(1)}, s32[]{:S(2)}) async-start(bf16[128,3072]{1,0:T(8,128)(2,1)} %param.15), calls=%async_computation.4 | async-start | bytes 983040 | tf_op jit(solution)/shard_map/slice | solution.py:342
  16.3 7.3 %collective-permute-start.1 = (bf16[2,16,3072]{2,1,0:T(8,128)(2,1)S(1)}, bf16[2,16,3072]{2,1,0:T(8,128)(2,1)S(1)}, u32[]{:S(2)}, u32[]{:S(2)}) collective-permute-start(bf16[2,16,3072]{2,1,0:T(8,128)(2,1)S(1)} %get-tuple-element.55), channel_id=1, source_target_pairs={{0,1},{1,32},{32,33},{33,0},{2,3},{3,34},{34,35},{35,2},{4,5},{5,3... | collective-permute-start | bytes 589832 | tf_op jit(solution)/shard_map/ppermute | solution.py:185
  17.6 11.3 %collective-permute-start.2 = (bf16[2,16,3072]{2,1,0:T(8,128)(2,1)S(1)}, bf16[2,16,3072]{2,1,0:T(8,128)(2,1)S(1)}, u32[]{:S(2)}, u32[]{:S(2)}) collective-permute-start(bf16[2,16,3072]{2,1,0:T(8,128)(2,1)S(1)} %get-tuple-element.56), channel_id=1, source_target_pairs={{0,32},{1,33},{32,0},{33,1},{2,34},{3,35},{34,2},{35,3},{4,36},{5,... | collective-permute-start | bytes 589832 | tf_op jit(solution)/shard_map/ppermute | solution.py:185
  20.0 8.9 %collective-permute-start.3 = (bf16[2,16,3072]{2,1,0:T(8,128)(2,1)S(1)}, bf16[2,16,3072]{2,1,0:T(8,128)(2,1)S(1)}, u32[]{:S(2)}, u32[]{:S(2)}) collective-permute-start(bf16[2,16,3072]{2,1,0:T(8,128)(2,1)S(1)} %get-tuple-element.53), channel_id=1, source_target_pairs={{0,33},{1,0},{32,1},{33,32},{2,35},{3,2},{34,3},{35,34},{4,37},{5,... | collective-permute-start | bytes 589832 | tf_op jit(solution)/shard_map/ppermute | solution.py:185
  23.7 5.2 %copy-start.10 = (bf16[2,16,3072]{2,1,0:T(8,128)(2,1)}, bf16[2,16,3072]{2,1,0:T(8,128)(2,1)S(1)}, u32[]{:S(2)}) copy-start(bf16[2,16,3072]{2,1,0:T(8,128)(2,1)S(1)} %collective-permute-done.1.refs_1_) | copy-start | bytes 589828
  28.9 0.7 copy-start.11
  28.9 0.7 copy-start.12
  31.8 24.3 %copy-start.13 = (bf16[16,384]{1,0:T(8,128)(2,1)S(1)}, bf16[16,384]{1,0:T(8,128)(2,1)}, u32[]{:S(2)}) copy-start(bf16[16,384]{1,0:T(8,128)(2,1)} %param.16) | copy-start | bytes 36868
  31.8 24.3 %copy-start.14 = (bf16[16,384]{1,0:T(8,128)(2,1)S(1)}, bf16[16,384]{1,0:T(8,128)(2,1)}, u32[]{:S(2)}) copy-start(bf16[16,384]{1,0:T(8,128)(2,1)} %param.25) | copy-start | bytes 36868
  31.8 24.3 %copy-start.15 = (bf16[16,384]{1,0:T(8,128)(2,1)S(1)}, bf16[16,384]{1,0:T(8,128)(2,1)}, u32[]{:S(2)}) copy-start(bf16[16,384]{1,0:T(8,128)(2,1)} %param.24) | copy-start | bytes 36868
  31.8 5.1 %collective-permute-start.4 = (bf16[16,3072]{1,0:T(8,128)(2,1)}, bf16[16,3072]{1,0:T(8,128)(2,1)S(1)}, u32[]{:S(2)}, u32[]{:S(2)}) collective-permute-start(bf16[16,3072]{1,0:T(8,128)(2,1)} %get-tuple-element.25), channel_id=1, source_target_pairs={{0,64},{64,128},{128,192},{192,0},{1,65},{65,129},{129,193},{193,1... | collective-permute-start | bytes 294920 | tf_op jit(solution)/shard_map/ppermute | solution.py:185
  33.2 6.6 %collective-permute-start.5 = (bf16[16,3072]{1,0:T(8,128)(2,1)}, bf16[16,3072]{1,0:T(8,128)(2,1)S(1)}, u32[]{:S(2)}, u32[]{:S(2)}) collective-permute-start(bf16[16,3072]{1,0:T(8,128)(2,1)} %get-tuple-element.26), channel_id=1, source_target_pairs={{0,128},{64,192},{128,0},{192,64},{1,129},{65,193},{129,1},{193,65... | collective-permute-start | bytes 294920 | tf_op jit(solution)/shard_map/ppermute | solution.py:185
  35.8 4.8 %collective-permute-start.6 = (bf16[16,3072]{1,0:T(8,128)(2,1)}, bf16[16,3072]{1,0:T(8,128)(2,1)S(1)}, u32[]{:S(2)}, u32[]{:S(2)}) collective-permute-start(bf16[16,3072]{1,0:T(8,128)(2,1)} %get-tuple-element.27), channel_id=1, source_target_pairs={{0,192},{64,0},{128,64},{192,128},{1,193},{65,1},{129,65},{193,129... | collective-permute-start | bytes 294920 | tf_op jit(solution)/shard_map/ppermute | solution.py:185
  43.7 12.3 %all-to-all-start.1 = ((bf16[8,16,384]{2,1,0:T(8,128)(2,1)}), bf16[8,16,384]{2,1,0:T(8,128)(2,1)S(1)}, u32[]{:S(2)}, u32[]{:S(2)}) async-start(bf16[8,16,384]{2,1,0:T(8,128)(2,1)} %copy.51), calls=%async_computation.1 | async-start | bytes 196608 | tf_op jit(solution)/shard_map/all_to_all | solution.py:178
  56.1 8.0 %collective-permute-start.7 = (bf16[4,16,384]{2,1,0:T(8,128)(2,1)S(1)}, bf16[4,16,384]{2,1,0:T(8,128)(2,1)S(1)}, u32[]{:S(2)}, u32[]{:S(2)}) collective-permute-start(bf16[4,16,384]{2,1,0:T(8,128)(2,1)S(1)} %pad_maximum_fusion.2), channel_id=1, source_target_pairs={{0,64},{64,128},{128,192},{192,0},{1,65},{65,129},{129,193},{193,1... | collective-permute-start | bytes 147464 | tf_op jit(solution)/shard_map/ppermute | solution.py:185
  56.2 7.9 %collective-permute-start.8 = (bf16[4,16,384]{2,1,0:T(8,128)(2,1)S(1)}, bf16[4,16,384]{2,1,0:T(8,128)(2,1)S(1)}, u32[]{:S(2)}, u32[]{:S(2)}) collective-permute-start(bf16[4,16,384]{2,1,0:T(8,128)(2,1)S(1)} %pad_maximum_fusion.2), channel_id=1, source_target_pairs={{0,128},{64,192},{128,0},{192,64},{1,129},{65,193},{129,1},{193,65... | collective-permute-start | bytes 147464 | tf_op jit(solution)/shard_map/ppermute | solution.py:185
  60.4 3.7 %collective-permute-start.9 = (bf16[4,16,384]{2,1,0:T(8,128)(2,1)S(1)}, bf16[4,16,384]{2,1,0:T(8,128)(2,1)S(1)}, u32[]{:S(2)}, u32[]{:S(2)}) collective-permute-start(bf16[4,16,384]{2,1,0:T(8,128)(2,1)S(1)} %pad_maximum_fusion.2), channel_id=1, source_target_pairs={{0,192},{64,0},{128,64},{192,128},{1,193},{65,1},{129,65},{193,129... | collective-permute-start | bytes 147464 | tf_op jit(solution)/shard_map/ppermute | solution.py:185
  60.5 16.0 %all-to-all-start.2 = ((bf16[8,80,384]{2,1,0:T(8,128)(2,1)}), bf16[8,80,384]{2,1,0:T(8,128)(2,1)S(1)}, u32[]{:S(2)}, u32[]{:S(2)}) async-start(bf16[8,80,384]{2,1,0:T(8,128)(2,1)} %bitcast.142), calls=%async_computation.2 | async-start | bytes 983040 | tf_op jit(solution)/shard_map/all_to_all | solution.py:178
  64.0 17.7 %copy-start.16 = (f32[128]{0:T(128)S(1)}, f32[128]{0:T(128)}, u32[]{:S(2)}) copy-start(f32[128]{0:T(128)} %param.21) | copy-start | bytes 1540
  64.0 17.7 %copy-start.17 = (f32[128]{0:T(128)S(1)}, f32[128]{0:T(128)}, u32[]{:S(2)}) copy-start(f32[128]{0:T(128)} %param.19) | copy-start | bytes 1540
  64.0 17.6 %copy-start.18 = (f32[128]{0:T(128)S(1)}, f32[128]{0:T(128)}, u32[]{:S(2)}) copy-start(f32[128]{0:T(128)} %param.22) | copy-start | bytes 1540
  64.0 17.6 %copy-start.19 = (f32[128]{0:T(128)S(1)}, f32[128]{0:T(128)}, u32[]{:S(2)}) copy-start(f32[128]{0:T(128)} %param.20) | copy-start | bytes 1540
  64.2 5.8 %collective-permute-start.10 = (bf16[4,4,16,384]{3,2,0,1:T(8,128)(2,1)S(1)}, bf16[4,4,16,384]{3,2,0,1:T(8,128)(2,1)S(1)}, u32[]{:S(2)}, u32[]{:S(2)}) collective-permute-start(bf16[4,4,16,384]{3,2,0,1:T(8,128)(2,1)S(1)} %bitcast_dynamic-update-slice_fusion.6), channel_id=1, source_target_pairs={{0,1},{1,32},{32,33},{33,0},{2,3},{3,34},{34,35},{35,2},{4,5},{5,3... | collective-permute-start | bytes 589832 | tf_op jit(solution)/shard_map/ppermute | solution.py:185
  65.2 7.7 %collective-permute-start.11 = (bf16[4,4,16,384]{3,2,0,1:T(8,128)(2,1)S(1)}, bf16[4,4,16,384]{3,2,0,1:T(8,128)(2,1)S(1)}, u32[]{:S(2)}, u32[]{:S(2)}) collective-permute-start(bf16[4,4,16,384]{3,2,0,1:T(8,128)(2,1)S(1)} %bitcast_dynamic-update-slice_fusion.6), channel_id=1, source_target_pairs={{0,32},{1,33},{32,0},{33,1},{2,34},{3,35},{34,2},{35,3},{4,36},{5,... | collective-permute-start | bytes 589832 | tf_op jit(solution)/shard_map/ppermute | solution.py:185
  67.7 5.2 %collective-permute-start.12 = (bf16[4,4,16,384]{3,2,0,1:T(8,128)(2,1)S(1)}, bf16[4,4,16,384]{3,2,0,1:T(8,128)(2,1)S(1)}, u32[]{:S(2)}, u32[]{:S(2)}) collective-permute-start(bf16[4,4,16,384]{3,2,0,1:T(8,128)(2,1)S(1)} %bitcast_dynamic-update-slice_fusion.6), channel_id=1, source_target_pairs={{0,33},{1,0},{32,1},{33,32},{2,35},{3,2},{34,3},{35,34},{4,37},{5,... | collective-permute-start | bytes 589832 | tf_op jit(solution)/shard_map/ppermute | solution.py:185
  76.5 7.6 %copy-start = (bf16[8,80,384]{2,1,0:T(8,128)(2,1)}, bf16[8,80,384]{2,1,0:T(8,128)(2,1)S(1)}, u32[]{:S(2)}) copy-start(bf16[8,80,384]{2,1,0:T(8,128)(2,1)S(1)} %all-to-all-done.2.v_ref) | copy-start | bytes 1474564
  76.5 7.1 %collective-permute-start.13 = (bf16[4,4,4,16,384]{4,3,2,1,0:T(8,128)(2,1)S(1)}, bf16[4,4,4,16,384]{4,3,2,1,0:T(8,128)(2,1)S(1)}, u32[]{:S(2)}, u32[]{:S(2)}) collective-permute-start(bf16[4,4,4,16,384]{4,3,2,1,0:T(8,128)(2,1)S(1)} %bitcast.152), channel_id=1, source_target_pairs={{0,16},{16,0},{1,17},{17,1},{2,18},{18,2},{3,19},{19,3},{4,20},{20... | collective-permute-start | bytes 2359304 | tf_op jit(solution)/shard_map/ppermute | solution.py:185
  83.9 6.2 %copy-start.2 = (bf16[2,1,4,4,16,384]{5,4,3,2,0,1:T(8,128)(2,1)}, bf16[2,1,4,4,16,384]{5,4,3,2,0,1:T(8,128)(2,1)S(1)}, u32[]{:S(2)}) copy-start(bf16[2,1,4,4,16,384]{5,4,3,2,0,1:T(8,128)(2,1)S(1)} %get-tuple-element.48) | copy-start | bytes 1179652
  83.9 6.2 %copy-start.4 = (bf16[2,1,4,4,16,384]{5,4,3,2,0,1:T(8,128)(2,1)}, bf16[2,1,4,4,16,384]{5,4,3,2,0,1:T(8,128)(2,1)S(1)}, u32[]{:S(2)}) copy-start(bf16[2,1,4,4,16,384]{5,4,3,2,0,1:T(8,128)(2,1)S(1)} %get-tuple-element.49) | copy-start | bytes 1179652
  83.9 0.8 copy-start.6
  83.9 0.8 copy-start.7
  90.1 1.3 collective-permute-start.14
  91.5 4.2 %collective-permute-start.15 = (f32[3,2,1024]{2,1,0:T(2,128)S(1)}, f32[3,2,1024]{2,1,0:T(2,128)S(1)}, u32[]{:S(2)}, u32[]{:S(2)}) collective-permute-start(f32[3,2,1024]{2,1,0:T(2,128)S(1)} %add.109), channel_id=1, source_target_pairs={{0,1},{1,32},{32,33},{33,0},{2,3},{3,34},{34,35},{35,2},{4,5},{5,3... | collective-permute-start | bytes 73736 | tf_op jit(solution)/shard_map/ppermute | solution.py:185
  92.5 4.2 %collective-permute-start.16 = (f32[3,2,1024]{2,1,0:T(2,128)S(1)}, f32[3,2,1024]{2,1,0:T(2,128)S(1)}, u32[]{:S(2)}, u32[]{:S(2)}) collective-permute-start(f32[3,2,1024]{2,1,0:T(2,128)S(1)} %add.109), channel_id=1, source_target_pairs={{0,32},{1,33},{32,0},{33,1},{2,34},{3,35},{34,2},{35,3},{4,36},{5,... | collective-permute-start | bytes 73736 | tf_op jit(solution)/shard_map/ppermute | solution.py:185
  95.0 3.0 %collective-permute-start.17 = (f32[3,2,1024]{2,1,0:T(2,128)S(1)}, f32[3,2,1024]{2,1,0:T(2,128)S(1)}, u32[]{:S(2)}, u32[]{:S(2)}) collective-permute-start(f32[3,2,1024]{2,1,0:T(2,128)S(1)} %add.109), channel_id=1, source_target_pairs={{0,33},{1,0},{32,1},{33,32},{2,35},{3,2},{34,3},{35,34},{4,37},{5,... | collective-permute-start | bytes 73736 | tf_op jit(solution)/shard_map/ppermute | solution.py:185
  98.0 4.0 %collective-permute-start.18 = (f32[3,2,1024]{2,1,0:T(2,128)S(1)}, f32[3,2,1024]{2,1,0:T(2,128)S(1)}, u32[]{:S(2)}, u32[]{:S(2)}) collective-permute-start(f32[3,2,1024]{2,1,0:T(2,128)S(1)} %add_add_fusion.1), channel_id=1, source_target_pairs={{0,64},{64,128},{128,192},{192,0},{1,65},{65,129},{129,193},{193,1... | collective-permute-start | bytes 73736 | tf_op jit(solution)/shard_map/ppermute | solution.py:185
  99.2 4.2 %collective-permute-start.19 = (f32[3,2,1024]{2,1,0:T(2,128)S(1)}, f32[3,2,1024]{2,1,0:T(2,128)S(1)}, u32[]{:S(2)}, u32[]{:S(2)}) collective-permute-start(f32[3,2,1024]{2,1,0:T(2,128)S(1)} %add_add_fusion.1), channel_id=1, source_target_pairs={{0,128},{64,192},{128,0},{192,64},{1,129},{65,193},{129,1},{193,65... | collective-permute-start | bytes 73736 | tf_op jit(solution)/shard_map/ppermute | solution.py:185
  99.3 4.1 %collective-permute-start.20 = (f32[3,2,1024]{2,1,0:T(2,128)S(1)}, f32[3,2,1024]{2,1,0:T(2,128)S(1)}, u32[]{:S(2)}, u32[]{:S(2)}) collective-permute-start(f32[3,2,1024]{2,1,0:T(2,128)S(1)} %add_add_fusion.1), channel_id=1, source_target_pairs={{0,192},{64,0},{128,64},{192,128},{1,193},{65,1},{129,65},{193,129... | collective-permute-start | bytes 73736 | tf_op jit(solution)/shard_map/ppermute | solution.py:185
  103.4 1.0 copy-start.1
  104.5 1.0 copy-start.3
  105.5 1.0 copy-start.5
  119.7 7.2 %collective-permute-start.21 = (bf16[4,4,64,384]{3,2,1,0:T(8,128)(2,1)}, bf16[4,4,64,384]{3,2,1,0:T(8,128)(2,1)}, u32[]{:S(2)}, u32[]{:S(2)}) collective-permute-start(bf16[4,4,64,384]{3,2,1,0:T(8,128)(2,1)} %dynamic-slice_bitcast_fusion), channel_id=1, source_target_pairs={{0,16},{16,0},{1,17},{17,1},{2,18},{18,2},{3,19},{19,3},{4,20},{20... | collective-permute-start | bytes 2359304 | tf_op jit(solution)/shard_map/ppermute | solution.py:185
  122.7 44.6 %all-to-all-start.3 = ((bf16[8,256,384]{2,1,0:T(8,128)(2,1)}), bf16[8,256,384]{2,1,0:T(8,128)(2,1)S(1)}, u32[]{:S(2)}, u32[]{:S(2)}) async-start(bf16[8,256,384]{2,1,0:T(8,128)(2,1)} %get-tuple-element.35), calls=%async_computation.3 | async-start | bytes 3145728 | tf_op jit(solution)/shard_map/all_to_all | solution.py:178
  128.3 7.5 %collective-permute-start.22 = (bf16[4,64,384]{2,1,0:T(8,128)(2,1)S(1)}, bf16[4,64,384]{2,1,0:T(8,128)(2,1)S(1)}, u32[]{:S(2)}, u32[]{:S(2)}) collective-permute-start(bf16[4,64,384]{2,1,0:T(8,128)(2,1)S(1)} %get-tuple-element.50), channel_id=1, source_target_pairs={{0,1},{1,32},{32,33},{33,0},{2,3},{3,34},{34,35},{35,2},{4,5},{5,3... | collective-permute-start | bytes 589832 | tf_op jit(solution)/shard_map/ppermute | solution.py:185
  128.4 12.3 %collective-permute-start.23 = (bf16[4,64,384]{2,1,0:T(8,128)(2,1)S(1)}, bf16[4,64,384]{2,1,0:T(8,128)(2,1)S(1)}, u32[]{:S(2)}, u32[]{:S(2)}) collective-permute-start(bf16[4,64,384]{2,1,0:T(8,128)(2,1)S(1)} %get-tuple-element.52), channel_id=1, source_target_pairs={{0,32},{1,33},{32,0},{33,1},{2,34},{3,35},{34,2},{35,3},{4,36},{5,... | collective-permute-start | bytes 589832 | tf_op jit(solution)/shard_map/ppermute | solution.py:185
  131.7 9.0 %collective-permute-start.24 = (bf16[4,64,384]{2,1,0:T(8,128)(2,1)S(1)}, bf16[4,64,384]{2,1,0:T(8,128)(2,1)S(1)}, u32[]{:S(2)}, u32[]{:S(2)}) collective-permute-start(bf16[4,64,384]{2,1,0:T(8,128)(2,1)S(1)} %get-tuple-element.51), channel_id=1, source_target_pairs={{0,33},{1,0},{32,1},{33,32},{2,35},{3,2},{34,3},{35,34},{4,37},{5,... | collective-permute-start | bytes 589832 | tf_op jit(solution)/shard_map/ppermute | solution.py:185
  140.9 4.5 %collective-permute-start.25 = (bf16[64,384]{1,0:T(8,128)(2,1)S(1)}, bf16[64,384]{1,0:T(8,128)(2,1)S(1)}, u32[]{:S(2)}, u32[]{:S(2)}) collective-permute-start(bf16[64,384]{1,0:T(8,128)(2,1)S(1)} %get-tuple-element.59), channel_id=1, source_target_pairs={{0,64},{64,128},{128,192},{192,0},{1,65},{65,129},{129,193},{193,1... | collective-permute-start | bytes 147464 | tf_op jit(solution)/shard_map/ppermute | solution.py:185
  141.6 5.0 %collective-permute-start.26 = (bf16[64,384]{1,0:T(8,128)(2,1)S(1)}, bf16[64,384]{1,0:T(8,128)(2,1)S(1)}, u32[]{:S(2)}, u32[]{:S(2)}) collective-permute-start(bf16[64,384]{1,0:T(8,128)(2,1)S(1)} %get-tuple-element.61), channel_id=1, source_target_pairs={{0,128},{64,192},{128,0},{192,64},{1,129},{65,193},{129,1},{193,65... | collective-permute-start | bytes 147464 | tf_op jit(solution)/shard_map/ppermute | solution.py:185
  144.3 3.6 %collective-permute-start.27 = (bf16[64,384]{1,0:T(8,128)(2,1)S(1)}, bf16[64,384]{1,0:T(8,128)(2,1)S(1)}, u32[]{:S(2)}, u32[]{:S(2)}) collective-permute-start(bf16[64,384]{1,0:T(8,128)(2,1)S(1)} %get-tuple-element.60), channel_id=1, source_target_pairs={{0,192},{64,0},{128,64},{192,128},{1,193},{65,1},{129,65},{193,129... | collective-permute-start | bytes 147464 | tf_op jit(solution)/shard_map/ppermute | solution.py:185
  167.3 1.2 copy-start.8

commit v7 on v6

--- a/solution.py
+++ b/solution.py
@@ -16,7 +16,7 @@
 ROW = ("xh", "xl")
 KEY_BLOCK = 1024
 EARLY = 48
-VMEM = 48 * 1024 * 1024
+VMEM = 52 * 1024 * 1024
 NT = (((1,), (1,)), ((), ()))
 NN = (((1,), (0,)), ((), ()))
 TN = (((0,), (0,)), ((), ()))

time: 171 us -> 171 us (level)
  waiting for transfers between devices: 64.6 us -> 62 us
  local copies, waits for them, and re-layouts: 12.5 us -> 9.98 us
  starting transfers between devices: 64.6 us -> 66.4 us
    unnamed x43 -> x35, local copies, waits for them, and re-layouts: 5.72 us -> 2.02 us
    ppermute x28, starting transfers between devices: 43.2 us -> 45.3 us  [push(): lax.ppermute(array, axes, [(i, (i + step) % size) for i in range(size)])]
    all_to_all x4, waiting for transfers between devices: 29.6 us -> 27.8 us  [swap(): return lax.all_to_all(array, axes, split_axis=0, concat_axis=0, tiled=True)]
where the time goes in v7:
time: 171 us; the launch traced here: 170 us
  starting transfers between devices  66.4 us (39%)
  waiting for transfers between devices  62 us (36%)
  Pallas kernels  23.4 us (14%)
  local copies, waits for them, and re-layouts  9.98 us (6%)
  other arithmetic  6.76 us (4%)
    ppermute x28, starting transfers between devices, push(): lax.ppermute(array, axes, [(i, (i + step) % size) for i in range(size)])  45.3 us
    ppermute x28, waiting for transfers between devices, push(): lax.ppermute(array, axes, [(i, (i + step) % size) for i in range(size)])  34.3 us
    all_to_all x4, waiting for transfers between devices, swap(): return lax.all_to_all(array, axes, split_axis=0, concat_axis=0, tiled=True)  27.8 us
    all_to_all x4, starting transfers between devices, swap(): return lax.all_to_all(array, axes, split_axis=0, concat_axis=0, tiled=True)  21.1 us
    pallas_call x1, Pallas kernels, attention_grads(): pl.pallas_call(grads_kernel, grid=(heads,), in_specs=operand_specs(operan...  12.6 us
    pallas_call x1, Pallas kernels, attention_stats(): pl.pallas_call(stats_kernel, grid=(heads,), in_specs=operand_specs(operan...  5.99 us
  transfers between devices with their start and end apart: 32, of which 22 were waited for; matrix products, arithmetic and copies ran while one was open for 4% of the time, Pallas kernels for 1%

profile of v7, /device:TPU:1, one launch (start us, length us, event | category | flops | bytes accessed | tf_op | source)
XLA Modules:
  0.0 169.9 jit_solution(15185210470236192687)
XLA Ops:
  0.6 1.0 slice.40
  1.6 1.2 pad_maximum_fusion
  2.8 1.1 copy.73
  4.0 9.1 %all-to-all-start = ((bf16[8,176,384]{2,1,0:T(8,128)(2,1)}), bf16[8,176,384]{2,1,0:T(8,128)(2,1)S(1)}, u32[]{:S(2)}, u32[]{:S(2)}) async-start(bf16[8,176,384]{2,1,0:T(8,128)(2,1)} %bitcast.140), calls=%async_computation | async-start | bytes 2162688 | tf_op jit(solution)/shard_map/all_to_all | solution.py:178
  13.2 1.0 collective-permute-start
  14.3 1.3 collective-permute-done
  15.6 0.7 fusion.5
  16.4 1.2 collective-permute-start.1
  17.6 2.5 %collective-permute-start.2 = (bf16[2,16,3072]{2,1,0:T(8,128)(2,1)S(1)}, bf16[2,16,3072]{2,1,0:T(8,128)(2,1)S(1)}, u32[]{:S(2)}, u32[]{:S(2)}) collective-permute-start(bf16[2,16,3072]{2,1,0:T(8,128)(2,1)S(1)} %get-tuple-element.56), channel_id=1, source_target_pairs={{0,32},{1,33},{32,0},{33,1},{2,34},{3,35},{34,2},{35,3},{4,36},{5,... | collective-permute-start | bytes 589832 | tf_op jit(solution)/shard_map/ppermute | solution.py:185
  20.0 1.2 collective-permute-start.3
  21.8 1.8 %collective-permute-done.1.refs_1_ = bf16[2,16,3072]{2,1,0:T(8,128)(2,1)S(1)} collective-permute-done((bf16[2,16,3072]{2,1,0:T(8,128)(2,1)S(1)}, bf16[2,16,3072]{2,1,0:T(8,128)(2,1)S(1)}, u32[]{:S(2)}, u32[]{:S(2)}) %collective-permute-start.1) | collective-permute-done | bytes 196640 | tf_op jit(solution)/shard_map/ppermute | solution.py:185
  23.7 5.2 %collective-permute-done.2.refs_2_ = bf16[2,16,3072]{2,1,0:T(8,128)(2,1)S(1)} collective-permute-done((bf16[2,16,3072]{2,1,0:T(8,128)(2,1)S(1)}, bf16[2,16,3072]{2,1,0:T(8,128)(2,1)S(1)}, u32[]{:S(2)}, u32[]{:S(2)}) %collective-permute-start.2) | collective-permute-done | bytes 196640 | tf_op jit(solution)/shard_map/ppermute | solution.py:185
  28.9 0.7 copy-done.7
  29.7 2.2 %shard_map.188 = (bf16[16,3072]{1,0:T(8,128)(2,1)}, bf16[16,3072]{1,0:T(8,128)(2,1)}, bf16[16,3072]{1,0:T(8,128)(2,1)}, bf16[16,3072]{1,0:T(8,128)(2,1)}) custom-call(s32[4]{0:T(128)} %get-tuple-element.71.source_ref, bf16[2,16,3072]{2,1,0:T(8,128)(2,1)} %get-tuple-element.54.refs_0_, bf16[2,16,3072]{2,1,0:T(8,128)(2,1)} %copy-done.6, ...), custom_call_target="tpu_custom_call" | custom-call | tf_op jit(solution)/shard_map/pallas_call | solution.py:251
  31.8 1.4 collective-permute-start.4
  33.2 2.6 %collective-permute-start.5 = (bf16[16,3072]{1,0:T(8,128)(2,1)}, bf16[16,3072]{1,0:T(8,128)(2,1)S(1)}, u32[]{:S(2)}, u32[]{:S(2)}) collective-permute-start(bf16[16,3072]{1,0:T(8,128)(2,1)} %get-tuple-element.26), channel_id=1, source_target_pairs={{0,128},{64,192},{128,0},{192,64},{1,129},{65,193},{129,1},{193,65... | collective-permute-start | bytes 294920 | tf_op jit(solution)/shard_map/ppermute | solution.py:185
  35.8 1.1 collective-permute-start.6
  36.9 2.8 %collective-permute-done.5 = bf16[16,3072]{1,0:T(8,128)(2,1)S(1)} collective-permute-done((bf16[16,3072]{1,0:T(8,128)(2,1)}, bf16[16,3072]{1,0:T(8,128)(2,1)S(1)}, u32[]{:S(2)}, u32[]{:S(2)}) %collective-permute-start.5) | collective-permute-done | bytes 98336 | tf_op jit(solution)/shard_map/ppermute | solution.py:185
  39.8 0.9 collective-permute-done.6
  40.7 2.3 %all-to-all-done.k_ref = bf16[8,176,384]{2,1,0:T(8,128)(2,1)S(1)} async-done(((bf16[8,176,384]{2,1,0:T(8,128)(2,1)}), bf16[8,176,384]{2,1,0:T(8,128)(2,1)S(1)}, u32[]{:S(2)}, u32[]{:S(2)}) %all-to-all-start) | async-done | bytes 1081376 | tf_op jit(solution)/shard_map/all_to_all | solution.py:178
  43.1 0.7 copy.51
  43.8 4.7 %all-to-all-start.1 = ((bf16[8,16,384]{2,1,0:T(8,128)(2,1)}), bf16[8,16,384]{2,1,0:T(8,128)(2,1)S(1)}, u32[]{:S(2)}, u32[]{:S(2)}) async-start(bf16[8,16,384]{2,1,0:T(8,128)(2,1)} %copy.51), calls=%async_computation.1 | async-start | bytes 196608 | tf_op jit(solution)/shard_map/all_to_all | solution.py:178
  48.4 0.8 copy.74
  49.3 6.9 %all-to-all-done.1 = bf16[8,16,384]{2,1,0:T(8,128)(2,1)S(1)} async-done(((bf16[8,16,384]{2,1,0:T(8,128)(2,1)}), bf16[8,16,384]{2,1,0:T(8,128)(2,1)S(1)}, u32[]{:S(2)}, u32[]{:S(2)}) %all-to-all-start.1) | async-done | bytes 98336 | tf_op jit(solution)/shard_map/all_to_all | solution.py:178
  56.3 3.4 %collective-permute-start.8 = (bf16[4,16,384]{2,1,0:T(8,128)(2,1)S(1)}, bf16[4,16,384]{2,1,0:T(8,128)(2,1)S(1)}, u32[]{:S(2)}, u32[]{:S(2)}) collective-permute-start(bf16[4,16,384]{2,1,0:T(8,128)(2,1)S(1)} %pad_maximum_fusion.2), channel_id=1, source_target_pairs={{0,128},{64,192},{128,0},{192,64},{1,129},{65,193},{129,1},{193,65... | collective-permute-start | bytes 147464 | tf_op jit(solution)/shard_map/ppermute | solution.py:185
  59.9 3.5 %all-to-all-start.2 = ((bf16[8,80,384]{2,1,0:T(8,128)(2,1)}), bf16[8,80,384]{2,1,0:T(8,128)(2,1)S(1)}, u32[]{:S(2)}, u32[]{:S(2)}) async-start(bf16[8,80,384]{2,1,0:T(8,128)(2,1)} %bitcast.142), calls=%async_computation.2 | async-start | bytes 983040 | tf_op jit(solution)/shard_map/all_to_all | solution.py:178
  63.6 1.3 collective-permute-start.10
  64.9 2.9 %collective-permute-start.11 = (bf16[4,4,16,384]{3,2,0,1:T(8,128)(2,1)S(1)}, bf16[4,4,16,384]{3,2,0,1:T(8,128)(2,1)S(1)}, u32[]{:S(2)}, u32[]{:S(2)}) collective-permute-start(bf16[4,4,16,384]{3,2,0,1:T(8,128)(2,1)S(1)} %bitcast_dynamic-update-slice_fusion.6), channel_id=1, source_target_pairs={{0,32},{1,33},{32,0},{33,1},{2,34},{3,35},{34,2},{35,3},{4,36},{5,... | collective-permute-start | bytes 589832 | tf_op jit(solution)/shard_map/ppermute | solution.py:185
  67.8 0.6 collective-permute-start.12
  68.5 1.1 collective-permute-done.10
  69.7 3.4 %collective-permute-done.11 = bf16[4,4,16,384]{3,2,0,1:T(8,128)(2,1)S(1)} collective-permute-done((bf16[4,4,16,384]{3,2,0,1:T(8,128)(2,1)S(1)}, bf16[4,4,16,384]{3,2,0,1:T(8,128)(2,1)S(1)}, u32[]{:S(2)}, u32[]{:S(2)}) %collective-permute-start.11) | collective-permute-done | bytes 196640 | tf_op jit(solution)/shard_map/ppermute | solution.py:185
  73.1 1.6 all-to-all-done.2.v_ref
  74.8 6.4 %collective-permute-start.13 = (bf16[4,4,4,16,384]{4,3,2,1,0:T(8,128)(2,1)S(1)}, bf16[4,4,4,16,384]{4,3,2,1,0:T(8,128)(2,1)S(1)}, u32[]{:S(2)}, u32[]{:S(2)}) collective-permute-start(bf16[4,4,4,16,384]{4,3,2,1,0:T(8,128)(2,1)S(1)} %bitcast.150), channel_id=1, source_target_pairs={{0,16},{16,0},{1,17},{17,1},{2,18},{18,2},{3,19},{19,3},{4,20},{20... | collective-permute-start | bytes 2359304 | tf_op jit(solution)/shard_map/ppermute | solution.py:185
  81.5 1.5 collective-permute-done.13
  83.4 1.0 pad_maximum_fusion.1.cot_ref
  84.3 6.0 %shard_map.189 = f32[3,2,1024]{2,1,0:T(2,128)S(1)} custom-call(bf16[512,384]{1,0:T(8,128)(2,1)S(1)} %bitcast.147, bf16[512,384]{1,0:T(8,128)(2,1)S(1)} %bitcast.145, bf16[1024,384]{1,0:T(8,128)(2,1)} %pad_maximum_fusion.1.cot_ref, bf16[8,176,384]{2,1,0:T(8,128)(2,1)} %copy-done.4, bf16[8,80,384]{2,1,0:T(8,128)(2,1)S(1)} %all-to-all-done.2.v_ref, ...), custom_call_target="tpu_custom_call" | custom-call | flops 1610612736 | bytes 6000000 | tf_op jit(solution)/shard_map/pallas_call | solution.py:142
  90.8 0.8 collective-permute-done.14
  91.7 1.3 collective-permute-start.15
  93.0 2.9 %collective-permute-start.16 = (f32[3,2,1024]{2,1,0:T(2,128)S(1)}, f32[3,2,1024]{2,1,0:T(2,128)S(1)}, u32[]{:S(2)}, u32[]{:S(2)}) collective-permute-start(f32[3,2,1024]{2,1,0:T(2,128)S(1)} %add.109), channel_id=1, source_target_pairs={{0,32},{1,33},{32,0},{33,1},{2,34},{3,35},{34,2},{35,3},{4,36},{5,... | collective-permute-start | bytes 73736 | tf_op jit(solution)/shard_map/ppermute | solution.py:185
  95.8 0.6 collective-permute-start.17
  96.5 0.9 collective-permute-done.16
  97.3 1.2 collective-permute-done.17
  98.6 0.7 collective-permute-start.18
  99.2 0.7 collective-permute-start.19
  99.9 2.0 %collective-permute-start.20 = (f32[3,2,1024]{2,1,0:T(2,128)S(1)}, f32[3,2,1024]{2,1,0:T(2,128)S(1)}, u32[]{:S(2)}, u32[]{:S(2)}) collective-permute-start(f32[3,2,1024]{2,1,0:T(2,128)S(1)} %add_add_fusion.1), channel_id=1, source_target_pairs={{0,192},{64,0},{128,64},{192,128},{1,193},{65,1},{129,65},{193,129... | collective-permute-start | bytes 73736 | tf_op jit(solution)/shard_map/ppermute | solution.py:185
  101.9 0.7 collective-permute-done.18
  102.5 1.0 collective-permute-done.19
  103.5 12.6 %shard_map.190 = (bf16[32,64,384]{2,1,0:T(8,128)(2,1)}, bf16[8,256,384]{2,1,0:T(8,128)(2,1)}, bf16[16,384]{1,0:T(8,128)(2,1)}, bf16[16,384]{1,0:T(8,128)(2,1)}) custom-call(bf16[512,384]{1,0:T(8,128)(2,1)S(1)} %bitcast.148, bf16[512,384]{1,0:T(8,128)(2,1)S(1)} %bitcast.146, bf16[1024,384]{1,0:T(8,128)(2,1)} %pad_maximum_fusion.1.cot_ref, ...), custom_call_target="tpu_custom_call" | custom-call | flops 4831838208 | bytes 6000000 | tf_op jit(solution)/shard_map/pallas_call | solution.py:165
  116.2 2.1 %dynamic-slice_bitcast_fusion = bf16[4,4,64,384]{3,2,1,0:T(8,128)(2,1)} fusion(bf16[2,4,4,64,384]{4,3,2,1,0:T(8,128)(2,1)} %bitcast.152, s32[]{:T(128)S(6)} %and.87), kind=kLoop, calls=%fused_computation.15 | loop fusion | bytes 1572868 | tf_op jit(solution)/shard_map/jit(dynamic_index_in_dim)/squeeze | solution.py:189
  118.3 3.3 %collective-permute-start.21 = (bf16[4,4,64,384]{3,2,1,0:T(8,128)(2,1)}, bf16[4,4,64,384]{3,2,1,0:T(8,128)(2,1)}, u32[]{:S(2)}, u32[]{:S(2)}) collective-permute-start(bf16[4,4,64,384]{3,2,1,0:T(8,128)(2,1)} %dynamic-slice_bitcast_fusion), channel_id=1, source_target_pairs={{0,16},{16,0},{1,17},{17,1},{2,18},{18,2},{3,19},{19,3},{4,20},{20... | collective-permute-start | bytes 2359304 | tf_op jit(solution)/shard_map/ppermute | solution.py:185
  121.6 3.8 %all-to-all-start.3 = ((bf16[8,256,384]{2,1,0:T(8,128)(2,1)}), bf16[8,256,384]{2,1,0:T(8,128)(2,1)S(1)}, u32[]{:S(2)}, u32[]{:S(2)}) async-start(bf16[8,256,384]{2,1,0:T(8,128)(2,1)} %get-tuple-element.35), calls=%async_computation.3 | async-start | bytes 3145728 | tf_op jit(solution)/shard_map/all_to_all | solution.py:178
  125.5 1.4 fusion
  127.2 3.2 %collective-permute-start.23 = (bf16[4,64,384]{2,1,0:T(8,128)(2,1)S(1)}, bf16[4,64,384]{2,1,0:T(8,128)(2,1)S(1)}, u32[]{:S(2)}, u32[]{:S(2)}) collective-permute-start(bf16[4,64,384]{2,1,0:T(8,128)(2,1)S(1)} %get-tuple-element.52), channel_id=1, source_target_pairs={{0,32},{1,33},{32,0},{33,1},{2,34},{3,35},{34,2},{35,3},{4,36},{5,... | collective-permute-start | bytes 589832 | tf_op jit(solution)/shard_map/ppermute | solution.py:185
  130.5 4.1 %collective-permute-done.22 = bf16[4,64,384]{2,1,0:T(8,128)(2,1)S(1)} collective-permute-done((bf16[4,64,384]{2,1,0:T(8,128)(2,1)S(1)}, bf16[4,64,384]{2,1,0:T(8,128)(2,1)S(1)}, u32[]{:S(2)}, u32[]{:S(2)}) %collective-permute-start.22) | collective-permute-done | bytes 196640 | tf_op jit(solution)/shard_map/ppermute | solution.py:185
  134.6 4.7 %collective-permute-done.23 = bf16[4,64,384]{2,1,0:T(8,128)(2,1)S(1)} collective-permute-done((bf16[4,64,384]{2,1,0:T(8,128)(2,1)S(1)}, bf16[4,64,384]{2,1,0:T(8,128)(2,1)S(1)}, u32[]{:S(2)}, u32[]{:S(2)}) %collective-permute-start.23) | collective-permute-done | bytes 196640 | tf_op jit(solution)/shard_map/ppermute | solution.py:185
  139.5 1.6 collective-permute-start.25
  141.1 1.9 %collective-permute-start.26 = (bf16[64,384]{1,0:T(8,128)(2,1)S(1)}, bf16[64,384]{1,0:T(8,128)(2,1)S(1)}, u32[]{:S(2)}, u32[]{:S(2)}) collective-permute-start(bf16[64,384]{1,0:T(8,128)(2,1)S(1)} %get-tuple-element.61), channel_id=1, source_target_pairs={{0,128},{64,192},{128,0},{192,64},{1,129},{65,193},{129,1},{193,65... | collective-permute-start | bytes 147464 | tf_op jit(solution)/shard_map/ppermute | solution.py:185
  144.1 1.8 %collective-permute-done.26 = bf16[64,384]{1,0:T(8,128)(2,1)S(1)} collective-permute-done((bf16[64,384]{1,0:T(8,128)(2,1)S(1)}, bf16[64,384]{1,0:T(8,128)(2,1)S(1)}, u32[]{:S(2)}, u32[]{:S(2)}) %collective-permute-start.26) | collective-permute-done | bytes 49184 | tf_op jit(solution)/shard_map/ppermute | solution.py:185
  146.8 0.6 fusion.20
  147.5 0.6 fusion.27
  148.3 0.6 fusion.23
  148.9 17.0 %all-to-all-done.3.came_ref = bf16[8,256,384]{2,1,0:T(8,128)(2,1)S(1)} async-done(((bf16[8,256,384]{2,1,0:T(8,128)(2,1)}), bf16[8,256,384]{2,1,0:T(8,128)(2,1)S(1)}, u32[]{:S(2)}, u32[]{:S(2)}) %all-to-all-start.3) | async-done | bytes 1572896 | tf_op jit(solution)/shard_map/all_to_all | solution.py:178
  165.9 1.2 copy-done.2
  167.1 2.7 %shard_map.191 = (bf16[128,3072]{1,0:T(8,128)(2,1)}, bf16[128,3072]{1,0:T(8,128)(2,1)}) custom-call(bf16[8,256,384]{2,1,0:T(8,128)(2,1)} %copy-done.2), custom_call_target="tpu_custom_call" | custom-call | tf_op jit(solution)/shard_map/pallas_call | solution.py:320
  (96 shorter events, 5.8 us)
Async XLA Ops:
  4.0 9.2 %copy-start.5 = (bf16[128,3072]{1,0:T(8,128)(2,1)S(1)}, bf16[128,3072]{1,0:T(8,128)(2,1)}, u32[]{:S(2)}) copy-start(bf16[128,3072]{1,0:T(8,128)(2,1)} %param.13) | copy-start | bytes 2359300
  4.0 39.1 %all-to-all-start = ((bf16[8,176,384]{2,1,0:T(8,128)(2,1)}), bf16[8,176,384]{2,1,0:T(8,128)(2,1)S(1)}, u32[]{:S(2)}, u32[]{:S(2)}) async-start(bf16[8,176,384]{2,1,0:T(8,128)(2,1)} %bitcast.140), calls=%async_computation | async-start | bytes 2162688 | tf_op jit(solution)/shard_map/all_to_all | solution.py:178
  13.1 8.0 %copy-start.16 = (s32[4]{0:T(128)S(1)}, s32[4]{0:T(128)}, u32[]{:S(2)}) copy-start(s32[4]{0:T(128)} %param.23) | copy-start | bytes 52
  13.2 2.4 %collective-permute-start = (bf16[4,16,3072]{2,1,0:T(8,128)(2,1)S(1)}, bf16[4,16,3072]{2,1,0:T(8,128)(2,1)S(1)}, u32[]{:S(2)}, u32[]{:S(2)}) collective-permute-start(bf16[4,16,3072]{2,1,0:T(8,128)(2,1)S(1)} %bitcast.161), channel_id=1, source_target_pairs={{0,16},{16,0},{1,17},{17,1},{2,18},{18,2},{3,19},{19,3},{4,20},{20... | collective-permute-start | bytes 1179656 | tf_op jit(solution)/shard_map/ppermute | solution.py:185
  16.3 32.1 %slice-start = ((bf16[128,3072]{1,0:T(8,128)(2,1)}), bf16[80,3072]{1,0:T(8,128)(2,1)S(1)}, s32[]{:S(2)}) async-start(bf16[128,3072]{1,0:T(8,128)(2,1)} %param.15), calls=%async_computation.4 | async-start | bytes 983040 | tf_op jit(solution)/shard_map/slice | solution.py:342
  16.4 7.3 %collective-permute-start.1 = (bf16[2,16,3072]{2,1,0:T(8,128)(2,1)S(1)}, bf16[2,16,3072]{2,1,0:T(8,128)(2,1)S(1)}, u32[]{:S(2)}, u32[]{:S(2)}) collective-permute-start(bf16[2,16,3072]{2,1,0:T(8,128)(2,1)S(1)} %get-tuple-element.55), channel_id=1, source_target_pairs={{0,1},{1,32},{32,33},{33,0},{2,3},{3,34},{34,35},{35,2},{4,5},{5,3... | collective-permute-start | bytes 589832 | tf_op jit(solution)/shard_map/ppermute | solution.py:185
  17.6 11.3 %collective-permute-start.2 = (bf16[2,16,3072]{2,1,0:T(8,128)(2,1)S(1)}, bf16[2,16,3072]{2,1,0:T(8,128)(2,1)S(1)}, u32[]{:S(2)}, u32[]{:S(2)}) collective-permute-start(bf16[2,16,3072]{2,1,0:T(8,128)(2,1)S(1)} %get-tuple-element.56), channel_id=1, source_target_pairs={{0,32},{1,33},{32,0},{33,1},{2,34},{3,35},{34,2},{35,3},{4,36},{5,... | collective-permute-start | bytes 589832 | tf_op jit(solution)/shard_map/ppermute | solution.py:185
  20.0 8.9 %collective-permute-start.3 = (bf16[2,16,3072]{2,1,0:T(8,128)(2,1)S(1)}, bf16[2,16,3072]{2,1,0:T(8,128)(2,1)S(1)}, u32[]{:S(2)}, u32[]{:S(2)}) collective-permute-start(bf16[2,16,3072]{2,1,0:T(8,128)(2,1)S(1)} %get-tuple-element.53), channel_id=1, source_target_pairs={{0,33},{1,0},{32,1},{33,32},{2,35},{3,2},{34,3},{35,34},{4,37},{5,... | collective-permute-start | bytes 589832 | tf_op jit(solution)/shard_map/ppermute | solution.py:185
  23.7 5.2 %copy-start.6 = (bf16[2,16,3072]{2,1,0:T(8,128)(2,1)}, bf16[2,16,3072]{2,1,0:T(8,128)(2,1)S(1)}, u32[]{:S(2)}) copy-start(bf16[2,16,3072]{2,1,0:T(8,128)(2,1)S(1)} %collective-permute-done.1.refs_1_) | copy-start | bytes 589828
  28.9 0.7 copy-start.7
  28.9 0.8 copy-start.8
  31.8 24.3 %copy-start.9 = (bf16[16,384]{1,0:T(8,128)(2,1)S(1)}, bf16[16,384]{1,0:T(8,128)(2,1)}, u32[]{:S(2)}) copy-start(bf16[16,384]{1,0:T(8,128)(2,1)} %param.16) | copy-start | bytes 36868
  31.8 24.3 %copy-start.10 = (bf16[16,384]{1,0:T(8,128)(2,1)S(1)}, bf16[16,384]{1,0:T(8,128)(2,1)}, u32[]{:S(2)}) copy-start(bf16[16,384]{1,0:T(8,128)(2,1)} %param.25) | copy-start | bytes 36868
  31.8 24.4 %copy-start.11 = (bf16[16,384]{1,0:T(8,128)(2,1)S(1)}, bf16[16,384]{1,0:T(8,128)(2,1)}, u32[]{:S(2)}) copy-start(bf16[16,384]{1,0:T(8,128)(2,1)} %param.24) | copy-start | bytes 36868
  31.8 5.1 %collective-permute-start.4 = (bf16[16,3072]{1,0:T(8,128)(2,1)}, bf16[16,3072]{1,0:T(8,128)(2,1)S(1)}, u32[]{:S(2)}, u32[]{:S(2)}) collective-permute-start(bf16[16,3072]{1,0:T(8,128)(2,1)} %get-tuple-element.25), channel_id=1, source_target_pairs={{0,64},{64,128},{128,192},{192,0},{1,65},{65,129},{129,193},{193,1... | collective-permute-start | bytes 294920 | tf_op jit(solution)/shard_map/ppermute | solution.py:185
  33.2 6.6 %collective-permute-start.5 = (bf16[16,3072]{1,0:T(8,128)(2,1)}, bf16[16,3072]{1,0:T(8,128)(2,1)S(1)}, u32[]{:S(2)}, u32[]{:S(2)}) collective-permute-start(bf16[16,3072]{1,0:T(8,128)(2,1)} %get-tuple-element.26), channel_id=1, source_target_pairs={{0,128},{64,192},{128,0},{192,64},{1,129},{65,193},{129,1},{193,65... | collective-permute-start | bytes 294920 | tf_op jit(solution)/shard_map/ppermute | solution.py:185
  35.8 4.8 %collective-permute-start.6 = (bf16[16,3072]{1,0:T(8,128)(2,1)}, bf16[16,3072]{1,0:T(8,128)(2,1)S(1)}, u32[]{:S(2)}, u32[]{:S(2)}) collective-permute-start(bf16[16,3072]{1,0:T(8,128)(2,1)} %get-tuple-element.27), channel_id=1, source_target_pairs={{0,192},{64,0},{128,64},{192,128},{1,193},{65,1},{129,65},{193,129... | collective-permute-start | bytes 294920 | tf_op jit(solution)/shard_map/ppermute | solution.py:185
  43.0 16.9 %copy-start.4 = (bf16[8,176,384]{2,1,0:T(8,128)(2,1)}, bf16[8,176,384]{2,1,0:T(8,128)(2,1)S(1)}, u32[]{:S(2)}) copy-start(bf16[8,176,384]{2,1,0:T(8,128)(2,1)S(1)} %all-to-all-done.k_ref) | copy-start | bytes 3244036
  43.8 12.3 %all-to-all-start.1 = ((bf16[8,16,384]{2,1,0:T(8,128)(2,1)}), bf16[8,16,384]{2,1,0:T(8,128)(2,1)S(1)}, u32[]{:S(2)}, u32[]{:S(2)}) async-start(bf16[8,16,384]{2,1,0:T(8,128)(2,1)} %copy.51), calls=%async_computation.1 | async-start | bytes 196608 | tf_op jit(solution)/shard_map/all_to_all | solution.py:178
  56.2 7.3 %collective-permute-start.7 = (bf16[4,16,384]{2,1,0:T(8,128)(2,1)S(1)}, bf16[4,16,384]{2,1,0:T(8,128)(2,1)S(1)}, u32[]{:S(2)}, u32[]{:S(2)}) collective-permute-start(bf16[4,16,384]{2,1,0:T(8,128)(2,1)S(1)} %pad_maximum_fusion.2), channel_id=1, source_target_pairs={{0,64},{64,128},{128,192},{192,0},{1,65},{65,129},{129,193},{193,1... | collective-permute-start | bytes 147464 | tf_op jit(solution)/shard_map/ppermute | solution.py:185
  56.3 7.2 %collective-permute-start.8 = (bf16[4,16,384]{2,1,0:T(8,128)(2,1)S(1)}, bf16[4,16,384]{2,1,0:T(8,128)(2,1)S(1)}, u32[]{:S(2)}, u32[]{:S(2)}) collective-permute-start(bf16[4,16,384]{2,1,0:T(8,128)(2,1)S(1)} %pad_maximum_fusion.2), channel_id=1, source_target_pairs={{0,128},{64,192},{128,0},{192,64},{1,129},{65,193},{129,1},{193,65... | collective-permute-start | bytes 147464 | tf_op jit(solution)/shard_map/ppermute | solution.py:185
  59.7 3.9 %collective-permute-start.9 = (bf16[4,16,384]{2,1,0:T(8,128)(2,1)S(1)}, bf16[4,16,384]{2,1,0:T(8,128)(2,1)S(1)}, u32[]{:S(2)}, u32[]{:S(2)}) collective-permute-start(bf16[4,16,384]{2,1,0:T(8,128)(2,1)S(1)} %pad_maximum_fusion.2), channel_id=1, source_target_pairs={{0,192},{64,0},{128,64},{192,128},{1,193},{65,1},{129,65},{193,129... | collective-permute-start | bytes 147464 | tf_op jit(solution)/shard_map/ppermute | solution.py:185
  59.9 14.8 %all-to-all-start.2 = ((bf16[8,80,384]{2,1,0:T(8,128)(2,1)}), bf16[8,80,384]{2,1,0:T(8,128)(2,1)S(1)}, u32[]{:S(2)}, u32[]{:S(2)}) async-start(bf16[8,80,384]{2,1,0:T(8,128)(2,1)} %bitcast.142), calls=%async_computation.2 | async-start | bytes 983040 | tf_op jit(solution)/shard_map/all_to_all | solution.py:178
  63.4 17.7 %copy-start.12 = (f32[128]{0:T(128)S(1)}, f32[128]{0:T(128)}, u32[]{:S(2)}) copy-start(f32[128]{0:T(128)} %param.21) | copy-start | bytes 1540
  63.5 17.7 %copy-start.13 = (f32[128]{0:T(128)S(1)}, f32[128]{0:T(128)}, u32[]{:S(2)}) copy-start(f32[128]{0:T(128)} %param.19) | copy-start | bytes 1540
  63.5 17.6 %copy-start.14 = (f32[128]{0:T(128)S(1)}, f32[128]{0:T(128)}, u32[]{:S(2)}) copy-start(f32[128]{0:T(128)} %param.22) | copy-start | bytes 1540
  63.5 17.6 %copy-start.15 = (f32[128]{0:T(128)S(1)}, f32[128]{0:T(128)}, u32[]{:S(2)}) copy-start(f32[128]{0:T(128)} %param.20) | copy-start | bytes 1540
  63.6 6.1 %collective-permute-start.10 = (bf16[4,4,16,384]{3,2,0,1:T(8,128)(2,1)S(1)}, bf16[4,4,16,384]{3,2,0,1:T(8,128)(2,1)S(1)}, u32[]{:S(2)}, u32[]{:S(2)}) collective-permute-start(bf16[4,4,16,384]{3,2,0,1:T(8,128)(2,1)S(1)} %bitcast_dynamic-update-slice_fusion.6), channel_id=1, source_target_pairs={{0,1},{1,32},{32,33},{33,0},{2,3},{3,34},{34,35},{35,2},{4,5},{5,3... | collective-permute-start | bytes 589832 | tf_op jit(solution)/shard_map/ppermute | solution.py:185
  64.9 8.2 %collective-permute-start.11 = (bf16[4,4,16,384]{3,2,0,1:T(8,128)(2,1)S(1)}, bf16[4,4,16,384]{3,2,0,1:T(8,128)(2,1)S(1)}, u32[]{:S(2)}, u32[]{:S(2)}) collective-permute-start(bf16[4,4,16,384]{3,2,0,1:T(8,128)(2,1)S(1)} %bitcast_dynamic-update-slice_fusion.6), channel_id=1, source_target_pairs={{0,32},{1,33},{32,0},{33,1},{2,34},{3,35},{34,2},{35,3},{4,36},{5,... | collective-permute-start | bytes 589832 | tf_op jit(solution)/shard_map/ppermute | solution.py:185
  67.8 5.3 %collective-permute-start.12 = (bf16[4,4,16,384]{3,2,0,1:T(8,128)(2,1)S(1)}, bf16[4,4,16,384]{3,2,0,1:T(8,128)(2,1)S(1)}, u32[]{:S(2)}, u32[]{:S(2)}) collective-permute-start(bf16[4,4,16,384]{3,2,0,1:T(8,128)(2,1)S(1)} %bitcast_dynamic-update-slice_fusion.6), channel_id=1, source_target_pairs={{0,33},{1,0},{32,1},{33,32},{2,35},{3,2},{34,3},{35,34},{4,37},{5,... | collective-permute-start | bytes 589832 | tf_op jit(solution)/shard_map/ppermute | solution.py:185
  74.8 8.3 %collective-permute-start.13 = (bf16[4,4,4,16,384]{4,3,2,1,0:T(8,128)(2,1)S(1)}, bf16[4,4,4,16,384]{4,3,2,1,0:T(8,128)(2,1)S(1)}, u32[]{:S(2)}, u32[]{:S(2)}) collective-permute-start(bf16[4,4,4,16,384]{4,3,2,1,0:T(8,128)(2,1)S(1)} %bitcast.150), channel_id=1, source_target_pairs={{0,16},{16,0},{1,17},{17,1},{2,18},{18,2},{3,19},{19,3},{4,20},{20... | collective-permute-start | bytes 2359304 | tf_op jit(solution)/shard_map/ppermute | solution.py:185
  83.4 1.0 copy-start
  83.4 1.0 copy-start.1
  90.3 1.3 collective-permute-start.14
  91.7 4.8 %collective-permute-start.15 = (f32[3,2,1024]{2,1,0:T(2,128)S(1)}, f32[3,2,1024]{2,1,0:T(2,128)S(1)}, u32[]{:S(2)}, u32[]{:S(2)}) collective-permute-start(f32[3,2,1024]{2,1,0:T(2,128)S(1)} %add.109), channel_id=1, source_target_pairs={{0,1},{1,32},{32,33},{33,0},{2,3},{3,34},{34,35},{35,2},{4,5},{5,3... | collective-permute-start | bytes 73736 | tf_op jit(solution)/shard_map/ppermute | solution.py:185
  93.0 4.4 %collective-permute-start.16 = (f32[3,2,1024]{2,1,0:T(2,128)S(1)}, f32[3,2,1024]{2,1,0:T(2,128)S(1)}, u32[]{:S(2)}, u32[]{:S(2)}) collective-permute-start(f32[3,2,1024]{2,1,0:T(2,128)S(1)} %add.109), channel_id=1, source_target_pairs={{0,32},{1,33},{32,0},{33,1},{2,34},{3,35},{34,2},{35,3},{4,36},{5,... | collective-permute-start | bytes 73736 | tf_op jit(solution)/shard_map/ppermute | solution.py:185
  95.8 2.7 %collective-permute-start.17 = (f32[3,2,1024]{2,1,0:T(2,128)S(1)}, f32[3,2,1024]{2,1,0:T(2,128)S(1)}, u32[]{:S(2)}, u32[]{:S(2)}) collective-permute-start(f32[3,2,1024]{2,1,0:T(2,128)S(1)} %add.109), channel_id=1, source_target_pairs={{0,33},{1,0},{32,1},{33,32},{2,35},{3,2},{34,3},{35,34},{4,37},{5,... | collective-permute-start | bytes 73736 | tf_op jit(solution)/shard_map/ppermute | solution.py:185
  98.6 4.0 %collective-permute-start.18 = (f32[3,2,1024]{2,1,0:T(2,128)S(1)}, f32[3,2,1024]{2,1,0:T(2,128)S(1)}, u32[]{:S(2)}, u32[]{:S(2)}) collective-permute-start(f32[3,2,1024]{2,1,0:T(2,128)S(1)} %add_add_fusion.1), channel_id=1, source_target_pairs={{0,64},{64,128},{128,192},{192,0},{1,65},{65,129},{129,193},{193,1... | collective-permute-start | bytes 73736 | tf_op jit(solution)/shard_map/ppermute | solution.py:185
  99.2 4.3 %collective-permute-start.19 = (f32[3,2,1024]{2,1,0:T(2,128)S(1)}, f32[3,2,1024]{2,1,0:T(2,128)S(1)}, u32[]{:S(2)}, u32[]{:S(2)}) collective-permute-start(f32[3,2,1024]{2,1,0:T(2,128)S(1)} %add_add_fusion.1), channel_id=1, source_target_pairs={{0,128},{64,192},{128,0},{192,64},{1,129},{65,193},{129,1},{193,65... | collective-permute-start | bytes 73736 | tf_op jit(solution)/shard_map/ppermute | solution.py:185
  99.9 3.6 %collective-permute-start.20 = (f32[3,2,1024]{2,1,0:T(2,128)S(1)}, f32[3,2,1024]{2,1,0:T(2,128)S(1)}, u32[]{:S(2)}, u32[]{:S(2)}) collective-permute-start(f32[3,2,1024]{2,1,0:T(2,128)S(1)} %add_add_fusion.1), channel_id=1, source_target_pairs={{0,192},{64,0},{128,64},{192,128},{1,193},{65,1},{129,65},{193,129... | collective-permute-start | bytes 73736 | tf_op jit(solution)/shard_map/ppermute | solution.py:185
  118.3 7.2 %collective-permute-start.21 = (bf16[4,4,64,384]{3,2,1,0:T(8,128)(2,1)}, bf16[4,4,64,384]{3,2,1,0:T(8,128)(2,1)}, u32[]{:S(2)}, u32[]{:S(2)}) collective-permute-start(bf16[4,4,64,384]{3,2,1,0:T(8,128)(2,1)} %dynamic-slice_bitcast_fusion), channel_id=1, source_target_pairs={{0,16},{16,0},{1,17},{17,1},{2,18},{18,2},{3,19},{19,3},{4,20},{20... | collective-permute-start | bytes 2359304 | tf_op jit(solution)/shard_map/ppermute | solution.py:185
  121.6 3.9 %copy-start.3 = (bf16[32,64,384]{2,1,0:T(8,128)(2,1)S(1)}, bf16[32,64,384]{2,1,0:T(8,128)(2,1)}, u32[]{:S(2)}) copy-start(bf16[32,64,384]{2,1,0:T(8,128)(2,1)} %get-tuple-element.34) | copy-start | bytes 4718596
  121.6 44.3 %all-to-all-start.3 = ((bf16[8,256,384]{2,1,0:T(8,128)(2,1)}), bf16[8,256,384]{2,1,0:T(8,128)(2,1)S(1)}, u32[]{:S(2)}, u32[]{:S(2)}) async-start(bf16[8,256,384]{2,1,0:T(8,128)(2,1)} %get-tuple-element.35), calls=%async_computation.3 | async-start | bytes 3145728 | tf_op jit(solution)/shard_map/all_to_all | solution.py:178
  126.9 7.7 %collective-permute-start.22 = (bf16[4,64,384]{2,1,0:T(8,128)(2,1)S(1)}, bf16[4,64,384]{2,1,0:T(8,128)(2,1)S(1)}, u32[]{:S(2)}, u32[]{:S(2)}) collective-permute-start(bf16[4,64,384]{2,1,0:T(8,128)(2,1)S(1)} %get-tuple-element.50), channel_id=1, source_target_pairs={{0,1},{1,32},{32,33},{33,0},{2,3},{3,34},{34,35},{35,2},{4,5},{5,3... | collective-permute-start | bytes 589832 | tf_op jit(solution)/shard_map/ppermute | solution.py:185
  127.2 12.2 %collective-permute-start.23 = (bf16[4,64,384]{2,1,0:T(8,128)(2,1)S(1)}, bf16[4,64,384]{2,1,0:T(8,128)(2,1)S(1)}, u32[]{:S(2)}, u32[]{:S(2)}) collective-permute-start(bf16[4,64,384]{2,1,0:T(8,128)(2,1)S(1)} %get-tuple-element.52), channel_id=1, source_target_pairs={{0,32},{1,33},{32,0},{33,1},{2,34},{3,35},{34,2},{35,3},{4,36},{5,... | collective-permute-start | bytes 589832 | tf_op jit(solution)/shard_map/ppermute | solution.py:185
  130.4 9.0 %collective-permute-start.24 = (bf16[4,64,384]{2,1,0:T(8,128)(2,1)S(1)}, bf16[4,64,384]{2,1,0:T(8,128)(2,1)S(1)}, u32[]{:S(2)}, u32[]{:S(2)}) collective-permute-start(bf16[4,64,384]{2,1,0:T(8,128)(2,1)S(1)} %get-tuple-element.51), channel_id=1, source_target_pairs={{0,33},{1,0},{32,1},{33,32},{2,35},{3,2},{34,3},{35,34},{4,37},{5,... | collective-permute-start | bytes 589832 | tf_op jit(solution)/shard_map/ppermute | solution.py:185
  139.5 4.5 %collective-permute-start.25 = (bf16[64,384]{1,0:T(8,128)(2,1)S(1)}, bf16[64,384]{1,0:T(8,128)(2,1)S(1)}, u32[]{:S(2)}, u32[]{:S(2)}) collective-permute-start(bf16[64,384]{1,0:T(8,128)(2,1)S(1)} %get-tuple-element.59), channel_id=1, source_target_pairs={{0,64},{64,128},{128,192},{192,0},{1,65},{65,129},{129,193},{193,1... | collective-permute-start | bytes 147464 | tf_op jit(solution)/shard_map/ppermute | solution.py:185
  141.1 4.7 %collective-permute-start.26 = (bf16[64,384]{1,0:T(8,128)(2,1)S(1)}, bf16[64,384]{1,0:T(8,128)(2,1)S(1)}, u32[]{:S(2)}, u32[]{:S(2)}) collective-permute-start(bf16[64,384]{1,0:T(8,128)(2,1)S(1)} %get-tuple-element.61), channel_id=1, source_target_pairs={{0,128},{64,192},{128,0},{192,64},{1,129},{65,193},{129,1},{193,65... | collective-permute-start | bytes 147464 | tf_op jit(solution)/shard_map/ppermute | solution.py:185
  143.0 3.4 %collective-permute-start.27 = (bf16[64,384]{1,0:T(8,128)(2,1)S(1)}, bf16[64,384]{1,0:T(8,128)(2,1)S(1)}, u32[]{:S(2)}, u32[]{:S(2)}) collective-permute-start(bf16[64,384]{1,0:T(8,128)(2,1)S(1)} %get-tuple-element.60), channel_id=1, source_target_pairs={{0,192},{64,0},{128,64},{192,128},{1,193},{65,1},{129,65},{193,129... | collective-permute-start | bytes 147464 | tf_op jit(solution)/shard_map/ppermute | solution.py:185
  165.9 1.2 copy-start.2

commit v8 on v6

--- a/solution.py
+++ b/solution.py
@@ -82,7 +82,7 @@
 
 def grads_kernel(
     win_ref, tq_ref, cot_ref, k_ref, v_ref, tk_ref, tv_ref, gains_ref, stats_ref,
-    rows_ref, dkv_ref, dtk_ref, dtv_ref,
+    side_ref, own_ref, other_ref, dkv_ref, dtk_ref, dtv_ref,
 ):
     queries = normed_queries(win_ref, tq_ref, gains_ref)
     cot = cot_ref[...]
@@ -108,11 +108,17 @@
             dkv_ref[spots, :own] = dkey.reshape(-1, own, HD)
             dkv_ref[spots, own:] = dvalue.reshape(-1, own, HD)
     half = count // 2
-    outs = out_t.T.astype(BF16)
-    dqs = (dq_t * INV_ROOT).T.astype(BF16)
-    groups, part = rows_ref.shape[0], rows_ref.shape[1] // 4
+    outs = out_t.T
+    dqs = (dq_t * INV_ROOT).T
+    groups, part = own_ref.shape[0], own_ref.shape[1] // 4
+    is_first = side_ref[0] == 0
     for place, block in enumerate((outs[:half], outs[half:], dqs[:half], dqs[half:])):
-        rows_ref[:, place * part : (place + 1) * part] = block.reshape(groups, part, HD)
+        low, high = block[: half // 2], block[half // 2 :]
+        spot = slice(place * part, (place + 1) * part)
+        for ref, rows in (
+            (own_ref, jnp.where(is_first, low, high)), (other_ref, jnp.where(is_first, high, low))
+        ):
+            ref[:, spot] = rows.astype(BF16).reshape(groups, part, HD)
 
 
 def column_spec(shape):
@@ -154,8 +160,10 @@
     _, _, cot, moved_k, moved_v, text_k, _ = operands
     count = cot.shape[0]
     width = heads * HD
+    rows = jax.ShapeDtypeStruct((groups // 2, count // groups * 2, width), BF16)
     shapes = [
-        jax.ShapeDtypeStruct((groups, count // groups * 2, width), BF16),
+        rows,
+        rows,
         jax.ShapeDtypeStruct(
             (moved_k.shape[0], moved_k.shape[1] + moved_v.shape[1], width), BF16
         ),
@@ -166,12 +174,15 @@
         grads_kernel,
         grid=(heads,),
         in_specs=operand_specs(operands, gains)
-        + [pl.BlockSpec((1, 2, count), lambda head: (head, 0, 0))],
+        + [
+            pl.BlockSpec((1, 2, count), lambda head: (head, 0, 0)),
+            pl.BlockSpec(memory_space=pltpu.SMEM),
+        ],
         out_specs=[column_spec(s.shape) for s in shapes],
         out_shape=shapes,
         compiler_params=PARAMS,
         cost_estimate=cost(operands, heads, 6),
-    )(*operands, gains, stats)
+    )(*operands, gains, stats, lax.axis_index("c")[None])
 
 
 def swap(array, axes):
@@ -221,10 +232,9 @@
     return sum(piece.astype(F32) for piece in scatter_stage(pieces, axes))
 
 
-def reduce_row(pieces):
-    shape = pieces.shape[1:]
-    pieces = pieces.reshape((lax.axis_size("c"), lax.axis_size(ROW), lax.axis_size("y")) + shape)
-    pieces = sum_stage(pieces, "c").astype(BF16)
+def reduce_row(own, other):
+    pieces = (own.astype(F32) + push(other, "c", 1).astype(F32)).astype(BF16)
+    pieces = pieces.reshape((lax.axis_size(ROW), lax.axis_size("y")) + pieces.shape[1:])
     return sum_stage(pieces, ROW).astype(BF16)
 
 
@@ -356,9 +366,9 @@
     operands = (window_rows, text_rows, cotangent, moved_k, moved_v, text_k, text_v)
 
     stats = sum_plane(attention_stats(operands, gains, heads))
-    out, back, key_text, value_text = attention_grads(operands, gains, stats, heads, groups)
+    out, other, back, key_text, value_text = attention_grads(operands, gains, stats, heads, groups)
     back = swap(back, "z")
-    total = sum_stage(reduce_row(out), "y")
+    total = sum_stage(reduce_row(out, other), "y")
     grad_video_k, grad_video_v = merge(back)
 
     def query_grad(raw, gain, cot):

time: 171 us -> 166 us (0.971)
  local copies, waits for them, and re-layouts: 12.5 us -> 7.3 us
  waiting for transfers between devices: 64.6 us -> 61.2 us
  starting transfers between devices: 64.6 us -> 66.8 us
    all_to_all x4, waiting for transfers between devices: 29.6 us -> 25.1 us  [swap(): return lax.all_to_all(array, axes, split_axis=0, concat_axis=0, tiled=True)]
    unnamed x43 -> x29, local copies, waits for them, and re-layouts: 5.72 us -> 1.45 us
  transfers between devices with their start and end apart: 32 -> 32, of which waited for: 22 -> 24; matrix products, arithmetic and copies ran while one was open for 4% -> 4% of each run, Pallas kernels for 1% -> 1%
where the time goes in v8:
time: 166 us; the launch traced here: 165 us
  starting transfers between devices  66.8 us (40%)
  waiting for transfers between devices  61.2 us (37%)
  Pallas kernels  22.5 us (14%)
  local copies, waits for them, and re-layouts  7.3 us (4%)
  other arithmetic  5.64 us (3%)
    ppermute x28, starting transfers between devices, push(): lax.ppermute(array, axes, [(i, (i + step) % size) for i in range(size)])  44.4 us
    ppermute x28, waiting for transfers between devices, push(): lax.ppermute(array, axes, [(i, (i + step) % size) for i in range(size)])  36.1 us
    all_to_all x4, waiting for transfers between devices, swap(): return lax.all_to_all(array, axes, split_axis=0, concat_axis=0, tiled=True)  25.1 us
    all_to_all x4, starting transfers between devices, swap(): return lax.all_to_all(array, axes, split_axis=0, concat_axis=0, tiled=True)  22.4 us
    pallas_call x1, Pallas kernels, attention_grads(): pl.pallas_call(grads_kernel, grid=(heads,), in_specs=operand_specs(operan...  12.3 us
    pallas_call x1, Pallas kernels, attention_stats(): pl.pallas_call(stats_kernel, grid=(heads,), in_specs=operand_specs(operan...  5.37 us
  transfers between devices with their start and end apart: 32, of which 24 were waited for; matrix products, arithmetic and copies ran while one was open for 4% of the time, Pallas kernels for 1%

profile of v8, /device:TPU:1, one launch (start us, length us, event | category | flops | bytes accessed | tf_op | source)
XLA Modules:
  0.0 164.7 jit_solution(2931131358731400808)
XLA Ops:
  0.6 1.0 slice.40
  1.6 1.2 pad_maximum_fusion
  2.8 1.1 copy.73
  4.0 9.1 %all-to-all-start = ((bf16[8,176,384]{2,1,0:T(8,128)(2,1)}), bf16[8,176,384]{2,1,0:T(8,128)(2,1)S(1)}, u32[]{:S(2)}, u32[]{:S(2)}) async-start(bf16[8,176,384]{2,1,0:T(8,128)(2,1)} %bitcast.136), calls=%async_computation | async-start | bytes 2162688 | tf_op jit(solution)/shard_map/all_to_all | solution.py:189
  13.2 1.0 collective-permute-start
  14.3 1.3 collective-permute-done
  15.6 0.7 fusion.4
  16.4 1.2 collective-permute-start.1
  17.6 2.5 %collective-permute-start.2 = (bf16[2,16,3072]{2,1,0:T(8,128)(2,1)S(1)}, bf16[2,16,3072]{2,1,0:T(8,128)(2,1)S(1)}, u32[]{:S(2)}, u32[]{:S(2)}) collective-permute-start(bf16[2,16,3072]{2,1,0:T(8,128)(2,1)S(1)} %get-tuple-element.58), channel_id=1, source_target_pairs={{0,32},{1,33},{32,0},{33,1},{2,34},{3,35},{34,2},{35,3},{4,36},{5,... | collective-permute-start | bytes 589832 | tf_op jit(solution)/shard_map/ppermute | solution.py:196
  20.0 1.2 collective-permute-start.3
  21.2 0.6 shift-right-arithmetic_and_fusion
  21.8 1.8 %collective-permute-done.1.refs_1_ = bf16[2,16,3072]{2,1,0:T(8,128)(2,1)S(1)} collective-permute-done((bf16[2,16,3072]{2,1,0:T(8,128)(2,1)S(1)}, bf16[2,16,3072]{2,1,0:T(8,128)(2,1)S(1)}, u32[]{:S(2)}, u32[]{:S(2)}) %collective-permute-start.1) | collective-permute-done | bytes 196640 | tf_op jit(solution)/shard_map/ppermute | solution.py:196
  23.7 5.2 %collective-permute-done.2.refs_2_ = bf16[2,16,3072]{2,1,0:T(8,128)(2,1)S(1)} collective-permute-done((bf16[2,16,3072]{2,1,0:T(8,128)(2,1)S(1)}, bf16[2,16,3072]{2,1,0:T(8,128)(2,1)S(1)}, u32[]{:S(2)}, u32[]{:S(2)}) %collective-permute-start.2) | collective-permute-done | bytes 196640 | tf_op jit(solution)/shard_map/ppermute | solution.py:196
  28.9 0.7 copy-done.4
  29.7 2.1 %shard_map.188 = (bf16[16,3072]{1,0:T(8,128)(2,1)}, bf16[16,3072]{1,0:T(8,128)(2,1)}, bf16[16,3072]{1,0:T(8,128)(2,1)}, bf16[16,3072]{1,0:T(8,128)(2,1)}) custom-call(s32[4]{0:T(128)} %get-tuple-element.73.source_ref, bf16[2,16,3072]{2,1,0:T(8,128)(2,1)} %get-tuple-element.56.refs_0_, bf16[2,16,3072]{2,1,0:T(8,128)(2,1)} %copy-done.3, ...), custom_call_target="tpu_custom_call" | custom-call | tf_op jit(solution)/shard_map/pallas_call | solution.py:261
  31.8 1.4 collective-permute-start.4
  33.2 2.6 %collective-permute-start.5 = (bf16[16,3072]{1,0:T(8,128)(2,1)}, bf16[16,3072]{1,0:T(8,128)(2,1)S(1)}, u32[]{:S(2)}, u32[]{:S(2)}) collective-permute-start(bf16[16,3072]{1,0:T(8,128)(2,1)} %get-tuple-element.27), channel_id=1, source_target_pairs={{0,128},{64,192},{128,0},{192,64},{1,129},{65,193},{129,1},{193,65... | collective-permute-start | bytes 294920 | tf_op jit(solution)/shard_map/ppermute | solution.py:196
  35.8 1.1 collective-permute-start.6
  36.9 2.8 %collective-permute-done.5 = bf16[16,3072]{1,0:T(8,128)(2,1)S(1)} collective-permute-done((bf16[16,3072]{1,0:T(8,128)(2,1)}, bf16[16,3072]{1,0:T(8,128)(2,1)S(1)}, u32[]{:S(2)}, u32[]{:S(2)}) %collective-permute-start.5) | collective-permute-done | bytes 98336 | tf_op jit(solution)/shard_map/ppermute | solution.py:196
  39.7 0.9 collective-permute-done.6
  40.6 1.0 fusion.14
  41.6 1.4 all-to-all-done.k_ref
  43.1 0.7 copy.51
  43.7 5.5 %all-to-all-start.1 = ((bf16[8,16,384]{2,1,0:T(8,128)(2,1)}), bf16[8,16,384]{2,1,0:T(8,128)(2,1)S(1)}, u32[]{:S(2)}, u32[]{:S(2)}) async-start(bf16[8,16,384]{2,1,0:T(8,128)(2,1)} %copy.51), calls=%async_computation.1 | async-start | bytes 196608 | tf_op jit(solution)/shard_map/all_to_all | solution.py:189
  49.2 0.8 copy.74
  50.0 6.9 %all-to-all-done.1 = bf16[8,16,384]{2,1,0:T(8,128)(2,1)S(1)} async-done(((bf16[8,16,384]{2,1,0:T(8,128)(2,1)}), bf16[8,16,384]{2,1,0:T(8,128)(2,1)S(1)}, u32[]{:S(2)}, u32[]{:S(2)}) %all-to-all-start.1) | async-done | bytes 98336 | tf_op jit(solution)/shard_map/all_to_all | solution.py:189
  57.1 2.5 %collective-permute-start.8 = (bf16[4,16,384]{2,1,0:T(8,128)(2,1)S(1)}, bf16[4,16,384]{2,1,0:T(8,128)(2,1)S(1)}, u32[]{:S(2)}, u32[]{:S(2)}) collective-permute-start(bf16[4,16,384]{2,1,0:T(8,128)(2,1)S(1)} %pad_maximum_fusion.2), channel_id=1, source_target_pairs={{0,128},{64,192},{128,0},{192,64},{1,129},{65,193},{129,1},{193,65... | collective-permute-start | bytes 147464 | tf_op jit(solution)/shard_map/ppermute | solution.py:196
  60.1 3.5 %all-to-all-start.2 = ((bf16[8,80,384]{2,1,0:T(8,128)(2,1)}), bf16[8,80,384]{2,1,0:T(8,128)(2,1)S(1)}, u32[]{:S(2)}, u32[]{:S(2)}) async-start(bf16[8,80,384]{2,1,0:T(8,128)(2,1)} %bitcast.138), calls=%async_computation.2 | async-start | bytes 983040 | tf_op jit(solution)/shard_map/all_to_all | solution.py:189
  63.7 1.1 collective-permute-start.10
  64.8 3.8 %collective-permute-start.11 = (bf16[4,4,16,384]{3,2,0,1:T(8,128)(2,1)S(1)}, bf16[4,4,16,384]{3,2,0,1:T(8,128)(2,1)S(1)}, u32[]{:S(2)}, u32[]{:S(2)}) collective-permute-start(bf16[4,4,16,384]{3,2,0,1:T(8,128)(2,1)S(1)} %bitcast_dynamic-update-slice_fusion.6), channel_id=1, source_target_pairs={{0,32},{1,33},{32,0},{33,1},{2,34},{3,35},{34,2},{35,3},{4,36},{5,... | collective-permute-start | bytes 589832 | tf_op jit(solution)/shard_map/ppermute | solution.py:196
  68.7 1.7 %collective-permute-done.10 = bf16[4,4,16,384]{3,2,0,1:T(8,128)(2,1)S(1)} collective-permute-done((bf16[4,4,16,384]{3,2,0,1:T(8,128)(2,1)S(1)}, bf16[4,4,16,384]{3,2,0,1:T(8,128)(2,1)S(1)}, u32[]{:S(2)}, u32[]{:S(2)}) %collective-permute-start.10) | collective-permute-done | bytes 196640 | tf_op jit(solution)/shard_map/ppermute | solution.py:196
  70.5 3.4 %collective-permute-done.11 = bf16[4,4,16,384]{3,2,0,1:T(8,128)(2,1)S(1)} collective-permute-done((bf16[4,4,16,384]{3,2,0,1:T(8,128)(2,1)S(1)}, bf16[4,4,16,384]{3,2,0,1:T(8,128)(2,1)S(1)}, u32[]{:S(2)}, u32[]{:S(2)}) %collective-permute-start.11) | collective-permute-done | bytes 196640 | tf_op jit(solution)/shard_map/ppermute | solution.py:196
  73.9 1.4 all-to-all-done.2.v_ref
  75.4 5.9 %collective-permute-start.13 = (bf16[4,4,4,16,384]{4,3,2,1,0:T(8,128)(2,1)S(1)}, bf16[4,4,4,16,384]{4,3,2,1,0:T(8,128)(2,1)S(1)}, u32[]{:S(2)}, u32[]{:S(2)}) collective-permute-start(bf16[4,4,4,16,384]{4,3,2,1,0:T(8,128)(2,1)S(1)} %bitcast.148), channel_id=1, source_target_pairs={{0,16},{16,0},{1,17},{17,1},{2,18},{18,2},{3,19},{19,3},{4,20},{20... | collective-permute-start | bytes 2359304 | tf_op jit(solution)/shard_map/ppermute | solution.py:196
  81.7 1.5 collective-permute-done.13
  83.7 0.6 copy-done
  84.3 5.4 %shard_map.189 = f32[3,2,1024]{2,1,0:T(2,128)S(1)} custom-call(bf16[512,384]{1,0:T(8,128)(2,1)S(1)} %bitcast.143, bf16[512,384]{1,0:T(8,128)(2,1)S(1)} %bitcast.141, bf16[1024,384]{1,0:T(8,128)(2,1)S(1)} %pad_maximum_fusion.1.cot_ref, bf16[8,176,384]{2,1,0:T(8,128)(2,1)S(1)} %all-to-all-done.k_ref, bf16[8,80,384]{2,1,0:T(8,128)(2,1)S(1)} %all-to-all-done.2.v_ref, ...), custom_call_target="tpu_custom_call" | custom-call | flops 1610612736 | bytes 6000000 | tf_op jit(solution)/shard_map/pallas_call | solution.py:148
  89.7 0.5 collective-permute-start.14
  90.1 0.8 collective-permute-done.14
  91.0 1.0 collective-permute-start.15
  92.0 3.8 %collective-permute-start.16 = (f32[3,2,1024]{2,1,0:T(2,128)S(1)}, f32[3,2,1024]{2,1,0:T(2,128)S(1)}, u32[]{:S(2)}, u32[]{:S(2)}) collective-permute-start(f32[3,2,1024]{2,1,0:T(2,128)S(1)} %add.106), channel_id=1, source_target_pairs={{0,32},{1,33},{32,0},{33,1},{2,34},{3,35},{34,2},{35,3},{4,36},{5,... | collective-permute-start | bytes 73736 | tf_op jit(solution)/shard_map/ppermute | solution.py:196
  95.8 1.4 collective-permute-done.16
  97.3 1.2 collective-permute-done.17
  98.6 1.3 collective-permute-start.19
  99.8 2.0 %collective-permute-start.20 = (f32[3,2,1024]{2,1,0:T(2,128)S(1)}, f32[3,2,1024]{2,1,0:T(2,128)S(1)}, u32[]{:S(2)}, u32[]{:S(2)}) collective-permute-start(f32[3,2,1024]{2,1,0:T(2,128)S(1)} %add_add_fusion.1), channel_id=1, source_target_pairs={{0,192},{64,0},{128,64},{192,128},{1,193},{65,1},{129,65},{193,129... | collective-permute-start | bytes 73736 | tf_op jit(solution)/shard_map/ppermute | solution.py:196
  101.8 0.6 collective-permute-done.18
  103.3 12.3 %shard_map.190 = (bf16[16,64,384]{2,1,0:T(8,128)(2,1)S(1)}, bf16[16,64,384]{2,1,0:T(8,128)(2,1)S(1)}, bf16[8,256,384]{2,1,0:T(8,128)(2,1)}, bf16[16,384]{1,0:T(8,128)(2,1)}, bf16[16,384]{1,0:T(8,128)(2,1)}) custom-call(bf16[512,384]{1,0:T(8,128)(2,1)S(1)} %bitcast.144, bf16[512,384]{1,0:T(8,128)(2,1)S(1)} %bitcast.142, ...), custom_call_target="tpu_custom_call" | custom-call | flops 4831838208 | bytes 6000000 | tf_op jit(solution)/shard_map/pallas_call | solution.py:173
  115.6 3.5 %collective-permute-start.21 = (bf16[16,64,384]{2,1,0:T(8,128)(2,1)S(1)}, bf16[16,64,384]{2,1,0:T(8,128)(2,1)S(1)}, u32[]{:S(2)}, u32[]{:S(2)}) collective-permute-start(bf16[16,64,384]{2,1,0:T(8,128)(2,1)S(1)} %get-tuple-element.36), channel_id=1, source_target_pairs={{0,16},{16,0},{1,17},{17,1},{2,18},{18,2},{3,19},{19,3},{4,20},{20... | collective-permute-start | bytes 2359304 | tf_op jit(solution)/shard_map/ppermute | solution.py:196
  119.1 4.3 %all-to-all-start.3 = ((bf16[8,256,384]{2,1,0:T(8,128)(2,1)}), bf16[8,256,384]{2,1,0:T(8,128)(2,1)}, u32[]{:S(2)}, u32[]{:S(2)}) async-start(bf16[8,256,384]{2,1,0:T(8,128)(2,1)} %get-tuple-element.37), calls=%async_computation.3 | async-start | bytes 3145728 | tf_op jit(solution)/shard_map/all_to_all | solution.py:189
  124.1 2.4 %collective-permute-start.23 = (bf16[4,64,384]{2,1,0:T(8,128)(2,1)S(1)}, bf16[4,64,384]{2,1,0:T(8,128)(2,1)S(1)}, u32[]{:S(2)}, u32[]{:S(2)}) collective-permute-start(bf16[4,64,384]{2,1,0:T(8,128)(2,1)S(1)} %get-tuple-element.54), channel_id=1, source_target_pairs={{0,32},{1,33},{32,0},{33,1},{2,34},{3,35},{34,2},{35,3},{4,36},{5,... | collective-permute-start | bytes 589832 | tf_op jit(solution)/shard_map/ppermute | solution.py:196
  126.4 0.9 collective-permute-start.24
  127.3 4.8 %collective-permute-done.22 = bf16[4,64,384]{2,1,0:T(8,128)(2,1)S(1)} collective-permute-done((bf16[4,64,384]{2,1,0:T(8,128)(2,1)S(1)}, bf16[4,64,384]{2,1,0:T(8,128)(2,1)S(1)}, u32[]{:S(2)}, u32[]{:S(2)}) %collective-permute-start.22) | collective-permute-done | bytes 196640 | tf_op jit(solution)/shard_map/ppermute | solution.py:196
  132.2 3.7 %collective-permute-done.23 = bf16[4,64,384]{2,1,0:T(8,128)(2,1)S(1)} collective-permute-done((bf16[4,64,384]{2,1,0:T(8,128)(2,1)S(1)}, bf16[4,64,384]{2,1,0:T(8,128)(2,1)S(1)}, u32[]{:S(2)}, u32[]{:S(2)}) %collective-permute-start.23) | collective-permute-done | bytes 196640 | tf_op jit(solution)/shard_map/ppermute | solution.py:196
  135.9 0.5 collective-permute-done.24
  136.5 1.6 collective-permute-start.25
  138.1 2.1 %collective-permute-start.26 = (bf16[64,384]{1,0:T(8,128)(2,1)S(1)}, bf16[64,384]{1,0:T(8,128)(2,1)S(1)}, u32[]{:S(2)}, u32[]{:S(2)}) collective-permute-start(bf16[64,384]{1,0:T(8,128)(2,1)S(1)} %get-tuple-element.63), channel_id=1, source_target_pairs={{0,128},{64,192},{128,0},{192,64},{1,129},{65,193},{129,1},{193,65... | collective-permute-start | bytes 147464 | tf_op jit(solution)/shard_map/ppermute | solution.py:196
  140.6 0.5 collective-permute-done.25
  141.2 1.8 %collective-permute-done.26 = bf16[64,384]{1,0:T(8,128)(2,1)S(1)} collective-permute-done((bf16[64,384]{1,0:T(8,128)(2,1)S(1)}, bf16[64,384]{1,0:T(8,128)(2,1)S(1)}, u32[]{:S(2)}, u32[]{:S(2)}) %collective-permute-start.26) | collective-permute-done | bytes 49184 | tf_op jit(solution)/shard_map/ppermute | solution.py:196
  143.0 1.1 collective-permute-done.27
  144.4 0.6 fusion.19
  145.1 0.6 fusion.26
  145.9 0.6 fusion.22
  146.5 15.4 %all-to-all-done.3.came_ref = bf16[8,256,384]{2,1,0:T(8,128)(2,1)} async-done(((bf16[8,256,384]{2,1,0:T(8,128)(2,1)}), bf16[8,256,384]{2,1,0:T(8,128)(2,1)}, u32[]{:S(2)}, u32[]{:S(2)}) %all-to-all-start.3) | async-done | bytes 1572896 | tf_op jit(solution)/shard_map/all_to_all | solution.py:189
  161.9 2.7 %shard_map.191 = (bf16[128,3072]{1,0:T(8,128)(2,1)}, bf16[128,3072]{1,0:T(8,128)(2,1)}) custom-call(bf16[8,256,384]{2,1,0:T(8,128)(2,1)} %all-to-all-done.3.came_ref), custom_call_target="tpu_custom_call" | custom-call | tf_op jit(solution)/shard_map/pallas_call | solution.py:330
  (89 shorter events, 4.8 us)
Async XLA Ops:
  4.0 9.2 %copy-start.2 = (bf16[128,3072]{1,0:T(8,128)(2,1)S(1)}, bf16[128,3072]{1,0:T(8,128)(2,1)}, u32[]{:S(2)}) copy-start(bf16[128,3072]{1,0:T(8,128)(2,1)} %param.13) | copy-start | bytes 2359300
  4.0 39.1 %all-to-all-start = ((bf16[8,176,384]{2,1,0:T(8,128)(2,1)}), bf16[8,176,384]{2,1,0:T(8,128)(2,1)S(1)}, u32[]{:S(2)}, u32[]{:S(2)}) async-start(bf16[8,176,384]{2,1,0:T(8,128)(2,1)} %bitcast.136), calls=%async_computation | async-start | bytes 2162688 | tf_op jit(solution)/shard_map/all_to_all | solution.py:189
  13.1 8.0 %copy-start.13 = (s32[4]{0:T(128)S(1)}, s32[4]{0:T(128)}, u32[]{:S(2)}) copy-start(s32[4]{0:T(128)} %param.23) | copy-start | bytes 52
  13.2 2.4 %collective-permute-start = (bf16[4,16,3072]{2,1,0:T(8,128)(2,1)S(1)}, bf16[4,16,3072]{2,1,0:T(8,128)(2,1)S(1)}, u32[]{:S(2)}, u32[]{:S(2)}) collective-permute-start(bf16[4,16,3072]{2,1,0:T(8,128)(2,1)S(1)} %bitcast.157), channel_id=1, source_target_pairs={{0,16},{16,0},{1,17},{17,1},{2,18},{18,2},{3,19},{19,3},{4,20},{20... | collective-permute-start | bytes 1179656 | tf_op jit(solution)/shard_map/ppermute | solution.py:196
  16.3 32.9 %slice-start = ((bf16[128,3072]{1,0:T(8,128)(2,1)}), bf16[80,3072]{1,0:T(8,128)(2,1)S(1)}, s32[]{:S(2)}) async-start(bf16[128,3072]{1,0:T(8,128)(2,1)} %param.15), calls=%async_computation.4 | async-start | bytes 983040 | tf_op jit(solution)/shard_map/slice | solution.py:352
  16.4 7.3 %collective-permute-start.1 = (bf16[2,16,3072]{2,1,0:T(8,128)(2,1)S(1)}, bf16[2,16,3072]{2,1,0:T(8,128)(2,1)S(1)}, u32[]{:S(2)}, u32[]{:S(2)}) collective-permute-start(bf16[2,16,3072]{2,1,0:T(8,128)(2,1)S(1)} %get-tuple-element.57), channel_id=1, source_target_pairs={{0,1},{1,32},{32,33},{33,0},{2,3},{3,34},{34,35},{35,2},{4,5},{5,3... | collective-permute-start | bytes 589832 | tf_op jit(solution)/shard_map/ppermute | solution.py:196
  17.6 11.3 %collective-permute-start.2 = (bf16[2,16,3072]{2,1,0:T(8,128)(2,1)S(1)}, bf16[2,16,3072]{2,1,0:T(8,128)(2,1)S(1)}, u32[]{:S(2)}, u32[]{:S(2)}) collective-permute-start(bf16[2,16,3072]{2,1,0:T(8,128)(2,1)S(1)} %get-tuple-element.58), channel_id=1, source_target_pairs={{0,32},{1,33},{32,0},{33,1},{2,34},{3,35},{34,2},{35,3},{4,36},{5,... | collective-permute-start | bytes 589832 | tf_op jit(solution)/shard_map/ppermute | solution.py:196
  20.0 8.9 %collective-permute-start.3 = (bf16[2,16,3072]{2,1,0:T(8,128)(2,1)S(1)}, bf16[2,16,3072]{2,1,0:T(8,128)(2,1)S(1)}, u32[]{:S(2)}, u32[]{:S(2)}) collective-permute-start(bf16[2,16,3072]{2,1,0:T(8,128)(2,1)S(1)} %get-tuple-element.55), channel_id=1, source_target_pairs={{0,33},{1,0},{32,1},{33,32},{2,35},{3,2},{34,3},{35,34},{4,37},{5,... | collective-permute-start | bytes 589832 | tf_op jit(solution)/shard_map/ppermute | solution.py:196
  23.7 5.2 %copy-start.3 = (bf16[2,16,3072]{2,1,0:T(8,128)(2,1)}, bf16[2,16,3072]{2,1,0:T(8,128)(2,1)S(1)}, u32[]{:S(2)}) copy-start(bf16[2,16,3072]{2,1,0:T(8,128)(2,1)S(1)} %collective-permute-done.1.refs_1_) | copy-start | bytes 589828
  28.9 0.7 copy-start.4
  28.9 0.8 copy-start.5
  31.8 25.2 %copy-start.6 = (bf16[16,384]{1,0:T(8,128)(2,1)S(1)}, bf16[16,384]{1,0:T(8,128)(2,1)}, u32[]{:S(2)}) copy-start(bf16[16,384]{1,0:T(8,128)(2,1)} %param.16) | copy-start | bytes 36868
  31.8 25.2 %copy-start.7 = (bf16[16,384]{1,0:T(8,128)(2,1)S(1)}, bf16[16,384]{1,0:T(8,128)(2,1)}, u32[]{:S(2)}) copy-start(bf16[16,384]{1,0:T(8,128)(2,1)} %param.25) | copy-start | bytes 36868
  31.8 25.2 %copy-start.8 = (bf16[16,384]{1,0:T(8,128)(2,1)S(1)}, bf16[16,384]{1,0:T(8,128)(2,1)}, u32[]{:S(2)}) copy-start(bf16[16,384]{1,0:T(8,128)(2,1)} %param.24) | copy-start | bytes 36868
  31.8 5.1 %collective-permute-start.4 = (bf16[16,3072]{1,0:T(8,128)(2,1)}, bf16[16,3072]{1,0:T(8,128)(2,1)S(1)}, u32[]{:S(2)}, u32[]{:S(2)}) collective-permute-start(bf16[16,3072]{1,0:T(8,128)(2,1)} %get-tuple-element.26), channel_id=1, source_target_pairs={{0,64},{64,128},{128,192},{192,0},{1,65},{65,129},{129,193},{193,1... | collective-permute-start | bytes 294920 | tf_op jit(solution)/shard_map/ppermute | solution.py:196
  33.2 6.6 %collective-permute-start.5 = (bf16[16,3072]{1,0:T(8,128)(2,1)}, bf16[16,3072]{1,0:T(8,128)(2,1)S(1)}, u32[]{:S(2)}, u32[]{:S(2)}) collective-permute-start(bf16[16,3072]{1,0:T(8,128)(2,1)} %get-tuple-element.27), channel_id=1, source_target_pairs={{0,128},{64,192},{128,0},{192,64},{1,129},{65,193},{129,1},{193,65... | collective-permute-start | bytes 294920 | tf_op jit(solution)/shard_map/ppermute | solution.py:196
  35.8 4.8 %collective-permute-start.6 = (bf16[16,3072]{1,0:T(8,128)(2,1)}, bf16[16,3072]{1,0:T(8,128)(2,1)S(1)}, u32[]{:S(2)}, u32[]{:S(2)}) collective-permute-start(bf16[16,3072]{1,0:T(8,128)(2,1)} %get-tuple-element.28), channel_id=1, source_target_pairs={{0,192},{64,0},{128,64},{192,128},{1,193},{65,1},{129,65},{193,129... | collective-permute-start | bytes 294920 | tf_op jit(solution)/shard_map/ppermute | solution.py:196
  43.7 13.2 %all-to-all-start.1 = ((bf16[8,16,384]{2,1,0:T(8,128)(2,1)}), bf16[8,16,384]{2,1,0:T(8,128)(2,1)S(1)}, u32[]{:S(2)}, u32[]{:S(2)}) async-start(bf16[8,16,384]{2,1,0:T(8,128)(2,1)} %copy.51), calls=%async_computation.1 | async-start | bytes 196608 | tf_op jit(solution)/shard_map/all_to_all | solution.py:189
  57.0 6.6 %collective-permute-start.7 = (bf16[4,16,384]{2,1,0:T(8,128)(2,1)S(1)}, bf16[4,16,384]{2,1,0:T(8,128)(2,1)S(1)}, u32[]{:S(2)}, u32[]{:S(2)}) collective-permute-start(bf16[4,16,384]{2,1,0:T(8,128)(2,1)S(1)} %pad_maximum_fusion.2), channel_id=1, source_target_pairs={{0,64},{64,128},{128,192},{192,0},{1,65},{65,129},{129,193},{193,1... | collective-permute-start | bytes 147464 | tf_op jit(solution)/shard_map/ppermute | solution.py:196
  57.1 6.6 %collective-permute-start.8 = (bf16[4,16,384]{2,1,0:T(8,128)(2,1)S(1)}, bf16[4,16,384]{2,1,0:T(8,128)(2,1)S(1)}, u32[]{:S(2)}, u32[]{:S(2)}) collective-permute-start(bf16[4,16,384]{2,1,0:T(8,128)(2,1)S(1)} %pad_maximum_fusion.2), channel_id=1, source_target_pairs={{0,128},{64,192},{128,0},{192,64},{1,129},{65,193},{129,1},{193,65... | collective-permute-start | bytes 147464 | tf_op jit(solution)/shard_map/ppermute | solution.py:196
  59.6 4.1 %collective-permute-start.9 = (bf16[4,16,384]{2,1,0:T(8,128)(2,1)S(1)}, bf16[4,16,384]{2,1,0:T(8,128)(2,1)S(1)}, u32[]{:S(2)}, u32[]{:S(2)}) collective-permute-start(bf16[4,16,384]{2,1,0:T(8,128)(2,1)S(1)} %pad_maximum_fusion.2), channel_id=1, source_target_pairs={{0,192},{64,0},{128,64},{192,128},{1,193},{65,1},{129,65},{193,129... | collective-permute-start | bytes 147464 | tf_op jit(solution)/shard_map/ppermute | solution.py:196
  60.1 15.3 %all-to-all-start.2 = ((bf16[8,80,384]{2,1,0:T(8,128)(2,1)}), bf16[8,80,384]{2,1,0:T(8,128)(2,1)S(1)}, u32[]{:S(2)}, u32[]{:S(2)}) async-start(bf16[8,80,384]{2,1,0:T(8,128)(2,1)} %bitcast.138), calls=%async_computation.2 | async-start | bytes 983040 | tf_op jit(solution)/shard_map/all_to_all | solution.py:189
  63.6 17.7 %copy-start.9 = (f32[128]{0:T(128)S(1)}, f32[128]{0:T(128)}, u32[]{:S(2)}) copy-start(f32[128]{0:T(128)} %param.21) | copy-start | bytes 1540
  63.6 17.7 %copy-start.10 = (f32[128]{0:T(128)S(1)}, f32[128]{0:T(128)}, u32[]{:S(2)}) copy-start(f32[128]{0:T(128)} %param.19) | copy-start | bytes 1540
  63.6 17.7 %copy-start.11 = (f32[128]{0:T(128)S(1)}, f32[128]{0:T(128)}, u32[]{:S(2)}) copy-start(f32[128]{0:T(128)} %param.22) | copy-start | bytes 1540
  63.6 17.7 %copy-start.12 = (f32[128]{0:T(128)S(1)}, f32[128]{0:T(128)}, u32[]{:S(2)}) copy-start(f32[128]{0:T(128)} %param.20) | copy-start | bytes 1540
  63.7 6.7 %collective-permute-start.10 = (bf16[4,4,16,384]{3,2,0,1:T(8,128)(2,1)S(1)}, bf16[4,4,16,384]{3,2,0,1:T(8,128)(2,1)S(1)}, u32[]{:S(2)}, u32[]{:S(2)}) collective-permute-start(bf16[4,4,16,384]{3,2,0,1:T(8,128)(2,1)S(1)} %bitcast_dynamic-update-slice_fusion.6), channel_id=1, source_target_pairs={{0,1},{1,32},{32,33},{33,0},{2,3},{3,34},{34,35},{35,2},{4,5},{5,3... | collective-permute-start | bytes 589832 | tf_op jit(solution)/shard_map/ppermute | solution.py:196
  64.8 9.0 %collective-permute-start.11 = (bf16[4,4,16,384]{3,2,0,1:T(8,128)(2,1)S(1)}, bf16[4,4,16,384]{3,2,0,1:T(8,128)(2,1)S(1)}, u32[]{:S(2)}, u32[]{:S(2)}) collective-permute-start(bf16[4,4,16,384]{3,2,0,1:T(8,128)(2,1)S(1)} %bitcast_dynamic-update-slice_fusion.6), channel_id=1, source_target_pairs={{0,32},{1,33},{32,0},{33,1},{2,34},{3,35},{34,2},{35,3},{4,36},{5,... | collective-permute-start | bytes 589832 | tf_op jit(solution)/shard_map/ppermute | solution.py:196
  68.6 5.3 %collective-permute-start.12 = (bf16[4,4,16,384]{3,2,0,1:T(8,128)(2,1)S(1)}, bf16[4,4,16,384]{3,2,0,1:T(8,128)(2,1)S(1)}, u32[]{:S(2)}, u32[]{:S(2)}) collective-permute-start(bf16[4,4,16,384]{3,2,0,1:T(8,128)(2,1)S(1)} %bitcast_dynamic-update-slice_fusion.6), channel_id=1, source_target_pairs={{0,33},{1,0},{32,1},{33,32},{2,35},{3,2},{34,3},{35,34},{4,37},{5,... | collective-permute-start | bytes 589832 | tf_op jit(solution)/shard_map/ppermute | solution.py:196
  75.4 7.8 %collective-permute-start.13 = (bf16[4,4,4,16,384]{4,3,2,1,0:T(8,128)(2,1)S(1)}, bf16[4,4,4,16,384]{4,3,2,1,0:T(8,128)(2,1)S(1)}, u32[]{:S(2)}, u32[]{:S(2)}) collective-permute-start(bf16[4,4,4,16,384]{4,3,2,1,0:T(8,128)(2,1)S(1)} %bitcast.148), channel_id=1, source_target_pairs={{0,16},{16,0},{1,17},{17,1},{2,18},{18,2},{3,19},{19,3},{4,20},{20... | collective-permute-start | bytes 2359304 | tf_op jit(solution)/shard_map/ppermute | solution.py:196
  83.6 0.7 copy-start
  83.6 0.7 copy-start.1
  89.7 1.3 collective-permute-start.14
  91.0 4.8 %collective-permute-start.15 = (f32[3,2,1024]{2,1,0:T(2,128)S(1)}, f32[3,2,1024]{2,1,0:T(2,128)S(1)}, u32[]{:S(2)}, u32[]{:S(2)}) collective-permute-start(f32[3,2,1024]{2,1,0:T(2,128)S(1)} %add.106), channel_id=1, source_target_pairs={{0,1},{1,32},{32,33},{33,0},{2,3},{3,34},{34,35},{35,2},{4,5},{5,3... | collective-permute-start | bytes 73736 | tf_op jit(solution)/shard_map/ppermute | solution.py:196
  92.0 5.2 %collective-permute-start.16 = (f32[3,2,1024]{2,1,0:T(2,128)S(1)}, f32[3,2,1024]{2,1,0:T(2,128)S(1)}, u32[]{:S(2)}, u32[]{:S(2)}) collective-permute-start(f32[3,2,1024]{2,1,0:T(2,128)S(1)} %add.106), channel_id=1, source_target_pairs={{0,32},{1,33},{32,0},{33,1},{2,34},{3,35},{34,2},{35,3},{4,36},{5,... | collective-permute-start | bytes 73736 | tf_op jit(solution)/shard_map/ppermute | solution.py:196
  95.8 2.7 %collective-permute-start.17 = (f32[3,2,1024]{2,1,0:T(2,128)S(1)}, f32[3,2,1024]{2,1,0:T(2,128)S(1)}, u32[]{:S(2)}, u32[]{:S(2)}) collective-permute-start(f32[3,2,1024]{2,1,0:T(2,128)S(1)} %add.106), channel_id=1, source_target_pairs={{0,33},{1,0},{32,1},{33,32},{2,35},{3,2},{34,3},{35,34},{4,37},{5,... | collective-permute-start | bytes 73736 | tf_op jit(solution)/shard_map/ppermute | solution.py:196
  98.5 4.0 %collective-permute-start.18 = (f32[3,2,1024]{2,1,0:T(2,128)S(1)}, f32[3,2,1024]{2,1,0:T(2,128)S(1)}, u32[]{:S(2)}, u32[]{:S(2)}) collective-permute-start(f32[3,2,1024]{2,1,0:T(2,128)S(1)} %add_add_fusion.1), channel_id=1, source_target_pairs={{0,64},{64,128},{128,192},{192,0},{1,65},{65,129},{129,193},{193,1... | collective-permute-start | bytes 73736 | tf_op jit(solution)/shard_map/ppermute | solution.py:196
  98.6 4.3 %collective-permute-start.19 = (f32[3,2,1024]{2,1,0:T(2,128)S(1)}, f32[3,2,1024]{2,1,0:T(2,128)S(1)}, u32[]{:S(2)}, u32[]{:S(2)}) collective-permute-start(f32[3,2,1024]{2,1,0:T(2,128)S(1)} %add_add_fusion.1), channel_id=1, source_target_pairs={{0,128},{64,192},{128,0},{192,64},{1,129},{65,193},{129,1},{193,65... | collective-permute-start | bytes 73736 | tf_op jit(solution)/shard_map/ppermute | solution.py:196
  99.8 3.5 %collective-permute-start.20 = (f32[3,2,1024]{2,1,0:T(2,128)S(1)}, f32[3,2,1024]{2,1,0:T(2,128)S(1)}, u32[]{:S(2)}, u32[]{:S(2)}) collective-permute-start(f32[3,2,1024]{2,1,0:T(2,128)S(1)} %add_add_fusion.1), channel_id=1, source_target_pairs={{0,192},{64,0},{128,64},{192,128},{1,193},{65,1},{129,65},{193,129... | collective-permute-start | bytes 73736 | tf_op jit(solution)/shard_map/ppermute | solution.py:196
  115.6 7.8 %collective-permute-start.21 = (bf16[16,64,384]{2,1,0:T(8,128)(2,1)S(1)}, bf16[16,64,384]{2,1,0:T(8,128)(2,1)S(1)}, u32[]{:S(2)}, u32[]{:S(2)}) collective-permute-start(bf16[16,64,384]{2,1,0:T(8,128)(2,1)S(1)} %get-tuple-element.36), channel_id=1, source_target_pairs={{0,16},{16,0},{1,17},{17,1},{2,18},{18,2},{3,19},{19,3},{4,20},{20... | collective-permute-start | bytes 2359304 | tf_op jit(solution)/shard_map/ppermute | solution.py:196
  119.1 42.8 %all-to-all-start.3 = ((bf16[8,256,384]{2,1,0:T(8,128)(2,1)}), bf16[8,256,384]{2,1,0:T(8,128)(2,1)}, u32[]{:S(2)}, u32[]{:S(2)}) async-start(bf16[8,256,384]{2,1,0:T(8,128)(2,1)} %get-tuple-element.37), calls=%async_computation.3 | async-start | bytes 3145728 | tf_op jit(solution)/shard_map/all_to_all | solution.py:189
  123.7 8.4 %collective-permute-start.22 = (bf16[4,64,384]{2,1,0:T(8,128)(2,1)S(1)}, bf16[4,64,384]{2,1,0:T(8,128)(2,1)S(1)}, u32[]{:S(2)}, u32[]{:S(2)}) collective-permute-start(bf16[4,64,384]{2,1,0:T(8,128)(2,1)S(1)} %get-tuple-element.52), channel_id=1, source_target_pairs={{0,1},{1,32},{32,33},{33,0},{2,3},{3,34},{34,35},{35,2},{4,5},{5,3... | collective-permute-start | bytes 589832 | tf_op jit(solution)/shard_map/ppermute | solution.py:196
  124.1 11.8 %collective-permute-start.23 = (bf16[4,64,384]{2,1,0:T(8,128)(2,1)S(1)}, bf16[4,64,384]{2,1,0:T(8,128)(2,1)S(1)}, u32[]{:S(2)}, u32[]{:S(2)}) collective-permute-start(bf16[4,64,384]{2,1,0:T(8,128)(2,1)S(1)} %get-tuple-element.54), channel_id=1, source_target_pairs={{0,32},{1,33},{32,0},{33,1},{2,34},{3,35},{34,2},{35,3},{4,36},{5,... | collective-permute-start | bytes 589832 | tf_op jit(solution)/shard_map/ppermute | solution.py:196
  126.4 10.0 %collective-permute-start.24 = (bf16[4,64,384]{2,1,0:T(8,128)(2,1)S(1)}, bf16[4,64,384]{2,1,0:T(8,128)(2,1)S(1)}, u32[]{:S(2)}, u32[]{:S(2)}) collective-permute-start(bf16[4,64,384]{2,1,0:T(8,128)(2,1)S(1)} %get-tuple-element.53), channel_id=1, source_target_pairs={{0,33},{1,0},{32,1},{33,32},{2,35},{3,2},{34,3},{35,34},{4,37},{5,... | collective-permute-start | bytes 589832 | tf_op jit(solution)/shard_map/ppermute | solution.py:196
  136.5 4.6 %collective-permute-start.25 = (bf16[64,384]{1,0:T(8,128)(2,1)S(1)}, bf16[64,384]{1,0:T(8,128)(2,1)S(1)}, u32[]{:S(2)}, u32[]{:S(2)}) collective-permute-start(bf16[64,384]{1,0:T(8,128)(2,1)S(1)} %get-tuple-element.61), channel_id=1, source_target_pairs={{0,64},{64,128},{128,192},{192,0},{1,65},{65,129},{129,193},{193,1... | collective-permute-start | bytes 147464 | tf_op jit(solution)/shard_map/ppermute | solution.py:196
  138.1 4.8 %collective-permute-start.26 = (bf16[64,384]{1,0:T(8,128)(2,1)S(1)}, bf16[64,384]{1,0:T(8,128)(2,1)S(1)}, u32[]{:S(2)}, u32[]{:S(2)}) collective-permute-start(bf16[64,384]{1,0:T(8,128)(2,1)S(1)} %get-tuple-element.63), channel_id=1, source_target_pairs={{0,128},{64,192},{128,0},{192,64},{1,129},{65,193},{129,1},{193,65... | collective-permute-start | bytes 147464 | tf_op jit(solution)/shard_map/ppermute | solution.py:196
  140.2 3.8 %collective-permute-start.27 = (bf16[64,384]{1,0:T(8,128)(2,1)S(1)}, bf16[64,384]{1,0:T(8,128)(2,1)S(1)}, u32[]{:S(2)}, u32[]{:S(2)}) collective-permute-start(bf16[64,384]{1,0:T(8,128)(2,1)S(1)} %get-tuple-element.62), channel_id=1, source_target_pairs={{0,192},{64,0},{128,64},{192,128},{1,193},{65,1},{129,65},{193,129... | collective-permute-start | bytes 147464 | tf_op jit(solution)/shard_map/ppermute | solution.py:196
